TPU v7x, 32 devices: a whole 2x2x4 slice. The times are simulated.
32 devices in a mesh: lon: 8 (over z, x), freq: 4 (over y, core).
Axes of the slice: x: 2, y: 2, z: 4, core: 2. Of those that a mesh axis runs over, the one named last changes fastest.
Arguments:
- spectrum: float32 [32, 36, 24, 1024], P('freq', None, None, 'lon'), may hold values from 0.03 to 1
- east_wind: float32 [24, 1024], P(None, 'lon'), may hold values from -30 to 30
- north_wind: float32 [24, 1024], P(None, 'lon'), may hold values from -30 to 30
- land_sea: int32 [24, 1024], P(None, 'lon'), may hold values from 0 to 2
- edge_rows: int32 [2, 1024], P(None, 'lon'), may hold values from 1 to 3
Outputs:
- energy: float32 [32, 36, 24, 1024], P('freq', None, None, 'lon')
- mean_slope: float32 [24, 1024], P(None, 'lon')
All inputs are finite; a program needn't handle non-finite values.
Results may differ from a plain program's by a relative error of at most 0.0001.
Values sent between devices are 32-bit elements; how exact they have to be, the bound alone decides.
No kernel may reach another device: no remote copies, remote signals or barrier semaphores. Data moves between devices by JAX's collectives and lax.ppermute only.
A program may use at most 128 MiB of HBM per device.

v0:
```python
import math

import jax
import jax.numpy as jnp
from jax import lax
from jax.sharding import PartitionSpec as P

NF = 32
STEPS = 2


COURANT_MAX = 0.9
FREQ_RATIO = 1.1
WIND_REF = 8.0
WIND_CLIP = 2.0
GROWTH = 0.01
BREAKING = 0.3
SATURATION_REF = 0.4
CUMULATIVE = 2.0
SWELL_DAMP = 0.1
ICE_DAMP = 0.5


def carried_in(value, axis, join, neutral):
    count, mine = (lax.axis_size(axis), lax.axis_index(axis))
    pieces = lax.all_gather(value, axis)
    total = jnp.full_like(value, 0) + jnp.asarray(neutral, value.dtype)

    def turn(position, total):
        longer = join(total, pieces[position])
        return jnp.where(position < mine, longer, total)

    return lax.fori_loop(0, count - 1, turn, total)


def with_halo(cells, sides, width):
    for axis, dim in sides:
        count = lax.axis_size(axis)
        head = lax.slice_in_dim(cells, 0, width, axis=dim)
        tail = lax.slice_in_dim(cells, cells.shape[dim] - width, cells.shape[dim], axis=dim)
        cells = jnp.concatenate(
            [
                lax.ppermute(tail, axis, [(i, (i + 1) % count) for i in range(count)]),
                cells,
                lax.ppermute(head, axis, [((i + 1) % count, i) for i in range(count)]),
            ],
            axis=dim,
        )
    return cells


def beam_warming(padded, courant, along_axis):
    length = padded.shape[along_axis] - 4

    def cut_at(offset):
        return lax.slice_in_dim(padded, 2 + offset, 2 + offset + length, axis=along_axis)

    centre = cut_at(0)
    back_one = cut_at(-1)
    back_two = cut_at(-2)
    ahead_one = cut_at(1)
    ahead_two = cut_at(2)
    forward = jnp.maximum(courant, 0.0)
    backward = jnp.maximum(-courant, 0.0)
    return (
        centre
        - 0.5 * forward * (3.0 * centre - 4.0 * back_one + back_two)
        + 0.5 * forward * forward * (centre - 2.0 * back_one + back_two)
        - 0.5 * backward * (3.0 * centre - 4.0 * ahead_one + ahead_two)
        + 0.5 * backward * backward * (centre - 2.0 * ahead_one + ahead_two)
    )


def add_parts(earlier, later):
    return earlier + later


def per_device(spectrum, east_wind, north_wind, land_sea, edge_rows):
    bands, count, lat_rows, width = spectrum.shape
    band_order = (lax.axis_index("freq") * bands + jnp.arange(bands)).astype(jnp.float32)
    ratios = jnp.power(FREQ_RATIO, band_order)
    root_ratio = jnp.sqrt(ratios)
    all_ratios = jnp.power(FREQ_RATIO, jnp.arange(NF).astype(jnp.float32))
    norm_stress = jnp.sum(all_ratios * jnp.sqrt(all_ratios))
    norm_slope = jnp.sum(all_ratios * all_ratios)
    step_angle = 2.0 * math.pi / count
    angles = jnp.arange(count).astype(jnp.float32) * step_angle
    cosines = jnp.cos(angles)
    sines = jnp.sin(angles)
    differ = jnp.cos(angles[:, None] - angles[None, :])
    kernel = jnp.where(differ > 0.0, differ * differ, 0.0) * step_angle
    courant_lon = (COURANT_MAX * cosines[None, :] / ratios[:, None])[:, :, None, None]
    courant_lat = (0.5 * COURANT_MAX * sines[None, :] / ratios[:, None])[:, :, None, None]
    sea_mask = (land_sea != 0).astype(jnp.float32)
    ice_mask = (land_sea == 2).astype(jnp.float32)
    row_index = jnp.arange(lat_rows)[:, None]
    held_mask = (
        (row_index < edge_rows[0][None, :]) | (row_index >= lat_rows - edge_rows[1][None, :])
    ).astype(jnp.float32)
    fields = jnp.stack([east_wind, north_wind, sea_mask, ice_mask, held_mask])
    band_weight = root_ratio[:, None, None, None]
    energy = spectrum
    mean_slope = jnp.zeros((lat_rows, width), jnp.float32)
    for step_index in range(STEPS):
        padded = with_halo(energy, (("lon", 3),), 2)
        shifted = beam_warming(padded, courant_lon, 3)
        shifted = jnp.pad(shifted, ((0, 0), (0, 0), (2, 2), (0, 0)), mode="edge")
        shifted = beam_warming(shifted, courant_lat, 2)
        shifted = (
            jnp.where(fields[4][None, None] > 0.5, spectrum, jnp.maximum(shifted, 0.0))
            * fields[2][None, None]
        )
        wind_along = (
            cosines[:, None, None] * fields[0][None] + sines[:, None, None] * fields[1][None]
        )
        wind_drive = (
            jnp.minimum(jnp.maximum(wind_along, 0.0) / WIND_REF, WIND_CLIP) ** 2
            * (1.0 - fields[3])[None]
        )
        slope_part = jnp.sum(shifted * (ratios * ratios)[:, None, None, None], axis=(0, 1)) * (
            step_angle / norm_slope
        )
        stress_part = jnp.sum(
            shifted * wind_drive[None] * (ratios * root_ratio)[:, None, None, None], axis=(0, 1)
        ) * (step_angle / norm_stress)
        saturation = jnp.einsum("ij,kjlw->kilw", kernel, shifted, precision=lax.Precision.HIGHEST)
        excess = jnp.maximum(jnp.sqrt(saturation) - math.sqrt(SATURATION_REF), 0.0) ** 2
        band_total = jnp.sum(excess, 0)
        forcing_mean_slope, stress = lax.psum((slope_part, stress_part), "freq")
        prefix_sum = carried_in(band_total, "freq", add_parts, jnp.zeros_like(band_total))
        stress_gain = 1.0 + stress / (stress + 1.0)
        lower_sum = prefix_sum[None] + jnp.cumsum(excess, 0) - excess
        net_rate = (
            GROWTH * band_weight * wind_drive[None] * stress_gain[None, None]
            - BREAKING * band_weight * excess / SATURATION_REF
            - CUMULATIVE * band_weight * lower_sum / NF
            - SWELL_DAMP
            * band_weight
            * (forcing_mean_slope / (forcing_mean_slope + 1.0))[None, None]
            - ICE_DAMP * band_weight * fields[3][None, None]
        )
        energy = shifted * jnp.exp(net_rate)
        mean_slope = forcing_mean_slope
    return (energy, mean_slope)


def solution(mesh):
    in_specs = (
        P("freq", None, None, "lon"),
        P(None, "lon"),
        P(None, "lon"),
        P(None, "lon"),
        P(None, "lon"),
    )
    out_specs = (P("freq", None, None, "lon"), P(None, "lon"))
    return jax.shard_map(
        per_device, mesh=mesh, in_specs=in_specs, out_specs=out_specs, check_vma=False
    )
```

profile of v0, /device:TPU:0, one launch (start us, length us, event | category | flops | bytes accessed | tf_op | source)
XLA Modules:
  0.0 213.8 jit_solution(9349768869381515878)
XLA Ops:
  7.2 7.0 %fusion.63 = (f32[8,36,24,2]{3,2,1,0:T(8,128)}, f32[8,36,24,2]{3,2,1,0:T(8,128)}) fusion(f32[8,36,24,128]{3,2,1,0:T(8,128)} %param.9), kind=kLoop, calls=%fused_computation.146 | loop fusion | bytes 221184 | tf_op jit(solution)/shard_map/slice | solution.py:40
  14.2 3.8 %copy.42 = f32[8,36,24,2]{1,2,3,0:T(8,128)} copy(f32[8,36,24,2]{3,2,1,0:T(8,128)} %get-tuple-element.228) | data formatting | bytes 110592
  18.0 2.9 %collective-permute-start = (f32[8,36,24,2]{1,2,3,0:T(8,128)}, f32[8,36,24,2]{1,2,3,0:T(8,128)}, u32[]{:S(2)}, u32[]{:S(2)}) collective-permute-start(f32[8,36,24,2]{1,2,3,0:T(8,128)} %copy.42), channel_id=1, source_target_pairs={{0,4},{4,8},{8,12},{12,16},{16,20},{20,24},{24,28},{28,0},{1,5},{5... | collective-permute-start | bytes 165896 | tf_op jit(solution)/shard_map/ppermute | solution.py:43
  21.0 3.7 %copy.43 = f32[8,36,24,2]{1,2,3,0:T(8,128)} copy(f32[8,36,24,2]{3,2,1,0:T(8,128)} %get-tuple-element.229) | data formatting | bytes 110592
  24.6 3.0 %collective-permute-start.1 = (f32[8,36,24,2]{1,2,3,0:T(8,128)}, f32[8,36,24,2]{1,2,3,0:T(8,128)}, u32[]{:S(2)}, u32[]{:S(2)}) collective-permute-start(f32[8,36,24,2]{1,2,3,0:T(8,128)} %copy.43), channel_id=1, source_target_pairs={{4,0},{8,4},{12,8},{16,12},{20,16},{24,20},{28,24},{0,28},{5,1},{9... | collective-permute-start | bytes 165896 | tf_op jit(solution)/shard_map/ppermute | solution.py:45
  31.6 1.7 multiply_multiply_fusion.2
  33.9 2.5 %copy.37 = f32[8,36,24,128]{3,1,2,0:T(8,128)} copy(f32[8,36,24,128]{3,2,1,0:T(8,128)S(1)} %copy-done) | data formatting | bytes 7077888 | tf_op args[0]
  36.4 3.8 %copy.22 = f32[8,36,24,2]{3,1,2,0:T(8,128)} copy(f32[8,36,24,2]{1,2,3,0:T(8,128)} %collective-permute-done) | data formatting | bytes 110592 | tf_op jit(solution)/shard_map/ppermute | solution.py:43
  40.2 3.7 %copy.28 = f32[8,36,24,2]{3,1,2,0:T(8,128)} copy(f32[8,36,24,2]{1,2,3,0:T(8,128)} %collective-permute-done.1) | data formatting | bytes 110592 | tf_op jit(solution)/shard_map/ppermute | solution.py:45
  44.0 19.2 %multiply_add_fusion.1 = f32[8,36,24,128]{3,1,2,0:T(8,128)S(1)} fusion(f32[8,36,24,128]{3,1,2,0:T(8,128)} %copy.37, f32[8,36,24,2]{3,1,2,0:T(8,128)} %copy.28, f32[8,36,24,2]{3,1,2,0:T(8,128)} %copy.22, f32[8,36]{1,0:T(8,128)} %get-tuple-element.244, f32[8,36]{1,0:T(8,128)} %get-tuple-element.242, f32[8,36]{1,0:T(8,128)} %get-tuple-element.243, ...), kind=kLoop, calls=%fused_computation.73 | loop fusion | flops 22118400 | bytes 7193088 | tf_op jit(solution)/shard_map/add | solution.py:66
  63.3 5.2 %multiply_reduce_fusion.3 = (f32[24,128]{1,0:T(8,128)}, f32[24,128]{1,0:T(8,128)}, f32[8,36,24,128]{3,1,2,0:T(8,128)S(1)}) fusion(f32[8]{0:T(128)S(1)} %copy-done.25, f32[36,24,128]{2,0,1:T(8,128)S(1)} %copy-done.4, f32[8]{0:T(128)S(1)} %copy-done.27, f32[24,128]{1,0:T(8,128)S(1)} %get-tuple-element.231, f32[8,36,24,128]{3,1,2,0:T(8,128)S(1)} %multiply_add_fusion.1, ...), kind=kLoop, calls=%fused_computation.71 | loop fusion | flops 29190144 | bytes 11693632 | tf_op jit(solution)/shard_map/reduce_sum | solution.py:123
  68.6 7.3 %bitcast_reduce_fusion.1 = (f32[36,24,128]{2,0,1:T(8,128)S(1)}, f32[8,24,128,36]{2,3,1,0:T(8,128)}) fusion(f32[8,36,24,128]{3,1,2,0:T(8,128)S(1)} %get-tuple-element.221, f32[36]{0:T(128)S(1)} %copy-done.20), kind=kOutput, calls=%fused_computation.59 | convolution fusion | flops 385640768 | bytes 7520400 | tf_op jit(solution)/shard_map/ij,kjlw->kilw/dot_general | solution.py:126
  85.2 12.7 %all-reduce.1 = (f32[24,128]{1,0:T(8,128)}, f32[24,128]{1,0:T(8,128)}) all-reduce(f32[24,128]{1,0:T(8,128)} %broadcast_multiply_fusion.4, f32[24,128]{1,0:T(8,128)} %broadcast_multiply_fusion.6), channel_id=1, replica_groups=mesh['lon'=8,'freq'=4] {'freq'}, use_global_device_ids=true, to_apply=%region_9.10 | all-reduce | flops 6144 | bytes 49152 | tf_op jit(solution)/shard_map/psum | solution.py:129
  101.3 5.7 %while.28 = (s32[]{:T(128)}, f32[36,24,128]{2,1,0:T(8,128)}, s32[]{:T(128)}, f32[4,36,24,128]{3,2,1,0:T(8,128)}, s32[]{:T(128)}, /*index=5*/s32[]{:T(128)}) while((s32[]{:T(128)}, f32[36,24,128]{2,1,0:T(8,128)}, s32[]{:T(128)}, f32[4,36,24,128]{3,2,1,0:T(8,128)}, s32[]{:T(128)}, /*index=5*/s32[]{:T(128)}) %tuple.103), condition=%wide.region_5.6_spmd.clone, body=%wide.region_4.5_spmd.clone.sunk | while | flops 331780 | bytes 1327197 | solution.py:33
  101.3 1.8 add_select_fusion.4
  103.1 2.0 add_select_fusion.4
  105.1 2.0 add_select_fusion.4
  108.1 6.9 %fusion.9 = f32[8,36,24,128]{3,1,2,0:T(8,128)S(1)} fusion(f32[8,36,24,128]{3,1,2,0:T(8,128)} %copy-done.2, f32[8,24,128,36]{2,3,1,0:T(8,128)} %get-tuple-element.247, f32[8,24,128]{2,1,0:T(8,128)} %broadcast_multiply_fusion.1, f32[8,24,128]{2,1,0:T(8,128)} %broadcast_multiply_fusion.2, f32[36,24,128]{2,0,1:T(8,128)S(1)} %copy.32, f32[8]{0:T(128)} %get-tuple-element.252, ...), kind=kOutput, calls=%fused_computation.29 | output fusion | flops 17694720 | bytes 11710560 | tf_op jit(solution)/shard_map/jit(cumsum)/reduce_window_sum | solution.py:132
  115.0 4.4 %fusion.62 = (f32[8,36,24,2]{3,1,2,0:T(8,128)}, f32[8,36,24,2]{3,1,2,0:T(8,128)}) fusion(f32[8,36,24,128]{3,1,2,0:T(8,128)S(1)} %fusion.9), kind=kLoop, calls=%fused_computation.145 | loop fusion | bytes 221184 | tf_op jit(solution)/shard_map/slice | solution.py:40
  119.4 3.7 %copy.33 = f32[8,36,24,2]{1,2,3,0:T(8,128)} copy(f32[8,36,24,2]{3,1,2,0:T(8,128)} %get-tuple-element.224) | data formatting | bytes 110592 | tf_op jit(solution)/shard_map/slice | solution.py:40
  123.1 3.7 %copy.35 = f32[8,36,24,2]{1,2,3,0:T(8,128)} copy(f32[8,36,24,2]{3,1,2,0:T(8,128)} %get-tuple-element.225) | data formatting | bytes 110592 | tf_op jit(solution)/shard_map/slice | solution.py:39
  126.9 4.7 %collective-permute-start.3 = (f32[8,36,24,2]{1,2,3,0:T(8,128)}, f32[8,36,24,2]{1,2,3,0:T(8,128)}, u32[]{:S(2)}, u32[]{:S(2)}) collective-permute-start(f32[8,36,24,2]{1,2,3,0:T(8,128)} %copy.35), channel_id=1, source_target_pairs={{4,0},{8,4},{12,8},{16,12},{20,16},{24,20},{28,24},{0,28},{5,1},{9... | collective-permute-start | bytes 165896 | tf_op jit(solution)/shard_map/ppermute | solution.py:45
  132.7 3.8 %copy.34 = f32[8,36,24,2]{3,1,2,0:T(8,128)} copy(f32[8,36,24,2]{1,2,3,0:T(8,128)} %collective-permute-done.2) | data formatting | bytes 110592 | tf_op jit(solution)/shard_map/ppermute | solution.py:43
  136.9 3.7 %copy.36 = f32[8,36,24,2]{3,1,2,0:T(8,128)} copy(f32[8,36,24,2]{1,2,3,0:T(8,128)} %collective-permute-done.3) | data formatting | bytes 110592 | tf_op jit(solution)/shard_map/ppermute | solution.py:45
  140.6 19.2 %multiply_add_fusion = f32[8,36,24,128]{3,1,2,0:T(8,128)S(1)} fusion(f32[8,36,24,128]{3,1,2,0:T(8,128)} %copy-done.1, f32[8,36,24,2]{3,1,2,0:T(8,128)} %copy.36, f32[8,36,24,2]{3,1,2,0:T(8,128)} %copy.34, f32[8,36]{1,0:T(8,128)} %get-tuple-element.244, f32[8,36]{1,0:T(8,128)} %get-tuple-element.242, f32[8,36]{1,0:T(8,128)} %get-tuple-element.243, ...), kind=kLoop, calls=%fused_computation.68 | loop fusion | flops 22118400 | bytes 7193088 | tf_op jit(solution)/shard_map/add | solution.py:66
  160.0 5.2 %multiply_reduce_fusion.1 = (f32[24,128]{1,0:T(8,128)}, f32[24,128]{1,0:T(8,128)}, f32[8,36,24,128]{3,1,2,0:T(8,128)S(1)}) fusion(f32[8]{0:T(128)S(1)} %copy-done.26, f32[36,24,128]{2,0,1:T(8,128)S(1)} %copy-done.5, f32[8]{0:T(128)S(1)} %copy-done.28, f32[24,128]{1,0:T(8,128)S(1)} %get-tuple-element.231, f32[8,36,24,128]{3,1,2,0:T(8,128)S(1)} %multiply_add_fusion, ...), kind=kLoop, calls=%fused_computation.66 | loop fusion | flops 29190144 | bytes 11693632 | tf_op jit(solution)/shard_map/reduce_sum | solution.py:123
  165.3 7.3 %bitcast_reduce_fusion = (f32[36,24,128]{2,0,1:T(8,128)S(1)}, f32[8,24,128,36]{2,3,1,0:T(8,128)}) fusion(f32[8,36,24,128]{3,1,2,0:T(8,128)S(1)} %get-tuple-element.220, f32[36]{0:T(128)S(1)} %copy-done.21), kind=kOutput, calls=%fused_computation.51 | convolution fusion | flops 385640768 | bytes 7520400 | tf_op jit(solution)/shard_map/ij,kjlw->kilw/dot_general | solution.py:126
  173.4 10.6 %all-reduce = (f32[24,128]{1,0:T(8,128)S(1)}, f32[24,128]{1,0:T(8,128)S(1)}) all-reduce(f32[24,128]{1,0:T(8,128)S(1)} %broadcast_multiply_fusion.3, f32[24,128]{1,0:T(8,128)S(1)} %broadcast_multiply_fusion.5), channel_id=1, replica_groups=mesh['lon'=8,'freq'=4] {'freq'}, use_global_device_ids=true, to_apply=%region_17.18 | all-reduce | flops 6144 | bytes 49152 | tf_op jit(solution)/shard_map/psum | solution.py:129
  184.2 10.1 %all-gather.7.cloned.1.call-done = f32[144,24,128]{2,1,0:T(8,128)} async-done(((f32[36,24,128]{2,1,0:T(8,128)}), f32[144,24,128]{2,1,0:T(8,128)}) %all-gather.7.cloned.1.call-update) | async-done | bytes 1769488 | tf_op jit(solution)/shard_map/all_gather | solution.py:26
  194.3 3.4 %while.29 = (s32[]{:T(128)}, f32[36,24,128]{2,1,0:T(8,128)S(1)}, s32[]{:T(128)}, f32[4,36,24,128]{3,2,1,0:T(8,128)}, s32[]{:T(128)}, /*index=5*/s32[]{:T(128)}) while((s32[]{:T(128)}, f32[36,24,128]{2,1,0:T(8,128)S(1)}, s32[]{:T(128)}, f32[4,36,24,128]{3,2,1,0:T(8,128)}, s32[]{:T(128)}, /*index=5*/s32[]{:T(128)}) %tuple.104), condition=%wide.region_14.15_spmd.clone, body=%wide.region_13.14_spmd.clone.sunk | while | flops 331780 | bytes 1327197 | solution.py:33
  197.9 6.6 %fusion.15 = f32[8,36,24,128]{3,1,2,0:T(8,128)S(1)} fusion(f32[8,36,24,128]{3,1,2,0:T(8,128)} %copy-done.3, f32[8,24,128,36]{2,3,1,0:T(8,128)} %get-tuple-element.249, f32[8,24,128]{2,1,0:T(8,128)S(1)} %broadcast_multiply_fusion, f32[36,24,128]{2,0,1:T(8,128)S(1)} %copy.39, f32[24,128]{1,0:T(8,128)S(1)} %fusion.40, f32[8,24,128]{2,1,0:T(8,128)S(1)} %copy-done.7, ...), kind=kOutput, calls=%fused_computation.35 | output fusion | flops 17694720 | bytes 11710560 | tf_op jit(solution)/shard_map/jit(cumsum)/reduce_window_sum | solution.py:132
  204.6 2.4 %copy.40 = f32[8,36,24,128]{3,2,1,0:T(8,128)} copy(f32[8,36,24,128]{3,1,2,0:T(8,128)S(1)} %fusion.15) | data formatting | bytes 7077888
  (112 shorter events, 23.2 us)
Async XLA Ops:
  7.2 94.1 %all-gather.5.cloned.1.call-start = ((), (), s32[]{:S(2)}) async-start(), calls=%async_computation | async-start | bytes 2211840 | tf_op jit(solution)/shard_map/all_gather | solution.py:26
  14.2 14.7 %copy-start.8 = (s32[24,128]{1,0:T(8,128)S(1)}, s32[24,128]{1,0:T(8,128)}, u32[]{:S(2)}) copy-start(s32[24,128]{1,0:T(8,128)} %param.12) | copy-start | bytes 36868
  14.2 14.7 %copy-start.30 = (s32[2,128]{1,0:T(2,128)S(1)}, s32[2,128]{1,0:T(2,128)}, u32[]{:S(2)}) copy-start(s32[2,128]{1,0:T(2,128)} %param.13) | copy-start | bytes 3076
  14.2 19.7 %copy-start = (f32[8,36,24,128]{3,2,1,0:T(8,128)S(1)}, f32[8,36,24,128]{3,2,1,0:T(8,128)}, u32[]{:S(2)}) copy-start(f32[8,36,24,128]{3,2,1,0:T(8,128)} %param.9) | copy-start | bytes 10616836
  18.0 18.4 %collective-permute-start = (f32[8,36,24,2]{1,2,3,0:T(8,128)}, f32[8,36,24,2]{1,2,3,0:T(8,128)}, u32[]{:S(2)}, u32[]{:S(2)}) collective-permute-start(f32[8,36,24,2]{1,2,3,0:T(8,128)} %copy.42), channel_id=1, source_target_pairs={{0,4},{4,8},{8,12},{12,16},{16,20},{20,24},{24,28},{28,0},{1,5},{5... | collective-permute-start | bytes 165896 | tf_op jit(solution)/shard_map/ppermute | solution.py:43
  24.6 15.6 %collective-permute-start.1 = (f32[8,36,24,2]{1,2,3,0:T(8,128)}, f32[8,36,24,2]{1,2,3,0:T(8,128)}, u32[]{:S(2)}, u32[]{:S(2)}) collective-permute-start(f32[8,36,24,2]{1,2,3,0:T(8,128)} %copy.43), channel_id=1, source_target_pairs={{4,0},{8,4},{12,8},{16,12},{20,16},{24,20},{28,24},{0,28},{5,1},{9... | collective-permute-start | bytes 165896 | tf_op jit(solution)/shard_map/ppermute | solution.py:45
  43.9 19.3 %copy-start.4 = (f32[36,24,128]{2,0,1:T(8,128)S(1)}, f32[36,24,128]{2,0,1:T(8,128)}, u32[]{:S(2)}) copy-start(f32[36,24,128]{2,0,1:T(8,128)} %multiply_multiply_fusion.2) | copy-start | bytes 1327108
  43.9 19.3 %copy-start.11 = (f32[8,36]{1,0:T(8,128)S(1)}, f32[8,36]{1,0:T(8,128)}, u32[]{:S(2)}) copy-start(f32[8,36]{1,0:T(8,128)} %get-tuple-element.235) | copy-start | bytes 3460
  43.9 19.3 %copy-start.13 = (f32[8,36]{1,0:T(8,128)S(1)}, f32[8,36]{1,0:T(8,128)}, u32[]{:S(2)}) copy-start(f32[8,36]{1,0:T(8,128)} %get-tuple-element.236) | copy-start | bytes 3460
  43.9 19.3 %copy-start.15 = (f32[8,36]{1,0:T(8,128)S(1)}, f32[8,36]{1,0:T(8,128)}, u32[]{:S(2)}) copy-start(f32[8,36]{1,0:T(8,128)} %get-tuple-element.237) | copy-start | bytes 3460
  44.0 19.3 %copy-start.17 = (pred[24,128]{1,0:T(8,128)(4,1)S(1)}, pred[24,128]{1,0:T(8,128)(4,1)}, u32[]{:S(2)}) copy-start(pred[24,128]{1,0:T(8,128)(4,1)} %get-tuple-element.260) | copy-start | bytes 9220
  44.0 19.3 %copy-start.25 = (f32[8]{0:T(128)S(1)}, f32[8]{0:T(128)}, u32[]{:S(2)}) copy-start(f32[8]{0:T(128)} %get-tuple-element.254) | copy-start | bytes 100
  44.0 19.3 %copy-start.27 = (f32[8]{0:T(128)S(1)}, f32[8]{0:T(128)}, u32[]{:S(2)}) copy-start(f32[8]{0:T(128)} %get-tuple-element.255) | copy-start | bytes 100
  76.7 117.6 %all-gather.7.cloned.1.call-start = ((), (), s32[]{:S(2)}) async-start(), calls=%async_computation.1 | async-start | bytes 2211840 | tf_op jit(solution)/shard_map/all_gather | solution.py:26
  123.1 9.6 %collective-permute-start.2 = (f32[8,36,24,2]{1,2,3,0:T(8,128)}, f32[8,36,24,2]{1,2,3,0:T(8,128)}, u32[]{:S(2)}, u32[]{:S(2)}) collective-permute-start(f32[8,36,24,2]{1,2,3,0:T(8,128)} %copy.33), channel_id=1, source_target_pairs={{0,4},{4,8},{8,12},{12,16},{16,20},{20,24},{24,28},{28,0},{1,5},{5... | collective-permute-start | bytes 165896 | tf_op jit(solution)/shard_map/ppermute | solution.py:43
  126.9 10.0 %collective-permute-start.3 = (f32[8,36,24,2]{1,2,3,0:T(8,128)}, f32[8,36,24,2]{1,2,3,0:T(8,128)}, u32[]{:S(2)}, u32[]{:S(2)}) collective-permute-start(f32[8,36,24,2]{1,2,3,0:T(8,128)} %copy.35), channel_id=1, source_target_pairs={{4,0},{8,4},{12,8},{16,12},{20,16},{24,20},{28,24},{0,28},{5,1},{9... | collective-permute-start | bytes 165896 | tf_op jit(solution)/shard_map/ppermute | solution.py:45
  140.6 19.3 %copy-start.5 = (f32[36,24,128]{2,0,1:T(8,128)S(1)}, f32[36,24,128]{2,0,1:T(8,128)}, u32[]{:S(2)}) copy-start(f32[36,24,128]{2,0,1:T(8,128)} %multiply_multiply_fusion.2) | copy-start | bytes 1327108
  140.6 19.3 %copy-start.12 = (f32[8,36]{1,0:T(8,128)S(1)}, f32[8,36]{1,0:T(8,128)}, u32[]{:S(2)}) copy-start(f32[8,36]{1,0:T(8,128)} %get-tuple-element.235) | copy-start | bytes 3460
  140.6 19.3 %copy-start.14 = (f32[8,36]{1,0:T(8,128)S(1)}, f32[8,36]{1,0:T(8,128)}, u32[]{:S(2)}) copy-start(f32[8,36]{1,0:T(8,128)} %get-tuple-element.236) | copy-start | bytes 3460
  140.6 19.3 %copy-start.16 = (f32[8,36]{1,0:T(8,128)S(1)}, f32[8,36]{1,0:T(8,128)}, u32[]{:S(2)}) copy-start(f32[8,36]{1,0:T(8,128)} %get-tuple-element.237) | copy-start | bytes 3460
  140.6 19.3 %copy-start.18 = (pred[24,128]{1,0:T(8,128)(4,1)S(1)}, pred[24,128]{1,0:T(8,128)(4,1)}, u32[]{:S(2)}) copy-start(pred[24,128]{1,0:T(8,128)(4,1)} %get-tuple-element.260) | copy-start | bytes 9220
  140.6 19.3 %copy-start.26 = (f32[8]{0:T(128)S(1)}, f32[8]{0:T(128)}, u32[]{:S(2)}) copy-start(f32[8]{0:T(128)} %get-tuple-element.254) | copy-start | bytes 100
  140.6 19.3 %copy-start.28 = (f32[8]{0:T(128)S(1)}, f32[8]{0:T(128)}, u32[]{:S(2)}) copy-start(f32[8]{0:T(128)} %get-tuple-element.255) | copy-start | bytes 100
  165.2 8.2 %copy-start.10 = (f32[24,128]{1,0:T(8,128)S(1)}, f32[24,128]{1,0:T(8,128)}, u32[]{:S(2)}) copy-start(f32[24,128]{1,0:T(8,128)} %get-tuple-element.197) | copy-start | bytes 36868
  165.2 8.2 %copy-start.9 = (f32[24,128]{1,0:T(8,128)S(1)}, f32[24,128]{1,0:T(8,128)}, u32[]{:S(2)}) copy-start(f32[24,128]{1,0:T(8,128)} %get-tuple-element.196) | copy-start | bytes 36868
  165.2 18.9 %copy-start.29 = (f32[8]{0:T(128)S(1)}, f32[8]{0:T(128)}, u32[]{:S(2)}) copy-start(f32[8]{0:T(128)} %get-tuple-element.251) | copy-start | bytes 100
  184.1 13.8 %copy-start.19 = (f32[24,128]{1,0:T(8,128)}, f32[24,128]{1,0:T(8,128)S(1)}, u32[]{:S(2)}) copy-start(f32[24,128]{1,0:T(8,128)S(1)} %get-tuple-element.216) | copy-start | bytes 36868
  184.1 13.8 %copy-start.6 = (f32[36,24,128]{2,0,1:T(8,128)S(1)}, f32[36,24,128]{2,0,1:T(8,128)}, u32[]{:S(2)}) copy-start(f32[36,24,128]{2,0,1:T(8,128)} %multiply_multiply_fusion.2) | copy-start | bytes 1327108
  184.1 13.8 %copy-start.7 = (f32[8,24,128]{2,1,0:T(8,128)S(1)}, f32[8,24,128]{2,1,0:T(8,128)}, u32[]{:S(2)}) copy-start(f32[8,24,128]{2,1,0:T(8,128)} %broadcast_multiply_fusion.1) | copy-start | bytes 294916
  184.1 13.8 %copy-start.22 = (f32[8]{0:T(128)S(1)}, f32[8]{0:T(128)}, u32[]{:S(2)}) copy-start(f32[8]{0:T(128)} %broadcast_multiply_fusion.11) | copy-start | bytes 100
  184.1 13.8 %copy-start.23 = (f32[8]{0:T(128)S(1)}, f32[8]{0:T(128)}, u32[]{:S(2)}) copy-start(f32[8]{0:T(128)} %get-tuple-element.252) | copy-start | bytes 100
  184.1 13.8 %copy-start.24 = (f32[8]{0:T(128)S(1)}, f32[8]{0:T(128)}, u32[]{:S(2)}) copy-start(f32[8]{0:T(128)} %get-tuple-element.253) | copy-start | bytes 100
  (5 other events, 29.5 us)
Sparse Core Ops, SparseCore 0:
  76.9 19.8 all-gather.4
  173.5 20.7 all-gather.6
where the time goes:
time: 215 us; the launch traced here: 214 us
  other arithmetic  88.1 us (41%)
  local copies, waits for them, and re-layouts  49.5 us (23%)
  blocking collectives  23.3 us (11%)
  between operations  15.9 us (7%)
  matrix products  14.5 us (7%)
  waiting for transfers between devices  11.6 us (5%)
  starting transfers between devices  10.8 us (5%)
    add x2, other arithmetic, beam_warming(): centre - 0.5 * forward * (3.0 * centre - 4.0 * back_one + back_two)  38.3 us
    psum x2, blocking collectives, per_device(): forcing_mean_slope, stress = lax.psum((slope_part, stress_part), 'freq')  23.3 us
    slice x3, local copies, waits for them, and re-layouts, with_halo(): lax.slice_in_dim(cells, cells.shape[dim] - width, cells.shape[dim], axis=...  15.1 us
    dot_general x2, matrix products, per_device(): jnp.einsum('ij,kjlw->kilw', kernel, shifted, precision=lax.Precision.HIGH...  14.5 us
    another operation x2, other arithmetic, per_device(): lower_sum = prefix_sum[None] + jnp.cumsum(excess, 0) - excess  13.5 us
    unnamed x66, local copies, waits for them, and re-layouts  12.5 us
    reduce_sum x2, other arithmetic, per_device(): jnp.sum(shifted * wind_drive[None] * (ratios * root_ratio)[:, None, None,...  10.5 us
    all_gather x2, waiting for transfers between devices, carried_in(): pieces = lax.all_gather(value, axis)  10.1 us
  transfers between devices with their start and end apart: 6, of which 3 were waited for; matrix products, arithmetic and copies ran while one was open for 16% of the time, Pallas kernels for 0%

commit v1 on v0

v1 whole, which is shorter than its diff:
```python
import functools
import math

import jax
import jax.numpy as jnp
import numpy as np
from jax import lax
from jax.experimental import pallas as pl
from jax.experimental.pallas import tpu as pltpu
from jax.sharding import PartitionSpec as P

NF = 32
STEPS = 2

COURANT_MAX = 0.9
FREQ_RATIO = 1.1
WIND_REF = 8.0
WIND_CLIP = 2.0
GROWTH = 0.01
BREAKING = 0.3
SATURATION_REF = 0.4
CUMULATIVE = 2.0
SWELL_DAMP = 0.1
ICE_DAMP = 0.5

ND = 36
HALF = ND // 2
QUARTER = ND // 4
DTHETA = 2.0 * math.pi / ND
LOG2E = 1.0 / math.log(2.0)
ROOT_REF = math.sqrt(SATURATION_REF)
TILES = 3
LAT = 8 * TILES
WIDTH = 128
STRIDE = 6 * ND + 8

ANGLES = np.arange(ND) * DTHETA
COS = np.cos(ANGLES)
SIN = np.sin(ANGLES)
COS2 = np.cos(2.0 * ANGLES)
SIN2 = np.sin(2.0 * ANGLES)
BACK_LON = [bool(c >= 0.0) for c in COS]
BACK_LAT = [bool(s >= 0.0) for s in SIN]
RANK = [sum(BACK_LON[:j]) if BACK_LON[j] else j - sum(BACK_LON[:j]) for j in range(ND)]


def one_sided(courant):
    c = np.abs(courant)
    return 1.0 - 1.5 * c + 0.5 * c * c, 2.0 * c - c * c, 0.5 * c * c - 0.5 * c


def make_tables():
    ratios = FREQ_RATIO ** np.arange(NF)
    root = np.sqrt(ratios)
    lon = one_sided(COURANT_MAX * COS[None, :] / ratios[:, None])
    lat = one_sided(0.5 * COURANT_MAX * SIN[None, :] / ratios[:, None])
    scalars = np.zeros((NF, STRIDE))
    for i in range(3):
        scalars[:, i : 6 * ND : 6] = lon[i]
        scalars[:, 3 + i : 6 * ND : 6] = lat[i]
    extra = 6 * ND
    scalars[:, extra + 0] = -BREAKING / SATURATION_REF * root * LOG2E
    scalars[:, extra + 1] = -CUMULATIVE / NF * root * LOG2E
    scalars[:, extra + 2] = ratios * ratios * DTHETA / np.sum(ratios * ratios)
    scalars[:, extra + 3] = ratios * root * DTHETA / np.sum(ratios * root)
    scalars[:, extra + 4] = root * LOG2E
    edge = np.zeros((NF, 4, WIDTH))
    for j in range(ND):
        for r in range(TILES):
            lane = 2 * (TILES * RANK[j] + r)
            if BACK_LON[j]:
                edge[:, 0, lane] = edge[:, 0, lane + 1] = lon[2][:, j]
                edge[:, 1, lane] = lon[1][:, j]
            else:
                edge[:, 2, lane] = edge[:, 2, lane + 1] = lon[2][:, j]
                edge[:, 3, lane + 1] = lon[1][:, j]
    return scalars.reshape(-1).astype(np.float32), edge.astype(np.float32)


SCALARS, EDGE = make_tables()


def lanes():
    return lax.broadcasted_iota(jnp.int32, (8, WIDTH), 1)


def pack_edges(tile_of, right_ref, left_ref):
    pair = lanes() // 2
    for back, out in ((True, right_ref), (False, left_ref)):
        acc = jnp.zeros((8, WIDTH), jnp.float32)
        for j in range(ND):
            if BACK_LON[j] != back:
                continue
            for r in range(TILES):
                place = TILES * RANK[j] + r
                shift = (2 * place - (WIDTH - 2 if back else 0)) % WIDTH
                tile = tile_of(j, r)
                moved = tile if shift == 0 else pltpu.roll(tile, shift, 1)
                acc = jnp.where(pair == place, moved, acc)
        out[0] = acc


def pack_kernel(q_ref, right_ref, left_ref):
    pack_edges(lambda j, r: q_ref[0, j, 8 * r : 8 * r + 8, :], right_ref, left_ref)


def wind_drive_of(j, r, east_ref, north_ref, open_water):
    rows = slice(8 * r, 8 * r + 8)
    along = float(COS[j]) * east_ref[rows, :] + float(SIN[j]) * north_ref[rows, :]
    drive = jnp.minimum(jnp.maximum(along, 0.0) / WIND_REF, WIND_CLIP)
    return drive * drive * open_water


def saturation_of(p):
    half = 0.5 * DTHETA
    diff = [p[b] - p[b + HALF] for b in range(HALF)]
    both = [p[b] + p[b + HALF] for b in range(HALF)]
    total = both[0]
    for b in range(1, HALF):
        total = total + both[b]
    total = total * (0.5 * half)
    fold = [both[b] - both[b + QUARTER] for b in range(QUARTER)]
    total_c = fold[0] * float(0.5 * half * COS2[0])
    total_s = None
    for b in range(1, QUARTER):
        total_c = total_c + fold[b] * float(0.5 * half * COS2[b])
        term = fold[b] * float(0.5 * half * SIN2[b])
        total_s = term if total_s is None else total_s + term
    diff = [d * half for d in diff]
    diff_c = [diff[b] * float(COS2[b]) for b in range(HALF)]
    diff_s = [diff[b] * float(SIN2[b]) for b in range(HALF)]

    def start(x):
        front = x[0]
        for b in range(1, QUARTER):
            front = front + x[b]
        rear = x[QUARTER]
        for b in range(QUARTER + 1, HALF):
            rear = rear + x[b]
        return 0.5 * (front - rear)

    win, win_c, win_s = start(diff), start(diff_c), start(diff_s)
    out = [None] * ND
    level = [None] * HALF
    for a in range(QUARTER):
        turn = total_c * float(COS2[a])
        if a:
            turn = turn + total_s * float(SIN2[a])
        level[a] = total + turn
        level[a + QUARTER] = total - turn
    for a in range(HALF):
        odd = win + win_c * float(COS2[a])
        if a:
            odd = odd + win_s * float(SIN2[a])
        out[a] = level[a] + odd
        out[a + HALF] = level[a] - odd
        new = a + QUARTER
        if a + 1 < HALF:
            if new < HALF:
                win, win_c, win_s = win + diff[new], win_c + diff_c[new], win_s + diff_s[new]
            else:
                new -= HALF
                win, win_c, win_s = win - diff[new], win_c - diff_c[new], win_s - diff_s[new]
    return out


def source_kernel(
    same,
    scal_ref,
    edge_ref,
    q_ref,
    spec_ref,
    from_left_ref,
    from_right_ref,
    own_right_ref,
    own_left_ref,
    east_ref,
    north_ref,
    land_ref,
    rows_ref,
    out_ref,
    sums_ref,
    drive_ref,
    x_ref,
    p_ref,
):
    k = pl.program_id(0)
    band = lax.axis_index("freq") * pl.num_programs(0) + k
    base = band * STRIDE
    lane = lanes()

    @pl.when(k == 0)
    def _():
        sums_ref[...] = jnp.zeros_like(sums_ref)
        for r in range(TILES):
            water = jnp.where(land_ref[8 * r : 8 * r + 8, :] == 2, 0.0, 1.0)
            for j in range(ND):
                drive_ref[j, 8 * r : 8 * r + 8, :] = wind_drive_of(j, r, east_ref, north_ref, water)

    gap_right = from_left_ref[k] - own_right_ref[k]
    gap_left = from_right_ref[k] - own_left_ref[k]
    fix_back = edge_ref[band, 0:1, :] * gap_right + edge_ref[band, 1:2, :] * pltpu.roll(
        gap_right, WIDTH - 1, 1
    )
    fix_ahead = edge_ref[band, 2:3, :] * gap_left + edge_ref[band, 3:4, :] * pltpu.roll(
        gap_left, 1, 1
    )

    held, sea = [], []
    for r in range(TILES):
        row = lax.broadcasted_iota(jnp.int32, (8, WIDTH), 0) + 8 * r
        held.append((row < rows_ref[0:1, :]) | (row >= LAT - rows_ref[1:2, :]))
        sea.append(jnp.where(land_ref[8 * r : 8 * r + 8, :] != 0, 1.0, 0.0))
    slope = [jnp.zeros((8, WIDTH), jnp.float32) for _ in range(TILES)]
    stress = [jnp.zeros((8, WIDTH), jnp.float32) for _ in range(TILES)]
    at_start, at_end = lane < 2, lane >= WIDTH - 2
    for j in range(ND):
        c0, c1, c2, d0, d1, d2 = (scal_ref[base + 6 * j + i] for i in range(6))
        back = BACK_LON[j]
        lead = 8 if BACK_LAT[j] else 0
        for r in range(TILES):
            q = q_ref[0, j, 8 * r : 8 * r + 8, :]
            one = pltpu.roll(q, 1 if back else WIDTH - 1, 1)
            two = pltpu.roll(q, 2 if back else WIDTH - 2, 1)
            place = 2 * (TILES * RANK[j] + r)
            shift = (-place if back else WIDTH - 2 - place) % WIDTH
            fix = fix_back if back else fix_ahead
            fix = fix if shift == 0 else pltpu.roll(fix, shift, 1)
            x = c0 * q + c1 * one + c2 * two + jnp.where(at_start if back else at_end, fix, 0.0)
            x_ref[j, lead + 8 * r : lead + 8 * r + 8, :] = x
            if BACK_LAT[j] and r == 0:
                x_ref[j, 0:8, :] = jnp.broadcast_to(x[0:1, :], (8, WIDTH))
            if not BACK_LAT[j] and r == TILES - 1:
                x_ref[j, LAT : LAT + 8, :] = jnp.broadcast_to(x[7:8, :], (8, WIDTH))
        sign = -1 if BACK_LAT[j] else 1
        for r in range(TILES):
            at = lead + 8 * r
            y = (
                d0 * x_ref[j, at : at + 8, :]
                + d1 * x_ref[j, at + sign : at + sign + 8, :]
                + d2 * x_ref[j, at + 2 * sign : at + 2 * sign + 8, :]
            )
            spec = (q_ref if same else spec_ref)[0, j, 8 * r : 8 * r + 8, :]
            y = jnp.where(held[r], spec, jnp.maximum(y, 0.0)) * sea[r]
            p_ref[j, 8 * r : 8 * r + 8, :] = y
            slope[r] = slope[r] + y
            stress[r] = stress[r] + y * drive_ref[j, 8 * r : 8 * r + 8, :]

    extra = base + 6 * ND
    for r in range(TILES):
        rows = slice(8 * r, 8 * r + 8)
        sums_ref[ND, rows, :] += slope[r] * scal_ref[extra + 2]
        sums_ref[ND + 1, rows, :] += stress[r] * scal_ref[extra + 3]
        p = [p_ref[j, rows, :] for j in range(ND)]
        for j, saturation in enumerate(saturation_of(p)):
            capped = jnp.maximum(saturation, SATURATION_REF)
            excess = capped * lax.rsqrt(capped) - ROOT_REF
            excess = excess * excess
            lower = sums_ref[j, rows, :]
            rate = excess * scal_ref[extra] + lower * scal_ref[extra + 1]
            sums_ref[j, rows, :] = lower + excess
            out_ref[0, j, rows, :] = p_ref[j, rows, :] * jnp.exp2(rate)


def pair_kernel(sums_ref, other_ref, out_ref):
    first = (lax.axis_index("freq") % 2) * HALF
    for i in range(HALF):
        out_ref[i] = sums_ref[first + i] + other_ref[first + i]
    for i in range(2):
        out_ref[HALF + i] = sums_ref[ND + i] + other_ref[ND + i]


def growth_kernel(
    last,
    scal_ref,
    part_ref,
    sums_ref,
    other_ref,
    mine_ref,
    rest_ref,
    east_ref,
    north_ref,
    land_ref,
    out_ref,
    *refs,
):
    rate_ref = refs[-1]
    k = pl.program_id(0)
    freq = lax.axis_index("freq")
    band = freq * pl.num_programs(0) + k

    @pl.when(k == 0)
    def _():
        core = freq % 2
        odd = jnp.where(core == 1, 1.0, 0.0)
        upper = jnp.where(freq >= 2, 1.0, 0.0)
        for r in range(TILES):
            rows = slice(8 * r, 8 * r + 8)
            ice = jnp.where(land_ref[rows, :] == 2, 1.0, 0.0)
            slope = (sums_ref[ND, rows, :] + other_ref[ND, rows, :]) + mine_ref[HALF, rows, :]
            stress = (sums_ref[ND + 1, rows, :] + other_ref[ND + 1, rows, :]) + mine_ref[
                HALF + 1, rows, :
            ]
            if last:
                refs[0][rows, :] = slope
            gain = GROWTH * (1.0 + stress / (stress + 1.0))
            damp = SWELL_DAMP * (slope / (slope + 1.0)) + ICE_DAMP * ice
            for j in range(ND):
                local = j % HALF
                near, far = mine_ref[local, rows, :], rest_ref[local, rows, :]
                in_mine = core == (0 if j < HALF else 1)
                lower = odd * other_ref[j, rows, :] + upper * jnp.where(in_mine, near, far)
                drive = wind_drive_of(j, r, east_ref, north_ref, 1.0 - ice)
                rate_ref[j, rows, :] = gain * drive - damp - (CUMULATIVE / NF) * lower

    root = scal_ref[band * STRIDE + 6 * ND + 4]

    def tile(j, r):
        rows = slice(8 * r, 8 * r + 8)
        value = part_ref[0, j, rows, :] * jnp.exp2(rate_ref[j, rows, :] * root)
        out_ref[0, j, rows, :] = value
        return value

    if last:
        for j in range(ND):
            for r in range(TILES):
                tile(j, r)
    else:
        pack_edges(tile, refs[0], refs[1])


def whole(shape):
    return pl.BlockSpec(shape, lambda k: (0,) * len(shape))


def per_device(spectrum, east_wind, north_wind, land_sea, edge_rows):
    bands, count, lat_rows, width = spectrum.shape
    assert (count, lat_rows, width) == (ND, LAT, WIDTH)
    ring = lax.axis_size("lon")
    assert lax.axis_size("freq") == 4 and bands * 4 == NF
    f32 = jnp.float32
    field = jax.ShapeDtypeStruct(spectrum.shape, f32)
    edges = jax.ShapeDtypeStruct((bands, 8, WIDTH), f32)
    sums = jax.ShapeDtypeStruct((ND + 2, LAT, WIDTH), f32)
    halves = jax.ShapeDtypeStruct((HALF + 2, LAT, WIDTH), f32)
    plane = (LAT, WIDTH)
    band_spec = pl.BlockSpec((1, ND, LAT, WIDTH), lambda k: (k, 0, 0, 0))
    edge_spec = pl.BlockSpec((1, 8, WIDTH), lambda k: (k, 0, 0))
    smem = pl.BlockSpec(memory_space=pltpu.SMEM)
    params = pltpu.CompilerParams(
        dimension_semantics=("arbitrary",), vmem_limit_bytes=40 * 1024 * 1024
    )
    scalars, edge_table = jnp.asarray(SCALARS), jnp.asarray(EDGE)
    swap_core = [(0, 1), (1, 0), (2, 3), (3, 2)]
    swap_chip = [(0, 2), (2, 0), (1, 3), (3, 1)]

    right, left = pl.pallas_call(
        pack_kernel,
        grid=(bands,),
        in_specs=[band_spec],
        out_specs=[edge_spec, edge_spec],
        out_shape=[edges, edges],
        compiler_params=params,
        name="pack_columns",
    )(spectrum)

    energy = spectrum
    for step in range(STEPS):
        last = step == STEPS - 1
        from_left = lax.ppermute(right, "lon", [(i, (i + 1) % ring) for i in range(ring)])
        from_right = lax.ppermute(left, "lon", [((i + 1) % ring, i) for i in range(ring)])
        same = step == 0
        source = pl.BlockSpec((1, 8, 8, WIDTH), lambda k: (0, 0, 0, 0)) if same else band_spec
        part, mine = pl.pallas_call(
            functools.partial(source_kernel, same),
            grid=(bands,),
            in_specs=[smem, whole(EDGE.shape), band_spec, source]
            + [whole((bands, 8, WIDTH))] * 4
            + [whole(plane)] * 3
            + [whole((2, WIDTH))],
            out_specs=[band_spec, whole(sums.shape)],
            out_shape=[field, sums],
            scratch_shapes=[
                pltpu.VMEM((ND, LAT, WIDTH), f32),
                pltpu.VMEM((ND, LAT + 8, WIDTH), f32),
                pltpu.VMEM((ND, LAT, WIDTH), f32),
            ],
            compiler_params=params,
            name="propagate_and_break",
        )(
            scalars, edge_table, energy, spectrum, from_left, from_right, right, left,
            east_wind, north_wind, land_sea, edge_rows,
        )
        other = lax.ppermute(mine, "freq", swap_core)
        pair = pl.pallas_call(
            pair_kernel,
            in_specs=[pl.BlockSpec(memory_space=pltpu.VMEM)] * 2,
            out_specs=pl.BlockSpec(memory_space=pltpu.VMEM),
            out_shape=halves,
            name="pair_sums",
        )(mine, other)
        near = lax.ppermute(pair, "freq", swap_chip)
        far = lax.ppermute(near, "freq", swap_core)
        if last:
            more_specs, more_shapes = [whole(plane)], [jax.ShapeDtypeStruct(plane, f32)]
        else:
            more_specs, more_shapes = [edge_spec, edge_spec], [edges, edges]
        energy, *more = pl.pallas_call(
            functools.partial(growth_kernel, last),
            grid=(bands,),
            in_specs=[smem, band_spec]
            + [whole(sums.shape)] * 2
            + [whole(halves.shape)] * 2
            + [whole(plane)] * 3,
            out_specs=[band_spec] + more_specs,
            out_shape=[field] + more_shapes,
            scratch_shapes=[pltpu.VMEM((ND, LAT, WIDTH), f32)],
            compiler_params=params,
            name="grow",
        )(scalars, part, mine, other, near, far, east_wind, north_wind, land_sea)
        if not last:
            right, left = more
    return energy, more[0]


def solution(mesh):
    in_specs = (
        P("freq", None, None, "lon"),
        P(None, "lon"),
        P(None, "lon"),
        P(None, "lon"),
        P(None, "lon"),
    )
    out_specs = (P("freq", None, None, "lon"), P(None, "lon"))
    return jax.shard_map(
        per_device, mesh=mesh, in_specs=in_specs, out_specs=out_specs, check_vma=False
    )
```

time: 215 us -> 89.5 us (0.42)
  other arithmetic: 88.1 us -> 0 us
  Pallas kernels: 0 us -> 30.7 us
  local copies, waits for them, and re-layouts: 49.5 us -> 19.3 us
  blocking collectives: 23.3 us -> 0 us
  between operations: 15.9 us -> 0.8 us
  matrix products: 14.5 us -> 0 us
  waiting for transfers between devices: 11.6 us -> 23.5 us
  starting transfers between devices: 10.8 us -> 14.4 us
    add x4 -> x0, other arithmetic: 39.7 us -> none  [the longest x2 38.3 us: beam_warming(): centre - 0.5 * forward * (3.0 * centre - 4.0 * back_one + back_two)]
    pallas_call x0 -> x7, Pallas kernels: none -> 30.7 us  [the longest x2 17.5 us: per_device(): pl.pallas_call(functools.partial(source_kernel, same), grid=(bands,), in_...]
    psum x2 -> x0, blocking collectives: 23.3 us -> none  [per_device(): forcing_mean_slope, stress = lax.psum((slope_part, stress_part), 'freq')]
    ppermute x4 -> x10, waiting for transfers between devices: 1.51 us -> 23.5 us  [the longest x2 13.1 us: per_device(): near = lax.ppermute(pair, 'freq', swap_chip)]
    slice x6 -> x0, local copies, waits for them, and re-layouts: 18.9 us -> none  [the longest x3 15.1 us: with_halo(): lax.slice_in_dim(cells, cells.shape[dim] - width, cells.shape[dim], axis=...]
    ppermute x4 -> x0, local copies, waits for them, and re-layouts: 15 us -> none  [the longest x2 7.53 us: with_halo(): lax.ppermute(tail, axis, [(i, (i + 1) % count) for i in range(count)])]
    dot_general x2 -> x0, matrix products: 14.5 us -> none  [per_device(): jnp.einsum('ij,kjlw->kilw', kernel, shifted, precision=lax.Precision.HIGH...]
    another operation x2 -> x0, other arithmetic: 13.5 us -> none  [per_device(): lower_sum = prefix_sum[None] + jnp.cumsum(excess, 0) - excess]
  transfers between devices with their start and end apart: 6 -> 10, of which waited for: 3 -> 8; matrix products, arithmetic and copies ran while one was open for 16% -> 0% of each run, Pallas kernels for 0% -> 0%
where the time goes in v1:
time: 89.5 us; the launch traced here: 88.7 us
  Pallas kernels  30.7 us (34%)
  waiting for transfers between devices  23.5 us (26%)
  local copies, waits for them, and re-layouts  19.3 us (22%)
  starting transfers between devices  14.4 us (16%)
    unnamed x56, local copies, waits for them, and re-layouts  19.3 us
    pallas_call x2, Pallas kernels, per_device(): pl.pallas_call(functools.partial(source_kernel, same), grid=(bands,), in_...  17.5 us
    ppermute x2, waiting for transfers between devices, per_device(): near = lax.ppermute(pair, 'freq', swap_chip)  13.1 us
    pallas_call x2, Pallas kernels, per_device(): pl.pallas_call(functools.partial(growth_kernel, last), grid=(bands,), in_...  7.94 us
    ppermute x2, starting transfers between devices, per_device(): lax.ppermute(left, 'lon', [((i + 1) % ring, i) for i in range(ring)])  6.52 us
    ppermute x2, starting transfers between devices, per_device(): lax.ppermute(right, 'lon', [(i, (i + 1) % ring) for i in range(ring)])  4.46 us
    ppermute x2, waiting for transfers between devices, per_device(): other = lax.ppermute(mine, 'freq', swap_core)  3.78 us
    pallas_call x2, Pallas kernels, per_device(): pl.pallas_call(pair_kernel, in_specs=[pl.BlockSpec(memory_space=pltpu.VME...  3.76 us
  transfers between devices with their start and end apart: 10, of which 8 were waited for; matrix products, arithmetic and copies ran while one was open for 0% of the time, Pallas kernels for 0%

profile of v1, /device:TPU:0, one launch (start us, length us, event | category | flops | bytes accessed | tf_op | source)
XLA Modules:
  0.0 88.7 jit_solution(9428547360370371792)
XLA Ops:
  0.6 2.0 %copy-done = f32[8,36,24,128]{3,2,1,0:T(8,128)S(1)} copy-done((f32[8,36,24,128]{3,2,1,0:T(8,128)S(1)}, f32[8,36,24,128]{3,2,1,0:T(8,128)}, u32[]{:S(2)}) %copy-start) | copy-done | bytes 3538968
  2.7 1.5 %pack_columns.1 = (f32[8,8,128]{2,1,0:T(8,128)S(1)}, f32[8,8,128]{2,1,0:T(8,128)S(1)}) custom-call(f32[8,36,24,128]{3,2,1,0:T(8,128)S(1)} %copy-done), custom_call_target="tpu_custom_call" | custom-call | tf_op jit(solution)/shard_map/pack_columns/pallas_call | solution.py:357
  4.2 3.0 %collective-permute-start = (f32[8,8,128]{2,1,0:T(8,128)S(1)}, f32[8,8,128]{2,1,0:T(8,128)S(1)}, u32[]{:S(2)}, u32[]{:S(2)}) collective-permute-start(f32[8,8,128]{2,1,0:T(8,128)S(1)} %get-tuple-element.11.own_right_ref), channel_id=1, source_target_pairs={{0,4},{4,8},{8,12},{12,16},{16,20},{20,24},{24,28},{28,0},{1,5},{5... | collective-permute-start | bytes 98312 | tf_op jit(solution)/shard_map/ppermute | solution.py:370
  7.2 3.1 %collective-permute-start.1 = (f32[8,8,128]{2,1,0:T(8,128)S(1)}, f32[8,8,128]{2,1,0:T(8,128)S(1)}, u32[]{:S(2)}, u32[]{:S(2)}) collective-permute-start(f32[8,8,128]{2,1,0:T(8,128)S(1)} %get-tuple-element.12.own_left_ref), channel_id=1, source_target_pairs={{4,0},{8,4},{12,8},{16,12},{20,16},{24,20},{28,24},{0,28},{5,1},{9... | collective-permute-start | bytes 98312 | tf_op jit(solution)/shard_map/ppermute | solution.py:371
  10.3 1.8 %collective-permute-done.from_left_ref = f32[8,8,128]{2,1,0:T(8,128)S(1)} collective-permute-done((f32[8,8,128]{2,1,0:T(8,128)S(1)}, f32[8,8,128]{2,1,0:T(8,128)S(1)}, u32[]{:S(2)}, u32[]{:S(2)}) %collective-permute-start) | collective-permute-done | bytes 32800 | tf_op jit(solution)/shard_map/ppermute | solution.py:370
  12.1 8.7 %propagate_and_break.2 = (f32[8,36,24,128]{3,2,1,0:T(8,128)S(1)}, f32[38,24,128]{2,1,0:T(8,128)S(1)}) custom-call(f32[7168]{0:T(1024)S(1)} %copy-done.12, f32[32,4,128]{2,1,0:T(4,128)S(1)} %copy-done.16, f32[8,36,24,128]{3,2,1,0:T(8,128)S(1)} %copy-done, f32[8,36,24,128]{3,2,1,0:T(8,128)S(1)} %copy-done, ...), custom_call_target="tpu_custom_call" | custom-call | tf_op jit(solution)/shard_map/propagate_and_break/pallas_call | solution.py:374
  20.9 1.8 %copy-done.4 = f32[8,36,24,128]{3,2,1,0:T(8,128)} copy-done((f32[8,36,24,128]{3,2,1,0:T(8,128)}, f32[8,36,24,128]{3,2,1,0:T(8,128)S(1)}, u32[]{:S(2)}) %copy-start.4) | copy-done | bytes 3538968
  22.7 0.8 copy-done.8
  23.5 2.0 %collective-permute-done.2.other_ref = f32[38,24,128]{2,1,0:T(8,128)} collective-permute-done((f32[38,24,128]{2,1,0:T(8,128)S(1)}, f32[38,24,128]{2,1,0:T(8,128)}, u32[]{:S(2)}, u32[]{:S(2)}) %collective-permute-start.2) | collective-permute-done | bytes 466976 | tf_op jit(solution)/shard_map/ppermute | solution.py:394
  25.4 1.9 %pair_sums.2 = f32[20,24,128]{2,1,0:T(8,128)} custom-call(f32[38,24,128]{2,1,0:T(8,128)} %copy-done.8, f32[38,24,128]{2,1,0:T(8,128)} %collective-permute-done.2.other_ref), custom_call_target="tpu_custom_call" | custom-call | tf_op jit(solution)/shard_map/pair_sums/pallas_call | solution.py:395
  27.3 1.7 %collective-permute-start.3 = (f32[20,24,128]{2,1,0:T(8,128)}, f32[20,24,128]{2,1,0:T(8,128)S(1)}, u32[]{:S(2)}, u32[]{:S(2)}) collective-permute-start(f32[20,24,128]{2,1,0:T(8,128)} %pair_sums.2), channel_id=1, source_target_pairs={{0,2},{2,0},{1,3},{3,1},{4,6},{6,4},{5,7},{7,5},{8,10},{10,8},{9,1... | collective-permute-start | bytes 737288 | tf_op jit(solution)/shard_map/ppermute | solution.py:402
  29.0 6.5 %collective-permute-done.3.mine_ref = f32[20,24,128]{2,1,0:T(8,128)S(1)} collective-permute-done((f32[20,24,128]{2,1,0:T(8,128)}, f32[20,24,128]{2,1,0:T(8,128)S(1)}, u32[]{:S(2)}, u32[]{:S(2)}) %collective-permute-start.3) | collective-permute-done | bytes 245792 | tf_op jit(solution)/shard_map/ppermute | solution.py:402
  35.5 1.5 %collective-permute-done.4.rest_ref = f32[20,24,128]{2,1,0:T(8,128)S(1)} collective-permute-done((f32[20,24,128]{2,1,0:T(8,128)S(1)}, f32[20,24,128]{2,1,0:T(8,128)S(1)}, u32[]{:S(2)}, u32[]{:S(2)}) %collective-permute-start.4) | collective-permute-done | bytes 245792 | tf_op jit(solution)/shard_map/ppermute | solution.py:403
  37.0 2.0 %copy-done.5 = f32[8,36,24,128]{3,2,1,0:T(8,128)S(1)} copy-done((f32[8,36,24,128]{3,2,1,0:T(8,128)S(1)}, f32[8,36,24,128]{3,2,1,0:T(8,128)}, u32[]{:S(2)}) %copy-start.5) | copy-done | bytes 3538968
  39.0 1.0 %copy-done.9 = f32[38,24,128]{2,1,0:T(8,128)S(1)} copy-done((f32[38,24,128]{2,1,0:T(8,128)S(1)}, f32[38,24,128]{2,1,0:T(8,128)}, u32[]{:S(2)}) %copy-start.9) | copy-done | bytes 466968
  42.2 3.2 %grow.2 = (f32[8,36,24,128]{3,2,1,0:T(8,128)S(1)}, f32[8,8,128]{2,1,0:T(8,128)S(1)}, f32[8,8,128]{2,1,0:T(8,128)S(1)}) custom-call(f32[7168]{0:T(1024)S(1)} %copy-done.13, f32[8,36,24,128]{3,2,1,0:T(8,128)S(1)} %copy-done.5, f32[38,24,128]{2,1,0:T(8,128)S(1)} %copy-done.9, f32[38,24,128]{2,1,0:T(8,128)} %collective-permute-done.2.other_ref, ...), custom_call_target="tpu_custom_call" | custom-call | tf_op jit(solution)/shard_map/grow/pallas_call | solution.py:408
  45.4 1.5 %collective-permute-start.5 = (f32[8,8,128]{2,1,0:T(8,128)S(1)}, f32[8,8,128]{2,1,0:T(8,128)S(1)}, u32[]{:S(2)}, u32[]{:S(2)}) collective-permute-start(f32[8,8,128]{2,1,0:T(8,128)S(1)} %get-tuple-element.16.own_right_ref), channel_id=1, source_target_pairs={{0,4},{4,8},{8,12},{12,16},{16,20},{20,24},{24,28},{28,0},{1,5},{5... | collective-permute-start | bytes 98312 | tf_op jit(solution)/shard_map/ppermute | solution.py:370
  46.9 3.4 %collective-permute-start.6 = (f32[8,8,128]{2,1,0:T(8,128)S(1)}, f32[8,8,128]{2,1,0:T(8,128)S(1)}, u32[]{:S(2)}, u32[]{:S(2)}) collective-permute-start(f32[8,8,128]{2,1,0:T(8,128)S(1)} %get-tuple-element.17.own_left_ref), channel_id=1, source_target_pairs={{4,0},{8,4},{12,8},{16,12},{20,16},{24,20},{28,24},{0,28},{5,1},{9... | collective-permute-start | bytes 98312 | tf_op jit(solution)/shard_map/ppermute | solution.py:371
  50.3 1.8 %collective-permute-done.5.from_left_ref = f32[8,8,128]{2,1,0:T(8,128)S(1)} collective-permute-done((f32[8,8,128]{2,1,0:T(8,128)S(1)}, f32[8,8,128]{2,1,0:T(8,128)S(1)}, u32[]{:S(2)}, u32[]{:S(2)}) %collective-permute-start.5) | collective-permute-done | bytes 32800 | tf_op jit(solution)/shard_map/ppermute | solution.py:370
  52.2 8.8 %propagate_and_break.3 = (f32[8,36,24,128]{3,2,1,0:T(8,128)S(1)}, f32[38,24,128]{2,1,0:T(8,128)S(1)}) custom-call(f32[7168]{0:T(1024)S(1)} %copy-done.14, f32[32,4,128]{2,1,0:T(4,128)S(1)} %copy-done.17, f32[8,36,24,128]{3,2,1,0:T(8,128)S(1)} %get-tuple-element.15.q_ref, f32[8,36,24,128]{3,2,1,0:T(8,128)S(1)} %copy-done.1, ...), custom_call_target="tpu_custom_call" | custom-call | tf_op jit(solution)/shard_map/propagate_and_break/pallas_call | solution.py:374
  61.0 1.8 %copy-done.2 = f32[8,36,24,128]{3,2,1,0:T(8,128)} copy-done((f32[8,36,24,128]{3,2,1,0:T(8,128)}, f32[8,36,24,128]{3,2,1,0:T(8,128)S(1)}, u32[]{:S(2)}) %copy-start.2) | copy-done | bytes 3538968
  62.7 0.8 copy-done.6
  63.5 1.8 %collective-permute-done.7.other_ref = f32[38,24,128]{2,1,0:T(8,128)S(1)} collective-permute-done((f32[38,24,128]{2,1,0:T(8,128)S(1)}, f32[38,24,128]{2,1,0:T(8,128)S(1)}, u32[]{:S(2)}, u32[]{:S(2)}) %collective-permute-start.7) | collective-permute-done | bytes 466976 | tf_op jit(solution)/shard_map/ppermute | solution.py:394
  65.4 0.8 copy-done.10
  66.1 1.9 %pair_sums.3 = f32[20,24,128]{2,1,0:T(8,128)} custom-call(f32[38,24,128]{2,1,0:T(8,128)} %copy-done.6, f32[38,24,128]{2,1,0:T(8,128)} %copy-done.10), custom_call_target="tpu_custom_call" | custom-call | tf_op jit(solution)/shard_map/pair_sums/pallas_call | solution.py:395
  68.0 1.7 %collective-permute-start.8 = (f32[20,24,128]{2,1,0:T(8,128)}, f32[20,24,128]{2,1,0:T(8,128)S(1)}, u32[]{:S(2)}, u32[]{:S(2)}) collective-permute-start(f32[20,24,128]{2,1,0:T(8,128)} %pair_sums.3), channel_id=1, source_target_pairs={{0,2},{2,0},{1,3},{3,1},{4,6},{6,4},{5,7},{7,5},{8,10},{10,8},{9,1... | collective-permute-start | bytes 737288 | tf_op jit(solution)/shard_map/ppermute | solution.py:402
  69.7 6.6 %collective-permute-done.8.mine_ref = f32[20,24,128]{2,1,0:T(8,128)S(1)} collective-permute-done((f32[20,24,128]{2,1,0:T(8,128)}, f32[20,24,128]{2,1,0:T(8,128)S(1)}, u32[]{:S(2)}, u32[]{:S(2)}) %collective-permute-start.8) | collective-permute-done | bytes 245792 | tf_op jit(solution)/shard_map/ppermute | solution.py:402
  76.2 1.5 %collective-permute-done.9.rest_ref = f32[20,24,128]{2,1,0:T(8,128)S(1)} collective-permute-done((f32[20,24,128]{2,1,0:T(8,128)S(1)}, f32[20,24,128]{2,1,0:T(8,128)S(1)}, u32[]{:S(2)}, u32[]{:S(2)}) %collective-permute-start.9) | collective-permute-done | bytes 245792 | tf_op jit(solution)/shard_map/ppermute | solution.py:403
  77.7 2.0 %copy-done.3 = f32[8,36,24,128]{3,2,1,0:T(8,128)S(1)} copy-done((f32[8,36,24,128]{3,2,1,0:T(8,128)S(1)}, f32[8,36,24,128]{3,2,1,0:T(8,128)}, u32[]{:S(2)}) %copy-start.3) | copy-done | bytes 3538968
  79.7 1.0 %copy-done.7 = f32[38,24,128]{2,1,0:T(8,128)S(1)} copy-done((f32[38,24,128]{2,1,0:T(8,128)S(1)}, f32[38,24,128]{2,1,0:T(8,128)}, u32[]{:S(2)}) %copy-start.7) | copy-done | bytes 466968
  80.8 1.0 %copy-done.11 = f32[38,24,128]{2,1,0:T(8,128)S(1)} copy-done((f32[38,24,128]{2,1,0:T(8,128)S(1)}, f32[38,24,128]{2,1,0:T(8,128)}, u32[]{:S(2)}) %copy-start.11) | copy-done | bytes 466968
  83.9 4.8 %grow.3 = (f32[8,36,24,128]{3,2,1,0:T(8,128)}, f32[24,128]{1,0:T(8,128)}) custom-call(f32[7168]{0:T(1024)S(1)} %copy-done.15, f32[8,36,24,128]{3,2,1,0:T(8,128)S(1)} %copy-done.3, f32[38,24,128]{2,1,0:T(8,128)S(1)} %copy-done.7, f32[38,24,128]{2,1,0:T(8,128)S(1)} %copy-done.11, f32[20,24,128]{2,1,0:T(8,128)S(1)} %collective-permute-done.8.mine_ref, ...), custom_call_target="tpu_custom_call" | custom-call | tf_op jit(solution)/shard_map/grow/pallas_call | solution.py:408
  (51 shorter events, 4.4 us)
Async XLA Ops:
  0.6 2.0 %copy-start = (f32[8,36,24,128]{3,2,1,0:T(8,128)S(1)}, f32[8,36,24,128]{3,2,1,0:T(8,128)}, u32[]{:S(2)}) copy-start(f32[8,36,24,128]{3,2,1,0:T(8,128)} %spec_ref.3) | copy-start | bytes 10616836
  2.6 9.5 %copy-start.12 = (f32[7168]{0:T(1024)S(1)}, f32[7168]{0:T(1024)}, u32[]{:S(2)}) copy-start(f32[7168]{0:T(1024)} %constant.4.clone.scal_ref) | copy-start | bytes 86020
  2.6 9.5 %copy-start.16 = (f32[32,4,128]{2,1,0:T(4,128)S(1)}, f32[32,4,128]{2,1,0:T(4,128)}, u32[]{:S(2)}) copy-start(f32[32,4,128]{2,1,0:T(4,128)} %constant.5.clone.edge_ref) | copy-start | bytes 196612
  2.6 9.5 %copy-start.18 = (f32[24,128]{1,0:T(8,128)S(1)}, f32[24,128]{1,0:T(8,128)}, u32[]{:S(2)}) copy-start(f32[24,128]{1,0:T(8,128)} %east_ref.7) | copy-start | bytes 36868
  2.6 9.5 %copy-start.19 = (f32[24,128]{1,0:T(8,128)S(1)}, f32[24,128]{1,0:T(8,128)}, u32[]{:S(2)}) copy-start(f32[24,128]{1,0:T(8,128)} %north_ref.7) | copy-start | bytes 36868
  2.6 9.5 %copy-start.23 = (s32[24,128]{1,0:T(8,128)S(1)}, s32[24,128]{1,0:T(8,128)}, u32[]{:S(2)}) copy-start(s32[24,128]{1,0:T(8,128)} %land_ref.7) | copy-start | bytes 36868
  2.7 9.5 %copy-start.27 = (s32[2,128]{1,0:T(2,128)S(1)}, s32[2,128]{1,0:T(2,128)}, u32[]{:S(2)}) copy-start(s32[2,128]{1,0:T(2,128)} %rows_ref.3) | copy-start | bytes 3076
  4.2 7.9 %collective-permute-start = (f32[8,8,128]{2,1,0:T(8,128)S(1)}, f32[8,8,128]{2,1,0:T(8,128)S(1)}, u32[]{:S(2)}, u32[]{:S(2)}) collective-permute-start(f32[8,8,128]{2,1,0:T(8,128)S(1)} %get-tuple-element.11.own_right_ref), channel_id=1, source_target_pairs={{0,4},{4,8},{8,12},{12,16},{16,20},{20,24},{24,28},{28,0},{1,5},{5... | collective-permute-start | bytes 98312 | tf_op jit(solution)/shard_map/ppermute | solution.py:370
  7.2 4.9 %collective-permute-start.1 = (f32[8,8,128]{2,1,0:T(8,128)S(1)}, f32[8,8,128]{2,1,0:T(8,128)S(1)}, u32[]{:S(2)}, u32[]{:S(2)}) collective-permute-start(f32[8,8,128]{2,1,0:T(8,128)S(1)} %get-tuple-element.12.own_left_ref), channel_id=1, source_target_pairs={{4,0},{8,4},{12,8},{16,12},{20,16},{24,20},{28,24},{0,28},{5,1},{9... | collective-permute-start | bytes 98312 | tf_op jit(solution)/shard_map/ppermute | solution.py:371
  20.9 1.8 %copy-start.4 = (f32[8,36,24,128]{3,2,1,0:T(8,128)}, f32[8,36,24,128]{3,2,1,0:T(8,128)S(1)}, u32[]{:S(2)}) copy-start(f32[8,36,24,128]{3,2,1,0:T(8,128)S(1)} %get-tuple-element.13.part_ref) | copy-start | bytes 10616836
  22.7 0.8 copy-start.8
  22.7 29.4 %copy-start.1 = (f32[8,36,24,128]{3,2,1,0:T(8,128)S(1)}, f32[8,36,24,128]{3,2,1,0:T(8,128)}, u32[]{:S(2)}) copy-start(f32[8,36,24,128]{3,2,1,0:T(8,128)} %spec_ref.3) | copy-start | bytes 10616836
  23.5 2.0 %collective-permute-start.2 = (f32[38,24,128]{2,1,0:T(8,128)S(1)}, f32[38,24,128]{2,1,0:T(8,128)}, u32[]{:S(2)}, u32[]{:S(2)}) collective-permute-start(f32[38,24,128]{2,1,0:T(8,128)S(1)} %get-tuple-element.14.sums_ref), channel_id=1, source_target_pairs={{0,1},{1,0},{2,3},{3,2},{4,5},{5,4},{6,7},{7,6},{8,9},{9,8},{10,11... | collective-permute-start | bytes 1400840 | tf_op jit(solution)/shard_map/ppermute | solution.py:394
  27.3 8.2 %collective-permute-start.3 = (f32[20,24,128]{2,1,0:T(8,128)}, f32[20,24,128]{2,1,0:T(8,128)S(1)}, u32[]{:S(2)}, u32[]{:S(2)}) collective-permute-start(f32[20,24,128]{2,1,0:T(8,128)} %pair_sums.2), channel_id=1, source_target_pairs={{0,2},{2,0},{1,3},{3,1},{4,6},{6,4},{5,7},{7,5},{8,10},{10,8},{9,1... | collective-permute-start | bytes 737288 | tf_op jit(solution)/shard_map/ppermute | solution.py:402
  35.5 1.5 %collective-permute-start.4 = (f32[20,24,128]{2,1,0:T(8,128)S(1)}, f32[20,24,128]{2,1,0:T(8,128)S(1)}, u32[]{:S(2)}, u32[]{:S(2)}) collective-permute-start(f32[20,24,128]{2,1,0:T(8,128)S(1)} %collective-permute-done.3.mine_ref), channel_id=1, source_target_pairs={{0,1},{1,0},{2,3},{3,2},{4,5},{5,4},{6,7},{7,6},{8,9},{9,8},{10,11... | collective-permute-start | bytes 737288 | tf_op jit(solution)/shard_map/ppermute | solution.py:403
  37.0 2.0 %copy-start.5 = (f32[8,36,24,128]{3,2,1,0:T(8,128)S(1)}, f32[8,36,24,128]{3,2,1,0:T(8,128)}, u32[]{:S(2)}) copy-start(f32[8,36,24,128]{3,2,1,0:T(8,128)} %copy-done.4) | copy-start | bytes 10616836
  39.0 1.0 %copy-start.9 = (f32[38,24,128]{2,1,0:T(8,128)S(1)}, f32[38,24,128]{2,1,0:T(8,128)}, u32[]{:S(2)}) copy-start(f32[38,24,128]{2,1,0:T(8,128)} %copy-done.8) | copy-start | bytes 1400836
  42.2 9.9 %copy-start.14 = (f32[7168]{0:T(1024)S(1)}, f32[7168]{0:T(1024)}, u32[]{:S(2)}) copy-start(f32[7168]{0:T(1024)} %constant.4.clone.scal_ref) | copy-start | bytes 86020
  42.2 9.9 %copy-start.17 = (f32[32,4,128]{2,1,0:T(4,128)S(1)}, f32[32,4,128]{2,1,0:T(4,128)}, u32[]{:S(2)}) copy-start(f32[32,4,128]{2,1,0:T(4,128)} %constant.5.clone.edge_ref) | copy-start | bytes 196612
  42.2 9.9 %copy-start.21 = (f32[24,128]{1,0:T(8,128)S(1)}, f32[24,128]{1,0:T(8,128)}, u32[]{:S(2)}) copy-start(f32[24,128]{1,0:T(8,128)} %north_ref.7) | copy-start | bytes 36868
  42.2 9.9 %copy-start.25 = (s32[24,128]{1,0:T(8,128)S(1)}, s32[24,128]{1,0:T(8,128)}, u32[]{:S(2)}) copy-start(s32[24,128]{1,0:T(8,128)} %land_ref.7) | copy-start | bytes 36868
  45.4 6.7 %collective-permute-start.5 = (f32[8,8,128]{2,1,0:T(8,128)S(1)}, f32[8,8,128]{2,1,0:T(8,128)S(1)}, u32[]{:S(2)}, u32[]{:S(2)}) collective-permute-start(f32[8,8,128]{2,1,0:T(8,128)S(1)} %get-tuple-element.16.own_right_ref), channel_id=1, source_target_pairs={{0,4},{4,8},{8,12},{12,16},{16,20},{20,24},{24,28},{28,0},{1,5},{5... | collective-permute-start | bytes 98312 | tf_op jit(solution)/shard_map/ppermute | solution.py:370
  46.9 5.3 %collective-permute-start.6 = (f32[8,8,128]{2,1,0:T(8,128)S(1)}, f32[8,8,128]{2,1,0:T(8,128)S(1)}, u32[]{:S(2)}, u32[]{:S(2)}) collective-permute-start(f32[8,8,128]{2,1,0:T(8,128)S(1)} %get-tuple-element.17.own_left_ref), channel_id=1, source_target_pairs={{4,0},{8,4},{12,8},{16,12},{20,16},{24,20},{28,24},{0,28},{5,1},{9... | collective-permute-start | bytes 98312 | tf_op jit(solution)/shard_map/ppermute | solution.py:371
  60.9 1.8 %copy-start.2 = (f32[8,36,24,128]{3,2,1,0:T(8,128)}, f32[8,36,24,128]{3,2,1,0:T(8,128)S(1)}, u32[]{:S(2)}) copy-start(f32[8,36,24,128]{3,2,1,0:T(8,128)S(1)} %get-tuple-element.18.part_ref) | copy-start | bytes 10616836
  62.7 0.8 copy-start.6
  63.5 1.8 %collective-permute-start.7 = (f32[38,24,128]{2,1,0:T(8,128)S(1)}, f32[38,24,128]{2,1,0:T(8,128)S(1)}, u32[]{:S(2)}, u32[]{:S(2)}) collective-permute-start(f32[38,24,128]{2,1,0:T(8,128)S(1)} %get-tuple-element.19.sums_ref), channel_id=1, source_target_pairs={{0,1},{1,0},{2,3},{3,2},{4,5},{5,4},{6,7},{7,6},{8,9},{9,8},{10,11... | collective-permute-start | bytes 1400840 | tf_op jit(solution)/shard_map/ppermute | solution.py:394
  65.3 0.8 copy-start.10
  68.0 8.2 %collective-permute-start.8 = (f32[20,24,128]{2,1,0:T(8,128)}, f32[20,24,128]{2,1,0:T(8,128)S(1)}, u32[]{:S(2)}, u32[]{:S(2)}) collective-permute-start(f32[20,24,128]{2,1,0:T(8,128)} %pair_sums.3), channel_id=1, source_target_pairs={{0,2},{2,0},{1,3},{3,1},{4,6},{6,4},{5,7},{7,5},{8,10},{10,8},{9,1... | collective-permute-start | bytes 737288 | tf_op jit(solution)/shard_map/ppermute | solution.py:402
  76.2 1.5 %collective-permute-start.9 = (f32[20,24,128]{2,1,0:T(8,128)S(1)}, f32[20,24,128]{2,1,0:T(8,128)S(1)}, u32[]{:S(2)}, u32[]{:S(2)}) collective-permute-start(f32[20,24,128]{2,1,0:T(8,128)S(1)} %collective-permute-done.8.mine_ref), channel_id=1, source_target_pairs={{0,1},{1,0},{2,3},{3,2},{4,5},{5,4},{6,7},{7,6},{8,9},{9,8},{10,11... | collective-permute-start | bytes 737288 | tf_op jit(solution)/shard_map/ppermute | solution.py:403
  77.7 2.0 %copy-start.3 = (f32[8,36,24,128]{3,2,1,0:T(8,128)S(1)}, f32[8,36,24,128]{3,2,1,0:T(8,128)}, u32[]{:S(2)}) copy-start(f32[8,36,24,128]{3,2,1,0:T(8,128)} %copy-done.2) | copy-start | bytes 10616836
  79.7 1.0 %copy-start.7 = (f32[38,24,128]{2,1,0:T(8,128)S(1)}, f32[38,24,128]{2,1,0:T(8,128)}, u32[]{:S(2)}) copy-start(f32[38,24,128]{2,1,0:T(8,128)} %copy-done.6) | copy-start | bytes 1400836
  80.8 1.0 %copy-start.11 = (f32[38,24,128]{2,1,0:T(8,128)S(1)}, f32[38,24,128]{2,1,0:T(8,128)}, u32[]{:S(2)}) copy-start(f32[38,24,128]{2,1,0:T(8,128)} %copy-done.10) | copy-start | bytes 1400836
  (6 other events, 4.3 us)

commit v2 on v1

--- a/solution.py
+++ b/solution.py
@@ -84,7 +84,7 @@
     return lax.broadcasted_iota(jnp.int32, (8, WIDTH), 1)
 
 
-def pack_edges(tile_of, right_ref, left_ref):
+def pack_edges(tile_of, k, right_ref, left_ref):
     pair = lanes() // 2
     for back, out in ((True, right_ref), (False, left_ref)):
         acc = jnp.zeros((8, WIDTH), jnp.float32)
@@ -97,11 +97,24 @@
                 tile = tile_of(j, r)
                 moved = tile if shift == 0 else pltpu.roll(tile, shift, 1)
                 acc = jnp.where(pair == place, moved, acc)
-        out[0] = acc
-
-
-def pack_kernel(q_ref, right_ref, left_ref):
-    pack_edges(lambda j, r: q_ref[0, j, 8 * r : 8 * r + 8, :], right_ref, left_ref)
+        out[k] = acc
+
+
+def pack_kernel(spec_ref, copy_ref, right_ref, left_ref, arrived):
+    bands = copy_ref.shape[0]
+
+    def fetch(k):
+        return pltpu.make_async_copy(spec_ref.at[k], copy_ref.at[k], arrived.at[k])
+
+    for k in range(bands):
+        fetch(k).start()
+
+    def band(k, carry):
+        fetch(k).wait()
+        pack_edges(lambda j, r: copy_ref[k, j, 8 * r : 8 * r + 8, :], k, right_ref, left_ref)
+        return carry
+
+    lax.fori_loop(0, bands, band, 0)
 
 
 def wind_drive_of(j, r, east_ref, north_ref, open_water):
@@ -165,7 +178,6 @@
 
 
 def source_kernel(
-    same,
     scal_ref,
     edge_ref,
     q_ref,
@@ -184,19 +196,31 @@
     x_ref,
     p_ref,
 ):
-    k = pl.program_id(0)
-    band = lax.axis_index("freq") * pl.num_programs(0) + k
+    bands = q_ref.shape[0]
+    sums_ref[...] = jnp.zeros_like(sums_ref)
+    for r in range(TILES):
+        water = jnp.where(land_ref[8 * r : 8 * r + 8, :] == 2, 0.0, 1.0)
+        for j in range(ND):
+            drive_ref[j, 8 * r : 8 * r + 8, :] = wind_drive_of(j, r, east_ref, north_ref, water)
+
+    def step(k, carry):
+        source_band(
+            k, lax.axis_index("freq") * bands + k, scal_ref, edge_ref, q_ref, spec_ref,
+            from_left_ref, from_right_ref, own_right_ref, own_left_ref, land_ref, rows_ref,
+            out_ref, sums_ref, drive_ref, x_ref, p_ref,
+        )
+        return carry
+
+    lax.fori_loop(0, bands, step, 0)
+
+
+def source_band(
+    k, band, scal_ref, edge_ref, q_ref, spec_ref,
+    from_left_ref, from_right_ref, own_right_ref, own_left_ref, land_ref, rows_ref,
+    out_ref, sums_ref, drive_ref, x_ref, p_ref,
+):
     base = band * STRIDE
     lane = lanes()
-
-    @pl.when(k == 0)
-    def _():
-        sums_ref[...] = jnp.zeros_like(sums_ref)
-        for r in range(TILES):
-            water = jnp.where(land_ref[8 * r : 8 * r + 8, :] == 2, 0.0, 1.0)
-            for j in range(ND):
-                drive_ref[j, 8 * r : 8 * r + 8, :] = wind_drive_of(j, r, east_ref, north_ref, water)
-
     gap_right = from_left_ref[k] - own_right_ref[k]
     gap_left = from_right_ref[k] - own_left_ref[k]
     fix_back = edge_ref[band, 0:1, :] * gap_right + edge_ref[band, 1:2, :] * pltpu.roll(
@@ -219,7 +243,7 @@
         back = BACK_LON[j]
         lead = 8 if BACK_LAT[j] else 0
         for r in range(TILES):
-            q = q_ref[0, j, 8 * r : 8 * r + 8, :]
+            q = q_ref[k, j, 8 * r : 8 * r + 8, :]
             one = pltpu.roll(q, 1 if back else WIDTH - 1, 1)
             two = pltpu.roll(q, 2 if back else WIDTH - 2, 1)
             place = 2 * (TILES * RANK[j] + r)
@@ -240,7 +264,7 @@
                 + d1 * x_ref[j, at + sign : at + sign + 8, :]
                 + d2 * x_ref[j, at + 2 * sign : at + 2 * sign + 8, :]
             )
-            spec = (q_ref if same else spec_ref)[0, j, 8 * r : 8 * r + 8, :]
+            spec = spec_ref[k, j, 8 * r : 8 * r + 8, :]
             y = jnp.where(held[r], spec, jnp.maximum(y, 0.0)) * sea[r]
             p_ref[j, 8 * r : 8 * r + 8, :] = y
             slope[r] = slope[r] + y
@@ -259,7 +283,7 @@
             lower = sums_ref[j, rows, :]
             rate = excess * scal_ref[extra] + lower * scal_ref[extra + 1]
             sums_ref[j, rows, :] = lower + excess
-            out_ref[0, j, rows, :] = p_ref[j, rows, :] * jnp.exp2(rate)
+            out_ref[k, j, rows, :] = p_ref[j, rows, :] * jnp.exp2(rate)
 
 
 def pair_kernel(sums_ref, other_ref, out_ref):
@@ -284,53 +308,60 @@
     out_ref,
     *refs,
 ):
-    rate_ref = refs[-1]
-    k = pl.program_id(0)
+    rate_ref = refs[2]
+    bands = part_ref.shape[0]
     freq = lax.axis_index("freq")
-    band = freq * pl.num_programs(0) + k
-
-    @pl.when(k == 0)
-    def _():
-        core = freq % 2
-        odd = jnp.where(core == 1, 1.0, 0.0)
-        upper = jnp.where(freq >= 2, 1.0, 0.0)
-        for r in range(TILES):
+    core = freq % 2
+    odd = jnp.where(core == 1, 1.0, 0.0)
+    upper = jnp.where(freq >= 2, 1.0, 0.0)
+    for r in range(TILES):
+        rows = slice(8 * r, 8 * r + 8)
+        ice = jnp.where(land_ref[rows, :] == 2, 1.0, 0.0)
+        slope = (sums_ref[ND, rows, :] + other_ref[ND, rows, :]) + mine_ref[HALF, rows, :]
+        stress = (sums_ref[ND + 1, rows, :] + other_ref[ND + 1, rows, :]) + mine_ref[
+            HALF + 1, rows, :
+        ]
+        if last:
+            refs[0][rows, :] = slope
+        gain = GROWTH * (1.0 + stress / (stress + 1.0))
+        damp = SWELL_DAMP * (slope / (slope + 1.0)) + ICE_DAMP * ice
+        for j in range(ND):
+            local = j % HALF
+            near, far = mine_ref[local, rows, :], rest_ref[local, rows, :]
+            in_mine = core == (0 if j < HALF else 1)
+            lower = odd * other_ref[j, rows, :] + upper * jnp.where(in_mine, near, far)
+            drive = wind_drive_of(j, r, east_ref, north_ref, 1.0 - ice)
+            rate_ref[j, rows, :] = gain * drive - damp - (CUMULATIVE / NF) * lower
+
+    if last:
+        field_ref, sent = refs[3], refs[4]
+
+        def send(k):
+            return pltpu.make_async_copy(field_ref.at[k], out_ref.at[k], sent.at[k])
+
+    def step(k, carry):
+        root = scal_ref[(freq * bands + k) * STRIDE + 6 * ND + 4]
+        target = field_ref if last else out_ref
+
+        def tile(j, r):
             rows = slice(8 * r, 8 * r + 8)
-            ice = jnp.where(land_ref[rows, :] == 2, 1.0, 0.0)
-            slope = (sums_ref[ND, rows, :] + other_ref[ND, rows, :]) + mine_ref[HALF, rows, :]
-            stress = (sums_ref[ND + 1, rows, :] + other_ref[ND + 1, rows, :]) + mine_ref[
-                HALF + 1, rows, :
-            ]
-            if last:
-                refs[0][rows, :] = slope
-            gain = GROWTH * (1.0 + stress / (stress + 1.0))
-            damp = SWELL_DAMP * (slope / (slope + 1.0)) + ICE_DAMP * ice
+            value = part_ref[k, j, rows, :] * jnp.exp2(rate_ref[j, rows, :] * root)
+            target[k, j, rows, :] = value
+            return value
+
+        if last:
             for j in range(ND):
-                local = j % HALF
-                near, far = mine_ref[local, rows, :], rest_ref[local, rows, :]
-                in_mine = core == (0 if j < HALF else 1)
-                lower = odd * other_ref[j, rows, :] + upper * jnp.where(in_mine, near, far)
-                drive = wind_drive_of(j, r, east_ref, north_ref, 1.0 - ice)
-                rate_ref[j, rows, :] = gain * drive - damp - (CUMULATIVE / NF) * lower
-
-    root = scal_ref[band * STRIDE + 6 * ND + 4]
-
-    def tile(j, r):
-        rows = slice(8 * r, 8 * r + 8)
-        value = part_ref[0, j, rows, :] * jnp.exp2(rate_ref[j, rows, :] * root)
-        out_ref[0, j, rows, :] = value
-        return value
-
+                for r in range(TILES):
+                    tile(j, r)
+            send(k).start()
+        else:
+            pack_edges(tile, k, refs[0], refs[1])
+        return carry
+
+    lax.fori_loop(0, bands, step, 0)
     if last:
-        for j in range(ND):
-            for r in range(TILES):
-                tile(j, r)
-    else:
-        pack_edges(tile, refs[0], refs[1])
-
-
-def whole(shape):
-    return pl.BlockSpec(shape, lambda k: (0,) * len(shape))
+        for k in range(bands):
+            send(k).wait()
 
 
 def per_device(spectrum, east_wind, north_wind, land_sea, edge_rows):
@@ -343,42 +374,34 @@
     edges = jax.ShapeDtypeStruct((bands, 8, WIDTH), f32)
     sums = jax.ShapeDtypeStruct((ND + 2, LAT, WIDTH), f32)
     halves = jax.ShapeDtypeStruct((HALF + 2, LAT, WIDTH), f32)
-    plane = (LAT, WIDTH)
-    band_spec = pl.BlockSpec((1, ND, LAT, WIDTH), lambda k: (k, 0, 0, 0))
-    edge_spec = pl.BlockSpec((1, 8, WIDTH), lambda k: (k, 0, 0))
+    plane = jax.ShapeDtypeStruct((LAT, WIDTH), f32)
     smem = pl.BlockSpec(memory_space=pltpu.SMEM)
-    params = pltpu.CompilerParams(
-        dimension_semantics=("arbitrary",), vmem_limit_bytes=40 * 1024 * 1024
-    )
+    vmem = pl.BlockSpec(memory_space=pltpu.VMEM)
+    hbm = pl.BlockSpec(memory_space=pltpu.HBM)
+    params = pltpu.CompilerParams(vmem_limit_bytes=24 * 1024 * 1024)
     scalars, edge_table = jnp.asarray(SCALARS), jnp.asarray(EDGE)
     swap_core = [(0, 1), (1, 0), (2, 3), (3, 2)]
     swap_chip = [(0, 2), (2, 0), (1, 3), (3, 1)]
 
-    right, left = pl.pallas_call(
+    spectrum, right, left = pl.pallas_call(
         pack_kernel,
-        grid=(bands,),
-        in_specs=[band_spec],
-        out_specs=[edge_spec, edge_spec],
-        out_shape=[edges, edges],
+        in_specs=[hbm],
+        out_specs=[vmem] * 3,
+        out_shape=[field, edges, edges],
+        scratch_shapes=[pltpu.SemaphoreType.DMA((bands,))],
         compiler_params=params,
         name="pack_columns",
-    )(spectrum)
+    )(pltpu.with_memory_space_constraint(spectrum, pltpu.HBM))
 
     energy = spectrum
     for step in range(STEPS):
         last = step == STEPS - 1
         from_left = lax.ppermute(right, "lon", [(i, (i + 1) % ring) for i in range(ring)])
         from_right = lax.ppermute(left, "lon", [((i + 1) % ring, i) for i in range(ring)])
-        same = step == 0
-        source = pl.BlockSpec((1, 8, 8, WIDTH), lambda k: (0, 0, 0, 0)) if same else band_spec
         part, mine = pl.pallas_call(
-            functools.partial(source_kernel, same),
-            grid=(bands,),
-            in_specs=[smem, whole(EDGE.shape), band_spec, source]
-            + [whole((bands, 8, WIDTH))] * 4
-            + [whole(plane)] * 3
-            + [whole((2, WIDTH))],
-            out_specs=[band_spec, whole(sums.shape)],
+            source_kernel,
+            in_specs=[smem] + [vmem] * 11,
+            out_specs=[vmem] * 2,
             out_shape=[field, sums],
             scratch_shapes=[
                 pltpu.VMEM((ND, LAT, WIDTH), f32),
@@ -394,27 +417,24 @@
         other = lax.ppermute(mine, "freq", swap_core)
         pair = pl.pallas_call(
             pair_kernel,
-            in_specs=[pl.BlockSpec(memory_space=pltpu.VMEM)] * 2,
-            out_specs=pl.BlockSpec(memory_space=pltpu.VMEM),
+            in_specs=[vmem] * 2,
+            out_specs=vmem,
             out_shape=halves,
+            compiler_params=params,
             name="pair_sums",
         )(mine, other)
         near = lax.ppermute(pair, "freq", swap_chip)
         far = lax.ppermute(near, "freq", swap_core)
+        scratch = [pltpu.VMEM((ND, LAT, WIDTH), f32)]
         if last:
-            more_specs, more_shapes = [whole(plane)], [jax.ShapeDtypeStruct(plane, f32)]
-        else:
-            more_specs, more_shapes = [edge_spec, edge_spec], [edges, edges]
+            scratch += [pltpu.VMEM(spectrum.shape, f32), pltpu.SemaphoreType.DMA((bands,))]
+        more = [plane, plane] if last else [edges, edges]
         energy, *more = pl.pallas_call(
             functools.partial(growth_kernel, last),
-            grid=(bands,),
-            in_specs=[smem, band_spec]
-            + [whole(sums.shape)] * 2
-            + [whole(halves.shape)] * 2
-            + [whole(plane)] * 3,
-            out_specs=[band_spec] + more_specs,
-            out_shape=[field] + more_shapes,
-            scratch_shapes=[pltpu.VMEM((ND, LAT, WIDTH), f32)],
+            in_specs=[smem] + [vmem] * 8,
+            out_specs=[hbm if last else vmem, vmem, vmem],
+            out_shape=[field] + more,
+            scratch_shapes=scratch,
             compiler_params=params,
             name="grow",
         )(scalars, part, mine, other, near, far, east_wind, north_wind, land_sea)

time: 89.5 us -> 64.5 us (0.72)
  local copies, waits for them, and re-layouts: 19.3 us -> 0.03 us
  Pallas kernels: 30.7 us -> 26 us
    unnamed x56 -> x12, local copies, waits for them, and re-layouts: 19.3 us -> 0.03 us
    pallas_call x7, Pallas kernels: 30.7 us -> 26 us  [the longest x2 16.6 us: per_device(): pl.pallas_call(source_kernel, in_specs=[smem] + [vmem] * 11, out_specs=[v...]
where the time goes in v2:
time: 64.5 us; the launch traced here: 64.3 us
  Pallas kernels  26 us (40%)
  waiting for transfers between devices  22.9 us (36%)
  starting transfers between devices  14.6 us (23%)
  between operations  0.77 us (1%)
    pallas_call x2, Pallas kernels, per_device(): pl.pallas_call(source_kernel, in_specs=[smem] + [vmem] * 11, out_specs=[v...  16.6 us
    ppermute x2, waiting for transfers between devices, per_device(): near = lax.ppermute(pair, 'freq', swap_chip)  12.6 us
    pallas_call x2, Pallas kernels, per_device(): pl.pallas_call(functools.partial(growth_kernel, last), in_specs=[smem] +...  6.73 us
    ppermute x2, starting transfers between devices, per_device(): lax.ppermute(left, 'lon', [((i + 1) % ring, i) for i in range(ring)])  6.52 us
    ppermute x2, starting transfers between devices, per_device(): lax.ppermute(right, 'lon', [(i, (i + 1) % ring) for i in range(ring)])  4.46 us
    ppermute x2, waiting for transfers between devices, per_device(): lax.ppermute(right, 'lon', [(i, (i + 1) % ring) for i in range(ring)])  3.66 us
    ppermute x2, waiting for transfers between devices, per_device(): other = lax.ppermute(mine, 'freq', swap_core)  3.63 us
    ppermute x2, starting transfers between devices, per_device(): near = lax.ppermute(pair, 'freq', swap_chip)  3.49 us
  transfers between devices with their start and end apart: 10, of which 8 were waited for; matrix products, arithmetic and copies ran while one was open for 0% of the time, Pallas kernels for 0%

profile of v2, /device:TPU:0, one launch (start us, length us, event | category | flops | bytes accessed | tf_op | source)
XLA Modules:
  0.0 64.3 jit_solution(10391008670736542308)
XLA Ops:
  0.6 0.0 copy-start
  0.6 0.0 copy-start.1
  0.7 0.0 copy-start.4
  0.7 0.0 copy-start.3
  0.7 0.0 copy-start.2
  0.7 0.0 copy-start.5
  0.7 2.6 %pack_columns.1 = (f32[8,36,24,128]{3,2,1,0:T(8,128)S(1)}, f32[8,8,128]{2,1,0:T(8,128)S(1)}, f32[8,8,128]{2,1,0:T(8,128)S(1)}) custom-call(f32[8,36,24,128]{3,2,1,0:T(8,128)} %spec_ref.1), custom_call_target="tpu_custom_call" | custom-call | tf_op jit(solution)/shard_map/pack_columns/pallas_call | solution.py:386
  3.3 3.0 %collective-permute-start = (f32[8,8,128]{2,1,0:T(8,128)S(1)}, f32[8,8,128]{2,1,0:T(8,128)S(1)}, u32[]{:S(2)}, u32[]{:S(2)}) collective-permute-start(f32[8,8,128]{2,1,0:T(8,128)S(1)} %get-tuple-element.15.own_right_ref), channel_id=1, source_target_pairs={{0,4},{4,8},{8,12},{12,16},{16,20},{20,24},{24,28},{28,0},{1,5},{5... | collective-permute-start | bytes 98312 | tf_op jit(solution)/shard_map/ppermute | solution.py:399
  6.3 3.1 %collective-permute-start.1 = (f32[8,8,128]{2,1,0:T(8,128)S(1)}, f32[8,8,128]{2,1,0:T(8,128)S(1)}, u32[]{:S(2)}, u32[]{:S(2)}) collective-permute-start(f32[8,8,128]{2,1,0:T(8,128)S(1)} %get-tuple-element.16.own_left_ref), channel_id=1, source_target_pairs={{4,0},{8,4},{12,8},{16,12},{20,16},{24,20},{28,24},{0,28},{5,1},{9... | collective-permute-start | bytes 98312 | tf_op jit(solution)/shard_map/ppermute | solution.py:400
  9.4 1.8 %collective-permute-done.from_left_ref = f32[8,8,128]{2,1,0:T(8,128)S(1)} collective-permute-done((f32[8,8,128]{2,1,0:T(8,128)S(1)}, f32[8,8,128]{2,1,0:T(8,128)S(1)}, u32[]{:S(2)}, u32[]{:S(2)}) %collective-permute-start) | collective-permute-done | bytes 32800 | tf_op jit(solution)/shard_map/ppermute | solution.py:399
  11.2 0.0 collective-permute-done.1.from_right_ref
  11.2 0.0 copy-done.1
  11.3 8.3 %propagate_and_break.2 = (f32[8,36,24,128]{3,2,1,0:T(8,128)S(1)}, f32[38,24,128]{2,1,0:T(8,128)S(1)}) custom-call(f32[7168]{0:T(1024)S(1)} %copy-done, f32[32,4,128]{2,1,0:T(4,128)S(1)} %copy-done.1, f32[8,36,24,128]{3,2,1,0:T(8,128)S(1)} %get-tuple-element.14.q_ref.spec_ref, f32[8,36,24,128]{3,2,1,0:T(8,128)S(1)} %get-tuple-element.14.q_ref.spec_ref, ...), custom_call_target="tpu_custom_call" | custom-call | tf_op jit(solution)/shard_map/propagate_and_break/pallas_call | solution.py:401
  19.6 0.1 collective-permute-start.2
  19.6 1.8 %collective-permute-done.2.other_ref = f32[38,24,128]{2,1,0:T(8,128)S(1)} collective-permute-done((f32[38,24,128]{2,1,0:T(8,128)S(1)}, f32[38,24,128]{2,1,0:T(8,128)S(1)}, u32[]{:S(2)}, u32[]{:S(2)}) %collective-permute-start.2) | collective-permute-done | bytes 466976 | tf_op jit(solution)/shard_map/ppermute | solution.py:417
  21.5 1.8 %collective-permute-start.3 = (f32[20,24,128]{2,1,0:T(8,128)S(1)}, f32[20,24,128]{2,1,0:T(8,128)S(1)}, u32[]{:S(2)}, u32[]{:S(2)}) collective-permute-start(f32[20,24,128]{2,1,0:T(8,128)S(1)} %pair_sums.2), channel_id=1, source_target_pairs={{0,2},{2,0},{1,3},{3,1},{4,6},{6,4},{5,7},{7,5},{8,10},{10,8},{9,1... | collective-permute-start | bytes 737288 | tf_op jit(solution)/shard_map/ppermute | solution.py:426
  23.3 6.3 %collective-permute-done.3.mine_ref = f32[20,24,128]{2,1,0:T(8,128)S(1)} collective-permute-done((f32[20,24,128]{2,1,0:T(8,128)S(1)}, f32[20,24,128]{2,1,0:T(8,128)S(1)}, u32[]{:S(2)}, u32[]{:S(2)}) %collective-permute-start.3) | collective-permute-done | bytes 245792 | tf_op jit(solution)/shard_map/ppermute | solution.py:426
  29.5 0.0 collective-permute-start.4
  29.6 1.5 %collective-permute-done.4.rest_ref = f32[20,24,128]{2,1,0:T(8,128)S(1)} collective-permute-done((f32[20,24,128]{2,1,0:T(8,128)S(1)}, f32[20,24,128]{2,1,0:T(8,128)S(1)}, u32[]{:S(2)}, u32[]{:S(2)}) %collective-permute-start.4) | collective-permute-done | bytes 245792 | tf_op jit(solution)/shard_map/ppermute | solution.py:427
  31.1 2.9 %grow.2 = (f32[8,36,24,128]{3,2,1,0:T(8,128)S(1)}, f32[8,8,128]{2,1,0:T(8,128)S(1)}, f32[8,8,128]{2,1,0:T(8,128)S(1)}) custom-call(f32[7168]{0:T(1024)S(1)} %copy-done, f32[8,36,24,128]{3,2,1,0:T(8,128)S(1)} %get-tuple-element.17.part_ref, f32[38,24,128]{2,1,0:T(8,128)S(1)} %get-tuple-element.18.sums_ref, ...), custom_call_target="tpu_custom_call" | custom-call | tf_op jit(solution)/shard_map/grow/pallas_call | solution.py:432
  34.0 1.5 %collective-permute-start.5 = (f32[8,8,128]{2,1,0:T(8,128)S(1)}, f32[8,8,128]{2,1,0:T(8,128)S(1)}, u32[]{:S(2)}, u32[]{:S(2)}) collective-permute-start(f32[8,8,128]{2,1,0:T(8,128)S(1)} %get-tuple-element.20.own_right_ref), channel_id=1, source_target_pairs={{0,4},{4,8},{8,12},{12,16},{16,20},{20,24},{24,28},{28,0},{1,5},{5... | collective-permute-start | bytes 98312 | tf_op jit(solution)/shard_map/ppermute | solution.py:399
  35.5 3.4 %collective-permute-start.6 = (f32[8,8,128]{2,1,0:T(8,128)S(1)}, f32[8,8,128]{2,1,0:T(8,128)S(1)}, u32[]{:S(2)}, u32[]{:S(2)}) collective-permute-start(f32[8,8,128]{2,1,0:T(8,128)S(1)} %get-tuple-element.21.own_left_ref), channel_id=1, source_target_pairs={{4,0},{8,4},{12,8},{16,12},{20,16},{24,20},{28,24},{0,28},{5,1},{9... | collective-permute-start | bytes 98312 | tf_op jit(solution)/shard_map/ppermute | solution.py:400
  38.9 1.8 %collective-permute-done.5.from_left_ref = f32[8,8,128]{2,1,0:T(8,128)S(1)} collective-permute-done((f32[8,8,128]{2,1,0:T(8,128)S(1)}, f32[8,8,128]{2,1,0:T(8,128)S(1)}, u32[]{:S(2)}, u32[]{:S(2)}) %collective-permute-start.5) | collective-permute-done | bytes 32800 | tf_op jit(solution)/shard_map/ppermute | solution.py:399
  40.7 0.0 collective-permute-done.6.from_right_ref
  40.7 8.3 %propagate_and_break.3 = (f32[8,36,24,128]{3,2,1,0:T(8,128)S(1)}, f32[38,24,128]{2,1,0:T(8,128)S(1)}) custom-call(f32[7168]{0:T(1024)S(1)} %copy-done, f32[32,4,128]{2,1,0:T(4,128)S(1)} %copy-done.1, f32[8,36,24,128]{3,2,1,0:T(8,128)S(1)} %get-tuple-element.19.q_ref, f32[8,36,24,128]{3,2,1,0:T(8,128)S(1)} %get-tuple-element.14.q_ref.spec_ref, ...), custom_call_target="tpu_custom_call" | custom-call | tf_op jit(solution)/shard_map/propagate_and_break/pallas_call | solution.py:401
  49.0 0.1 collective-permute-start.7
  49.1 1.8 %collective-permute-done.7.other_ref = f32[38,24,128]{2,1,0:T(8,128)S(1)} collective-permute-done((f32[38,24,128]{2,1,0:T(8,128)S(1)}, f32[38,24,128]{2,1,0:T(8,128)S(1)}, u32[]{:S(2)}, u32[]{:S(2)}) %collective-permute-start.7) | collective-permute-done | bytes 466976 | tf_op jit(solution)/shard_map/ppermute | solution.py:417
  51.0 1.7 %collective-permute-start.8 = (f32[20,24,128]{2,1,0:T(8,128)S(1)}, f32[20,24,128]{2,1,0:T(8,128)S(1)}, u32[]{:S(2)}, u32[]{:S(2)}) collective-permute-start(f32[20,24,128]{2,1,0:T(8,128)S(1)} %pair_sums.3), channel_id=1, source_target_pairs={{0,2},{2,0},{1,3},{3,1},{4,6},{6,4},{5,7},{7,5},{8,10},{10,8},{9,1... | collective-permute-start | bytes 737288 | tf_op jit(solution)/shard_map/ppermute | solution.py:426
  52.7 6.3 %collective-permute-done.8.mine_ref = f32[20,24,128]{2,1,0:T(8,128)S(1)} collective-permute-done((f32[20,24,128]{2,1,0:T(8,128)S(1)}, f32[20,24,128]{2,1,0:T(8,128)S(1)}, u32[]{:S(2)}, u32[]{:S(2)}) %collective-permute-start.8) | collective-permute-done | bytes 245792 | tf_op jit(solution)/shard_map/ppermute | solution.py:426
  59.0 0.0 collective-permute-start.9
  59.0 1.5 %collective-permute-done.9.rest_ref = f32[20,24,128]{2,1,0:T(8,128)S(1)} collective-permute-done((f32[20,24,128]{2,1,0:T(8,128)S(1)}, f32[20,24,128]{2,1,0:T(8,128)S(1)}, u32[]{:S(2)}, u32[]{:S(2)}) %collective-permute-start.9) | collective-permute-done | bytes 245792 | tf_op jit(solution)/shard_map/ppermute | solution.py:427
  60.5 3.8 %grow.3 = (f32[8,36,24,128]{3,2,1,0:T(8,128)}, f32[24,128]{1,0:T(8,128)}, f32[24,128]{1,0:T(8,128)}) custom-call(f32[7168]{0:T(1024)S(1)} %copy-done, f32[8,36,24,128]{3,2,1,0:T(8,128)S(1)} %get-tuple-element.22.part_ref, f32[38,24,128]{2,1,0:T(8,128)S(1)} %get-tuple-element.23.sums_ref, f32[38,24,128]{2,1,0:T(8,128)S(1)} %collective-permute-done.7.other_ref, ...), custom_call_target="tpu_custom_call" | custom-call | tf_op jit(solution)/shard_map/grow/pallas_call | solution.py:432
  (7 shorter events, 0.1 us)
Async XLA Ops:
  0.6 10.6 %copy-start = (f32[7168]{0:T(1024)S(1)}, f32[7168]{0:T(1024)}, u32[]{:S(2)}) copy-start(f32[7168]{0:T(1024)} %constant.4.clone.scal_ref) | copy-start | bytes 86020
  0.6 10.6 %copy-start.1 = (f32[32,4,128]{2,1,0:T(4,128)S(1)}, f32[32,4,128]{2,1,0:T(4,128)}, u32[]{:S(2)}) copy-start(f32[32,4,128]{2,1,0:T(4,128)} %constant.5.clone.edge_ref) | copy-start | bytes 196612
  0.7 10.6 %copy-start.4 = (s32[24,128]{1,0:T(8,128)S(1)}, s32[24,128]{1,0:T(8,128)}, u32[]{:S(2)}) copy-start(s32[24,128]{1,0:T(8,128)} %land_ref.7) | copy-start | bytes 36868
  0.7 10.6 %copy-start.3 = (f32[24,128]{1,0:T(8,128)S(1)}, f32[24,128]{1,0:T(8,128)}, u32[]{:S(2)}) copy-start(f32[24,128]{1,0:T(8,128)} %north_ref.7) | copy-start | bytes 36868
  0.7 10.6 %copy-start.2 = (f32[24,128]{1,0:T(8,128)S(1)}, f32[24,128]{1,0:T(8,128)}, u32[]{:S(2)}) copy-start(f32[24,128]{1,0:T(8,128)} %east_ref.7) | copy-start | bytes 36868
  0.7 10.6 %copy-start.5 = (s32[2,128]{1,0:T(2,128)S(1)}, s32[2,128]{1,0:T(2,128)}, u32[]{:S(2)}) copy-start(s32[2,128]{1,0:T(2,128)} %rows_ref.3) | copy-start | bytes 3076
  3.3 7.9 %collective-permute-start = (f32[8,8,128]{2,1,0:T(8,128)S(1)}, f32[8,8,128]{2,1,0:T(8,128)S(1)}, u32[]{:S(2)}, u32[]{:S(2)}) collective-permute-start(f32[8,8,128]{2,1,0:T(8,128)S(1)} %get-tuple-element.15.own_right_ref), channel_id=1, source_target_pairs={{0,4},{4,8},{8,12},{12,16},{16,20},{20,24},{24,28},{28,0},{1,5},{5... | collective-permute-start | bytes 98312 | tf_op jit(solution)/shard_map/ppermute | solution.py:399
  6.3 4.9 %collective-permute-start.1 = (f32[8,8,128]{2,1,0:T(8,128)S(1)}, f32[8,8,128]{2,1,0:T(8,128)S(1)}, u32[]{:S(2)}, u32[]{:S(2)}) collective-permute-start(f32[8,8,128]{2,1,0:T(8,128)S(1)} %get-tuple-element.16.own_left_ref), channel_id=1, source_target_pairs={{4,0},{8,4},{12,8},{16,12},{20,16},{24,20},{28,24},{0,28},{5,1},{9... | collective-permute-start | bytes 98312 | tf_op jit(solution)/shard_map/ppermute | solution.py:400
  19.6 1.9 %collective-permute-start.2 = (f32[38,24,128]{2,1,0:T(8,128)S(1)}, f32[38,24,128]{2,1,0:T(8,128)S(1)}, u32[]{:S(2)}, u32[]{:S(2)}) collective-permute-start(f32[38,24,128]{2,1,0:T(8,128)S(1)} %get-tuple-element.18.sums_ref), channel_id=1, source_target_pairs={{0,1},{1,0},{2,3},{3,2},{4,5},{5,4},{6,7},{7,6},{8,9},{9,8},{10,11... | collective-permute-start | bytes 1400840 | tf_op jit(solution)/shard_map/ppermute | solution.py:417
  21.5 8.1 %collective-permute-start.3 = (f32[20,24,128]{2,1,0:T(8,128)S(1)}, f32[20,24,128]{2,1,0:T(8,128)S(1)}, u32[]{:S(2)}, u32[]{:S(2)}) collective-permute-start(f32[20,24,128]{2,1,0:T(8,128)S(1)} %pair_sums.2), channel_id=1, source_target_pairs={{0,2},{2,0},{1,3},{3,1},{4,6},{6,4},{5,7},{7,5},{8,10},{10,8},{9,1... | collective-permute-start | bytes 737288 | tf_op jit(solution)/shard_map/ppermute | solution.py:426
  29.5 1.5 %collective-permute-start.4 = (f32[20,24,128]{2,1,0:T(8,128)S(1)}, f32[20,24,128]{2,1,0:T(8,128)S(1)}, u32[]{:S(2)}, u32[]{:S(2)}) collective-permute-start(f32[20,24,128]{2,1,0:T(8,128)S(1)} %collective-permute-done.3.mine_ref), channel_id=1, source_target_pairs={{0,1},{1,0},{2,3},{3,2},{4,5},{5,4},{6,7},{7,6},{8,9},{9,8},{10,11... | collective-permute-start | bytes 737288 | tf_op jit(solution)/shard_map/ppermute | solution.py:427
  34.0 6.7 %collective-permute-start.5 = (f32[8,8,128]{2,1,0:T(8,128)S(1)}, f32[8,8,128]{2,1,0:T(8,128)S(1)}, u32[]{:S(2)}, u32[]{:S(2)}) collective-permute-start(f32[8,8,128]{2,1,0:T(8,128)S(1)} %get-tuple-element.20.own_right_ref), channel_id=1, source_target_pairs={{0,4},{4,8},{8,12},{12,16},{16,20},{20,24},{24,28},{28,0},{1,5},{5... | collective-permute-start | bytes 98312 | tf_op jit(solution)/shard_map/ppermute | solution.py:399
  35.5 5.3 %collective-permute-start.6 = (f32[8,8,128]{2,1,0:T(8,128)S(1)}, f32[8,8,128]{2,1,0:T(8,128)S(1)}, u32[]{:S(2)}, u32[]{:S(2)}) collective-permute-start(f32[8,8,128]{2,1,0:T(8,128)S(1)} %get-tuple-element.21.own_left_ref), channel_id=1, source_target_pairs={{4,0},{8,4},{12,8},{16,12},{20,16},{24,20},{28,24},{0,28},{5,1},{9... | collective-permute-start | bytes 98312 | tf_op jit(solution)/shard_map/ppermute | solution.py:400
  49.0 1.9 %collective-permute-start.7 = (f32[38,24,128]{2,1,0:T(8,128)S(1)}, f32[38,24,128]{2,1,0:T(8,128)S(1)}, u32[]{:S(2)}, u32[]{:S(2)}) collective-permute-start(f32[38,24,128]{2,1,0:T(8,128)S(1)} %get-tuple-element.23.sums_ref), channel_id=1, source_target_pairs={{0,1},{1,0},{2,3},{3,2},{4,5},{5,4},{6,7},{7,6},{8,9},{9,8},{10,11... | collective-permute-start | bytes 1400840 | tf_op jit(solution)/shard_map/ppermute | solution.py:417
  51.0 8.1 %collective-permute-start.8 = (f32[20,24,128]{2,1,0:T(8,128)S(1)}, f32[20,24,128]{2,1,0:T(8,128)S(1)}, u32[]{:S(2)}, u32[]{:S(2)}) collective-permute-start(f32[20,24,128]{2,1,0:T(8,128)S(1)} %pair_sums.3), channel_id=1, source_target_pairs={{0,2},{2,0},{1,3},{3,1},{4,6},{6,4},{5,7},{7,5},{8,10},{10,8},{9,1... | collective-permute-start | bytes 737288 | tf_op jit(solution)/shard_map/ppermute | solution.py:426
  59.0 1.5 %collective-permute-start.9 = (f32[20,24,128]{2,1,0:T(8,128)S(1)}, f32[20,24,128]{2,1,0:T(8,128)S(1)}, u32[]{:S(2)}, u32[]{:S(2)}) collective-permute-start(f32[20,24,128]{2,1,0:T(8,128)S(1)} %collective-permute-done.8.mine_ref), channel_id=1, source_target_pairs={{0,1},{1,0},{2,3},{3,2},{4,5},{5,4},{6,7},{7,6},{8,9},{9,8},{10,11... | collective-permute-start | bytes 737288 | tf_op jit(solution)/shard_map/ppermute | solution.py:427

commit v3 on v2

v3 whole, which is shorter than its diff:
```python
import functools
import math

import jax
import jax.numpy as jnp
import numpy as np
from jax import lax
from jax.experimental import pallas as pl
from jax.experimental.pallas import tpu as pltpu
from jax.sharding import PartitionSpec as P

NF = 32
STEPS = 2

COURANT_MAX = 0.9
FREQ_RATIO = 1.1
WIND_REF = 8.0
WIND_CLIP = 2.0
GROWTH = 0.01
BREAKING = 0.3
SATURATION_REF = 0.4
CUMULATIVE = 2.0
SWELL_DAMP = 0.1
ICE_DAMP = 0.5

ND = 36
HALF = ND // 2
QUARTER = ND // 4
DTHETA = 2.0 * math.pi / ND
LOG2E = 1.0 / math.log(2.0)
ROOT_REF = math.sqrt(SATURATION_REF)
TILES = 3
LAT = 8 * TILES
WIDTH = 128
STRIDE = 6 * ND + 8

ANGLES = np.arange(ND) * DTHETA
COS = np.cos(ANGLES)
SIN = np.sin(ANGLES)
COS2 = np.cos(2.0 * ANGLES)
SIN2 = np.sin(2.0 * ANGLES)
BACK_LON = [bool(c >= 0.0) for c in COS]
BACK_LAT = [bool(s >= 0.0) for s in SIN]
RANK = [sum(BACK_LON[:j]) if BACK_LON[j] else j - sum(BACK_LON[:j]) for j in range(ND)]


def one_sided(courant):
    c = np.abs(courant)
    return 1.0 - 1.5 * c + 0.5 * c * c, 2.0 * c - c * c, 0.5 * c * c - 0.5 * c


GROUP = 32
BANDS = 8
PACKED = ND + 1
SENT = HALF + QUARTER + 1
FIELDS = 5
SLOPE_AT = ND * TILES
STRESS_AT = SLOPE_AT + TILES
PACKED_AT = STRESS_AT + TILES
PACKED_SUMS = 5
SUMS = PACKED_AT + PACKED_SUMS
HALF_SUMS = HALF * TILES + 2 * TILES + PACKED_SUMS


def make_tables():
    ratios = FREQ_RATIO ** np.arange(NF)
    root = np.sqrt(ratios)
    lon = one_sided(COURANT_MAX * COS[None, :] / ratios[:, None])
    lat = one_sided(0.5 * COURANT_MAX * SIN[None, :] / ratios[:, None])
    scalars = np.zeros((NF, STRIDE))
    for i in range(3):
        scalars[:, i : 6 * ND : 6] = lon[i]
        scalars[:, 3 + i : 6 * ND : 6] = lat[i]
    rest = [
        -BREAKING / SATURATION_REF * root,
        -CUMULATIVE / NF * root,
        ratios * ratios * DTHETA / np.sum(ratios * ratios),
        ratios * root * DTHETA / np.sum(ratios * root),
        root,
    ]
    packed = np.zeros((NF // BANDS, PACKED, 8, WIDTH))
    for i, value in enumerate(rest):
        scalars[:, 6 * ND + i] = value
    for lane in range(TILES * GROUP):
        slot, k = lane % 4, lane // 4 % BANDS
        for i in range(3):
            packed[:, :ND, i, lane] = lon[i][k::BANDS]
            packed[:, :ND, 3 + i, lane] = lat[i][k::BANDS]
        for j in range(ND):
            if slot == (0 if BACK_LON[j] else 3):
                packed[:, j, 6, lane] = lon[1][k::BANDS, j]
        for i, value in enumerate(rest):
            packed[:, ND, i, lane] = value[k::BANDS]
    return scalars.reshape(-1).astype(np.float32), packed.astype(np.float32)


SCALARS, PACKED_TABLE = make_tables()


def lanes():
    return lax.broadcasted_iota(jnp.int32, (8, WIDTH), 1)


def sublanes():
    return lax.broadcasted_iota(jnp.int32, (8, WIDTH), 0)


def turn(tile, shift):
    shift = shift % WIDTH
    return tile if shift == 0 else pltpu.roll(tile, shift, 1)


def tile_rows(r):
    return slice(8 * r, 8 * r + 8)


CHUNK = 4


def pack_kernel(spec_ref, *refs):
    sources, (copy_ref, right_ref, left_ref), held_refs = refs[:4], refs[4:7], refs[7:11]
    arrived = refs[11]

    def fetch(c):
        part = pl.ds(CHUNK * c, CHUNK)
        return pltpu.make_async_copy(spec_ref.at[:, part], copy_ref.at[:, part], arrived.at[c])

    small = [
        pltpu.make_async_copy(source, target, arrived.at[ND // CHUNK + i])
        for i, (source, target) in enumerate(zip(sources, held_refs))
    ]
    for c in range(ND // CHUNK):
        fetch(c).start()
    for copy in small:
        copy.start()
    lane = lanes()
    zero = jnp.zeros((8, WIDTH), jnp.float32)
    held = [zero, zero]
    for j in range(ND):
        if j % CHUNK == 0:
            fetch(j // CHUNK).wait()
        wide, narrow = (right_ref, left_ref) if BACK_LON[j] else (left_ref, right_ref)
        half = RANK[j] % 2
        four = zero
        two = zero
        for r in range(TILES):
            for k in range(BANDS):
                tile = copy_ref[k, j, tile_rows(r), :]
                place = GROUP * r + 4 * k
                first, pair = (WIDTH - 4, 0) if BACK_LON[j] else (0, WIDTH - 2)
                four = jnp.where(lane // 4 == place // 4, turn(tile, place - first), four)
                place = place + 2 * half
                two = jnp.where(lane // 2 == place // 2, turn(tile, place - pair), two)
        wide[RANK[j]] = four
        if half:
            slot = lane % 4 < 2
            two = jnp.where(slot, held[BACK_LON[j]], two)
            narrow[HALF + RANK[j] // 2] = two
        else:
            held[BACK_LON[j]] = two
    for copy in small:
        copy.wait()
    east_ref, north_ref, land_ref, rows_ref = held_refs
    fields = [
        [f(r) for r in range(TILES)]
        for f in (
            lambda r: east_ref[tile_rows(r), :],
            lambda r: north_ref[tile_rows(r), :],
            lambda r: land_ref[tile_rows(r), :].astype(jnp.float32),
            lambda r: jnp.broadcast_to(rows_ref[0:1, :].astype(jnp.float32), (8, WIDTH)),
            lambda r: jnp.broadcast_to(rows_ref[1:2, :].astype(jnp.float32), (8, WIDTH)),
        )
    ]
    to_right, to_left = zero, zero
    for i in range(FIELDS):
        for r in range(TILES):
            place = GROUP * r + 4 * i
            here = lane // 2 == place // 2
            to_right = jnp.where(here, turn(fields[i][r], place - (WIDTH - 2)), to_right)
            to_left = jnp.where(here, turn(fields[i][r], place), to_left)
    right_ref[SENT - 1] = to_right
    left_ref[SENT - 1] = to_left


def wind_drive_of(j, r, east_ref, north_ref, open_water):
    rows = tile_rows(r)
    along = float(COS[j]) * east_ref[rows, :] + float(SIN[j]) * north_ref[rows, :]
    drive = jnp.minimum(jnp.maximum(along, 0.0) / WIND_REF, WIND_CLIP)
    return drive * drive * open_water


def saturation_of(p):
    half = 0.5 * DTHETA
    diff = [p[b] - p[b + HALF] for b in range(HALF)]
    both = [p[b] + p[b + HALF] for b in range(HALF)]
    total = both[0]
    for b in range(1, HALF):
        total = total + both[b]
    total = total * (0.5 * half)
    fold = [both[b] - both[b + QUARTER] for b in range(QUARTER)]
    total_c = fold[0] * float(0.5 * half * COS2[0])
    total_s = None
    for b in range(1, QUARTER):
        total_c = total_c + fold[b] * float(0.5 * half * COS2[b])
        term = fold[b] * float(0.5 * half * SIN2[b])
        total_s = term if total_s is None else total_s + term
    diff = [d * half for d in diff]
    diff_c = [diff[b] * float(COS2[b]) for b in range(HALF)]
    diff_s = [diff[b] * float(SIN2[b]) for b in range(HALF)]

    def start(x):
        front = x[0]
        for b in range(1, QUARTER):
            front = front + x[b]
        rear = x[QUARTER]
        for b in range(QUARTER + 1, HALF):
            rear = rear + x[b]
        return 0.5 * (front - rear)

    win, win_c, win_s = start(diff), start(diff_c), start(diff_s)
    out = [None] * ND
    level = [None] * HALF
    for a in range(QUARTER):
        turn = total_c * float(COS2[a])
        if a:
            turn = turn + total_s * float(SIN2[a])
        level[a] = total + turn
        level[a + QUARTER] = total - turn
    for a in range(HALF):
        odd = win + win_c * float(COS2[a])
        if a:
            odd = odd + win_s * float(SIN2[a])
        out[a] = level[a] + odd
        out[a + HALF] = level[a] - odd
        new = a + QUARTER
        if a + 1 < HALF:
            if new < HALF:
                win, win_c, win_s = win + diff[new], win_c + diff_c[new], win_s + diff_s[new]
            else:
                new -= HALF
                win, win_c, win_s = win - diff[new], win_c - diff_c[new], win_s - diff_s[new]
    return out


def drift_kernel(scal_ref, q_ref, out_ref, x_ref):
    bands = q_ref.shape[0]
    lane = lanes()
    one = jnp.ones((8, WIDTH), jnp.float32)
    inside = {
        (True, 1): jnp.where(lane >= 1, one, 0.0),
        (True, 2): jnp.where(lane >= 2, one, 0.0),
        (False, 1): jnp.where(lane < WIDTH - 1, one, 0.0),
        (False, 2): jnp.where(lane < WIDTH - 2, one, 0.0),
    }

    def band(k, carry):
        base = (lax.axis_index("freq") * bands + k) * STRIDE
        for j in range(ND):
            c0, c1, c2, d0, d1, d2 = (scal_ref[base + 6 * j + i] for i in range(6))
            side = 1 if BACK_LON[j] else -1
            c1 = c1 * inside[BACK_LON[j], 1]
            c2 = c2 * inside[BACK_LON[j], 2]
            lead = 8 if BACK_LAT[j] else 0
            for r in range(TILES):
                q = q_ref[k, j, tile_rows(r), :]
                x = c0 * q + c1 * turn(q, side) + c2 * turn(q, 2 * side)
                x_ref[j, lead + 8 * r : lead + 8 * r + 8, :] = x
                if BACK_LAT[j] and r == 0:
                    x_ref[j, 0:8, :] = jnp.broadcast_to(x[0:1, :], (8, WIDTH))
                if not BACK_LAT[j] and r == TILES - 1:
                    x_ref[j, LAT : LAT + 8, :] = jnp.broadcast_to(x[7:8, :], (8, WIDTH))
            sign = -1 if BACK_LAT[j] else 1
            for r in range(TILES):
                at = lead + 8 * r
                out_ref[k, j, tile_rows(r), :] = (
                    d0 * x_ref[j, at : at + 8, :]
                    + d1 * x_ref[j, at + sign : at + sign + 8, :]
                    + d2 * x_ref[j, at + 2 * sign : at + 2 * sign + 8, :]
                )
        return carry

    lax.fori_loop(0, bands, band, 0)


def packed_lat(j, x, d0, d1, d2):
    lane, row = lanes(), sublanes()

    def shifted(x):
        if BACK_LAT[j]:
            moved = pltpu.roll(x, 1, 0)
            over = jnp.where(lane < GROUP, x, turn(moved, GROUP))
            return jnp.where(row >= 1, moved, over)
        moved = pltpu.roll(x, 7, 0)
        over = jnp.where(lane >= (TILES - 1) * GROUP, x, turn(moved, -GROUP))
        return jnp.where(row <= 6, moved, over)

    near = shifted(x)
    return d0 * x + d1 * near + d2 * shifted(near)


def spread(tile, position):
    at_first = lanes() // 4 % BANDS == 0
    tile = jnp.where(at_first, turn(tile, -4 * position), 0.0)
    for step in (1, 2, 4):
        tile = tile + turn(tile, 4 * step)
    return tile


def packed_fix(freq, table_ref, columns_ref, fix_ref):
    for j in range(ND):
        row = [table_ref[freq, j, i : i + 1, :] for i in range(7)]
        tile = columns_ref[j]
        first = row[2] * tile + row[6] * turn(tile, -1 if BACK_LON[j] else 1)
        fix_ref[j] = packed_lat(j, first, *row[3:6])


def packed_start(mine_right_ref, mine_left_ref, left_ref, right_ref, columns_ref, side_refs):
    near_ref, far_ref = side_refs
    lane = lanes()
    slot = lane % 4
    for j in range(ND):
        half = RANK[j] % 2
        narrow = HALF + RANK[j] // 2
        if BACK_LON[j]:
            wide, own = left_ref[RANK[j]], mine_right_ref[RANK[j]]
            other = turn(right_ref[narrow], 2 - 2 * half)
            centre = jnp.where(slot < 2, turn(wide, -2), other)
            near = jnp.where(slot == 2, turn(own, -1), turn(centre, 1))
            near = jnp.where(slot < 2, turn(wide, -1), near)
            far = jnp.where(slot < 2, wide, own)
        else:
            wide, own = right_ref[RANK[j]], mine_left_ref[RANK[j]]
            other = turn(left_ref[narrow], -2 * half)
            centre = jnp.where(slot < 2, other, turn(wide, 2))
            near = jnp.where(slot == 1, turn(own, 1), turn(centre, -1))
            near = jnp.where(slot >= 2, turn(wide, 1), near)
            far = jnp.where(slot < 2, own, wide)
        used = lane < TILES * GROUP
        columns_ref[j] = jnp.where(used, centre, 0.0)
        near_ref[j] = jnp.where(used, near, 0.0)
        far_ref[j] = jnp.where(used, far, 0.0)


def packed_source(
    freq, table_ref, left_ref, right_ref, columns_ref, side_refs,
    sums_ref, part_ref, drive_ref, ice_ref, p_ref,
):
    near_ref, far_ref = side_refs
    lane = lanes()
    slot, place = lane % 4, lane // 4 % BANDS
    both = jnp.where(slot < 2, left_ref[SENT - 1], turn(right_ref[SENT - 1], 2))
    east, north, land, south_rows, north_rows = (spread(both, i) for i in range(FIELDS))
    row = lane // GROUP * 8 + sublanes()
    row = row.astype(jnp.float32)
    held = (row < south_rows) | (row >= LAT - north_rows)
    sea = jnp.where(land > 0.5, 1.0, 0.0)
    ice = jnp.where(land > 1.5, 1.0, 0.0)
    ice_ref[...] = ice
    slope = jnp.zeros((8, WIDTH), jnp.float32)
    stress = slope
    for j in range(ND):
        coef = [table_ref[freq, j, i : i + 1, :] for i in range(6)]
        centre = columns_ref[j]
        x = coef[0] * centre + coef[1] * near_ref[j] + coef[2] * far_ref[j]
        x = packed_lat(j, x, *coef[3:])
        p = jnp.where(held, centre, jnp.maximum(x, 0.0)) * sea
        along = float(COS[j]) * east + float(SIN[j]) * north
        drive = jnp.minimum(jnp.maximum(along, 0.0) / WIND_REF, WIND_CLIP)
        drive = drive * drive * (1.0 - ice)
        drive_ref[j] = drive
        p_ref[j] = p
        slope = slope + p
        stress = stress + p * drive
    coef = [table_ref[freq, ND, i : i + 1, :] for i in range(5)]

    def running(tile):
        for step in (1, 2, 4):
            tile = tile + jnp.where(place >= step, turn(tile, 4 * step), 0.0)
        return tile

    out = [jnp.zeros((8, WIDTH), jnp.float32) for _ in range(PACKED_SUMS)]

    def put(index, tile):
        position = index % BANDS
        moved = turn(tile, 4 * (position - (BANDS - 1)))
        out[index // BANDS] = jnp.where(place == position, moved, out[index // BANDS])

    for j, excess in enumerate(excess_of([p_ref[j] for j in range(ND)])):
        total = running(excess)
        put(j, total)
        rate = excess * coef[0] + (total - excess) * coef[1]
        part_ref[j] = p_ref[j] * jnp.exp(rate)
    put(ND, running(slope * coef[2]))
    put(ND + 1, running(stress * coef[3]))
    for i in range(PACKED_SUMS):
        sums_ref[PACKED_AT + i] = out[i]


def excess_of(p):
    out = []
    for saturation in saturation_of(p):
        capped = jnp.maximum(saturation, SATURATION_REF)
        excess = capped * lax.rsqrt(capped) - ROOT_REF
        out.append(excess * excess)
    return out


def source_kernel(first, *refs):
    scal_ref, table_ref, x_ref, spec_ref, east_ref, north_ref, land_ref, rows_ref = refs[:8]
    refs = refs[8:]
    freq = lax.axis_index("freq")
    bands = x_ref.shape[0]
    if first:
        mine_right_ref, mine_left_ref, left_ref, right_ref = refs[:4]
        p_ref, excess_ref, sums_ref, part_ref, packed_drive_ref, ice_ref = refs[4:10]
        drive_ref, fix_ref, columns_ref, near_ref, far_ref, packed_ref = refs[10:]
        sides = (near_ref, far_ref)
        packed_start(mine_right_ref, mine_left_ref, left_ref, right_ref, columns_ref, sides)
        packed_source(
            freq, table_ref, left_ref, right_ref, columns_ref, sides,
            sums_ref, part_ref, packed_drive_ref, ice_ref, packed_ref,
        )
    else:
        columns_ref, p_ref, excess_ref, sums_ref, drive_ref, fix_ref = refs
        for i in range(PACKED_SUMS):
            sums_ref[PACKED_AT + i] = jnp.zeros((8, WIDTH), jnp.float32)
    packed_fix(freq, table_ref, columns_ref, fix_ref)
    for i in range(PACKED_AT):
        sums_ref[i] = jnp.zeros((8, WIDTH), jnp.float32)
    for r in range(TILES):
        water = jnp.where(land_ref[tile_rows(r), :] == 2, 0.0, 1.0)
        for j in range(ND):
            drive_ref[j, tile_rows(r), :] = wind_drive_of(j, r, east_ref, north_ref, water)

    lane = lanes()
    at_edge = {True: lane < 2, False: lane >= WIDTH - 2}

    def band(k, carry):
        extra = (freq * bands + k) * STRIDE + 6 * ND
        for r in range(TILES):
            rows = tile_rows(r)
            row = sublanes() + 8 * r
            held = (row < rows_ref[0:1, :]) | (row >= LAT - rows_ref[1:2, :])
            sea = jnp.where(land_ref[rows, :] != 0, 1.0, 0.0)
            slope = jnp.zeros((8, WIDTH), jnp.float32)
            stress = slope
            shift = {
                True: jnp.bitwise_and(WIDTH - GROUP * r - 4 * k, WIDTH - 1),
                False: WIDTH - 4 - GROUP * r - 4 * k,
            }
            for j in range(ND):
                back = BACK_LON[j]
                moved = pltpu.roll(fix_ref[j], shift[back], 1)
                p = x_ref[k, j, rows, :] + jnp.where(at_edge[back], moved, 0.0)
                p = jnp.where(held, spec_ref[k, j, rows, :], jnp.maximum(p, 0.0)) * sea
                p_ref[k, j, rows, :] = p
                slope = slope + p
                stress = stress + p * drive_ref[j, rows, :]
            sums_ref[SLOPE_AT + r] += slope * scal_ref[extra + 2]
            sums_ref[STRESS_AT + r] += stress * scal_ref[extra + 3]
            for j, excess in enumerate(excess_of([p_ref[k, j, rows, :] for j in range(ND)])):
                excess_ref[k, j, rows, :] = excess
                sums_ref[TILES * j + r] += excess
        return carry

    lax.fori_loop(0, bands, band, 0)


def local_kernel(scal_ref, p_ref, excess_ref, out_ref):
    bands = p_ref.shape[0]
    first = (lax.axis_index("freq") * bands) * STRIDE + 6 * ND

    def direction(j, carry):
        for r in range(TILES):
            rows = tile_rows(r)
            lower = jnp.zeros((8, WIDTH), jnp.float32)
            for k in range(bands):
                excess = excess_ref[k, j, rows, :]
                at = first + k * STRIDE
                rate = excess * scal_ref[at] + lower * scal_ref[at + 1]
                out_ref[k, j, rows, :] = p_ref[k, j, rows, :] * jnp.exp(rate)
                lower = lower + excess
        return carry

    lax.fori_loop(0, ND, direction, 0)


def pair_kernel(sums_ref, other_ref, out_ref):
    count = HALF * TILES
    first = (lax.axis_index("freq") % 2) * count
    for i in range(count):
        out_ref[i] = sums_ref[first + i] + other_ref[first + i]
    for i in range(HALF_SUMS - count):
        out_ref[count + i] = sums_ref[SLOPE_AT + i] + other_ref[SLOPE_AT + i]


def damp_and_gain(slope, stress, ice):
    damp = SWELL_DAMP * (slope / (slope + 1.0)) + ICE_DAMP * ice
    return damp, GROWTH * (1.0 + stress / (stress + 1.0))


def growth_kernel(last, *refs):
    scal_ref, part_ref, sums_ref, other_ref, mine_ref, rest_ref = refs[:6]
    east_ref, north_ref, land_ref = refs[6:9]
    bands = part_ref.shape[0]
    freq = lax.axis_index("freq")
    core = freq % 2
    odd = jnp.where(core == 1, 1.0, 0.0)
    upper = jnp.where(freq >= 2, 1.0, 0.0)
    after = SLOPE_AT - HALF * TILES
    if last:
        out_ref, slope_ref, rate_ref, field_ref, sent = refs[9:]
    else:
        table_ref, packed_part_ref, packed_drive_ref, ice_ref = refs[9:13]
        out_ref, columns_ref, rate_ref = refs[13:]
        coef = table_ref[freq, ND, 4:5, :]
        total, lower = [], []
        for i in range(PACKED_AT, SUMS):
            total.append((sums_ref[i] + other_ref[i]) + mine_ref[i - after])
            lower.append(odd * other_ref[i] + upper * mine_ref[i - after])
        slope, stress = (spread(total[i // BANDS], i % BANDS) for i in (ND, ND + 1))
        damp, gain = damp_and_gain(slope, stress, ice_ref[...])
        for j in range(ND):
            under = spread(lower[j // BANDS], j % BANDS)
            rate = gain * packed_drive_ref[j] - damp - (CUMULATIVE / NF) * under
            columns_ref[j] = packed_part_ref[j] * jnp.exp(coef * rate)
    for r in range(TILES):
        rows = tile_rows(r)
        ice = jnp.where(land_ref[rows, :] == 2, 1.0, 0.0)
        slope, stress = (
            (sums_ref[at + r] + other_ref[at + r]) + mine_ref[at + r - after]
            for at in (SLOPE_AT, STRESS_AT)
        )
        if last:
            slope_ref[rows, :] = slope
        damp, gain = damp_and_gain(slope, stress, ice)
        for j in range(ND):
            local = (j % HALF) * TILES + r
            near, far = mine_ref[local], rest_ref[local]
            in_mine = core == (0 if j < HALF else 1)
            lower = odd * other_ref[TILES * j + r] + upper * jnp.where(in_mine, near, far)
            drive = wind_drive_of(j, r, east_ref, north_ref, 1.0 - ice)
            rate_ref[j, rows, :] = gain * drive - damp - (CUMULATIVE / NF) * lower

    def send(k):
        return pltpu.make_async_copy(field_ref.at[k], out_ref.at[k], sent.at[k])

    def band(k, carry):
        root = scal_ref[(freq * bands + k) * STRIDE + 6 * ND + 4]
        target = field_ref if last else out_ref
        for j in range(ND):
            for r in range(TILES):
                rows = tile_rows(r)
                factor = jnp.exp(rate_ref[j, rows, :] * root)
                target[k, j, rows, :] = part_ref[k, j, rows, :] * factor
        if last:
            send(k).start()
        return carry

    lax.fori_loop(0, bands, band, 0)
    if last:
        for k in range(bands):
            send(k).wait()


def cost(tiles, ops, moves):
    return pl.CostEstimate(
        flops=tiles * ops * 8 * WIDTH, bytes_accessed=tiles * moves * 32 * WIDTH, transcendentals=0
    )


def per_device(spectrum, east_wind, north_wind, land_sea, edge_rows):
    bands, count, lat_rows, width = spectrum.shape
    assert (bands, count, lat_rows, width) == (BANDS, ND, LAT, WIDTH)
    ring = lax.axis_size("lon")
    assert lax.axis_size("freq") == 4 and bands * 4 == NF
    f32 = jnp.float32

    def tiles(count):
        return jax.ShapeDtypeStruct((count, 8, WIDTH), f32)

    field = jax.ShapeDtypeStruct(spectrum.shape, f32)
    plane = jax.ShapeDtypeStruct((LAT, WIDTH), f32)
    tile = jax.ShapeDtypeStruct((8, WIDTH), f32)
    smem = pl.BlockSpec(memory_space=pltpu.SMEM)
    vmem = pl.BlockSpec(memory_space=pltpu.VMEM)
    hbm = pl.BlockSpec(memory_space=pltpu.HBM)
    params = pltpu.CompilerParams(vmem_limit_bytes=16 * 1024 * 1024)
    scalars, table = jnp.asarray(SCALARS), jnp.asarray(PACKED_TABLE)
    swap_core = [(0, 1), (1, 0), (2, 3), (3, 2)]
    swap_chip = [(0, 2), (2, 0), (1, 3), (3, 1)]
    whole = bands * ND * TILES
    by_direction = pltpu.VMEM((ND, LAT, WIDTH), f32)
    packed = pltpu.VMEM((ND, 8, WIDTH), f32)

    arguments = [spectrum, east_wind, north_wind, land_sea, edge_rows]
    spectrum, right, left, east_wind, north_wind, land_sea, edge_rows = pl.pallas_call(
        pack_kernel,
        in_specs=[hbm] * 5,
        out_specs=[vmem] * 7,
        out_shape=[field, tiles(SENT), tiles(SENT)]
        + [jax.ShapeDtypeStruct(x.shape, x.dtype) for x in arguments[1:]],
        scratch_shapes=[pltpu.SemaphoreType.DMA((ND // CHUNK + 4,))],
        compiler_params=params,
        cost_estimate=cost(whole, 6, 2),
        name="pack_columns",
    )(*(pltpu.with_memory_space_constraint(x, pltpu.HBM) for x in arguments))
    from_left = lax.ppermute(right, "lon", [(i, (i + 1) % ring) for i in range(ring)])
    from_right = lax.ppermute(left, "lon", [((i + 1) % ring, i) for i in range(ring)])

    energy = spectrum
    for step in range(STEPS):
        first, last = step == 0, step == STEPS - 1
        drifted = pl.pallas_call(
            drift_kernel,
            in_specs=[smem, vmem],
            out_specs=vmem,
            out_shape=field,
            scratch_shapes=[pltpu.VMEM((ND, LAT + 8, WIDTH), f32)],
            compiler_params=params,
            cost_estimate=cost(whole, 12, 2),
            name="drift",
        )(scalars, energy)
        operands = [scalars, table, drifted, spectrum, east_wind, north_wind, land_sea, edge_rows]
        operands += [right, left, from_left, from_right] if first else [columns]
        p, excess, mine, *packed_state = pl.pallas_call(
            functools.partial(source_kernel, first),
            in_specs=[smem] + [vmem] * (len(operands) - 1),
            out_specs=[vmem] * (6 if first else 3),
            out_shape=[field, field, tiles(SUMS)] + ([tiles(ND), tiles(ND), tile] if first else []),
            scratch_shapes=[by_direction, packed] + ([packed] * 4 if first else []),
            compiler_params=params,
            cost_estimate=cost(whole, 30, 3),
            name="sources",
        )(*operands)
        other = lax.ppermute(mine, "freq", swap_core)
        pair = pl.pallas_call(
            pair_kernel,
            in_specs=[vmem] * 2,
            out_specs=vmem,
            out_shape=tiles(HALF_SUMS),
            compiler_params=params,
            cost_estimate=cost(HALF_SUMS, 1, 3),
            name="pair_sums",
        )(mine, other)
        near = lax.ppermute(pair, "freq", swap_chip)
        excess, _ = lax.optimization_barrier((excess, pair))
        part = pl.pallas_call(
            local_kernel,
            in_specs=[smem] + [vmem] * 2,
            out_specs=vmem,
            out_shape=field,
            compiler_params=params,
            cost_estimate=cost(whole, 8, 3),
            name="local_rate",
        )(scalars, p, excess)
        near, part = lax.optimization_barrier((near, part))
        far = lax.ppermute(near, "freq", swap_core)
        operands = [scalars, part, mine, other, near, far, east_wind, north_wind, land_sea]
        scratch = [by_direction]
        if last:
            scratch += [pltpu.VMEM(spectrum.shape, f32), pltpu.SemaphoreType.DMA((bands,))]
        else:
            operands += [table] + packed_state
        energy, columns = pl.pallas_call(
            functools.partial(growth_kernel, last),
            in_specs=[smem] + [vmem] * (len(operands) - 1),
            out_specs=[hbm if last else vmem, vmem],
            out_shape=[field, plane if last else tiles(ND)],
            scratch_shapes=scratch,
            compiler_params=params,
            cost_estimate=cost(whole, 6, 2),
            name="grow",
        )(*operands)
    return energy, columns


def solution(mesh):
    in_specs = (
        P("freq", None, None, "lon"),
        P(None, "lon"),
        P(None, "lon"),
        P(None, "lon"),
        P(None, "lon"),
    )
    out_specs = (P("freq", None, None, "lon"), P(None, "lon"))
    return jax.shard_map(
        per_device, mesh=mesh, in_specs=in_specs, out_specs=out_specs, check_vma=False
    )
```

time: 64.5 us -> 61.3 us (0.950)
  Pallas kernels: 26 us -> 35.5 us
  waiting for transfers between devices: 22.9 us -> 15.2 us
  starting transfers between devices: 14.6 us -> 9.63 us
    pallas_call x3 -> x7, Pallas kernels: 19.2 us -> 29.5 us  [the longest x2 12.6 us: per_device(): pl.pallas_call(functools.partial(source_kernel, first), in_specs=[smem] +...]
    ppermute x2, waiting for transfers between devices: 12.6 us -> 8.45 us  [per_device(): near = lax.ppermute(pair, 'freq', swap_chip)]
    ppermute x2 -> x1, waiting for transfers between devices: 3.66 us -> 0.01 us  [per_device(): lax.ppermute(right, 'lon', [(i, (i + 1) % ring) for i in range(ring)])]
    ppermute x2 -> x1, starting transfers between devices: 6.52 us -> 3.1 us  [per_device(): lax.ppermute(left, 'lon', [((i + 1) % ring, i) for i in range(ring)])]
    ppermute x2 -> x1, starting transfers between devices: 4.46 us -> 2.99 us  [per_device(): lax.ppermute(right, 'lon', [(i, (i + 1) % ring) for i in range(ring)])]
    pallas_call x2, Pallas kernels: 6.73 us -> 5.95 us  [per_device(): pl.pallas_call(functools.partial(growth_kernel, last), in_specs=[smem] +...]
  transfers between devices with their start and end apart: 10 -> 8, of which waited for: 8 -> 7; matrix products, arithmetic and copies ran while one was open for 0% -> 0% of each run, Pallas kernels for 0% -> 15%
where the time goes in v3:
time: 61.3 us; the launch traced here: 61.1 us
  Pallas kernels  35.5 us (58%)
  waiting for transfers between devices  15.2 us (25%)
  starting transfers between devices  9.63 us (16%)
  between operations  0.73 us (1%)
    pallas_call x2, Pallas kernels, per_device(): pl.pallas_call(functools.partial(source_kernel, first), in_specs=[smem] +...  12.6 us
    ppermute x2, waiting for transfers between devices, per_device(): near = lax.ppermute(pair, 'freq', swap_chip)  8.45 us
    pallas_call x2, Pallas kernels, per_device(): pl.pallas_call(drift_kernel, in_specs=[smem, vmem], out_specs=vmem, out_s...  8.01 us
    pallas_call x2, Pallas kernels, per_device(): pl.pallas_call(functools.partial(growth_kernel, last), in_specs=[smem] +...  5.95 us
    pallas_call x2, Pallas kernels, per_device(): pl.pallas_call(local_kernel, in_specs=[smem] + [vmem] * 2, out_specs=vmem...  5.28 us
    pallas_call x1, Pallas kernels, per_device(): pl.pallas_call(pack_kernel, in_specs=[hbm] * 5, out_specs=[vmem] * 7, out...  3.64 us
    ppermute x2, waiting for transfers between devices, per_device(): other = lax.ppermute(mine, 'freq', swap_core)  3.57 us
    ppermute x2, starting transfers between devices, per_device(): near = lax.ppermute(pair, 'freq', swap_chip)  3.25 us
  transfers between devices with their start and end apart: 8, of which 7 were waited for; matrix products, arithmetic and copies ran while one was open for 0% of the time, Pallas kernels for 15%

profile of v3, /device:TPU:0, one launch (start us, length us, event | category | flops | bytes accessed | tf_op | source)
XLA Modules:
  0.0 61.1 jit_solution(4683121920417554224)
XLA Ops:
  0.6 0.0 copy-start.1
  0.6 3.6 %pack_columns.1 = (f32[8,36,24,128]{3,2,1,0:T(8,128)S(1)}, f32[28,8,128]{2,1,0:T(8,128)S(1)}, f32[28,8,128]{2,1,0:T(8,128)S(1)}, f32[24,128]{1,0:T(8,128)S(1)}, ...) custom-call(f32[8,36,24,128]{3,2,1,0:T(8,128)} %spec_ref.1, f32[24,128]{1,0:T(8,128)} %refs_0_.5, ...), custom_call_target="tpu_custom_call" | custom-call | flops 5308416 | bytes 7077888 | tf_op jit(solution)/shard_map/pack_columns/pallas_call | solution.py:597
  4.3 3.0 %collective-permute-start = (f32[28,8,128]{2,1,0:T(8,128)S(1)}, f32[28,8,128]{2,1,0:T(8,128)S(1)}, u32[]{:S(2)}, u32[]{:S(2)}) collective-permute-start(f32[28,8,128]{2,1,0:T(8,128)S(1)} %get-tuple-element.31.refs_8_), channel_id=1, source_target_pairs={{0,4},{4,8},{8,12},{12,16},{16,20},{20,24},{24,28},{28,0},{1,5},{5... | collective-permute-start | bytes 344072 | tf_op jit(solution)/shard_map/ppermute | solution.py:608
  7.3 3.1 %collective-permute-start.1 = (f32[28,8,128]{2,1,0:T(8,128)S(1)}, f32[28,8,128]{2,1,0:T(8,128)S(1)}, u32[]{:S(2)}, u32[]{:S(2)}) collective-permute-start(f32[28,8,128]{2,1,0:T(8,128)S(1)} %get-tuple-element.32.refs_9_), channel_id=1, source_target_pairs={{4,0},{8,4},{12,8},{16,12},{20,16},{24,20},{28,24},{0,28},{5,1},{9... | collective-permute-start | bytes 344072 | tf_op jit(solution)/shard_map/ppermute | solution.py:609
  10.4 0.0 copy-done.1
  10.4 0.0 copy-start
  10.4 4.0 %drift.2.refs_2_ = f32[8,36,24,128]{3,2,1,0:T(8,128)S(1)} custom-call(f32[7168]{0:T(1024)S(1)} %copy-done.1, f32[8,36,24,128]{3,2,1,0:T(8,128)S(1)} %get-tuple-element.26.q_ref.refs_3_), custom_call_target="tpu_custom_call" | custom-call | flops 10616832 | bytes 7077888 | tf_op jit(solution)/shard_map/drift/pallas_call | solution.py:614
  14.4 0.0 collective-permute-done.refs_10_
  14.4 0.1 collective-permute-done.1.refs_11_
  14.5 0.0 copy-done
  14.5 7.4 %sources.2 = (f32[8,36,24,128]{3,2,1,0:T(8,128)S(1)}, f32[8,36,24,128]{3,2,1,0:T(8,128)S(1)}, f32[119,8,128]{2,1,0:T(8,128)S(1)}, f32[36,8,128]{2,1,0:T(8,128)S(...) custom-call(f32[7168]{0:T(1024)S(1)} %copy-done.1, f32[4,37,8,128]{3,2,1,0:T(8,128)S(1)} %copy-done, ...), custom_call_target="tpu_custom_call" | custom-call | flops 26542080 | bytes 10616832 | tf_op jit(solution)/shard_map/sources/pallas_call | solution.py:626
  22.0 0.1 collective-permute-start.2
  22.1 1.8 %collective-permute-done.2.other_ref.refs_3_ = f32[119,8,128]{2,1,0:T(8,128)S(1)} collective-permute-done((f32[119,8,128]{2,1,0:T(8,128)S(1)}, f32[119,8,128]{2,1,0:T(8,128)S(1)}, u32[]{:S(2)}, u32[]{:S(2)}) %collective-permute-start.2) | collective-permute-done | bytes 487456 | tf_op jit(solution)/shard_map/ppermute | solution.py:636
  23.9 1.6 %collective-permute-start.3 = (f32[65,8,128]{2,1,0:T(8,128)S(1)}, f32[65,8,128]{2,1,0:T(8,128)S(1)}, u32[]{:S(2)}, u32[]{:S(2)}) collective-permute-start(f32[65,8,128]{2,1,0:T(8,128)S(1)} %pair_sums.2), channel_id=1, source_target_pairs={{0,2},{2,0},{1,3},{3,1},{4,6},{6,4},{5,7},{7,5},{8,10},{10,8},{9,1... | collective-permute-start | bytes 798728 | tf_op jit(solution)/shard_map/ppermute | solution.py:646
  25.6 2.6 %local_rate.2.refs_1_ = f32[8,36,24,128]{3,2,1,0:T(8,128)S(1)} custom-call(f32[7168]{0:T(1024)S(1)} %copy-done.1, f32[8,36,24,128]{3,2,1,0:T(8,128)S(1)} %get-tuple-element.34.p_ref, f32[8,36,24,128]{3,2,1,0:T(8,128)S(1)} %get-tuple-element.36.excess_ref), custom_call_target="tpu_custom_call" | custom-call | flops 7077888 | bytes 10616832 | tf_op jit(solution)/shard_map/local_rate/pallas_call | solution.py:648
  28.2 4.2 %collective-permute-done.3.refs_4_ = f32[65,8,128]{2,1,0:T(8,128)S(1)} collective-permute-done((f32[65,8,128]{2,1,0:T(8,128)S(1)}, f32[65,8,128]{2,1,0:T(8,128)S(1)}, u32[]{:S(2)}, u32[]{:S(2)}) %collective-permute-start.3) | collective-permute-done | bytes 266272 | tf_op jit(solution)/shard_map/ppermute | solution.py:646
  32.4 0.0 collective-permute-start.4
  32.4 1.5 %collective-permute-done.4.refs_5_ = f32[65,8,128]{2,1,0:T(8,128)S(1)} collective-permute-done((f32[65,8,128]{2,1,0:T(8,128)S(1)}, f32[65,8,128]{2,1,0:T(8,128)S(1)}, u32[]{:S(2)}, u32[]{:S(2)}) %collective-permute-start.4) | collective-permute-done | bytes 266272 | tf_op jit(solution)/shard_map/ppermute | solution.py:658
  34.0 2.1 %grow.2 = (f32[8,36,24,128]{3,2,1,0:T(8,128)S(1)}, f32[36,8,128]{2,1,0:T(8,128)S(1)}) custom-call(f32[7168]{0:T(1024)S(1)} %copy-done.1, f32[8,36,24,128]{3,2,1,0:T(8,128)S(1)} %local_rate.2.refs_1_, f32[119,8,128]{2,1,0:T(8,128)S(1)} %get-tuple-element.33.sums_ref.refs_2_, f32[119,8,128]{2,1,0:T(8,128)S(1)} %collective-permute-done.2.other_ref.refs_3_, ...), custom_call_target="tpu_custom_call" | custom-call | flops 5308416 | bytes 7077888 | tf_op jit(solution)/shard_map/grow/pallas_call | solution.py:665
  36.1 4.0 %drift.3.refs_2_ = f32[8,36,24,128]{3,2,1,0:T(8,128)S(1)} custom-call(f32[7168]{0:T(1024)S(1)} %copy-done.1, f32[8,36,24,128]{3,2,1,0:T(8,128)S(1)} %get-tuple-element.42.q_ref), custom_call_target="tpu_custom_call" | custom-call | flops 10616832 | bytes 7077888 | tf_op jit(solution)/shard_map/drift/pallas_call | solution.py:614
  40.1 5.1 %sources.3 = (f32[8,36,24,128]{3,2,1,0:T(8,128)S(1)}, f32[8,36,24,128]{3,2,1,0:T(8,128)S(1)}, f32[119,8,128]{2,1,0:T(8,128)S(1)}) custom-call(f32[7168]{0:T(1024)S(1)} %copy-done.1, f32[4,37,8,128]{3,2,1,0:T(8,128)S(1)} %copy-done, f32[8,36,24,128]{3,2,1,0:T(8,128)S(1)} %drift.3.refs_2_, f32[8,36,24,128]{3,2,1,0:T(8,128)S(1)} %get-tuple-element.26.q_ref.refs_3_, ...), custom_call_target="tpu_custom_call" | custom-call | flops 26542080 | bytes 10616832 | tf_op jit(solution)/shard_map/sources/pallas_call | solution.py:626
  45.3 0.2 collective-permute-start.5
  45.5 1.7 %collective-permute-done.5.other_ref.refs_3_ = f32[119,8,128]{2,1,0:T(8,128)S(1)} collective-permute-done((f32[119,8,128]{2,1,0:T(8,128)S(1)}, f32[119,8,128]{2,1,0:T(8,128)S(1)}, u32[]{:S(2)}, u32[]{:S(2)}) %collective-permute-start.5) | collective-permute-done | bytes 487456 | tf_op jit(solution)/shard_map/ppermute | solution.py:636
  47.3 1.6 %collective-permute-start.6 = (f32[65,8,128]{2,1,0:T(8,128)S(1)}, f32[65,8,128]{2,1,0:T(8,128)S(1)}, u32[]{:S(2)}, u32[]{:S(2)}) collective-permute-start(f32[65,8,128]{2,1,0:T(8,128)S(1)} %pair_sums.3), channel_id=1, source_target_pairs={{0,2},{2,0},{1,3},{3,1},{4,6},{6,4},{5,7},{7,5},{8,10},{10,8},{9,1... | collective-permute-start | bytes 798728 | tf_op jit(solution)/shard_map/ppermute | solution.py:646
  48.9 2.6 %local_rate.3.refs_1_ = f32[8,36,24,128]{3,2,1,0:T(8,128)S(1)} custom-call(f32[7168]{0:T(1024)S(1)} %copy-done.1, f32[8,36,24,128]{3,2,1,0:T(8,128)S(1)} %get-tuple-element.45.p_ref, f32[8,36,24,128]{3,2,1,0:T(8,128)S(1)} %get-tuple-element.47.excess_ref), custom_call_target="tpu_custom_call" | custom-call | flops 7077888 | bytes 10616832 | tf_op jit(solution)/shard_map/local_rate/pallas_call | solution.py:648
  51.5 4.2 %collective-permute-done.6.refs_4_ = f32[65,8,128]{2,1,0:T(8,128)S(1)} collective-permute-done((f32[65,8,128]{2,1,0:T(8,128)S(1)}, f32[65,8,128]{2,1,0:T(8,128)S(1)}, u32[]{:S(2)}, u32[]{:S(2)}) %collective-permute-start.6) | collective-permute-done | bytes 266272 | tf_op jit(solution)/shard_map/ppermute | solution.py:646
  55.8 0.0 collective-permute-start.7
  55.8 1.5 %collective-permute-done.7.refs_5_ = f32[65,8,128]{2,1,0:T(8,128)S(1)} collective-permute-done((f32[65,8,128]{2,1,0:T(8,128)S(1)}, f32[65,8,128]{2,1,0:T(8,128)S(1)}, u32[]{:S(2)}, u32[]{:S(2)}) %collective-permute-start.7) | collective-permute-done | bytes 266272 | tf_op jit(solution)/shard_map/ppermute | solution.py:658
  57.3 3.8 %grow.3 = (f32[8,36,24,128]{3,2,1,0:T(8,128)}, f32[24,128]{1,0:T(8,128)}) custom-call(f32[7168]{0:T(1024)S(1)} %copy-done.1, f32[8,36,24,128]{3,2,1,0:T(8,128)S(1)} %local_rate.3.refs_1_, f32[119,8,128]{2,1,0:T(8,128)S(1)} %get-tuple-element.44.sums_ref.refs_2_, f32[119,8,128]{2,1,0:T(8,128)S(1)} %collective-permute-done.5.other_ref.refs_3_, ...), custom_call_target="tpu_custom_call" | custom-call | flops 5308416 | bytes 7077888 | tf_op jit(solution)/shard_map/grow/pallas_call | solution.py:665
  (2 shorter events, 0.1 us)
Async XLA Ops:
  0.6 9.8 %copy-start.1 = (f32[7168]{0:T(1024)S(1)}, f32[7168]{0:T(1024)}, u32[]{:S(2)}) copy-start(f32[7168]{0:T(1024)} %constant.4.clone.scal_ref.refs_0_) | copy-start | bytes 86020
  4.3 10.1 %collective-permute-start = (f32[28,8,128]{2,1,0:T(8,128)S(1)}, f32[28,8,128]{2,1,0:T(8,128)S(1)}, u32[]{:S(2)}, u32[]{:S(2)}) collective-permute-start(f32[28,8,128]{2,1,0:T(8,128)S(1)} %get-tuple-element.31.refs_8_), channel_id=1, source_target_pairs={{0,4},{4,8},{8,12},{12,16},{16,20},{20,24},{24,28},{28,0},{1,5},{5... | collective-permute-start | bytes 344072 | tf_op jit(solution)/shard_map/ppermute | solution.py:608
  7.3 7.2 %collective-permute-start.1 = (f32[28,8,128]{2,1,0:T(8,128)S(1)}, f32[28,8,128]{2,1,0:T(8,128)S(1)}, u32[]{:S(2)}, u32[]{:S(2)}) collective-permute-start(f32[28,8,128]{2,1,0:T(8,128)S(1)} %get-tuple-element.32.refs_9_), channel_id=1, source_target_pairs={{4,0},{8,4},{12,8},{16,12},{20,16},{24,20},{28,24},{0,28},{5,1},{9... | collective-permute-start | bytes 344072 | tf_op jit(solution)/shard_map/ppermute | solution.py:609
  10.4 4.1 %copy-start = (f32[4,37,8,128]{3,2,1,0:T(8,128)S(1)}, f32[4,37,8,128]{3,2,1,0:T(8,128)}, u32[]{:S(2)}) copy-start(f32[4,37,8,128]{3,2,1,0:T(8,128)} %constant.5.clone.refs_1_.refs_9_) | copy-start | bytes 1818628
  22.0 1.9 %collective-permute-start.2 = (f32[119,8,128]{2,1,0:T(8,128)S(1)}, f32[119,8,128]{2,1,0:T(8,128)S(1)}, u32[]{:S(2)}, u32[]{:S(2)}) collective-permute-start(f32[119,8,128]{2,1,0:T(8,128)S(1)} %get-tuple-element.33.sums_ref.refs_2_), channel_id=1, source_target_pairs={{0,1},{1,0},{2,3},{3,2},{4,5},{5,4},{6,7},{7,6},{8,9},{9,8},{10,11... | collective-permute-start | bytes 1462280 | tf_op jit(solution)/shard_map/ppermute | solution.py:636
  23.9 8.5 %collective-permute-start.3 = (f32[65,8,128]{2,1,0:T(8,128)S(1)}, f32[65,8,128]{2,1,0:T(8,128)S(1)}, u32[]{:S(2)}, u32[]{:S(2)}) collective-permute-start(f32[65,8,128]{2,1,0:T(8,128)S(1)} %pair_sums.2), channel_id=1, source_target_pairs={{0,2},{2,0},{1,3},{3,1},{4,6},{6,4},{5,7},{7,5},{8,10},{10,8},{9,1... | collective-permute-start | bytes 798728 | tf_op jit(solution)/shard_map/ppermute | solution.py:646
  32.4 1.5 %collective-permute-start.4 = (f32[65,8,128]{2,1,0:T(8,128)S(1)}, f32[65,8,128]{2,1,0:T(8,128)S(1)}, u32[]{:S(2)}, u32[]{:S(2)}) collective-permute-start(f32[65,8,128]{2,1,0:T(8,128)S(1)} %collective-permute-done.3.refs_4_), channel_id=1, source_target_pairs={{0,1},{1,0},{2,3},{3,2},{4,5},{5,4},{6,7},{7,6},{8,9},{9,8},{10,11... | collective-permute-start | bytes 798728 | tf_op jit(solution)/shard_map/ppermute | solution.py:658
  45.3 1.9 %collective-permute-start.5 = (f32[119,8,128]{2,1,0:T(8,128)S(1)}, f32[119,8,128]{2,1,0:T(8,128)S(1)}, u32[]{:S(2)}, u32[]{:S(2)}) collective-permute-start(f32[119,8,128]{2,1,0:T(8,128)S(1)} %get-tuple-element.44.sums_ref.refs_2_), channel_id=1, source_target_pairs={{0,1},{1,0},{2,3},{3,2},{4,5},{5,4},{6,7},{7,6},{8,9},{9,8},{10,11... | collective-permute-start | bytes 1462280 | tf_op jit(solution)/shard_map/ppermute | solution.py:636
  47.3 8.5 %collective-permute-start.6 = (f32[65,8,128]{2,1,0:T(8,128)S(1)}, f32[65,8,128]{2,1,0:T(8,128)S(1)}, u32[]{:S(2)}, u32[]{:S(2)}) collective-permute-start(f32[65,8,128]{2,1,0:T(8,128)S(1)} %pair_sums.3), channel_id=1, source_target_pairs={{0,2},{2,0},{1,3},{3,1},{4,6},{6,4},{5,7},{7,5},{8,10},{10,8},{9,1... | collective-permute-start | bytes 798728 | tf_op jit(solution)/shard_map/ppermute | solution.py:646
  55.8 1.5 %collective-permute-start.7 = (f32[65,8,128]{2,1,0:T(8,128)S(1)}, f32[65,8,128]{2,1,0:T(8,128)S(1)}, u32[]{:S(2)}, u32[]{:S(2)}) collective-permute-start(f32[65,8,128]{2,1,0:T(8,128)S(1)} %collective-permute-done.6.refs_4_), channel_id=1, source_target_pairs={{0,1},{1,0},{2,3},{3,2},{4,5},{5,4},{6,7},{7,6},{8,9},{9,8},{10,11... | collective-permute-start | bytes 798728 | tf_op jit(solution)/shard_map/ppermute | solution.py:658

commit v4 on v3

v4 whole, which is shorter than its diff:
```python
import functools
import math

import jax
import jax.numpy as jnp
import numpy as np
from jax import lax
from jax.experimental import pallas as pl
from jax.experimental.pallas import tpu as pltpu
from jax.sharding import PartitionSpec as P

NF = 32
STEPS = 2

COURANT_MAX = 0.9
FREQ_RATIO = 1.1
WIND_REF = 8.0
WIND_CLIP = 2.0
GROWTH = 0.01
BREAKING = 0.3
SATURATION_REF = 0.4
CUMULATIVE = 2.0
SWELL_DAMP = 0.1
ICE_DAMP = 0.5

ND = 36
HALF = ND // 2
QUARTER = ND // 4
DTHETA = 2.0 * math.pi / ND
LOG2E = 1.0 / math.log(2.0)
ROOT_REF = math.sqrt(SATURATION_REF)
TILES = 3
LAT = 8 * TILES
WIDTH = 128
STRIDE = 6 * ND + 8

ANGLES = np.arange(ND) * DTHETA
COS = np.cos(ANGLES)
SIN = np.sin(ANGLES)
COS2 = np.cos(2.0 * ANGLES)
SIN2 = np.sin(2.0 * ANGLES)
BACK_LON = [bool(c >= 0.0) for c in COS]
BACK_LAT = [bool(s >= 0.0) for s in SIN]
RANK = [sum(BACK_LON[:j]) if BACK_LON[j] else j - sum(BACK_LON[:j]) for j in range(ND)]


def one_sided(courant):
    c = np.abs(courant)
    return 1.0 - 1.5 * c + 0.5 * c * c, 2.0 * c - c * c, 0.5 * c * c - 0.5 * c


GROUP = 32
BANDS = 8
SENT = HALF + QUARTER + 1
FIELDS = 5
SLOPE_AT = ND * TILES
STRESS_AT = SLOPE_AT + TILES
PACKED_AT = STRESS_AT + TILES
PACKED_SUMS = 5
HALF_TILES = HALF * TILES
SCALE = 0.25 * DTHETA
CAP = SATURATION_REF / SCALE
ROOT_CAP = math.sqrt(CAP)
LOWER = CUMULATIVE / NF * SCALE


def make_tables():
    ratios = FREQ_RATIO ** np.arange(NF)
    root = np.sqrt(ratios)
    lon = one_sided(COURANT_MAX * COS[None, :] / ratios[:, None])
    lat = one_sided(0.5 * COURANT_MAX * SIN[None, :] / ratios[:, None])
    scalars = np.zeros((NF, STRIDE))
    for i in range(3):
        scalars[:, i : 6 * ND : 6] = lon[i]
        scalars[:, 3 + i : 6 * ND : 6] = lat[i]
    rest = [
        -BREAKING / SATURATION_REF * SCALE * root,
        -LOWER * root,
        ratios * ratios * DTHETA / np.sum(ratios * ratios),
        ratios * root * DTHETA / np.sum(ratios * root),
        root,
        1.0 / ratios,
    ]
    packed = np.zeros((NF // BANDS, len(rest), 8, WIDTH))
    for i, value in enumerate(rest):
        scalars[:, 6 * ND + i] = value
        for lane in range(TILES * GROUP):
            packed[:, i, :, lane] = value[lane // 4 % BANDS :: BANDS, None]
    return scalars.reshape(-1).astype(np.float32), packed.astype(np.float32)


SCALARS, PACKED_TABLE = make_tables()


def lanes():
    return lax.broadcasted_iota(jnp.int32, (8, WIDTH), 1)


def sublanes():
    return lax.broadcasted_iota(jnp.int32, (8, WIDTH), 0)


def turn(tile, shift):
    shift = shift % WIDTH
    return tile if shift == 0 else pltpu.roll(tile, shift, 1)


def tile_rows(r):
    return pl.ds(r, 8, stride=TILES)


CHUNK = 4


def pack_kernel(spec_ref, *refs):
    sources, (copy_ref, right_ref, left_ref), held_refs = refs[:4], refs[4:7], refs[7:11]
    to_even_ref, to_odd_ref, arrived = refs[11:]

    def fetch(c):
        part = pl.ds(CHUNK * c, CHUNK)
        return pltpu.make_async_copy(spec_ref.at[:, part], copy_ref.at[:, part], arrived.at[c])

    small = [
        pltpu.make_async_copy(source, target, arrived.at[ND // CHUNK + i])
        for i, (source, target) in enumerate(zip(sources, held_refs))
    ]
    for c in range(ND // CHUNK):
        fetch(c).start()
    for copy in small:
        copy.start()
    lane = lanes()
    zero = jnp.zeros((8, WIDTH), jnp.float32)
    held = [zero, zero]
    for j in range(ND):
        if j % CHUNK == 0:
            fetch(j // CHUNK).wait()
        back = BACK_LON[j]
        wide, narrow = (right_ref, left_ref) if back else (left_ref, right_ref)
        half = RANK[j] % 2
        first, aside = (WIDTH - 4, 4) if back else (0, -2)
        four = zero
        two = zero
        for r in range(TILES):
            for k in range(BANDS):
                place = GROUP * r + 4 * k
                tile = turn(copy_ref[k, j, tile_rows(r), :], place - first)
                four = jnp.where(lane // 4 == place // 4, tile, four)
                two = jnp.where(lane // 2 == (place + aside) % WIDTH // 2, tile, two)
        wide[RANK[j]] = four
        two = turn(two, 2 * half - aside)
        if half:
            narrow[HALF + RANK[j] // 2] = jnp.where(lane % 4 < 2, held[back], two)
        else:
            held[back] = two
    for copy in small:
        copy.wait()
    east_ref, north_ref, land_ref, rows_ref = held_refs
    fields = [
        [f(r) for r in range(TILES)]
        for f in (
            lambda r: east_ref[tile_rows(r), :],
            lambda r: north_ref[tile_rows(r), :],
            lambda r: land_ref[tile_rows(r), :].astype(jnp.float32),
            lambda r: jnp.broadcast_to(rows_ref[0:1, :].astype(jnp.float32), (8, WIDTH)),
            lambda r: jnp.broadcast_to(rows_ref[1:2, :].astype(jnp.float32), (8, WIDTH)),
        )
    ]
    to_right, to_left = zero, zero
    for i in range(FIELDS):
        for r in range(TILES):
            place = GROUP * r + 4 * i
            here = lane // 2 == place // 2
            to_right = jnp.where(here, turn(fields[i][r], place - (WIDTH - 2)), to_right)
            to_left = jnp.where(here, turn(fields[i][r], place), to_left)
    right_ref[SENT - 1] = to_right
    left_ref[SENT - 1] = to_left
    odd = lax.axis_index("lon") % 2 == 1
    for i in range(SENT):
        right, left = right_ref[i], left_ref[i]
        to_even_ref[i] = jnp.where(odd, left, right)
        to_odd_ref[i] = jnp.where(odd, right, left)


def drive_of(j, east, north, open_water):
    along = float(COS[j]) * east + float(SIN[j]) * north
    drive = jnp.minimum(jnp.maximum(along, 0.0) / WIND_REF, WIND_CLIP)
    return drive * drive * open_water


def saturation_of(p):
    diff = [p[b] - p[b + HALF] for b in range(HALF)]
    both = [p[b] + p[b + HALF] for b in range(HALF)]
    total = both[0]
    for b in range(1, HALF):
        total = total + both[b]
    fold = [both[b] - both[b + QUARTER] for b in range(QUARTER)]
    total_c, total_s = fold[0], None
    for b in range(1, QUARTER):
        total_c = total_c + fold[b] * float(COS2[b])
        term = fold[b] * float(SIN2[b])
        total_s = term if total_s is None else total_s + term
    level = [None] * HALF
    for a in range(QUARTER):
        wave = total_c * float(COS2[a])
        if a:
            wave = wave + total_s * float(SIN2[a])
        level[a] = total + wave
        level[a + QUARTER] = total - wave

    def at(b):
        return diff[b % HALF], b // HALF % 2 == 1

    def plus(x, b):
        value, negative = at(b)
        return x - value if negative else x + value

    def minus(x, b):
        value, negative = at(b)
        return x + value if negative else x - value

    plain, waves = diff[0], []
    for a in range(2):
        wave = diff[a]
        for d in range(1, QUARTER):
            pair = minus(diff[a + d], a - d + HALF)
            wave = wave + pair * float(COS2[d])
            if a == 0:
                plain = plain + pair
        waves.append(wave)
    twice = float(2.0 * COS2[1])
    odd = [None] * HALF
    odd[0] = plain + waves[0]
    window, before, now = plain, waves[0], waves[1]
    for a in range(1, QUARTER + 1):
        window = plus(minus(window, a - 9), a + 8)
        odd[a] = window + now
        if a < QUARTER:
            step = minus(plus(twice * now - before, a + 8), a + 10)
            before, now = now, step
    window, after, now = plain, waves[1], waves[0]
    for a in range(0, -(QUARTER - 1), -1):
        step = minus(plus(twice * now - after, a + 8), a + 10)
        after, now = now, step
        window = minus(plus(window, a - 9 + 2 * HALF), a + 8)
        odd[a - 1 + HALF] = -(window + now)
    out = [None] * ND
    for a in range(HALF):
        out[a] = level[a] + odd[a]
        out[a + HALF] = level[a] - odd[a]
    return out


def inside_masks():
    lane = lanes()
    one = jnp.ones((8, WIDTH), jnp.float32)
    return {
        (True, 1): jnp.where(lane >= 1, one, 0.0),
        (True, 2): jnp.where(lane >= 2, one, 0.0),
        (False, 1): jnp.where(lane < WIDTH - 1, one, 0.0),
        (False, 2): jnp.where(lane < WIDTH - 2, one, 0.0),
    }


def drift(j, base, tiles, scal_ref, inside):
    c0, c1, c2, d0, d1, d2 = (scal_ref[base + 6 * j + i] for i in range(6))
    side = 1 if BACK_LON[j] else -1
    c1 = c1 * inside[BACK_LON[j], 1]
    c2 = c2 * inside[BACK_LON[j], 2]
    x = [c0 * q + c1 * turn(q, side) + c2 * turn(q, 2 * side) for q in tiles]
    row = sublanes()
    if BACK_LAT[j]:
        over = [jnp.where(row == 0, x[0], pltpu.roll(x[r], 1, 0)) for r in (1, 2)]
        near = [over[1], x[0], x[1]]
        far = [over[0], over[1], x[0]]
    else:
        over = [jnp.where(row == 7, x[2], pltpu.roll(x[r], 7, 0)) for r in (0, 1)]
        near = [x[1], x[2], over[0]]
        far = [x[2], over[0], over[1]]
    return [d0 * x[r] + d1 * near[r] + d2 * far[r] for r in range(TILES)]


def drift_kernel(scal_ref, q_ref, out_ref):
    bands = q_ref.shape[0]
    inside = inside_masks()

    def band(k, carry):
        base = (lax.axis_index("freq") * bands + k) * STRIDE
        for j in range(ND):
            tiles = [q_ref[k, j, tile_rows(r), :] for r in range(TILES)]
            for r, tile in enumerate(drift(j, base, tiles, scal_ref, inside)):
                out_ref[k, j, r] = tile
        return carry

    lax.fori_loop(0, bands, band, 0)


def packed_lat(j, x, d0, d1, d2):
    lane, row = lanes(), sublanes()
    first, last = lane < GROUP, lane >= (TILES - 1) * GROUP
    if BACK_LAT[j]:
        moved, one = pltpu.roll(x, 1, 0), turn(x, GROUP)
        near = jnp.where(first, jnp.where(row == 0, x, turn(moved, -2 * GROUP)), one)
        far = jnp.where(row == 0, jnp.where(first, x, one), turn(moved, -GROUP))
        far = jnp.where(last, turn(x, 2 * GROUP), far)
    else:
        moved, one = pltpu.roll(x, 7, 0), turn(x, -GROUP)
        near = jnp.where(last, jnp.where(row == 7, x, turn(moved, 2 * GROUP)), one)
        far = jnp.where(row == 7, jnp.where(last, x, one), turn(moved, GROUP))
        far = jnp.where(first, turn(x, -2 * GROUP), far)
    return d0 * x + d1 * near + d2 * far


def spread(tile, position):
    at_first = lanes() // 4 % BANDS == 0
    tile = jnp.where(at_first, turn(tile, -4 * position), 0.0)
    for step in (1, 2, 4):
        tile = tile + turn(tile, 4 * step)
    return tile


def packed_coefficients(inverse, speed):
    c = inverse * abs(float(speed))
    return 1.0 + c * (0.5 * c - 1.5), c * (2.0 - c), c * (0.5 * c - 0.5)


def packed_fix(table, columns_ref, fix_ref):
    slot = lanes() % 4
    inverse = table(5)
    for j in range(ND):
        back = BACK_LON[j]
        _, c1, c2 = packed_coefficients(inverse, COURANT_MAX * COS[j])
        tile = columns_ref[j]
        next_one = jnp.where(slot == (0 if back else 3), turn(tile, -1 if back else 1), 0.0)
        first = c2 * tile + c1 * next_one
        lat = packed_coefficients(inverse, 0.5 * COURANT_MAX * SIN[j])
        fix_ref[j] = packed_lat(j, first, *lat)


def packed_start(mine_right_ref, mine_left_ref, left_ref, right_ref, columns_ref, side_refs):
    near_ref, far_ref = side_refs
    lane = lanes()
    slot = lane % 4
    used = lane < TILES * GROUP
    for j in range(ND):
        half = RANK[j] % 2
        narrow = HALF + RANK[j] // 2
        if BACK_LON[j]:
            wide, own = left_ref[RANK[j]], mine_right_ref[RANK[j]]
            other = turn(right_ref[narrow], 2 - 2 * half)
            centre = jnp.where(slot < 2, turn(wide, -2), other)
            near = jnp.where(slot == 2, turn(own, -1), turn(centre, 1))
            near = jnp.where(slot < 2, turn(wide, -1), near)
            far = jnp.where(slot < 2, wide, own)
        else:
            wide, own = right_ref[RANK[j]], mine_left_ref[RANK[j]]
            other = turn(left_ref[narrow], -2 * half)
            centre = jnp.where(slot < 2, other, turn(wide, 2))
            near = jnp.where(slot == 1, turn(own, 1), turn(centre, -1))
            near = jnp.where(slot >= 2, turn(wide, 1), near)
            far = jnp.where(slot < 2, own, wide)
        columns_ref[j] = jnp.where(used, centre, 0.0)
        near_ref[j] = jnp.where(used, near, 0.0)
        far_ref[j] = jnp.where(used, far, 0.0)


def packed_source(
    table, left_ref, right_ref, columns_ref, side_refs, sums_ref, part_ref, drive_ref, ice_ref, p_ref
):
    near_ref, far_ref = side_refs
    lane = lanes()
    slot, place = lane % 4, lane // 4 % BANDS
    both = jnp.where(slot < 2, left_ref[SENT - 1], turn(right_ref[SENT - 1], 2))
    east, north, land, south_rows, north_rows = (spread(both, i) for i in range(FIELDS))
    row = (TILES * sublanes() + lane // GROUP).astype(jnp.float32)
    held = (row < south_rows) | (row >= LAT - north_rows)
    sea = jnp.where(land > 0.5, 1.0, 0.0)
    ice = jnp.where(land > 1.5, 1.0, 0.0)
    ice_ref[...] = ice
    inverse = table(5)
    slope = jnp.zeros((8, WIDTH), jnp.float32)
    stress = slope
    for j in range(ND):
        lon = packed_coefficients(inverse, COURANT_MAX * COS[j])
        lat = packed_coefficients(inverse, 0.5 * COURANT_MAX * SIN[j])
        centre = columns_ref[j]
        x = lon[0] * centre + lon[1] * near_ref[j] + lon[2] * far_ref[j]
        x = packed_lat(j, x, *lat)
        p = jnp.where(held, centre, jnp.maximum(x, 0.0)) * sea
        drive = drive_of(j, east, north, 1.0 - ice)
        drive_ref[j] = drive
        p_ref[j] = p
        slope = slope + p
        stress = stress + p * drive

    def running(tile):
        for step in (1, 2, 4):
            tile = tile + jnp.where(place >= step, turn(tile, 4 * step), 0.0)
        return tile

    out = [jnp.zeros((8, WIDTH), jnp.float32) for _ in range(PACKED_SUMS)]

    def put(index, tile):
        position = index % BANDS
        moved = turn(tile, 4 * (position - (BANDS - 1)))
        out[index // BANDS] = jnp.where(place == position, moved, out[index // BANDS])

    for j, excess in enumerate(excess_of([p_ref[j] for j in range(ND)])):
        total = running(excess)
        put(j, total)
        rate = excess * table(0) + (total - excess) * table(1)
        part_ref[j] = p_ref[j] * jnp.exp(rate)
    put(ND, running(slope * table(2)))
    put(ND + 1, running(stress * table(3)))
    for i in range(PACKED_SUMS):
        sums_ref[PACKED_AT + i] = out[i]


def excess_of(p):
    out = []
    for saturation in saturation_of(p):
        capped = jnp.maximum(saturation, CAP)
        excess = capped * lax.rsqrt(capped) - ROOT_CAP
        out.append(excess * excess)
    return out


def source_kernel(first, *refs):
    scal_ref, table_ref, x_ref, spec_ref, east_ref, north_ref, land_ref, rows_ref = refs[:8]
    refs = refs[8:]
    freq = lax.axis_index("freq")
    bands = x_ref.shape[0]

    def table(i):
        return table_ref[freq, i]

    if first:
        mine_right_ref, mine_left_ref, even_ref, odd_ref = refs[:4]
        p_ref, excess_ref, sums_ref, part_ref, packed_drive_ref, ice_ref = refs[4:10]
        drive_ref, fix_ref, left_ref, right_ref, columns_ref, near_ref, far_ref, packed_ref = refs[10:]
        odd = lax.axis_index("lon") % 2 == 1
        for i in range(SENT):
            even, other = even_ref[i], odd_ref[i]
            left_ref[i] = jnp.where(odd, even, other)
            right_ref[i] = jnp.where(odd, other, even)
        sides = (near_ref, far_ref)
        packed_start(mine_right_ref, mine_left_ref, left_ref, right_ref, columns_ref, sides)
        packed_source(
            table, left_ref, right_ref, columns_ref, sides,
            sums_ref, part_ref, packed_drive_ref, ice_ref, packed_ref,
        )
    else:
        columns_ref, p_ref, excess_ref, sums_ref, drive_ref, fix_ref = refs
    packed_fix(table, columns_ref, fix_ref)
    for i in range(PACKED_AT):
        sums_ref[i] = jnp.zeros((8, WIDTH), jnp.float32)
    for r in range(TILES):
        rows = tile_rows(r)
        water = jnp.where(land_ref[rows, :] == 2, 0.0, 1.0)
        east, north = east_ref[rows, :], north_ref[rows, :]
        for j in range(ND):
            drive_ref[j, r] = drive_of(j, east, north, water)

    lane = lanes()
    at_edge = {True: lane < 2, False: lane >= WIDTH - 2}

    def band(k, carry):
        extra = (freq * bands + k) * STRIDE + 6 * ND
        for r in range(TILES):
            rows = tile_rows(r)
            row = TILES * sublanes() + r
            held = (row < rows_ref[0:1, :]) | (row >= LAT - rows_ref[1:2, :])
            sea = jnp.where(land_ref[rows, :] != 0, 1.0, 0.0)
            slope = jnp.zeros((8, WIDTH), jnp.float32)
            stress = slope
            shift = {
                True: jnp.bitwise_and(WIDTH - GROUP * r - 4 * k, WIDTH - 1),
                False: WIDTH - 4 - GROUP * r - 4 * k,
            }
            for j in range(ND):
                back = BACK_LON[j]
                moved = pltpu.roll(fix_ref[j], shift[back], 1)
                p = x_ref[k, j, r] + jnp.where(at_edge[back], moved, 0.0)
                p = jnp.where(held, spec_ref[k, j, rows, :], jnp.maximum(p, 0.0)) * sea
                p_ref[k, j, r] = p
                slope = slope + p
                stress = stress + p * drive_ref[j, r]
            sums_ref[SLOPE_AT + r] += slope * scal_ref[extra + 2]
            sums_ref[STRESS_AT + r] += stress * scal_ref[extra + 3]
            for j, excess in enumerate(excess_of([p_ref[k, j, r] for j in range(ND)])):
                excess_ref[k, j, r] = excess
                sums_ref[TILES * j + r] += excess
        return carry

    lax.fori_loop(0, bands, band, 0)


def local_kernel(scal_ref, p_ref, excess_ref, out_ref):
    bands = p_ref.shape[0]
    first = (lax.axis_index("freq") * bands) * STRIDE + 6 * ND
    some = 6

    def directions(group, carry):
        for i in range(some):
            j = group * some + i
            for r in range(TILES):
                lower = jnp.zeros((8, WIDTH), jnp.float32)
                for k in range(bands):
                    excess = excess_ref[k, j, r]
                    at = first + k * STRIDE
                    rate = excess * scal_ref[at] + lower * scal_ref[at + 1]
                    out_ref[k, j, r] = p_ref[k, j, r] * jnp.exp(rate)
                    lower = lower + excess
        return carry

    lax.fori_loop(0, ND // some, directions, 0)


def pair_kernel(sums_ref, other_ref, out_ref):
    first = (lax.axis_index("freq") % 2) * HALF_TILES
    for i in range(HALF_TILES):
        out_ref[i] = sums_ref[first + i] + other_ref[first + i]
    for i in range(out_ref.shape[0] - HALF_TILES):
        out_ref[HALF_TILES + i] = sums_ref[SLOPE_AT + i] + other_ref[SLOPE_AT + i]


def damp_and_gain(slope, stress, ice):
    damp = SWELL_DAMP * (slope / (slope + 1.0)) + ICE_DAMP * ice
    return damp, GROWTH * (1.0 + stress / (stress + 1.0))


def grow_half(half, last, near, refs):
    scal_ref, part_ref, sums_ref, other_ref, mine_ref, lower_ref = refs[:6]
    east_ref, north_ref, land_ref, out_ref, rate_ref, field_ref, sent = refs[6:]
    bands = part_ref.shape[0]
    freq = lax.axis_index("freq")
    odd = jnp.where(freq % 2 == 1, 1.0, 0.0)
    upper = jnp.where(freq >= 2, 1.0, 0.0)
    after = SLOPE_AT - HALF_TILES
    for r in range(TILES):
        rows = tile_rows(r)
        ice = jnp.where(land_ref[rows, :] == 2, 1.0, 0.0)
        slope, stress = (
            (sums_ref[at + r] + other_ref[at + r]) + mine_ref[at + r - after]
            for at in (SLOPE_AT, STRESS_AT)
        )
        damp, gain = damp_and_gain(slope, stress, ice)
        east, north = east_ref[rows, :], north_ref[rows, :]
        for i in range(HALF):
            j = half * HALF + i
            lower = odd * other_ref[TILES * j + r] + upper * lower_ref[TILES * i + r]
            drive = drive_of(j, east, north, 1.0 - ice)
            rate_ref[i, r] = gain * drive - damp - LOWER * lower

    inside = None if last else inside_masks()

    def send(k):
        place = pl.ds(half * HALF, HALF)
        return pltpu.make_async_copy(field_ref.at[k], out_ref.at[k, place], sent.at[k])

    def band(k, carry):
        base = (freq * bands + k) * STRIDE
        root = scal_ref[base + 6 * ND + 4]
        for i in range(HALF):
            j = half * HALF + i
            tiles = [part_ref[k, j, r] * jnp.exp(rate_ref[i, r] * root) for r in range(TILES)]
            if last:
                for r in range(TILES):
                    field_ref[k, i, tile_rows(r), :] = tiles[r]
            else:
                for r, tile in enumerate(drift(j, base, tiles, scal_ref, inside)):
                    out_ref[k, j, r] = tile
        if last:
            send(k).start()
        return carry

    lax.fori_loop(0, bands, band, 0)
    if last:
        for k in range(bands):
            send(k).wait()


def growth_kernel(last, near, *refs):
    operands, refs = refs[:9], refs[9:]
    scal_ref, part_ref, sums_ref, other_ref, mine_ref = operands[:5]
    freq = lax.axis_index("freq")
    rest = (None, None)
    if near and last:
        out_ref, slope_ref, rate_ref, *rest = refs
        for r in range(TILES):
            at = SLOPE_AT + r
            total = (sums_ref[at] + other_ref[at]) + mine_ref[at - SLOPE_AT + HALF_TILES]
            slope_ref[tile_rows(r), :] = total
    elif near:
        table_ref, packed_part_ref, packed_drive_ref, ice_ref, out_ref, columns_ref, rate_ref = refs
        odd = jnp.where(freq % 2 == 1, 1.0, 0.0)
        upper = jnp.where(freq >= 2, 1.0, 0.0)
        total, lower = [], []
        for i in range(PACKED_SUMS):
            here, there = PACKED_AT + i, HALF_TILES + 2 * TILES + i
            total.append((sums_ref[here] + other_ref[here]) + mine_ref[there])
            lower.append(odd * other_ref[here] + upper * mine_ref[there])
        slope, stress = (spread(total[i // BANDS], i % BANDS) for i in (ND, ND + 1))
        damp, gain = damp_and_gain(slope, stress, ice_ref[...])
        root = table_ref[freq, 4]
        for j in range(ND):
            under = spread(lower[j // BANDS], j % BANDS)
            rate = gain * packed_drive_ref[j] - damp - LOWER * under
            columns_ref[j] = packed_part_ref[j] * jnp.exp(root * rate)
    else:
        _, out_ref, rate_ref, *rest = refs
        rest = rest or (None, None)
    for half in range(2):

        @pl.when(freq % 2 == (half if near else 1 - half))
        def _():
            grow_half(half, last, near, operands + (out_ref, rate_ref, *rest))


def cost(tiles, ops, moves):
    return pl.CostEstimate(
        flops=tiles * ops * 8 * WIDTH, bytes_accessed=tiles * moves * 32 * WIDTH, transcendentals=0
    )


def per_device(spectrum, east_wind, north_wind, land_sea, edge_rows):
    bands, count, lat_rows, width = spectrum.shape
    assert (bands, count, lat_rows, width) == (BANDS, ND, LAT, WIDTH)
    ring = lax.axis_size("lon")
    assert lax.axis_size("freq") == 4 and bands * 4 == NF and ring % 2 == 0
    f32 = jnp.float32

    def tiles(count):
        return jax.ShapeDtypeStruct((count, 8, WIDTH), f32)

    field = jax.ShapeDtypeStruct(spectrum.shape, f32)
    spread_field = jax.ShapeDtypeStruct((bands, ND, TILES, 8, WIDTH), f32)
    plane = jax.ShapeDtypeStruct((LAT, WIDTH), f32)
    tile = jax.ShapeDtypeStruct((8, WIDTH), f32)
    smem = pl.BlockSpec(memory_space=pltpu.SMEM)
    vmem = pl.BlockSpec(memory_space=pltpu.VMEM)
    hbm = pl.BlockSpec(memory_space=pltpu.HBM)
    params = pltpu.CompilerParams(vmem_limit_bytes=16 * 1024 * 1024)
    scalars, table = jnp.asarray(SCALARS), jnp.asarray(PACKED_TABLE)
    swap_core = [(0, 1), (1, 0), (2, 3), (3, 2)]
    swap_chip = [(0, 2), (2, 0), (1, 3), (3, 1)]
    swap_even = [(i, i ^ 1) for i in range(ring)]
    swap_odd = [(i, (i + (1 if i % 2 else -1)) % ring) for i in range(ring)]
    whole = bands * ND * TILES
    by_direction = pltpu.VMEM((ND, TILES, 8, WIDTH), f32)
    packed = pltpu.VMEM((ND, 8, WIDTH), f32)
    received = pltpu.VMEM((SENT, 8, WIDTH), f32)

    arguments = [spectrum, east_wind, north_wind, land_sea, edge_rows]
    spectrum, right, left, east_wind, north_wind, land_sea, edge_rows, even, odd = pl.pallas_call(
        pack_kernel,
        in_specs=[hbm] * 5,
        out_specs=[vmem] * 9,
        out_shape=[field, tiles(SENT), tiles(SENT)]
        + [jax.ShapeDtypeStruct(x.shape, x.dtype) for x in arguments[1:]]
        + [tiles(SENT), tiles(SENT)],
        scratch_shapes=[pltpu.SemaphoreType.DMA((ND // CHUNK + 4,))],
        compiler_params=params,
        cost_estimate=cost(whole, 6, 2),
        name="pack_columns",
    )(*(pltpu.with_memory_space_constraint(x, pltpu.HBM) for x in arguments))
    even = lax.ppermute(even, "lon", swap_even)
    odd = lax.ppermute(odd, "lon", swap_odd)
    drifted = pl.pallas_call(
        drift_kernel,
        in_specs=[smem, vmem],
        out_specs=vmem,
        out_shape=spread_field,
        compiler_params=params,
        cost_estimate=cost(whole, 12, 2),
        name="drift",
    )(scalars, spectrum)

    fields = [east_wind, north_wind, land_sea]
    for step in range(STEPS):
        first, last = step == 0, step == STEPS - 1
        sums = PACKED_AT + (PACKED_SUMS if first else 0)
        half_sums = sums - SLOPE_AT + HALF_TILES
        operands = [scalars, table, drifted, spectrum, *fields, edge_rows]
        operands += [right, left, even, odd] if first else [columns]
        p, excess, mine, *packed_state = pl.pallas_call(
            functools.partial(source_kernel, first),
            in_specs=[smem] + [vmem] * (len(operands) - 1),
            out_specs=[vmem] * (6 if first else 3),
            out_shape=[spread_field, spread_field, tiles(sums)]
            + ([tiles(ND), tiles(ND), tile] if first else []),
            scratch_shapes=[by_direction, packed]
            + ([received] * 2 + [packed] * 4 if first else []),
            compiler_params=params,
            cost_estimate=cost(whole, 30, 3),
            name="sources",
        )(*operands)
        other = lax.ppermute(mine, "freq", swap_core)
        pair = pl.pallas_call(
            pair_kernel,
            in_specs=[vmem] * 2,
            out_specs=vmem,
            out_shape=tiles(half_sums),
            compiler_params=params,
            cost_estimate=cost(half_sums, 1, 3),
            name="pair_sums",
        )(mine, other)
        near = lax.ppermute(pair, "freq", swap_chip)
        excess, _ = lax.optimization_barrier((excess, pair))
        part = pl.pallas_call(
            local_kernel,
            in_specs=[smem] + [vmem] * 2,
            out_specs=vmem,
            out_shape=spread_field,
            compiler_params=params,
            cost_estimate=cost(whole, 8, 3),
            name="local_rate",
        )(scalars, p, excess)
        near, part = lax.optimization_barrier((near, part))
        far = lax.ppermute(near, "freq", swap_core)

        def grow(is_near, lower, extra, more_specs, more_shapes, alias):
            operands = [scalars, part, mine, other, near, lower, *fields] + extra
            scratch = [pltpu.VMEM((HALF, TILES, 8, WIDTH), f32)]
            if last:
                scratch += [
                    pltpu.VMEM((bands, HALF, LAT, WIDTH), f32),
                    pltpu.SemaphoreType.DMA((bands,)),
                ]
            specs = [smem] + [vmem] * (len(operands) - 1)
            if alias and last:
                specs[-1] = hbm
            return pl.pallas_call(
                functools.partial(growth_kernel, last, is_near),
                in_specs=specs,
                out_specs=[hbm if last else vmem] + more_specs,
                out_shape=[field if last else spread_field] + more_shapes,
                input_output_aliases={len(operands) - 1: 0} if alias else {},
                scratch_shapes=scratch,
                compiler_params=params,
                cost_estimate=cost(whole, 6 if last else 12, 1),
                name="grow_near" if is_near else "grow_far",
            )(*operands)

        extra = [] if last else [table, *packed_state]
        made, columns = grow(True, near, extra, [vmem], [plane if last else tiles(ND)], False)
        (drifted,) = grow(False, far, [made], [], [], True)
    return drifted, columns


def solution(mesh):
    in_specs = (
        P("freq", None, None, "lon"),
        P(None, "lon"),
        P(None, "lon"),
        P(None, "lon"),
        P(None, "lon"),
    )
    out_specs = (P("freq", None, None, "lon"), P(None, "lon"))
    return jax.shard_map(
        per_device, mesh=mesh, in_specs=in_specs, out_specs=out_specs, check_vma=False
    )
```

time: 61.3 us -> 61 us (level)
  waiting for transfers between devices: 15.2 us -> 13.1 us
  Pallas kernels: 35.5 us -> 36.6 us
  starting transfers between devices: 9.63 us -> 10.4 us
    pallas_call x3 -> x5, Pallas kernels: 9.59 us -> 14.8 us  [the longest x4 11.4 us: grow(): pl.pallas_call(functools.partial(growth_kernel, last, is_near), in_specs=...]
    pallas_call x2 -> x1, Pallas kernels: 8.01 us -> 3.48 us  [per_device(): pl.pallas_call(drift_kernel, in_specs=[smem, vmem], out_specs=vmem, out_s...]
    ppermute x2, waiting for transfers between devices: 3.08 us -> 0.01 us  [per_device(): far = lax.ppermute(near, 'freq', swap_core)]
    pallas_call x2, Pallas kernels: 12.6 us -> 14 us  [per_device(): pl.pallas_call(functools.partial(source_kernel, first), in_specs=[smem] +...]
    pallas_call x2, Pallas kernels: 5.28 us -> 4.23 us  [per_device(): pl.pallas_call(local_kernel, in_specs=[smem] + [vmem] * 2, out_specs=vmem...]
    ppermute x2, waiting for transfers between devices: 8.45 us -> 9.37 us  [per_device(): near = lax.ppermute(pair, 'freq', swap_chip)]
  transfers between devices with their start and end apart: 8 -> 8, of which waited for: 7 -> 5; matrix products, arithmetic and copies ran while one was open for 0% -> 0% of each run, Pallas kernels for 15% -> 23%
where the time goes in v4:
time: 61 us; the launch traced here: 60.8 us
  Pallas kernels  36.6 us (60%)
  waiting for transfers between devices  13.1 us (21%)
  starting transfers between devices  10.4 us (17%)
  between operations  0.75 us (1%)
    pallas_call x2, Pallas kernels, per_device(): pl.pallas_call(functools.partial(source_kernel, first), in_specs=[smem] +...  14 us
    pallas_call x4, Pallas kernels, grow(): pl.pallas_call(functools.partial(growth_kernel, last, is_near), in_specs=...  11.4 us
    ppermute x2, waiting for transfers between devices, per_device(): near = lax.ppermute(pair, 'freq', swap_chip)  9.37 us
    pallas_call x2, Pallas kernels, per_device(): pl.pallas_call(local_kernel, in_specs=[smem] + [vmem] * 2, out_specs=vmem...  4.23 us
    ppermute x1, starting transfers between devices, per_device(): odd = lax.ppermute(odd, 'lon', swap_odd)  3.57 us
    pallas_call x1, Pallas kernels, per_device(): pl.pallas_call(drift_kernel, in_specs=[smem, vmem], out_specs=vmem, out_s...  3.48 us
    pallas_call x1, Pallas kernels, per_device(): pl.pallas_call(pack_kernel, in_specs=[hbm] * 5, out_specs=[vmem] * 9, out...  3.34 us
    ppermute x2, waiting for transfers between devices, per_device(): other = lax.ppermute(mine, 'freq', swap_core)  3.3 us
  transfers between devices with their start and end apart: 8, of which 5 were waited for; matrix products, arithmetic and copies ran while one was open for 0% of the time, Pallas kernels for 23%

profile of v4, /device:TPU:0, one launch (start us, length us, event | category | flops | bytes accessed | tf_op | source)
XLA Modules:
  0.0 60.8 jit_solution(12591310298017704656)
XLA Ops:
  0.6 0.0 copy-start
  0.6 3.3 %pack_columns.1 = (f32[8,36,24,128]{3,2,1,0:T(8,128)S(1)}, f32[28,8,128]{2,1,0:T(8,128)S(1)}, f32[28,8,128]{2,1,0:T(8,128)S(1)}, f32[24,128]{1,0:T(8,128)S(1)}, ...) custom-call(f32[8,36,24,128]{3,2,1,0:T(8,128)} %spec_ref.1, ...), custom_call_target="tpu_custom_call" | custom-call | flops 5308416 | bytes 7077888 | tf_op jit(solution)/shard_map/pack_columns/pallas_call | solution.py:654
  4.0 3.0 %collective-permute-start = (f32[28,8,128]{2,1,0:T(8,128)S(1)}, f32[28,8,128]{2,1,0:T(8,128)S(1)}, u32[]{:S(2)}, u32[]{:S(2)}) collective-permute-start(f32[28,8,128]{2,1,0:T(8,128)S(1)} %get-tuple-element.37), channel_id=1, source_target_pairs={{0,4},{4,0},{8,12},{12,8},{16,20},{20,16},{24,28},{28,24},{1,5},{5... | collective-permute-start | bytes 344072 | tf_op jit(solution)/shard_map/ppermute | solution.py:666
  7.0 3.6 %collective-permute-start.1 = (f32[28,8,128]{2,1,0:T(8,128)S(1)}, f32[28,8,128]{2,1,0:T(8,128)S(1)}, u32[]{:S(2)}, u32[]{:S(2)}) collective-permute-start(f32[28,8,128]{2,1,0:T(8,128)S(1)} %get-tuple-element.38), channel_id=1, source_target_pairs={{0,28},{4,8},{8,4},{12,16},{16,12},{20,24},{24,20},{28,0},{1,29},{... | collective-permute-start | bytes 344072 | tf_op jit(solution)/shard_map/ppermute | solution.py:667
  10.6 0.0 copy-done
  10.6 0.0 copy-start.1
  10.6 3.5 %drift.1.refs_2_ = f32[8,36,3,8,128]{4,3,2,1,0:T(8,128)S(1)} custom-call(f32[7168]{0:T(1024)S(1)} %copy-done, f32[8,36,24,128]{3,2,1,0:T(8,128)S(1)} %get-tuple-element.30.q_ref.refs_3_), custom_call_target="tpu_custom_call" | custom-call | flops 10616832 | bytes 7077888 | tf_op jit(solution)/shard_map/drift/pallas_call | solution.py:668
  14.1 0.0 collective-permute-done.refs_10_
  14.1 0.4 collective-permute-done.1.refs_11_
  14.5 0.0 copy-done.1
  14.5 8.4 %sources.2 = (f32[8,36,3,8,128]{4,3,2,1,0:T(8,128)S(1)}, f32[8,36,3,8,128]{4,3,2,1,0:T(8,128)S(1)}, f32[119,8,128]{2,1,0:T(8,128)S(1)}, f32[36,8,128]{2,1,0:T(8,...) custom-call(f32[7168]{0:T(1024)S(1)} %copy-done, f32[4,6,8,128]{3,2,1,0:T(8,128)S(1)} %copy-done.1, ...), custom_call_target="tpu_custom_call" | custom-call | flops 26542080 | bytes 10616832 | tf_op jit(solution)/shard_map/sources/pallas_call | solution.py:685
  22.9 0.1 collective-permute-start.2
  23.0 1.8 %collective-permute-done.2.other_ref.refs_3_ = f32[119,8,128]{2,1,0:T(8,128)S(1)} collective-permute-done((f32[119,8,128]{2,1,0:T(8,128)S(1)}, f32[119,8,128]{2,1,0:T(8,128)S(1)}, u32[]{:S(2)}, u32[]{:S(2)}) %collective-permute-start.2) | collective-permute-done | bytes 487456 | tf_op jit(solution)/shard_map/ppermute | solution.py:697
  24.8 1.6 %collective-permute-start.3 = (f32[65,8,128]{2,1,0:T(8,128)S(1)}, f32[65,8,128]{2,1,0:T(8,128)S(1)}, u32[]{:S(2)}, u32[]{:S(2)}) collective-permute-start(f32[65,8,128]{2,1,0:T(8,128)S(1)} %pair_sums.2), channel_id=1, source_target_pairs={{0,2},{2,0},{1,3},{3,1},{4,6},{6,4},{5,7},{7,5},{8,10},{10,8},{9,1... | collective-permute-start | bytes 798728 | tf_op jit(solution)/shard_map/ppermute | solution.py:707
  26.4 2.1 %local_rate.2.refs_1_ = f32[8,36,3,8,128]{4,3,2,1,0:T(8,128)S(1)} custom-call(f32[7168]{0:T(1024)S(1)} %copy-done, f32[8,36,3,8,128]{4,3,2,1,0:T(8,128)S(1)} %get-tuple-element.40.p_ref, f32[8,36,3,8,128]{4,3,2,1,0:T(8,128)S(1)} %get-tuple-element.42.excess_ref), custom_call_target="tpu_custom_call" | custom-call | flops 7077888 | bytes 10616832 | tf_op jit(solution)/shard_map/local_rate/pallas_call | solution.py:709
  28.5 4.8 %collective-permute-done.3.refs_4_.refs_5_ = f32[65,8,128]{2,1,0:T(8,128)S(1)} collective-permute-done((f32[65,8,128]{2,1,0:T(8,128)S(1)}, f32[65,8,128]{2,1,0:T(8,128)S(1)}, u32[]{:S(2)}, u32[]{:S(2)}) %collective-permute-start.3) | collective-permute-done | bytes 266272 | tf_op jit(solution)/shard_map/ppermute | solution.py:707
  33.3 0.0 collective-permute-start.4
  33.3 3.1 %grow_near.2 = (f32[8,36,3,8,128]{4,3,2,1,0:T(8,128)S(1)}, f32[36,8,128]{2,1,0:T(8,128)S(1)}) custom-call(f32[7168]{0:T(1024)S(1)} %copy-done, f32[8,36,3,8,128]{4,3,2,1,0:T(8,128)S(1)} %local_rate.2.refs_1_, f32[119,8,128]{2,1,0:T(8,128)S(1)} %get-tuple-element.39.sums_ref.refs_2_, f32[119,8,128]{2,1,0:T(8,128)S(1)} %collective-permute-done.2.other_ref.refs_3_, ...), custom_call_target="tpu_custom_call" | custom-call | flops 10616832 | bytes 3538944 | tf_op jit(solution)/shard_map/grow_near/pallas_call | solution.py:732
  36.5 0.0 collective-permute-done.4.refs_5_
  36.5 2.8 %grow_far.2.refs_2_ = f32[8,36,3,8,128]{4,3,2,1,0:T(8,128)S(1)} custom-call(f32[7168]{0:T(1024)S(1)} %copy-done, f32[8,36,3,8,128]{4,3,2,1,0:T(8,128)S(1)} %local_rate.2.refs_1_, f32[119,8,128]{2,1,0:T(8,128)S(1)} %get-tuple-element.39.sums_ref.refs_2_, f32[119,8,128]{2,1,0:T(8,128)S(1)} %collective-permute-done.2.other_ref.refs_3_, ...), custom_call_target="tpu_custom_call", output_to_operand_aliasing={{}: (9, {})} | custom-call | flops 10616832 | bytes 3538944 | tf_op jit(solution)/shard_map/grow_far/pallas_call | solution.py:732
  39.3 5.7 %sources.3 = (f32[8,36,3,8,128]{4,3,2,1,0:T(8,128)S(1)}, f32[8,36,3,8,128]{4,3,2,1,0:T(8,128)S(1)}, f32[114,8,128]{2,1,0:T(8,128)S(1)}) custom-call(f32[7168]{0:T(1024)S(1)} %copy-done, f32[4,6,8,128]{3,2,1,0:T(8,128)S(1)} %copy-done.1, f32[8,36,3,8,128]{4,3,2,1,0:T(8,128)S(1)} %grow_far.2.refs_2_, f32[8,36,24,128]{3,2,1,0:T(8,128)S(1)} %get-tuple-element.30.q_ref.refs_3_, ...), custom_call_target="tpu_custom_call" | custom-call | flops 26542080 | bytes 10616832 | tf_op jit(solution)/shard_map/sources/pallas_call | solution.py:685
  45.0 0.6 collective-permute-start.5
  45.5 1.5 %collective-permute-done.5.other_ref.refs_3_ = f32[114,8,128]{2,1,0:T(8,128)S(1)} collective-permute-done((f32[114,8,128]{2,1,0:T(8,128)S(1)}, f32[114,8,128]{2,1,0:T(8,128)S(1)}, u32[]{:S(2)}, u32[]{:S(2)}) %collective-permute-start.5) | collective-permute-done | bytes 466976 | tf_op jit(solution)/shard_map/ppermute | solution.py:697
  47.0 1.6 %collective-permute-start.6 = (f32[60,8,128]{2,1,0:T(8,128)S(1)}, f32[60,8,128]{2,1,0:T(8,128)S(1)}, u32[]{:S(2)}, u32[]{:S(2)}) collective-permute-start(f32[60,8,128]{2,1,0:T(8,128)S(1)} %pair_sums.3), channel_id=1, source_target_pairs={{0,2},{2,0},{1,3},{3,1},{4,6},{6,4},{5,7},{7,5},{8,10},{10,8},{9,1... | collective-permute-start | bytes 737288 | tf_op jit(solution)/shard_map/ppermute | solution.py:707
  48.6 2.1 %local_rate.3.refs_1_ = f32[8,36,3,8,128]{4,3,2,1,0:T(8,128)S(1)} custom-call(f32[7168]{0:T(1024)S(1)} %copy-done, f32[8,36,3,8,128]{4,3,2,1,0:T(8,128)S(1)} %get-tuple-element.51.p_ref, f32[8,36,3,8,128]{4,3,2,1,0:T(8,128)S(1)} %get-tuple-element.53.excess_ref), custom_call_target="tpu_custom_call" | custom-call | flops 7077888 | bytes 10616832 | tf_op jit(solution)/shard_map/local_rate/pallas_call | solution.py:709
  50.7 4.6 %collective-permute-done.6.refs_4_.refs_5_ = f32[60,8,128]{2,1,0:T(8,128)S(1)} collective-permute-done((f32[60,8,128]{2,1,0:T(8,128)S(1)}, f32[60,8,128]{2,1,0:T(8,128)S(1)}, u32[]{:S(2)}, u32[]{:S(2)}) %collective-permute-start.6) | collective-permute-done | bytes 245792 | tf_op jit(solution)/shard_map/ppermute | solution.py:707
  55.3 0.0 collective-permute-start.7
  55.3 3.1 %grow_near.3 = (f32[8,36,24,128]{3,2,1,0:T(8,128)}, f32[24,128]{1,0:T(8,128)}) custom-call(f32[7168]{0:T(1024)S(1)} %copy-done, f32[8,36,3,8,128]{4,3,2,1,0:T(8,128)S(1)} %local_rate.3.refs_1_, f32[114,8,128]{2,1,0:T(8,128)S(1)} %get-tuple-element.50.sums_ref.refs_2_, f32[114,8,128]{2,1,0:T(8,128)S(1)} %collective-permute-done.5.other_ref.refs_3_, ...), custom_call_target="tpu_custom_call" | custom-call | flops 5308416 | bytes 3538944 | tf_op jit(solution)/shard_map/grow_near/pallas_call | solution.py:732
  58.4 0.0 collective-permute-done.7.refs_5_
  58.4 2.5 %grow_far.3 = f32[8,36,24,128]{3,2,1,0:T(8,128)} custom-call(f32[7168]{0:T(1024)S(1)} %copy-done, f32[8,36,3,8,128]{4,3,2,1,0:T(8,128)S(1)} %local_rate.3.refs_1_, f32[114,8,128]{2,1,0:T(8,128)S(1)} %get-tuple-element.50.sums_ref.refs_2_, f32[114,8,128]{2,1,0:T(8,128)S(1)} %collective-permute-done.5.other_ref.refs_3_, ...), custom_call_target="tpu_custom_call", output_to_operand_aliasing={{}: (9, {})} | custom-call | flops 5308416 | bytes 3538944 | tf_op jit(solution)/shard_map/grow_far/pallas_call | solution.py:732
  (2 shorter events, 0.1 us)
Async XLA Ops:
  0.6 9.9 %copy-start = (f32[7168]{0:T(1024)S(1)}, f32[7168]{0:T(1024)}, u32[]{:S(2)}) copy-start(f32[7168]{0:T(1024)} %constant.4.clone.scal_ref.refs_0_) | copy-start | bytes 86020
  4.0 10.1 %collective-permute-start = (f32[28,8,128]{2,1,0:T(8,128)S(1)}, f32[28,8,128]{2,1,0:T(8,128)S(1)}, u32[]{:S(2)}, u32[]{:S(2)}) collective-permute-start(f32[28,8,128]{2,1,0:T(8,128)S(1)} %get-tuple-element.37), channel_id=1, source_target_pairs={{0,4},{4,0},{8,12},{12,8},{16,20},{20,16},{24,28},{28,24},{1,5},{5... | collective-permute-start | bytes 344072 | tf_op jit(solution)/shard_map/ppermute | solution.py:666
  7.0 7.5 %collective-permute-start.1 = (f32[28,8,128]{2,1,0:T(8,128)S(1)}, f32[28,8,128]{2,1,0:T(8,128)S(1)}, u32[]{:S(2)}, u32[]{:S(2)}) collective-permute-start(f32[28,8,128]{2,1,0:T(8,128)S(1)} %get-tuple-element.38), channel_id=1, source_target_pairs={{0,28},{4,8},{8,4},{12,16},{16,12},{20,24},{24,20},{28,0},{1,29},{... | collective-permute-start | bytes 344072 | tf_op jit(solution)/shard_map/ppermute | solution.py:667
  10.6 3.9 %copy-start.1 = (f32[4,6,8,128]{3,2,1,0:T(8,128)S(1)}, f32[4,6,8,128]{3,2,1,0:T(8,128)}, u32[]{:S(2)}) copy-start(f32[4,6,8,128]{3,2,1,0:T(8,128)} %constant.5.clone.refs_1_.refs_9_) | copy-start | bytes 294916
  22.9 1.9 %collective-permute-start.2 = (f32[119,8,128]{2,1,0:T(8,128)S(1)}, f32[119,8,128]{2,1,0:T(8,128)S(1)}, u32[]{:S(2)}, u32[]{:S(2)}) collective-permute-start(f32[119,8,128]{2,1,0:T(8,128)S(1)} %get-tuple-element.39.sums_ref.refs_2_), channel_id=1, source_target_pairs={{0,1},{1,0},{2,3},{3,2},{4,5},{5,4},{6,7},{7,6},{8,9},{9,8},{10,11... | collective-permute-start | bytes 1462280 | tf_op jit(solution)/shard_map/ppermute | solution.py:697
  24.8 8.5 %collective-permute-start.3 = (f32[65,8,128]{2,1,0:T(8,128)S(1)}, f32[65,8,128]{2,1,0:T(8,128)S(1)}, u32[]{:S(2)}, u32[]{:S(2)}) collective-permute-start(f32[65,8,128]{2,1,0:T(8,128)S(1)} %pair_sums.2), channel_id=1, source_target_pairs={{0,2},{2,0},{1,3},{3,1},{4,6},{6,4},{5,7},{7,5},{8,10},{10,8},{9,1... | collective-permute-start | bytes 798728 | tf_op jit(solution)/shard_map/ppermute | solution.py:707
  33.3 3.1 %collective-permute-start.4 = (f32[65,8,128]{2,1,0:T(8,128)S(1)}, f32[65,8,128]{2,1,0:T(8,128)S(1)}, u32[]{:S(2)}, u32[]{:S(2)}) collective-permute-start(f32[65,8,128]{2,1,0:T(8,128)S(1)} %collective-permute-done.3.refs_4_.refs_5_), channel_id=1, source_target_pairs={{0,1},{1,0},{2,3},{3,2},{4,5},{5,4},{6,7},{7,6},{8,9},{9,8},{10,11... | collective-permute-start | bytes 798728 | tf_op jit(solution)/shard_map/ppermute | solution.py:719
  45.0 2.0 %collective-permute-start.5 = (f32[114,8,128]{2,1,0:T(8,128)S(1)}, f32[114,8,128]{2,1,0:T(8,128)S(1)}, u32[]{:S(2)}, u32[]{:S(2)}) collective-permute-start(f32[114,8,128]{2,1,0:T(8,128)S(1)} %get-tuple-element.50.sums_ref.refs_2_), channel_id=1, source_target_pairs={{0,1},{1,0},{2,3},{3,2},{4,5},{5,4},{6,7},{7,6},{8,9},{9,8},{10,11... | collective-permute-start | bytes 1400840 | tf_op jit(solution)/shard_map/ppermute | solution.py:697
  47.0 8.3 %collective-permute-start.6 = (f32[60,8,128]{2,1,0:T(8,128)S(1)}, f32[60,8,128]{2,1,0:T(8,128)S(1)}, u32[]{:S(2)}, u32[]{:S(2)}) collective-permute-start(f32[60,8,128]{2,1,0:T(8,128)S(1)} %pair_sums.3), channel_id=1, source_target_pairs={{0,2},{2,0},{1,3},{3,1},{4,6},{6,4},{5,7},{7,5},{8,10},{10,8},{9,1... | collective-permute-start | bytes 737288 | tf_op jit(solution)/shard_map/ppermute | solution.py:707
  55.3 3.1 %collective-permute-start.7 = (f32[60,8,128]{2,1,0:T(8,128)S(1)}, f32[60,8,128]{2,1,0:T(8,128)S(1)}, u32[]{:S(2)}, u32[]{:S(2)}) collective-permute-start(f32[60,8,128]{2,1,0:T(8,128)S(1)} %collective-permute-done.6.refs_4_.refs_5_), channel_id=1, source_target_pairs={{0,1},{1,0},{2,3},{3,2},{4,5},{5,4},{6,7},{7,6},{8,9},{9,8},{10,11... | collective-permute-start | bytes 737288 | tf_op jit(solution)/shard_map/ppermute | solution.py:719

commit v5 on v4

--- a/solution.py
+++ b/solution.py
@@ -187,18 +187,21 @@
     return drive * drive * open_water
 
 
+def tree(values):
+    values = list(values)
+    while len(values) > 1:
+        values = [sum(values[i + 1 : i + 2], values[i]) for i in range(0, len(values), 2)]
+    return values[0]
+
+
 def saturation_of(p):
     diff = [p[b] - p[b + HALF] for b in range(HALF)]
     both = [p[b] + p[b + HALF] for b in range(HALF)]
-    total = both[0]
-    for b in range(1, HALF):
-        total = total + both[b]
+    folded = [both[b] + both[b + QUARTER] for b in range(QUARTER)]
+    total = tree(folded)
     fold = [both[b] - both[b + QUARTER] for b in range(QUARTER)]
-    total_c, total_s = fold[0], None
-    for b in range(1, QUARTER):
-        total_c = total_c + fold[b] * float(COS2[b])
-        term = fold[b] * float(SIN2[b])
-        total_s = term if total_s is None else total_s + term
+    total_c = tree([fold[0]] + [fold[b] * float(COS2[b]) for b in range(1, QUARTER)])
+    total_s = tree([fold[b] * float(SIN2[b]) for b in range(1, QUARTER)])
     level = [None] * HALF
     for a in range(QUARTER):
         wave = total_c * float(COS2[a])
@@ -210,43 +213,48 @@
     def at(b):
         return diff[b % HALF], b // HALF % 2 == 1
 
-    def plus(x, b):
-        value, negative = at(b)
-        return x - value if negative else x + value
-
-    def minus(x, b):
-        value, negative = at(b)
-        return x + value if negative else x - value
-
-    plain, waves = diff[0], []
+    def minus(a, b):
+        x, flip_x = at(a)
+        y, flip_y = at(b)
+        if flip_x:
+            return y - x if flip_y else None, (x, y)
+        return x + y if flip_y else x - y, None
+
+    def plus_minus(value, a, b):
+        gap, opposite = minus(a, b)
+        if gap is None:
+            return value - (opposite[0] + opposite[1])
+        return value + gap
+
+    waves = []
     for a in range(2):
-        wave = diff[a]
-        for d in range(1, QUARTER):
-            pair = minus(diff[a + d], a - d + HALF)
-            wave = wave + pair * float(COS2[d])
-            if a == 0:
-                plain = plain + pair
-        waves.append(wave)
+        pairs = [minus(a + d, a - d + HALF)[0] for d in range(1, QUARTER)]
+        weighted = [pairs[d - 1] * float(COS2[d]) for d in range(1, QUARTER)]
+        waves.append(tree([diff[a]] + weighted))
+        if a == 0:
+            plain = tree([diff[0]] + pairs)
     twice = float(2.0 * COS2[1])
-    odd = [None] * HALF
+    odd, below = [None] * HALF, [None] * HALF
     odd[0] = plain + waves[0]
     window, before, now = plain, waves[0], waves[1]
     for a in range(1, QUARTER + 1):
-        window = plus(minus(window, a - 9), a + 8)
+        window = plus_minus(window, a + 8, a - 9)
         odd[a] = window + now
         if a < QUARTER:
-            step = minus(plus(twice * now - before, a + 8), a + 10)
-            before, now = now, step
+            rest = plus_minus(before, a + 10, a + 8)
+            before, now = now, twice * now - rest
     window, after, now = plain, waves[1], waves[0]
     for a in range(0, -(QUARTER - 1), -1):
-        step = minus(plus(twice * now - after, a + 8), a + 10)
-        after, now = now, step
-        window = minus(plus(window, a - 9 + 2 * HALF), a + 8)
-        odd[a - 1 + HALF] = -(window + now)
+        rest = plus_minus(after, a + 10, a + 8)
+        after, now = now, twice * now - rest
+        window = plus_minus(window, a - 9 + 2 * HALF, a + 8)
+        below[a - 1 + HALF] = window + now
     out = [None] * ND
     for a in range(HALF):
-        out[a] = level[a] + odd[a]
-        out[a + HALF] = level[a] - odd[a]
+        if odd[a] is not None:
+            out[a], out[a + HALF] = level[a] + odd[a], level[a] - odd[a]
+        else:
+            out[a], out[a + HALF] = level[a] - below[a], level[a] + below[a]
     return out
 
 
@@ -323,17 +331,25 @@
     return 1.0 + c * (0.5 * c - 1.5), c * (2.0 - c), c * (0.5 * c - 0.5)
 
 
+AHEAD = [j for j in range(ND) if not BACK_LON[j]]
+BACK = [j for j in range(ND) if BACK_LON[j]]
+
+
 def packed_fix(table, columns_ref, fix_ref):
     slot = lanes() % 4
     inverse = table(5)
-    for j in range(ND):
+
+    def one(j):
         back = BACK_LON[j]
         _, c1, c2 = packed_coefficients(inverse, COURANT_MAX * COS[j])
         tile = columns_ref[j]
         next_one = jnp.where(slot == (0 if back else 3), turn(tile, -1 if back else 1), 0.0)
         first = c2 * tile + c1 * next_one
         lat = packed_coefficients(inverse, 0.5 * COURANT_MAX * SIN[j])
-        fix_ref[j] = packed_lat(j, first, *lat)
+        return packed_lat(j, first, *lat)
+
+    for i in range(HALF):
+        fix_ref[i] = jnp.where(slot < 2, one(BACK[i]), turn(one(AHEAD[i]), -4))
 
 
 def packed_start(mine_right_ref, mine_left_ref, left_ref, right_ref, columns_ref, side_refs):
@@ -348,15 +364,15 @@
             wide, own = left_ref[RANK[j]], mine_right_ref[RANK[j]]
             other = turn(right_ref[narrow], 2 - 2 * half)
             centre = jnp.where(slot < 2, turn(wide, -2), other)
-            near = jnp.where(slot == 2, turn(own, -1), turn(centre, 1))
-            near = jnp.where(slot < 2, turn(wide, -1), near)
+            near = turn(jnp.where(slot == 3, own, wide), -1)
+            near = jnp.where(slot == 3, turn(centre, 1), near)
             far = jnp.where(slot < 2, wide, own)
         else:
             wide, own = right_ref[RANK[j]], mine_left_ref[RANK[j]]
             other = turn(left_ref[narrow], -2 * half)
             centre = jnp.where(slot < 2, other, turn(wide, 2))
-            near = jnp.where(slot == 1, turn(own, 1), turn(centre, -1))
-            near = jnp.where(slot >= 2, turn(wide, 1), near)
+            near = turn(jnp.where(slot == 0, own, wide), 1)
+            near = jnp.where(slot == 0, turn(centre, -1), near)
             far = jnp.where(slot < 2, own, wide)
         columns_ref[j] = jnp.where(used, centre, 0.0)
         near_ref[j] = jnp.where(used, near, 0.0)
@@ -364,7 +380,7 @@
 
 
 def packed_source(
-    table, left_ref, right_ref, columns_ref, side_refs, sums_ref, part_ref, drive_ref, ice_ref, p_ref
+    table, left_ref, right_ref, columns_ref, side_refs, sums_ref, part_ref, drive_ref, ice_ref
 ):
     near_ref, far_ref = side_refs
     lane = lanes()
@@ -377,20 +393,18 @@
     ice = jnp.where(land > 1.5, 1.0, 0.0)
     ice_ref[...] = ice
     inverse = table(5)
-    slope = jnp.zeros((8, WIDTH), jnp.float32)
-    stress = slope
+    p, stress = [], []
     for j in range(ND):
         lon = packed_coefficients(inverse, COURANT_MAX * COS[j])
         lat = packed_coefficients(inverse, 0.5 * COURANT_MAX * SIN[j])
         centre = columns_ref[j]
         x = lon[0] * centre + lon[1] * near_ref[j] + lon[2] * far_ref[j]
         x = packed_lat(j, x, *lat)
-        p = jnp.where(held, centre, jnp.maximum(x, 0.0)) * sea
+        p.append(jnp.where(held, centre, jnp.maximum(x, 0.0)) * sea)
         drive = drive_of(j, east, north, 1.0 - ice)
         drive_ref[j] = drive
-        p_ref[j] = p
-        slope = slope + p
-        stress = stress + p * drive
+        stress.append(p[j] * drive)
+    slope, stress = tree(p), tree(stress)
 
     def running(tile):
         for step in (1, 2, 4):
@@ -404,11 +418,11 @@
         moved = turn(tile, 4 * (position - (BANDS - 1)))
         out[index // BANDS] = jnp.where(place == position, moved, out[index // BANDS])
 
-    for j, excess in enumerate(excess_of([p_ref[j] for j in range(ND)])):
+    for j, excess in enumerate(excess_of(p)):
         total = running(excess)
         put(j, total)
         rate = excess * table(0) + (total - excess) * table(1)
-        part_ref[j] = p_ref[j] * jnp.exp(rate)
+        part_ref[j] = p[j] * jnp.exp(rate)
     put(ND, running(slope * table(2)))
     put(ND + 1, running(stress * table(3)))
     for i in range(PACKED_SUMS):
@@ -436,7 +450,7 @@
     if first:
         mine_right_ref, mine_left_ref, even_ref, odd_ref = refs[:4]
         p_ref, excess_ref, sums_ref, part_ref, packed_drive_ref, ice_ref = refs[4:10]
-        drive_ref, fix_ref, left_ref, right_ref, columns_ref, near_ref, far_ref, packed_ref = refs[10:]
+        drive_ref, fix_ref, left_ref, right_ref, columns_ref, near_ref, far_ref = refs[10:]
         odd = lax.axis_index("lon") % 2 == 1
         for i in range(SENT):
             even, other = even_ref[i], odd_ref[i]
@@ -446,7 +460,7 @@
         packed_start(mine_right_ref, mine_left_ref, left_ref, right_ref, columns_ref, sides)
         packed_source(
             table, left_ref, right_ref, columns_ref, sides,
-            sums_ref, part_ref, packed_drive_ref, ice_ref, packed_ref,
+            sums_ref, part_ref, packed_drive_ref, ice_ref,
         )
     else:
         columns_ref, p_ref, excess_ref, sums_ref, drive_ref, fix_ref = refs
@@ -470,23 +484,20 @@
             row = TILES * sublanes() + r
             held = (row < rows_ref[0:1, :]) | (row >= LAT - rows_ref[1:2, :])
             sea = jnp.where(land_ref[rows, :] != 0, 1.0, 0.0)
-            slope = jnp.zeros((8, WIDTH), jnp.float32)
-            stress = slope
-            shift = {
-                True: jnp.bitwise_and(WIDTH - GROUP * r - 4 * k, WIDTH - 1),
-                False: WIDTH - 4 - GROUP * r - 4 * k,
-            }
-            for j in range(ND):
-                back = BACK_LON[j]
-                moved = pltpu.roll(fix_ref[j], shift[back], 1)
-                p = x_ref[k, j, r] + jnp.where(at_edge[back], moved, 0.0)
-                p = jnp.where(held, spec_ref[k, j, rows, :], jnp.maximum(p, 0.0)) * sea
-                p_ref[k, j, r] = p
-                slope = slope + p
-                stress = stress + p * drive_ref[j, r]
+            shift = jnp.bitwise_and(WIDTH - GROUP * r - 4 * k, WIDTH - 1)
+            p = [None] * ND
+            for i in range(HALF):
+                moved = pltpu.roll(fix_ref[i], shift, 1)
+                for j in (BACK[i], AHEAD[i]):
+                    x = x_ref[k, j, r] + jnp.where(at_edge[BACK_LON[j]], moved, 0.0)
+                    x = jnp.where(held, spec_ref[k, j, rows, :], jnp.maximum(x, 0.0)) * sea
+                    p_ref[k, j, r] = x
+                    p[j] = x
+            slope = tree(p)
+            stress = tree([p[j] * drive_ref[j, r] for j in range(ND)])
             sums_ref[SLOPE_AT + r] += slope * scal_ref[extra + 2]
             sums_ref[STRESS_AT + r] += stress * scal_ref[extra + 3]
-            for j, excess in enumerate(excess_of([p_ref[k, j, r] for j in range(ND)])):
+            for j, excess in enumerate(excess_of(p)):
                 excess_ref[k, j, r] = excess
                 sums_ref[TILES * j + r] += excess
         return carry
@@ -530,7 +541,7 @@
 
 def grow_half(half, last, near, refs):
     scal_ref, part_ref, sums_ref, other_ref, mine_ref, lower_ref = refs[:6]
-    east_ref, north_ref, land_ref, out_ref, rate_ref, field_ref, sent = refs[6:]
+    east_ref, north_ref, land_ref, out_ref, rate_ref, near_ref, field_ref, sent = refs[6:]
     bands = part_ref.shape[0]
     freq = lax.axis_index("freq")
     odd = jnp.where(freq % 2 == 1, 1.0, 0.0)
@@ -552,10 +563,12 @@
             rate_ref[i, r] = gain * drive - damp - LOWER * lower
 
     inside = None if last else inside_masks()
-
-    def send(k):
-        place = pl.ds(half * HALF, HALF)
-        return pltpu.make_async_copy(field_ref.at[k], out_ref.at[k, place], sent.at[k])
+    target_ref = out_ref if near else field_ref
+
+    def send(k, mine):
+        source, which = (field_ref, half) if mine else (near_ref, 1 - half)
+        place = out_ref.at[k, pl.ds(which * HALF, HALF)]
+        return pltpu.make_async_copy(source.at[k], place, sent.at[int(mine), k])
 
     def band(k, carry):
         base = (freq * bands + k) * STRIDE
@@ -565,27 +578,32 @@
             tiles = [part_ref[k, j, r] * jnp.exp(rate_ref[i, r] * root) for r in range(TILES)]
             if last:
                 for r in range(TILES):
-                    field_ref[k, i, tile_rows(r), :] = tiles[r]
+                    target_ref[k, i, tile_rows(r), :] = tiles[r]
             else:
                 for r, tile in enumerate(drift(j, base, tiles, scal_ref, inside)):
                     out_ref[k, j, r] = tile
-        if last:
-            send(k).start()
+        if last and not near:
+            send(k, True).start()
         return carry
 
+    write = last and not near
+    if write:
+        for k in range(bands):
+            send(k, False).start()
     lax.fori_loop(0, bands, band, 0)
-    if last:
+    if write:
         for k in range(bands):
-            send(k).wait()
+            send(k, False).wait()
+            send(k, True).wait()
 
 
 def growth_kernel(last, near, *refs):
     operands, refs = refs[:9], refs[9:]
     scal_ref, part_ref, sums_ref, other_ref, mine_ref = operands[:5]
     freq = lax.axis_index("freq")
-    rest = (None, None)
+    rest = (None,) * 3
     if near and last:
-        out_ref, slope_ref, rate_ref, *rest = refs
+        out_ref, slope_ref, rate_ref = refs
         for r in range(TILES):
             at = SLOPE_AT + r
             total = (sums_ref[at] + other_ref[at]) + mine_ref[at - SLOPE_AT + HALF_TILES]
@@ -607,8 +625,8 @@
             rate = gain * packed_drive_ref[j] - damp - LOWER * under
             columns_ref[j] = packed_part_ref[j] * jnp.exp(root * rate)
     else:
-        _, out_ref, rate_ref, *rest = refs
-        rest = rest or (None, None)
+        before_ref, out_ref, rate_ref, *rest = refs
+        rest = (before_ref, *rest) if last else (None,) * 3
     for half in range(2):
 
         @pl.when(freq % 2 == (half if near else 1 - half))
@@ -689,7 +707,7 @@
             out_shape=[spread_field, spread_field, tiles(sums)]
             + ([tiles(ND), tiles(ND), tile] if first else []),
             scratch_shapes=[by_direction, packed]
-            + ([received] * 2 + [packed] * 4 if first else []),
+            + ([received] * 2 + [packed] * 3 if first else []),
             compiler_params=params,
             cost_estimate=cost(whole, 30, 3),
             name="sources",
@@ -718,22 +736,19 @@
         near, part = lax.optimization_barrier((near, part))
         far = lax.ppermute(near, "freq", swap_core)
 
-        def grow(is_near, lower, extra, more_specs, more_shapes, alias):
-            operands = [scalars, part, mine, other, near, lower, *fields] + extra
+        near_half = jax.ShapeDtypeStruct((bands, HALF, LAT, WIDTH), f32)
+
+        def grow(is_near, operands, shapes):
+            write = last and not is_near
             scratch = [pltpu.VMEM((HALF, TILES, 8, WIDTH), f32)]
-            if last:
-                scratch += [
-                    pltpu.VMEM((bands, HALF, LAT, WIDTH), f32),
-                    pltpu.SemaphoreType.DMA((bands,)),
-                ]
-            specs = [smem] + [vmem] * (len(operands) - 1)
-            if alias and last:
-                specs[-1] = hbm
+            if write:
+                scratch += [pltpu.VMEM(near_half.shape, f32), pltpu.SemaphoreType.DMA((2, bands))]
+            alias = not last and not is_near
             return pl.pallas_call(
                 functools.partial(growth_kernel, last, is_near),
-                in_specs=specs,
-                out_specs=[hbm if last else vmem] + more_specs,
-                out_shape=[field if last else spread_field] + more_shapes,
+                in_specs=[smem] + [vmem] * (len(operands) - 1),
+                out_specs=[hbm if write else vmem] * len(shapes),
+                out_shape=shapes,
                 input_output_aliases={len(operands) - 1: 0} if alias else {},
                 scratch_shapes=scratch,
                 compiler_params=params,
@@ -741,9 +756,12 @@
                 name="grow_near" if is_near else "grow_far",
             )(*operands)
 
+        operands = [scalars, part, mine, other, near]
         extra = [] if last else [table, *packed_state]
-        made, columns = grow(True, near, extra, [vmem], [plane if last else tiles(ND)], False)
-        (drifted,) = grow(False, far, [made], [], [], True)
+        shapes = [near_half, plane] if last else [spread_field, tiles(ND)]
+        made, columns = grow(True, operands + [near, *fields, *extra], shapes)
+        shapes = [field if last else spread_field]
+        (drifted,) = grow(False, operands + [far, *fields, made], shapes)
     return drifted, columns
 
 

time: 61 us -> 59 us (0.967)
  Pallas kernels: 36.6 us -> 34.6 us
    pallas_call x2, Pallas kernels: 14 us -> 12.5 us  [per_device(): pl.pallas_call(functools.partial(source_kernel, first), in_specs=[smem] +...]
  transfers between devices with their start and end apart: 8 -> 8, of which waited for: 5 -> 5; matrix products, arithmetic and copies ran while one was open for 0% -> 0% of each run, Pallas kernels for 23% -> 22%
where the time goes in v5:
time: 59 us; the launch traced here: 58.9 us
  Pallas kernels  34.6 us (59%)
  waiting for transfers between devices  13.1 us (22%)
  starting transfers between devices  10.4 us (18%)
  between operations  0.74 us (1%)
    pallas_call x2, Pallas kernels, per_device(): pl.pallas_call(functools.partial(source_kernel, first), in_specs=[smem] +...  12.5 us
    pallas_call x4, Pallas kernels, grow(): pl.pallas_call(functools.partial(growth_kernel, last, is_near), in_specs=...  11 us
    ppermute x2, waiting for transfers between devices, per_device(): near = lax.ppermute(pair, 'freq', swap_chip)  9.37 us
    pallas_call x2, Pallas kernels, per_device(): pl.pallas_call(local_kernel, in_specs=[smem] + [vmem] * 2, out_specs=vmem...  4.23 us
    ppermute x1, starting transfers between devices, per_device(): odd = lax.ppermute(odd, 'lon', swap_odd)  3.57 us
    pallas_call x1, Pallas kernels, per_device(): pl.pallas_call(drift_kernel, in_specs=[smem, vmem], out_specs=vmem, out_s...  3.48 us
    pallas_call x1, Pallas kernels, per_device(): pl.pallas_call(pack_kernel, in_specs=[hbm] * 5, out_specs=[vmem] * 9, out...  3.34 us
    ppermute x2, waiting for transfers between devices, per_device(): other = lax.ppermute(mine, 'freq', swap_core)  3.3 us
  transfers between devices with their start and end apart: 8, of which 5 were waited for; matrix products, arithmetic and copies ran while one was open for 0% of the time, Pallas kernels for 22%

profile of v5, /device:TPU:0, one launch (start us, length us, event | category | flops | bytes accessed | tf_op | source)
XLA Modules:
  0.0 58.9 jit_solution(2860213057344891072)
XLA Ops:
  0.6 0.0 copy-start
  0.6 3.3 %pack_columns.1 = (f32[8,36,24,128]{3,2,1,0:T(8,128)S(1)}, f32[28,8,128]{2,1,0:T(8,128)S(1)}, f32[28,8,128]{2,1,0:T(8,128)S(1)}, f32[24,128]{1,0:T(8,128)S(1)}, ...) custom-call(f32[8,36,24,128]{3,2,1,0:T(8,128)} %spec_ref.1, ...), custom_call_target="tpu_custom_call" | custom-call | flops 5308416 | bytes 7077888 | tf_op jit(solution)/shard_map/pack_columns/pallas_call | solution.py:672
  4.0 3.0 %collective-permute-start = (f32[28,8,128]{2,1,0:T(8,128)S(1)}, f32[28,8,128]{2,1,0:T(8,128)S(1)}, u32[]{:S(2)}, u32[]{:S(2)}) collective-permute-start(f32[28,8,128]{2,1,0:T(8,128)S(1)} %get-tuple-element.37), channel_id=1, source_target_pairs={{0,4},{4,0},{8,12},{12,8},{16,20},{20,16},{24,28},{28,24},{1,5},{5... | collective-permute-start | bytes 344072 | tf_op jit(solution)/shard_map/ppermute | solution.py:684
  7.0 3.6 %collective-permute-start.1 = (f32[28,8,128]{2,1,0:T(8,128)S(1)}, f32[28,8,128]{2,1,0:T(8,128)S(1)}, u32[]{:S(2)}, u32[]{:S(2)}) collective-permute-start(f32[28,8,128]{2,1,0:T(8,128)S(1)} %get-tuple-element.38), channel_id=1, source_target_pairs={{0,28},{4,8},{8,4},{12,16},{16,12},{20,24},{24,20},{28,0},{1,29},{... | collective-permute-start | bytes 344072 | tf_op jit(solution)/shard_map/ppermute | solution.py:685
  10.6 0.0 copy-done
  10.6 0.0 copy-start.1
  10.6 3.5 %drift.1.refs_2_ = f32[8,36,3,8,128]{4,3,2,1,0:T(8,128)S(1)} custom-call(f32[7168]{0:T(1024)S(1)} %copy-done, f32[8,36,24,128]{3,2,1,0:T(8,128)S(1)} %get-tuple-element.30.q_ref.refs_3_), custom_call_target="tpu_custom_call" | custom-call | flops 10616832 | bytes 7077888 | tf_op jit(solution)/shard_map/drift/pallas_call | solution.py:686
  14.1 0.0 collective-permute-done.refs_10_
  14.1 0.4 collective-permute-done.1.refs_11_
  14.5 0.0 copy-done.1
  14.5 7.3 %sources.2 = (f32[8,36,3,8,128]{4,3,2,1,0:T(8,128)S(1)}, f32[8,36,3,8,128]{4,3,2,1,0:T(8,128)S(1)}, f32[119,8,128]{2,1,0:T(8,128)S(1)}, f32[36,8,128]{2,1,0:T(8,...) custom-call(f32[7168]{0:T(1024)S(1)} %copy-done, f32[4,6,8,128]{3,2,1,0:T(8,128)S(1)} %copy-done.1, ...), custom_call_target="tpu_custom_call" | custom-call | flops 26542080 | bytes 10616832 | tf_op jit(solution)/shard_map/sources/pallas_call | solution.py:703
  21.8 0.1 collective-permute-start.2
  21.8 1.8 %collective-permute-done.2.other_ref.refs_3_ = f32[119,8,128]{2,1,0:T(8,128)S(1)} collective-permute-done((f32[119,8,128]{2,1,0:T(8,128)S(1)}, f32[119,8,128]{2,1,0:T(8,128)S(1)}, u32[]{:S(2)}, u32[]{:S(2)}) %collective-permute-start.2) | collective-permute-done | bytes 487456 | tf_op jit(solution)/shard_map/ppermute | solution.py:715
  23.7 1.6 %collective-permute-start.3 = (f32[65,8,128]{2,1,0:T(8,128)S(1)}, f32[65,8,128]{2,1,0:T(8,128)S(1)}, u32[]{:S(2)}, u32[]{:S(2)}) collective-permute-start(f32[65,8,128]{2,1,0:T(8,128)S(1)} %pair_sums.2), channel_id=1, source_target_pairs={{0,2},{2,0},{1,3},{3,1},{4,6},{6,4},{5,7},{7,5},{8,10},{10,8},{9,1... | collective-permute-start | bytes 798728 | tf_op jit(solution)/shard_map/ppermute | solution.py:725
  25.3 2.1 %local_rate.2.refs_1_ = f32[8,36,3,8,128]{4,3,2,1,0:T(8,128)S(1)} custom-call(f32[7168]{0:T(1024)S(1)} %copy-done, f32[8,36,3,8,128]{4,3,2,1,0:T(8,128)S(1)} %get-tuple-element.40.p_ref, f32[8,36,3,8,128]{4,3,2,1,0:T(8,128)S(1)} %get-tuple-element.42.excess_ref), custom_call_target="tpu_custom_call" | custom-call | flops 7077888 | bytes 10616832 | tf_op jit(solution)/shard_map/local_rate/pallas_call | solution.py:727
  27.4 4.8 %collective-permute-done.3.refs_4_.refs_5_ = f32[65,8,128]{2,1,0:T(8,128)S(1)} collective-permute-done((f32[65,8,128]{2,1,0:T(8,128)S(1)}, f32[65,8,128]{2,1,0:T(8,128)S(1)}, u32[]{:S(2)}, u32[]{:S(2)}) %collective-permute-start.3) | collective-permute-done | bytes 266272 | tf_op jit(solution)/shard_map/ppermute | solution.py:725
  32.2 0.0 collective-permute-start.4
  32.2 3.1 %grow_near.2 = (f32[8,36,3,8,128]{4,3,2,1,0:T(8,128)S(1)}, f32[36,8,128]{2,1,0:T(8,128)S(1)}) custom-call(f32[7168]{0:T(1024)S(1)} %copy-done, f32[8,36,3,8,128]{4,3,2,1,0:T(8,128)S(1)} %local_rate.2.refs_1_, f32[119,8,128]{2,1,0:T(8,128)S(1)} %get-tuple-element.39.sums_ref.refs_2_, f32[119,8,128]{2,1,0:T(8,128)S(1)} %collective-permute-done.2.other_ref.refs_3_, ...), custom_call_target="tpu_custom_call" | custom-call | flops 10616832 | bytes 3538944 | tf_op jit(solution)/shard_map/grow_near/pallas_call | solution.py:747
  35.3 0.0 collective-permute-done.4.refs_5_
  35.4 2.8 %grow_far.2.refs_2_ = f32[8,36,3,8,128]{4,3,2,1,0:T(8,128)S(1)} custom-call(f32[7168]{0:T(1024)S(1)} %copy-done, f32[8,36,3,8,128]{4,3,2,1,0:T(8,128)S(1)} %local_rate.2.refs_1_, f32[119,8,128]{2,1,0:T(8,128)S(1)} %get-tuple-element.39.sums_ref.refs_2_, f32[119,8,128]{2,1,0:T(8,128)S(1)} %collective-permute-done.2.other_ref.refs_3_, ...), custom_call_target="tpu_custom_call", output_to_operand_aliasing={{}: (9, {})} | custom-call | flops 10616832 | bytes 3538944 | tf_op jit(solution)/shard_map/grow_far/pallas_call | solution.py:747
  38.2 5.2 %sources.3 = (f32[8,36,3,8,128]{4,3,2,1,0:T(8,128)S(1)}, f32[8,36,3,8,128]{4,3,2,1,0:T(8,128)S(1)}, f32[114,8,128]{2,1,0:T(8,128)S(1)}) custom-call(f32[7168]{0:T(1024)S(1)} %copy-done, f32[4,6,8,128]{3,2,1,0:T(8,128)S(1)} %copy-done.1, f32[8,36,3,8,128]{4,3,2,1,0:T(8,128)S(1)} %grow_far.2.refs_2_, f32[8,36,24,128]{3,2,1,0:T(8,128)S(1)} %get-tuple-element.30.q_ref.refs_3_, ...), custom_call_target="tpu_custom_call" | custom-call | flops 26542080 | bytes 10616832 | tf_op jit(solution)/shard_map/sources/pallas_call | solution.py:703
  43.4 0.6 collective-permute-start.5
  44.0 1.5 %collective-permute-done.5.other_ref.refs_3_ = f32[114,8,128]{2,1,0:T(8,128)S(1)} collective-permute-done((f32[114,8,128]{2,1,0:T(8,128)S(1)}, f32[114,8,128]{2,1,0:T(8,128)S(1)}, u32[]{:S(2)}, u32[]{:S(2)}) %collective-permute-start.5) | collective-permute-done | bytes 466976 | tf_op jit(solution)/shard_map/ppermute | solution.py:715
  45.5 1.6 %collective-permute-start.6 = (f32[60,8,128]{2,1,0:T(8,128)S(1)}, f32[60,8,128]{2,1,0:T(8,128)S(1)}, u32[]{:S(2)}, u32[]{:S(2)}) collective-permute-start(f32[60,8,128]{2,1,0:T(8,128)S(1)} %pair_sums.3), channel_id=1, source_target_pairs={{0,2},{2,0},{1,3},{3,1},{4,6},{6,4},{5,7},{7,5},{8,10},{10,8},{9,1... | collective-permute-start | bytes 737288 | tf_op jit(solution)/shard_map/ppermute | solution.py:725
  47.1 2.1 %local_rate.3.refs_1_ = f32[8,36,3,8,128]{4,3,2,1,0:T(8,128)S(1)} custom-call(f32[7168]{0:T(1024)S(1)} %copy-done, f32[8,36,3,8,128]{4,3,2,1,0:T(8,128)S(1)} %get-tuple-element.51.p_ref, f32[8,36,3,8,128]{4,3,2,1,0:T(8,128)S(1)} %get-tuple-element.53.excess_ref), custom_call_target="tpu_custom_call" | custom-call | flops 7077888 | bytes 10616832 | tf_op jit(solution)/shard_map/local_rate/pallas_call | solution.py:727
  49.2 4.6 %collective-permute-done.6.refs_4_.refs_5_ = f32[60,8,128]{2,1,0:T(8,128)S(1)} collective-permute-done((f32[60,8,128]{2,1,0:T(8,128)S(1)}, f32[60,8,128]{2,1,0:T(8,128)S(1)}, u32[]{:S(2)}, u32[]{:S(2)}) %collective-permute-start.6) | collective-permute-done | bytes 245792 | tf_op jit(solution)/shard_map/ppermute | solution.py:725
  53.8 0.0 collective-permute-start.7
  53.8 2.2 %grow_near.3 = (f32[8,18,24,128]{3,2,1,0:T(8,128)S(1)}, f32[24,128]{1,0:T(8,128)}) custom-call(f32[7168]{0:T(1024)S(1)} %copy-done, f32[8,36,3,8,128]{4,3,2,1,0:T(8,128)S(1)} %local_rate.3.refs_1_, f32[114,8,128]{2,1,0:T(8,128)S(1)} %get-tuple-element.50.sums_ref.refs_2_, f32[114,8,128]{2,1,0:T(8,128)S(1)} %collective-permute-done.5.other_ref.refs_3_, ...), custom_call_target="tpu_custom_call" | custom-call | flops 5308416 | bytes 3538944 | tf_op jit(solution)/shard_map/grow_near/pallas_call | solution.py:747
  55.9 0.0 collective-permute-done.7.refs_5_
  55.9 2.9 %grow_far.3 = f32[8,36,24,128]{3,2,1,0:T(8,128)} custom-call(f32[7168]{0:T(1024)S(1)} %copy-done, f32[8,36,3,8,128]{4,3,2,1,0:T(8,128)S(1)} %local_rate.3.refs_1_, f32[114,8,128]{2,1,0:T(8,128)S(1)} %get-tuple-element.50.sums_ref.refs_2_, f32[114,8,128]{2,1,0:T(8,128)S(1)} %collective-permute-done.5.other_ref.refs_3_, ...), custom_call_target="tpu_custom_call" | custom-call | flops 5308416 | bytes 3538944 | tf_op jit(solution)/shard_map/grow_far/pallas_call | solution.py:747
  (2 shorter events, 0.1 us)
Async XLA Ops:
  0.6 9.9 %copy-start = (f32[7168]{0:T(1024)S(1)}, f32[7168]{0:T(1024)}, u32[]{:S(2)}) copy-start(f32[7168]{0:T(1024)} %constant.4.clone.scal_ref.refs_0_) | copy-start | bytes 86020
  4.0 10.1 %collective-permute-start = (f32[28,8,128]{2,1,0:T(8,128)S(1)}, f32[28,8,128]{2,1,0:T(8,128)S(1)}, u32[]{:S(2)}, u32[]{:S(2)}) collective-permute-start(f32[28,8,128]{2,1,0:T(8,128)S(1)} %get-tuple-element.37), channel_id=1, source_target_pairs={{0,4},{4,0},{8,12},{12,8},{16,20},{20,16},{24,28},{28,24},{1,5},{5... | collective-permute-start | bytes 344072 | tf_op jit(solution)/shard_map/ppermute | solution.py:684
  7.0 7.5 %collective-permute-start.1 = (f32[28,8,128]{2,1,0:T(8,128)S(1)}, f32[28,8,128]{2,1,0:T(8,128)S(1)}, u32[]{:S(2)}, u32[]{:S(2)}) collective-permute-start(f32[28,8,128]{2,1,0:T(8,128)S(1)} %get-tuple-element.38), channel_id=1, source_target_pairs={{0,28},{4,8},{8,4},{12,16},{16,12},{20,24},{24,20},{28,0},{1,29},{... | collective-permute-start | bytes 344072 | tf_op jit(solution)/shard_map/ppermute | solution.py:685
  10.6 3.9 %copy-start.1 = (f32[4,6,8,128]{3,2,1,0:T(8,128)S(1)}, f32[4,6,8,128]{3,2,1,0:T(8,128)}, u32[]{:S(2)}) copy-start(f32[4,6,8,128]{3,2,1,0:T(8,128)} %constant.5.clone.refs_1_.refs_9_) | copy-start | bytes 294916
  21.8 1.9 %collective-permute-start.2 = (f32[119,8,128]{2,1,0:T(8,128)S(1)}, f32[119,8,128]{2,1,0:T(8,128)S(1)}, u32[]{:S(2)}, u32[]{:S(2)}) collective-permute-start(f32[119,8,128]{2,1,0:T(8,128)S(1)} %get-tuple-element.39.sums_ref.refs_2_), channel_id=1, source_target_pairs={{0,1},{1,0},{2,3},{3,2},{4,5},{5,4},{6,7},{7,6},{8,9},{9,8},{10,11... | collective-permute-start | bytes 1462280 | tf_op jit(solution)/shard_map/ppermute | solution.py:715
  23.7 8.5 %collective-permute-start.3 = (f32[65,8,128]{2,1,0:T(8,128)S(1)}, f32[65,8,128]{2,1,0:T(8,128)S(1)}, u32[]{:S(2)}, u32[]{:S(2)}) collective-permute-start(f32[65,8,128]{2,1,0:T(8,128)S(1)} %pair_sums.2), channel_id=1, source_target_pairs={{0,2},{2,0},{1,3},{3,1},{4,6},{6,4},{5,7},{7,5},{8,10},{10,8},{9,1... | collective-permute-start | bytes 798728 | tf_op jit(solution)/shard_map/ppermute | solution.py:725
  32.2 3.1 %collective-permute-start.4 = (f32[65,8,128]{2,1,0:T(8,128)S(1)}, f32[65,8,128]{2,1,0:T(8,128)S(1)}, u32[]{:S(2)}, u32[]{:S(2)}) collective-permute-start(f32[65,8,128]{2,1,0:T(8,128)S(1)} %collective-permute-done.3.refs_4_.refs_5_), channel_id=1, source_target_pairs={{0,1},{1,0},{2,3},{3,2},{4,5},{5,4},{6,7},{7,6},{8,9},{9,8},{10,11... | collective-permute-start | bytes 798728 | tf_op jit(solution)/shard_map/ppermute | solution.py:737
  43.4 2.0 %collective-permute-start.5 = (f32[114,8,128]{2,1,0:T(8,128)S(1)}, f32[114,8,128]{2,1,0:T(8,128)S(1)}, u32[]{:S(2)}, u32[]{:S(2)}) collective-permute-start(f32[114,8,128]{2,1,0:T(8,128)S(1)} %get-tuple-element.50.sums_ref.refs_2_), channel_id=1, source_target_pairs={{0,1},{1,0},{2,3},{3,2},{4,5},{5,4},{6,7},{7,6},{8,9},{9,8},{10,11... | collective-permute-start | bytes 1400840 | tf_op jit(solution)/shard_map/ppermute | solution.py:715
  45.5 8.3 %collective-permute-start.6 = (f32[60,8,128]{2,1,0:T(8,128)S(1)}, f32[60,8,128]{2,1,0:T(8,128)S(1)}, u32[]{:S(2)}, u32[]{:S(2)}) collective-permute-start(f32[60,8,128]{2,1,0:T(8,128)S(1)} %pair_sums.3), channel_id=1, source_target_pairs={{0,2},{2,0},{1,3},{3,1},{4,6},{6,4},{5,7},{7,5},{8,10},{10,8},{9,1... | collective-permute-start | bytes 737288 | tf_op jit(solution)/shard_map/ppermute | solution.py:725
  53.8 2.2 %collective-permute-start.7 = (f32[60,8,128]{2,1,0:T(8,128)S(1)}, f32[60,8,128]{2,1,0:T(8,128)S(1)}, u32[]{:S(2)}, u32[]{:S(2)}) collective-permute-start(f32[60,8,128]{2,1,0:T(8,128)S(1)} %collective-permute-done.6.refs_4_.refs_5_), channel_id=1, source_target_pairs={{0,1},{1,0},{2,3},{3,2},{4,5},{5,4},{6,7},{7,6},{8,9},{9,8},{10,11... | collective-permute-start | bytes 737288 | tf_op jit(solution)/shard_map/ppermute | solution.py:737

commit v6 on v5

--- a/solution.py
+++ b/solution.py
@@ -70,9 +70,10 @@
     lon = one_sided(COURANT_MAX * COS[None, :] / ratios[:, None])
     lat = one_sided(0.5 * COURANT_MAX * SIN[None, :] / ratios[:, None])
     scalars = np.zeros((NF, STRIDE))
-    for i in range(3):
-        scalars[:, i : 6 * ND : 6] = lon[i]
-        scalars[:, 3 + i : 6 * ND : 6] = lat[i]
+    for i, value in enumerate(
+        (lon[1] / lon[0], lon[2] / lon[0], lat[1] / lat[0], lat[2] / lat[0], lon[0] * lat[0])
+    ):
+        scalars[:, i : 6 * ND : 6] = value
     rest = [
         -BREAKING / SATURATION_REF * SCALE * root,
         -LOWER * root,
@@ -106,7 +107,7 @@
 
 
 def tile_rows(r):
-    return pl.ds(r, 8, stride=TILES)
+    return slice(8 * r, 8 * r + 8)
 
 
 CHUNK = 4
@@ -270,21 +271,26 @@
 
 
 def drift(j, base, tiles, scal_ref, inside):
-    c0, c1, c2, d0, d1, d2 = (scal_ref[base + 6 * j + i] for i in range(6))
+    c1, c2, d1, d2 = (scal_ref[base + 6 * j + i] for i in range(4))
     side = 1 if BACK_LON[j] else -1
     c1 = c1 * inside[BACK_LON[j], 1]
     c2 = c2 * inside[BACK_LON[j], 2]
-    x = [c0 * q + c1 * turn(q, side) + c2 * turn(q, 2 * side) for q in tiles]
+    x = [q + c1 * turn(q, side) + c2 * turn(q, 2 * side) for q in tiles]
     row = sublanes()
-    if BACK_LAT[j]:
-        over = [jnp.where(row == 0, x[0], pltpu.roll(x[r], 1, 0)) for r in (1, 2)]
-        near = [over[1], x[0], x[1]]
-        far = [over[0], over[1], x[0]]
-    else:
-        over = [jnp.where(row == 7, x[2], pltpu.roll(x[r], 7, 0)) for r in (0, 1)]
-        near = [x[1], x[2], over[0]]
-        far = [x[2], over[0], over[1]]
-    return [d0 * x[r] + d1 * near[r] + d2 * far[r] for r in range(TILES)]
+    one, two = (1, 2) if BACK_LAT[j] else (7, 6)
+    at_edge = (row < 1, row < 2) if BACK_LAT[j] else (row >= 7, row >= 6)
+    order = range(TILES) if BACK_LAT[j] else range(TILES - 1, -1, -1)
+    moved = [[pltpu.roll(tile, by, 0) for tile in x] for by in (one, two)]
+    y = [None] * TILES
+    before = None
+    for r in order:
+        first = x[r] if before is None else moved[0][before]
+        near = jnp.where(at_edge[0], first, moved[0][r])
+        second = near if before is None else moved[1][before]
+        far = jnp.where(at_edge[1], second, moved[1][r])
+        y[r] = x[r] + d1 * near + d2 * far
+        before = r
+    return y
 
 
 def drift_kernel(scal_ref, q_ref, out_ref):
@@ -294,7 +300,8 @@
     def band(k, carry):
         base = (lax.axis_index("freq") * bands + k) * STRIDE
         for j in range(ND):
-            tiles = [q_ref[k, j, tile_rows(r), :] for r in range(TILES)]
+            factor = scal_ref[base + 6 * j + 4]
+            tiles = [q_ref[k, j, tile_rows(r), :] * factor for r in range(TILES)]
             for r, tile in enumerate(drift(j, base, tiles, scal_ref, inside)):
                 out_ref[k, j, r] = tile
         return carry
@@ -304,18 +311,18 @@
 
 def packed_lat(j, x, d0, d1, d2):
     lane, row = lanes(), sublanes()
-    first, last = lane < GROUP, lane >= (TILES - 1) * GROUP
-    if BACK_LAT[j]:
-        moved, one = pltpu.roll(x, 1, 0), turn(x, GROUP)
-        near = jnp.where(first, jnp.where(row == 0, x, turn(moved, -2 * GROUP)), one)
-        far = jnp.where(row == 0, jnp.where(first, x, one), turn(moved, -GROUP))
-        far = jnp.where(last, turn(x, 2 * GROUP), far)
-    else:
-        moved, one = pltpu.roll(x, 7, 0), turn(x, -GROUP)
-        near = jnp.where(last, jnp.where(row == 7, x, turn(moved, 2 * GROUP)), one)
-        far = jnp.where(row == 7, jnp.where(last, x, one), turn(moved, GROUP))
-        far = jnp.where(first, turn(x, -2 * GROUP), far)
-    return d0 * x + d1 * near + d2 * far
+
+    def shifted(x):
+        if BACK_LAT[j]:
+            moved = pltpu.roll(x, 1, 0)
+            over = jnp.where(lane < GROUP, x, turn(moved, GROUP))
+            return jnp.where(row >= 1, moved, over)
+        moved = pltpu.roll(x, 7, 0)
+        over = jnp.where(lane >= (TILES - 1) * GROUP, x, turn(moved, -GROUP))
+        return jnp.where(row <= 6, moved, over)
+
+    near = shifted(x)
+    return d0 * x + d1 * near + d2 * shifted(near)
 
 
 def spread(tile, position):
@@ -387,7 +394,7 @@
     slot, place = lane % 4, lane // 4 % BANDS
     both = jnp.where(slot < 2, left_ref[SENT - 1], turn(right_ref[SENT - 1], 2))
     east, north, land, south_rows, north_rows = (spread(both, i) for i in range(FIELDS))
-    row = (TILES * sublanes() + lane // GROUP).astype(jnp.float32)
+    row = (sublanes() + lane // GROUP * 8).astype(jnp.float32)
     held = (row < south_rows) | (row >= LAT - north_rows)
     sea = jnp.where(land > 0.5, 1.0, 0.0)
     ice = jnp.where(land > 1.5, 1.0, 0.0)
@@ -436,6 +443,12 @@
         excess = capped * lax.rsqrt(capped) - ROOT_CAP
         out.append(excess * excess)
     return out
+
+
+def held_and_sea(r, land_ref, rows_ref):
+    row = sublanes() + 8 * r
+    held = (row < rows_ref[0:1, :]) | (row >= LAT - rows_ref[1:2, :])
+    return held, jnp.where(land_ref[tile_rows(r), :] != 0, 1.0, 0.0)
 
 
 def source_kernel(first, *refs):
@@ -481,16 +494,19 @@
         extra = (freq * bands + k) * STRIDE + 6 * ND
         for r in range(TILES):
             rows = tile_rows(r)
-            row = TILES * sublanes() + r
-            held = (row < rows_ref[0:1, :]) | (row >= LAT - rows_ref[1:2, :])
-            sea = jnp.where(land_ref[rows, :] != 0, 1.0, 0.0)
+            held, sea = held_and_sea(r, land_ref, rows_ref)
+            if not first:
+                free = jnp.where(held, 0.0, sea)
             shift = jnp.bitwise_and(WIDTH - GROUP * r - 4 * k, WIDTH - 1)
             p = [None] * ND
             for i in range(HALF):
                 moved = pltpu.roll(fix_ref[i], shift, 1)
                 for j in (BACK[i], AHEAD[i]):
                     x = x_ref[k, j, r] + jnp.where(at_edge[BACK_LON[j]], moved, 0.0)
-                    x = jnp.where(held, spec_ref[k, j, rows, :], jnp.maximum(x, 0.0)) * sea
+                    if first:
+                        x = jnp.where(held, spec_ref[k, j, rows, :], jnp.maximum(x, 0.0)) * sea
+                    else:
+                        x = jnp.maximum(x * free, spec_ref[k, j, r])
                     p_ref[k, j, r] = x
                     p[j] = x
             slope = tree(p)
@@ -505,21 +521,33 @@
     lax.fori_loop(0, bands, band, 0)
 
 
-def local_kernel(scal_ref, p_ref, excess_ref, out_ref):
+def local_kernel(last, scal_ref, p_ref, excess_ref, *refs):
+    if last:
+        (out_ref,) = refs
+    else:
+        spec_ref, land_ref, rows_ref, out_ref, held_ref = refs
     bands = p_ref.shape[0]
-    first = (lax.axis_index("freq") * bands) * STRIDE + 6 * ND
+    first = (lax.axis_index("freq") * bands) * STRIDE
+    extra = first + 6 * ND
     some = 6
 
     def directions(group, carry):
-        for i in range(some):
-            j = group * some + i
-            for r in range(TILES):
+        for r in range(TILES):
+            if not last:
+                held, sea = held_and_sea(r, land_ref, rows_ref)
+                kept = jnp.where(held, sea, 0.0)
+            for i in range(some):
+                j = group * some + i
                 lower = jnp.zeros((8, WIDTH), jnp.float32)
                 for k in range(bands):
                     excess = excess_ref[k, j, r]
-                    at = first + k * STRIDE
+                    at = extra + k * STRIDE
                     rate = excess * scal_ref[at] + lower * scal_ref[at + 1]
-                    out_ref[k, j, r] = p_ref[k, j, r] * jnp.exp(rate)
+                    value = p_ref[k, j, r] * jnp.exp(rate)
+                    if not last:
+                        value = value * scal_ref[first + k * STRIDE + 6 * j + 4]
+                        held_ref[k, j, r] = spec_ref[k, j, tile_rows(r), :] * kept
+                    out_ref[k, j, r] = value
                     lower = lower + excess
         return carry
 
@@ -698,7 +726,7 @@
         first, last = step == 0, step == STEPS - 1
         sums = PACKED_AT + (PACKED_SUMS if first else 0)
         half_sums = sums - SLOPE_AT + HALF_TILES
-        operands = [scalars, table, drifted, spectrum, *fields, edge_rows]
+        operands = [scalars, table, drifted, spectrum if first else kept, *fields, edge_rows]
         operands += [right, left, even, odd] if first else [columns]
         p, excess, mine, *packed_state = pl.pallas_call(
             functools.partial(source_kernel, first),
@@ -724,15 +752,17 @@
         )(mine, other)
         near = lax.ppermute(pair, "freq", swap_chip)
         excess, _ = lax.optimization_barrier((excess, pair))
-        part = pl.pallas_call(
-            local_kernel,
-            in_specs=[smem] + [vmem] * 2,
-            out_specs=vmem,
-            out_shape=spread_field,
+        operands = [scalars, p, excess] + ([] if last else [spectrum, land_sea, edge_rows])
+        part, *kept = pl.pallas_call(
+            functools.partial(local_kernel, last),
+            in_specs=[smem] + [vmem] * (len(operands) - 1),
+            out_specs=[vmem] * (1 if last else 2),
+            out_shape=[spread_field] * (1 if last else 2),
             compiler_params=params,
             cost_estimate=cost(whole, 8, 3),
             name="local_rate",
-        )(scalars, p, excess)
+        )(*operands)
+        kept = None if last else kept[0]
         near, part = lax.optimization_barrier((near, part))
         far = lax.ppermute(near, "freq", swap_core)
 

time: 59 us -> 57.4 us (0.973)
  waiting for transfers between devices: 13.1 us -> 12 us
    pallas_call x2, Pallas kernels: 12.5 us -> 10.8 us  [per_device(): pl.pallas_call(functools.partial(source_kernel, first), in_specs=[smem] +...]
    pallas_call x2, Pallas kernels: 4.23 us -> 5.24 us  [per_device(): pl.pallas_call(functools.partial(local_kernel, last), in_specs=[smem] + [...]
    ppermute x2, waiting for transfers between devices: 9.37 us -> 8.36 us  [per_device(): near = lax.ppermute(pair, 'freq', swap_chip)]
  transfers between devices with their start and end apart: 8 -> 8, of which waited for: 5 -> 5; matrix products, arithmetic and copies ran while one was open for 0% -> 0% of each run, Pallas kernels for 22% -> 25%
where the time goes in v6:
time: 57.4 us; the launch traced here: 57.3 us
  Pallas kernels  34.1 us (59%)
  waiting for transfers between devices  12 us (21%)
  starting transfers between devices  10.4 us (18%)
  between operations  0.74 us (1%)
    pallas_call x4, Pallas kernels, grow(): pl.pallas_call(functools.partial(growth_kernel, last, is_near), in_specs=...  11.1 us
    pallas_call x2, Pallas kernels, per_device(): pl.pallas_call(functools.partial(source_kernel, first), in_specs=[smem] +...  10.8 us
    ppermute x2, waiting for transfers between devices, per_device(): near = lax.ppermute(pair, 'freq', swap_chip)  8.36 us
    pallas_call x2, Pallas kernels, per_device(): pl.pallas_call(functools.partial(local_kernel, last), in_specs=[smem] + [...  5.24 us
    ppermute x1, starting transfers between devices, per_device(): odd = lax.ppermute(odd, 'lon', swap_odd)  3.57 us
    pallas_call x1, Pallas kernels, per_device(): pl.pallas_call(drift_kernel, in_specs=[smem, vmem], out_specs=vmem, out_s...  3.53 us
    pallas_call x1, Pallas kernels, per_device(): pl.pallas_call(pack_kernel, in_specs=[hbm] * 5, out_specs=[vmem] * 9, out...  3.34 us
    ppermute x2, waiting for transfers between devices, per_device(): other = lax.ppermute(mine, 'freq', swap_core)  3.3 us
  transfers between devices with their start and end apart: 8, of which 5 were waited for; matrix products, arithmetic and copies ran while one was open for 0% of the time, Pallas kernels for 25%

profile of v6, /device:TPU:0, one launch (start us, length us, event | category | flops | bytes accessed | tf_op | source)
XLA Modules:
  0.0 57.3 jit_solution(16179066948565470611)
XLA Ops:
  0.6 0.0 copy-start
  0.6 3.3 %pack_columns.1 = (f32[8,36,24,128]{3,2,1,0:T(8,128)S(1)}, f32[28,8,128]{2,1,0:T(8,128)S(1)}, f32[28,8,128]{2,1,0:T(8,128)S(1)}, f32[24,128]{1,0:T(8,128)S(1)}, ...) custom-call(f32[8,36,24,128]{3,2,1,0:T(8,128)} %spec_ref.1, ...), custom_call_target="tpu_custom_call" | custom-call | flops 5308416 | bytes 7077888 | tf_op jit(solution)/shard_map/pack_columns/pallas_call | solution.py:700
  4.0 3.0 %collective-permute-start = (f32[28,8,128]{2,1,0:T(8,128)S(1)}, f32[28,8,128]{2,1,0:T(8,128)S(1)}, u32[]{:S(2)}, u32[]{:S(2)}) collective-permute-start(f32[28,8,128]{2,1,0:T(8,128)S(1)} %get-tuple-element.39), channel_id=1, source_target_pairs={{0,4},{4,0},{8,12},{12,8},{16,20},{20,16},{24,28},{28,24},{1,5},{5... | collective-permute-start | bytes 344072 | tf_op jit(solution)/shard_map/ppermute | solution.py:712
  7.0 3.6 %collective-permute-start.1 = (f32[28,8,128]{2,1,0:T(8,128)S(1)}, f32[28,8,128]{2,1,0:T(8,128)S(1)}, u32[]{:S(2)}, u32[]{:S(2)}) collective-permute-start(f32[28,8,128]{2,1,0:T(8,128)S(1)} %get-tuple-element.40), channel_id=1, source_target_pairs={{0,28},{4,8},{8,4},{12,16},{16,12},{20,24},{24,20},{28,0},{1,29},{... | collective-permute-start | bytes 344072 | tf_op jit(solution)/shard_map/ppermute | solution.py:713
  10.6 0.0 copy-done
  10.6 0.0 copy-start.1
  10.6 3.5 %drift.1.refs_2_ = f32[8,36,3,8,128]{4,3,2,1,0:T(8,128)S(1)} custom-call(f32[7168]{0:T(1024)S(1)} %copy-done, f32[8,36,24,128]{3,2,1,0:T(8,128)S(1)} %get-tuple-element.32.q_ref.refs_3_.refs_0_), custom_call_target="tpu_custom_call" | custom-call | flops 10616832 | bytes 7077888 | tf_op jit(solution)/shard_map/drift/pallas_call | solution.py:714
  14.1 0.0 collective-permute-done.refs_10_
  14.1 0.4 collective-permute-done.1.refs_11_
  14.5 0.0 copy-done.1
  14.5 6.1 %sources.2 = (f32[8,36,3,8,128]{4,3,2,1,0:T(8,128)S(1)}, f32[8,36,3,8,128]{4,3,2,1,0:T(8,128)S(1)}, f32[119,8,128]{2,1,0:T(8,128)S(1)}, f32[36,8,128]{2,1,0:T(8,...) custom-call(f32[7168]{0:T(1024)S(1)} %copy-done, f32[4,6,8,128]{3,2,1,0:T(8,128)S(1)} %copy-done.1, ...), custom_call_target="tpu_custom_call" | custom-call | flops 26542080 | bytes 10616832 | tf_op jit(solution)/shard_map/sources/pallas_call | solution.py:731
  20.6 0.1 collective-permute-start.2
  20.7 1.8 %collective-permute-done.2.other_ref.refs_3_ = f32[119,8,128]{2,1,0:T(8,128)S(1)} collective-permute-done((f32[119,8,128]{2,1,0:T(8,128)S(1)}, f32[119,8,128]{2,1,0:T(8,128)S(1)}, u32[]{:S(2)}, u32[]{:S(2)}) %collective-permute-start.2) | collective-permute-done | bytes 487456 | tf_op jit(solution)/shard_map/ppermute | solution.py:743
  22.6 1.6 %collective-permute-start.3 = (f32[65,8,128]{2,1,0:T(8,128)S(1)}, f32[65,8,128]{2,1,0:T(8,128)S(1)}, u32[]{:S(2)}, u32[]{:S(2)}) collective-permute-start(f32[65,8,128]{2,1,0:T(8,128)S(1)} %pair_sums.2), channel_id=1, source_target_pairs={{0,2},{2,0},{1,3},{3,1},{4,6},{6,4},{5,7},{7,5},{8,10},{10,8},{9,1... | collective-permute-start | bytes 798728 | tf_op jit(solution)/shard_map/ppermute | solution.py:753
  24.2 3.1 %local_rate.2 = (f32[8,36,3,8,128]{4,3,2,1,0:T(8,128)S(1)}, f32[8,36,3,8,128]{4,3,2,1,0:T(8,128)S(1)}) custom-call(f32[7168]{0:T(1024)S(1)} %copy-done, f32[8,36,3,8,128]{4,3,2,1,0:T(8,128)S(1)} %get-tuple-element.42.p_ref, f32[8,36,3,8,128]{4,3,2,1,0:T(8,128)S(1)} %get-tuple-element.44.excess_ref, ...), custom_call_target="tpu_custom_call" | custom-call | flops 7077888 | bytes 10616832 | tf_op jit(solution)/shard_map/local_rate/pallas_call | solution.py:756
  27.3 3.8 %collective-permute-done.3.refs_4_.refs_5_ = f32[65,8,128]{2,1,0:T(8,128)S(1)} collective-permute-done((f32[65,8,128]{2,1,0:T(8,128)S(1)}, f32[65,8,128]{2,1,0:T(8,128)S(1)}, u32[]{:S(2)}, u32[]{:S(2)}) %collective-permute-start.3) | collective-permute-done | bytes 266272 | tf_op jit(solution)/shard_map/ppermute | solution.py:753
  31.1 0.0 collective-permute-start.4
  31.1 3.1 %grow_near.2 = (f32[8,36,3,8,128]{4,3,2,1,0:T(8,128)S(1)}, f32[36,8,128]{2,1,0:T(8,128)S(1)}) custom-call(f32[7168]{0:T(1024)S(1)} %copy-done, f32[8,36,3,8,128]{4,3,2,1,0:T(8,128)S(1)} %get-tuple-element.46.refs_1_, f32[119,8,128]{2,1,0:T(8,128)S(1)} %get-tuple-element.41.sums_ref.refs_2_, f32[119,8,128]{2,1,0:T(8,128)S(1)} %collective-permute-done.2.other_ref.refs_3_, ...), custom_call_target="tpu_custom_call" | custom-call | flops 10616832 | bytes 3538944 | tf_op jit(solution)/shard_map/grow_near/pallas_call | solution.py:777
  34.2 0.0 collective-permute-done.4.refs_5_
  34.2 2.8 %grow_far.2.refs_2_ = f32[8,36,3,8,128]{4,3,2,1,0:T(8,128)S(1)} custom-call(f32[7168]{0:T(1024)S(1)} %copy-done, f32[8,36,3,8,128]{4,3,2,1,0:T(8,128)S(1)} %get-tuple-element.46.refs_1_, f32[119,8,128]{2,1,0:T(8,128)S(1)} %get-tuple-element.41.sums_ref.refs_2_, ...), custom_call_target="tpu_custom_call", output_to_operand_aliasing={{}: (9, {})} | custom-call | flops 10616832 | bytes 3538944 | tf_op jit(solution)/shard_map/grow_far/pallas_call | solution.py:777
  37.0 4.7 %sources.3 = (f32[8,36,3,8,128]{4,3,2,1,0:T(8,128)S(1)}, f32[8,36,3,8,128]{4,3,2,1,0:T(8,128)S(1)}, f32[114,8,128]{2,1,0:T(8,128)S(1)}) custom-call(f32[7168]{0:T(1024)S(1)} %copy-done, f32[4,6,8,128]{3,2,1,0:T(8,128)S(1)} %copy-done.1, f32[8,36,3,8,128]{4,3,2,1,0:T(8,128)S(1)} %grow_far.2.refs_2_, f32[8,36,3,8,128]{4,3,2,1,0:T(8,128)S(1)} %get-tuple-element.52.refs_3_, ...), custom_call_target="tpu_custom_call" | custom-call | flops 26542080 | bytes 10616832 | tf_op jit(solution)/shard_map/sources/pallas_call | solution.py:731
  41.8 0.6 collective-permute-start.5
  42.4 1.5 %collective-permute-done.5.other_ref.refs_3_ = f32[114,8,128]{2,1,0:T(8,128)S(1)} collective-permute-done((f32[114,8,128]{2,1,0:T(8,128)S(1)}, f32[114,8,128]{2,1,0:T(8,128)S(1)}, u32[]{:S(2)}, u32[]{:S(2)}) %collective-permute-start.5) | collective-permute-done | bytes 466976 | tf_op jit(solution)/shard_map/ppermute | solution.py:743
  43.8 1.6 %collective-permute-start.6 = (f32[60,8,128]{2,1,0:T(8,128)S(1)}, f32[60,8,128]{2,1,0:T(8,128)S(1)}, u32[]{:S(2)}, u32[]{:S(2)}) collective-permute-start(f32[60,8,128]{2,1,0:T(8,128)S(1)} %pair_sums.3), channel_id=1, source_target_pairs={{0,2},{2,0},{1,3},{3,1},{4,6},{6,4},{5,7},{7,5},{8,10},{10,8},{9,1... | collective-permute-start | bytes 737288 | tf_op jit(solution)/shard_map/ppermute | solution.py:753
  45.4 2.1 %local_rate.3.refs_1_ = f32[8,36,3,8,128]{4,3,2,1,0:T(8,128)S(1)} custom-call(f32[7168]{0:T(1024)S(1)} %copy-done, f32[8,36,3,8,128]{4,3,2,1,0:T(8,128)S(1)} %get-tuple-element.55.p_ref, f32[8,36,3,8,128]{4,3,2,1,0:T(8,128)S(1)} %get-tuple-element.57.excess_ref), custom_call_target="tpu_custom_call" | custom-call | flops 7077888 | bytes 10616832 | tf_op jit(solution)/shard_map/local_rate/pallas_call | solution.py:756
  47.6 4.6 %collective-permute-done.6.refs_4_.refs_5_ = f32[60,8,128]{2,1,0:T(8,128)S(1)} collective-permute-done((f32[60,8,128]{2,1,0:T(8,128)S(1)}, f32[60,8,128]{2,1,0:T(8,128)S(1)}, u32[]{:S(2)}, u32[]{:S(2)}) %collective-permute-start.6) | collective-permute-done | bytes 245792 | tf_op jit(solution)/shard_map/ppermute | solution.py:753
  52.1 0.0 collective-permute-start.7
  52.2 2.2 %grow_near.3 = (f32[8,18,24,128]{3,2,1,0:T(8,128)S(1)}, f32[24,128]{1,0:T(8,128)}) custom-call(f32[7168]{0:T(1024)S(1)} %copy-done, f32[8,36,3,8,128]{4,3,2,1,0:T(8,128)S(1)} %local_rate.3.refs_1_, f32[114,8,128]{2,1,0:T(8,128)S(1)} %get-tuple-element.54.sums_ref.refs_2_, f32[114,8,128]{2,1,0:T(8,128)S(1)} %collective-permute-done.5.other_ref.refs_3_, ...), custom_call_target="tpu_custom_call" | custom-call | flops 5308416 | bytes 3538944 | tf_op jit(solution)/shard_map/grow_near/pallas_call | solution.py:777
  54.3 0.0 collective-permute-done.7.refs_5_
  54.3 2.9 %grow_far.3 = f32[8,36,24,128]{3,2,1,0:T(8,128)} custom-call(f32[7168]{0:T(1024)S(1)} %copy-done, f32[8,36,3,8,128]{4,3,2,1,0:T(8,128)S(1)} %local_rate.3.refs_1_, f32[114,8,128]{2,1,0:T(8,128)S(1)} %get-tuple-element.54.sums_ref.refs_2_, f32[114,8,128]{2,1,0:T(8,128)S(1)} %collective-permute-done.5.other_ref.refs_3_, ...), custom_call_target="tpu_custom_call" | custom-call | flops 5308416 | bytes 3538944 | tf_op jit(solution)/shard_map/grow_far/pallas_call | solution.py:777
  (2 shorter events, 0.1 us)
Async XLA Ops:
  0.6 9.9 %copy-start = (f32[7168]{0:T(1024)S(1)}, f32[7168]{0:T(1024)}, u32[]{:S(2)}) copy-start(f32[7168]{0:T(1024)} %constant.4.clone.scal_ref.refs_0_) | copy-start | bytes 86020
  4.0 10.1 %collective-permute-start = (f32[28,8,128]{2,1,0:T(8,128)S(1)}, f32[28,8,128]{2,1,0:T(8,128)S(1)}, u32[]{:S(2)}, u32[]{:S(2)}) collective-permute-start(f32[28,8,128]{2,1,0:T(8,128)S(1)} %get-tuple-element.39), channel_id=1, source_target_pairs={{0,4},{4,0},{8,12},{12,8},{16,20},{20,16},{24,28},{28,24},{1,5},{5... | collective-permute-start | bytes 344072 | tf_op jit(solution)/shard_map/ppermute | solution.py:712
  7.0 7.5 %collective-permute-start.1 = (f32[28,8,128]{2,1,0:T(8,128)S(1)}, f32[28,8,128]{2,1,0:T(8,128)S(1)}, u32[]{:S(2)}, u32[]{:S(2)}) collective-permute-start(f32[28,8,128]{2,1,0:T(8,128)S(1)} %get-tuple-element.40), channel_id=1, source_target_pairs={{0,28},{4,8},{8,4},{12,16},{16,12},{20,24},{24,20},{28,0},{1,29},{... | collective-permute-start | bytes 344072 | tf_op jit(solution)/shard_map/ppermute | solution.py:713
  10.6 3.9 %copy-start.1 = (f32[4,6,8,128]{3,2,1,0:T(8,128)S(1)}, f32[4,6,8,128]{3,2,1,0:T(8,128)}, u32[]{:S(2)}) copy-start(f32[4,6,8,128]{3,2,1,0:T(8,128)} %constant.5.clone.refs_1_.refs_9_) | copy-start | bytes 294916
  20.6 1.9 %collective-permute-start.2 = (f32[119,8,128]{2,1,0:T(8,128)S(1)}, f32[119,8,128]{2,1,0:T(8,128)S(1)}, u32[]{:S(2)}, u32[]{:S(2)}) collective-permute-start(f32[119,8,128]{2,1,0:T(8,128)S(1)} %get-tuple-element.41.sums_ref.refs_2_), channel_id=1, source_target_pairs={{0,1},{1,0},{2,3},{3,2},{4,5},{5,4},{6,7},{7,6},{8,9},{9,8},{10,11... | collective-permute-start | bytes 1462280 | tf_op jit(solution)/shard_map/ppermute | solution.py:743
  22.6 8.5 %collective-permute-start.3 = (f32[65,8,128]{2,1,0:T(8,128)S(1)}, f32[65,8,128]{2,1,0:T(8,128)S(1)}, u32[]{:S(2)}, u32[]{:S(2)}) collective-permute-start(f32[65,8,128]{2,1,0:T(8,128)S(1)} %pair_sums.2), channel_id=1, source_target_pairs={{0,2},{2,0},{1,3},{3,1},{4,6},{6,4},{5,7},{7,5},{8,10},{10,8},{9,1... | collective-permute-start | bytes 798728 | tf_op jit(solution)/shard_map/ppermute | solution.py:753
  31.1 3.1 %collective-permute-start.4 = (f32[65,8,128]{2,1,0:T(8,128)S(1)}, f32[65,8,128]{2,1,0:T(8,128)S(1)}, u32[]{:S(2)}, u32[]{:S(2)}) collective-permute-start(f32[65,8,128]{2,1,0:T(8,128)S(1)} %collective-permute-done.3.refs_4_.refs_5_), channel_id=1, source_target_pairs={{0,1},{1,0},{2,3},{3,2},{4,5},{5,4},{6,7},{7,6},{8,9},{9,8},{10,11... | collective-permute-start | bytes 798728 | tf_op jit(solution)/shard_map/ppermute | solution.py:767
  41.8 2.0 %collective-permute-start.5 = (f32[114,8,128]{2,1,0:T(8,128)S(1)}, f32[114,8,128]{2,1,0:T(8,128)S(1)}, u32[]{:S(2)}, u32[]{:S(2)}) collective-permute-start(f32[114,8,128]{2,1,0:T(8,128)S(1)} %get-tuple-element.54.sums_ref.refs_2_), channel_id=1, source_target_pairs={{0,1},{1,0},{2,3},{3,2},{4,5},{5,4},{6,7},{7,6},{8,9},{9,8},{10,11... | collective-permute-start | bytes 1400840 | tf_op jit(solution)/shard_map/ppermute | solution.py:743
  43.8 8.3 %collective-permute-start.6 = (f32[60,8,128]{2,1,0:T(8,128)S(1)}, f32[60,8,128]{2,1,0:T(8,128)S(1)}, u32[]{:S(2)}, u32[]{:S(2)}) collective-permute-start(f32[60,8,128]{2,1,0:T(8,128)S(1)} %pair_sums.3), channel_id=1, source_target_pairs={{0,2},{2,0},{1,3},{3,1},{4,6},{6,4},{5,7},{7,5},{8,10},{10,8},{9,1... | collective-permute-start | bytes 737288 | tf_op jit(solution)/shard_map/ppermute | solution.py:753
  52.1 2.2 %collective-permute-start.7 = (f32[60,8,128]{2,1,0:T(8,128)S(1)}, f32[60,8,128]{2,1,0:T(8,128)S(1)}, u32[]{:S(2)}, u32[]{:S(2)}) collective-permute-start(f32[60,8,128]{2,1,0:T(8,128)S(1)} %collective-permute-done.6.refs_4_.refs_5_), channel_id=1, source_target_pairs={{0,1},{1,0},{2,3},{3,2},{4,5},{5,4},{6,7},{7,6},{8,9},{9,8},{10,11... | collective-permute-start | bytes 737288 | tf_op jit(solution)/shard_map/ppermute | solution.py:767

commit v7 on v6

--- a/solution.py
+++ b/solution.py
@@ -132,6 +132,7 @@
     lane = lanes()
     zero = jnp.zeros((8, WIDTH), jnp.float32)
     held = [zero, zero]
+    spot = {True: (lane + (WIDTH - 4)) % WIDTH, False: (lane + 2) % WIDTH}
     for j in range(ND):
         if j % CHUNK == 0:
             fetch(j // CHUNK).wait()
@@ -139,14 +140,21 @@
         wide, narrow = (right_ref, left_ref) if back else (left_ref, right_ref)
         half = RANK[j] % 2
         first, aside = (WIDTH - 4, 4) if back else (0, -2)
-        four = zero
-        two = zero
+        fours, twos = [], []
         for r in range(TILES):
+            four, two = zero, zero
             for k in range(BANDS):
                 place = GROUP * r + 4 * k
                 tile = turn(copy_ref[k, j, tile_rows(r), :], place - first)
-                four = jnp.where(lane // 4 == place // 4, tile, four)
-                two = jnp.where(lane // 2 == (place + aside) % WIDTH // 2, tile, two)
+                four = jnp.where(lane // 4 % BANDS == k, tile, four)
+                two = jnp.where(spot[back] // 4 % BANDS == k, tile, two)
+            fours.append(four)
+            twos.append(two)
+        four = jnp.where(lane < GROUP, fours[0], jnp.where(lane < 2 * GROUP, fours[1], fours[2]))
+        two = jnp.where(
+            spot[back] < GROUP, twos[0], jnp.where(spot[back] < 2 * GROUP, twos[1], twos[2])
+        )
+        four = jnp.where(lane < TILES * GROUP, four, 0.0)
         wide[RANK[j]] = four
         two = turn(two, 2 * half - aside)
         if half:
@@ -183,8 +191,8 @@
 
 
 def drive_of(j, east, north, open_water):
-    along = float(COS[j]) * east + float(SIN[j]) * north
-    drive = jnp.minimum(jnp.maximum(along, 0.0) / WIND_REF, WIND_CLIP)
+    along = float(COS[j] / WIND_REF) * east + float(SIN[j] / WIND_REF) * north
+    drive = jnp.minimum(jnp.maximum(along, 0.0), WIND_CLIP)
     return drive * drive * open_water
 
 
@@ -293,8 +301,14 @@
     return y
 
 
-def drift_kernel(scal_ref, q_ref, out_ref):
+def drift_kernel(scal_ref, q_ref, east_ref, north_ref, land_ref, out_ref, drive_ref):
     bands = q_ref.shape[0]
+    for r in range(TILES):
+        rows = tile_rows(r)
+        water = jnp.where(land_ref[rows, :] == 2, 0.0, 1.0)
+        east, north = east_ref[rows, :], north_ref[rows, :]
+        for j in range(ND):
+            drive_ref[j, r] = drive_of(j, east, north, water)
     inside = inside_masks()
 
     def band(k, carry):
@@ -452,8 +466,8 @@
 
 
 def source_kernel(first, *refs):
-    scal_ref, table_ref, x_ref, spec_ref, east_ref, north_ref, land_ref, rows_ref = refs[:8]
-    refs = refs[8:]
+    scal_ref, table_ref, x_ref, spec_ref, drive_ref, land_ref, rows_ref = refs[:7]
+    refs = refs[7:]
     freq = lax.axis_index("freq")
     bands = x_ref.shape[0]
 
@@ -463,7 +477,7 @@
     if first:
         mine_right_ref, mine_left_ref, even_ref, odd_ref = refs[:4]
         p_ref, excess_ref, sums_ref, part_ref, packed_drive_ref, ice_ref = refs[4:10]
-        drive_ref, fix_ref, left_ref, right_ref, columns_ref, near_ref, far_ref = refs[10:]
+        fix_ref, left_ref, right_ref, columns_ref, near_ref, far_ref = refs[10:]
         odd = lax.axis_index("lon") % 2 == 1
         for i in range(SENT):
             even, other = even_ref[i], odd_ref[i]
@@ -476,16 +490,10 @@
             sums_ref, part_ref, packed_drive_ref, ice_ref,
         )
     else:
-        columns_ref, p_ref, excess_ref, sums_ref, drive_ref, fix_ref = refs
+        columns_ref, p_ref, excess_ref, sums_ref, fix_ref = refs
     packed_fix(table, columns_ref, fix_ref)
     for i in range(PACKED_AT):
         sums_ref[i] = jnp.zeros((8, WIDTH), jnp.float32)
-    for r in range(TILES):
-        rows = tile_rows(r)
-        water = jnp.where(land_ref[rows, :] == 2, 0.0, 1.0)
-        east, north = east_ref[rows, :], north_ref[rows, :]
-        for j in range(ND):
-            drive_ref[j, r] = drive_of(j, east, north, water)
 
     lane = lanes()
     at_edge = {True: lane < 2, False: lane >= WIDTH - 2}
@@ -569,7 +577,7 @@
 
 def grow_half(half, last, near, refs):
     scal_ref, part_ref, sums_ref, other_ref, mine_ref, lower_ref = refs[:6]
-    east_ref, north_ref, land_ref, out_ref, rate_ref, near_ref, field_ref, sent = refs[6:]
+    drive_ref, land_ref, out_ref, rate_ref, near_ref, field_ref, sent = refs[6:]
     bands = part_ref.shape[0]
     freq = lax.axis_index("freq")
     odd = jnp.where(freq % 2 == 1, 1.0, 0.0)
@@ -583,12 +591,10 @@
             for at in (SLOPE_AT, STRESS_AT)
         )
         damp, gain = damp_and_gain(slope, stress, ice)
-        east, north = east_ref[rows, :], north_ref[rows, :]
         for i in range(HALF):
             j = half * HALF + i
             lower = odd * other_ref[TILES * j + r] + upper * lower_ref[TILES * i + r]
-            drive = drive_of(j, east, north, 1.0 - ice)
-            rate_ref[i, r] = gain * drive - damp - LOWER * lower
+            rate_ref[i, r] = gain * drive_ref[j, r] - damp - LOWER * lower
 
     inside = None if last else inside_masks()
     target_ref = out_ref if near else field_ref
@@ -626,16 +632,18 @@
 
 
 def growth_kernel(last, near, *refs):
-    operands, refs = refs[:9], refs[9:]
+    operands, refs = refs[:8], refs[8:]
     scal_ref, part_ref, sums_ref, other_ref, mine_ref = operands[:5]
     freq = lax.axis_index("freq")
     rest = (None,) * 3
     if near and last:
-        out_ref, slope_ref, rate_ref = refs
+        out_ref, slope_out_ref, rate_ref, slope_ref, slope_sent = refs
         for r in range(TILES):
             at = SLOPE_AT + r
             total = (sums_ref[at] + other_ref[at]) + mine_ref[at - SLOPE_AT + HALF_TILES]
             slope_ref[tile_rows(r), :] = total
+        slope_copy = pltpu.make_async_copy(slope_ref, slope_out_ref, slope_sent)
+        slope_copy.start()
     elif near:
         table_ref, packed_part_ref, packed_drive_ref, ice_ref, out_ref, columns_ref, rate_ref = refs
         odd = jnp.where(freq % 2 == 1, 1.0, 0.0)
@@ -661,6 +669,9 @@
         def _():
             grow_half(half, last, near, operands + (out_ref, rate_ref, *rest))
 
+    if near and last:
+        slope_copy.wait()
+
 
 def cost(tiles, ops, moves):
     return pl.CostEstimate(
@@ -692,7 +703,6 @@
     swap_even = [(i, i ^ 1) for i in range(ring)]
     swap_odd = [(i, (i + (1 if i % 2 else -1)) % ring) for i in range(ring)]
     whole = bands * ND * TILES
-    by_direction = pltpu.VMEM((ND, TILES, 8, WIDTH), f32)
     packed = pltpu.VMEM((ND, 8, WIDTH), f32)
     received = pltpu.VMEM((SENT, 8, WIDTH), f32)
 
@@ -711,17 +721,17 @@
     )(*(pltpu.with_memory_space_constraint(x, pltpu.HBM) for x in arguments))
     even = lax.ppermute(even, "lon", swap_even)
     odd = lax.ppermute(odd, "lon", swap_odd)
-    drifted = pl.pallas_call(
+    drifted, drive = pl.pallas_call(
         drift_kernel,
-        in_specs=[smem, vmem],
-        out_specs=vmem,
-        out_shape=spread_field,
+        in_specs=[smem] + [vmem] * 4,
+        out_specs=[vmem] * 2,
+        out_shape=[spread_field, jax.ShapeDtypeStruct((ND, TILES, 8, WIDTH), f32)],
         compiler_params=params,
         cost_estimate=cost(whole, 12, 2),
         name="drift",
-    )(scalars, spectrum)
-
-    fields = [east_wind, north_wind, land_sea]
+    )(scalars, spectrum, east_wind, north_wind, land_sea)
+
+    fields = [drive, land_sea]
     for step in range(STEPS):
         first, last = step == 0, step == STEPS - 1
         sums = PACKED_AT + (PACKED_SUMS if first else 0)
@@ -734,7 +744,7 @@
             out_specs=[vmem] * (6 if first else 3),
             out_shape=[spread_field, spread_field, tiles(sums)]
             + ([tiles(ND), tiles(ND), tile] if first else []),
-            scratch_shapes=[by_direction, packed]
+            scratch_shapes=[packed]
             + ([received] * 2 + [packed] * 3 if first else []),
             compiler_params=params,
             cost_estimate=cost(whole, 30, 3),
@@ -773,11 +783,13 @@
             scratch = [pltpu.VMEM((HALF, TILES, 8, WIDTH), f32)]
             if write:
                 scratch += [pltpu.VMEM(near_half.shape, f32), pltpu.SemaphoreType.DMA((2, bands))]
+            elif last:
+                scratch += [pltpu.VMEM(plane.shape, f32), pltpu.SemaphoreType.DMA(())]
             alias = not last and not is_near
             return pl.pallas_call(
                 functools.partial(growth_kernel, last, is_near),
                 in_specs=[smem] + [vmem] * (len(operands) - 1),
-                out_specs=[hbm if write else vmem] * len(shapes),
+                out_specs=[hbm] if write else [vmem, hbm if last else vmem][: len(shapes)],
                 out_shape=shapes,
                 input_output_aliases={len(operands) - 1: 0} if alias else {},
                 scratch_shapes=scratch,

time: 57.4 us -> 56.8 us (0.990)
  Pallas kernels: 34.1 us -> 33.5 us
    pallas_call x4, Pallas kernels: 11.1 us -> 10.4 us  [grow(): pl.pallas_call(functools.partial(growth_kernel, last, is_near), in_specs=...]
  transfers between devices with their start and end apart: 8 -> 8, of which waited for: 5 -> 5; matrix products, arithmetic and copies ran while one was open for 0% -> 0% of each run, Pallas kernels for 25% -> 24%
where the time goes in v7:
time: 56.8 us; the launch traced here: 56.6 us
  Pallas kernels  33.5 us (59%)
  waiting for transfers between devices  11.9 us (21%)
  starting transfers between devices  10.4 us (18%)
  between operations  0.76 us (1%)
    pallas_call x2, Pallas kernels, per_device(): pl.pallas_call(functools.partial(source_kernel, first), in_specs=[smem] +...  10.6 us
    pallas_call x4, Pallas kernels, grow(): pl.pallas_call(functools.partial(growth_kernel, last, is_near), in_specs=...  10.4 us
    ppermute x2, waiting for transfers between devices, per_device(): near = lax.ppermute(pair, 'freq', swap_chip)  8.31 us
    pallas_call x2, Pallas kernels, per_device(): pl.pallas_call(functools.partial(local_kernel, last), in_specs=[smem] + [...  5.29 us
    pallas_call x1, Pallas kernels, per_device(): pl.pallas_call(drift_kernel, in_specs=[smem] + [vmem] * 4, out_specs=[vme...  3.61 us
    ppermute x1, starting transfers between devices, per_device(): odd = lax.ppermute(odd, 'lon', swap_odd)  3.57 us
    pallas_call x1, Pallas kernels, per_device(): pl.pallas_call(pack_kernel, in_specs=[hbm] * 5, out_specs=[vmem] * 9, out...  3.54 us
    ppermute x2, waiting for transfers between devices, per_device(): other = lax.ppermute(mine, 'freq', swap_core)  3.3 us
  transfers between devices with their start and end apart: 8, of which 5 were waited for; matrix products, arithmetic and copies ran while one was open for 0% of the time, Pallas kernels for 24%

profile of v7, /device:TPU:0, one launch (start us, length us, event | category | flops | bytes accessed | tf_op | source)
XLA Modules:
  0.0 56.6 jit_solution(2198941595762592155)
XLA Ops:
  0.6 0.0 copy-start
  0.6 0.0 copy-start.1
  0.7 3.5 %pack_columns.1 = (f32[8,36,24,128]{3,2,1,0:T(8,128)S(1)}, f32[28,8,128]{2,1,0:T(8,128)S(1)}, f32[28,8,128]{2,1,0:T(8,128)S(1)}, f32[24,128]{1,0:T(8,128)S(1)}, ...) custom-call(f32[8,36,24,128]{3,2,1,0:T(8,128)} %spec_ref.1, ...), custom_call_target="tpu_custom_call" | custom-call | flops 5308416 | bytes 7077888 | tf_op jit(solution)/shard_map/pack_columns/pallas_call | solution.py:710
  4.2 3.0 %collective-permute-start = (f32[28,8,128]{2,1,0:T(8,128)S(1)}, f32[28,8,128]{2,1,0:T(8,128)S(1)}, u32[]{:S(2)}, u32[]{:S(2)}) collective-permute-start(f32[28,8,128]{2,1,0:T(8,128)S(1)} %get-tuple-element.43), channel_id=1, source_target_pairs={{0,4},{4,0},{8,12},{12,8},{16,20},{20,16},{24,28},{28,24},{1,5},{5... | collective-permute-start | bytes 344072 | tf_op jit(solution)/shard_map/ppermute | solution.py:722
  7.2 3.6 %collective-permute-start.1 = (f32[28,8,128]{2,1,0:T(8,128)S(1)}, f32[28,8,128]{2,1,0:T(8,128)S(1)}, u32[]{:S(2)}, u32[]{:S(2)}) collective-permute-start(f32[28,8,128]{2,1,0:T(8,128)S(1)} %get-tuple-element.44), channel_id=1, source_target_pairs={{0,28},{4,8},{8,4},{12,16},{16,12},{20,24},{24,20},{28,0},{1,29},{... | collective-permute-start | bytes 344072 | tf_op jit(solution)/shard_map/ppermute | solution.py:723
  10.8 0.0 copy-done
  10.8 3.6 %drift.1 = (f32[8,36,3,8,128]{4,3,2,1,0:T(8,128)S(1)}, f32[36,3,8,128]{3,2,1,0:T(8,128)S(1)}) custom-call(f32[7168]{0:T(1024)S(1)} %copy-done, f32[8,36,24,128]{3,2,1,0:T(8,128)S(1)} %get-tuple-element.34.q_ref.refs_3_.refs_0_, f32[24,128]{1,0:T(8,128)S(1)} %get-tuple-element.35.east_ref, f32[24,128]{1,0:T(8,128)S(1)} %get-tuple-element.36.north_ref, ...), custom_call_target="tpu_custom_call" | custom-call | flops 10616832 | bytes 7077888 | tf_op jit(solution)/shard_map/drift/pallas_call | solution.py:724
  14.4 0.0 collective-permute-done.refs_9_
  14.4 0.3 collective-permute-done.1.refs_10_
  14.7 0.0 copy-done.1
  14.7 6.0 %sources.2 = (f32[8,36,3,8,128]{4,3,2,1,0:T(8,128)S(1)}, f32[8,36,3,8,128]{4,3,2,1,0:T(8,128)S(1)}, f32[119,8,128]{2,1,0:T(8,128)S(1)}, f32[36,8,128]{2,1,0:T(8,...) custom-call(f32[7168]{0:T(1024)S(1)} %copy-done, f32[4,6,8,128]{3,2,1,0:T(8,128)S(1)} %copy-done.1, ...), custom_call_target="tpu_custom_call" | custom-call | flops 26542080 | bytes 10616832 | tf_op jit(solution)/shard_map/sources/pallas_call | solution.py:741
  20.7 0.1 collective-permute-start.2
  20.8 1.8 %collective-permute-done.2.other_ref.refs_3_ = f32[119,8,128]{2,1,0:T(8,128)S(1)} collective-permute-done((f32[119,8,128]{2,1,0:T(8,128)S(1)}, f32[119,8,128]{2,1,0:T(8,128)S(1)}, u32[]{:S(2)}, u32[]{:S(2)}) %collective-permute-start.2) | collective-permute-done | bytes 487456 | tf_op jit(solution)/shard_map/ppermute | solution.py:753
  22.6 1.6 %collective-permute-start.3 = (f32[65,8,128]{2,1,0:T(8,128)S(1)}, f32[65,8,128]{2,1,0:T(8,128)S(1)}, u32[]{:S(2)}, u32[]{:S(2)}) collective-permute-start(f32[65,8,128]{2,1,0:T(8,128)S(1)} %pair_sums.2), channel_id=1, source_target_pairs={{0,2},{2,0},{1,3},{3,1},{4,6},{6,4},{5,7},{7,5},{8,10},{10,8},{9,1... | collective-permute-start | bytes 798728 | tf_op jit(solution)/shard_map/ppermute | solution.py:763
  24.2 3.1 %local_rate.2 = (f32[8,36,3,8,128]{4,3,2,1,0:T(8,128)S(1)}, f32[8,36,3,8,128]{4,3,2,1,0:T(8,128)S(1)}) custom-call(f32[7168]{0:T(1024)S(1)} %copy-done, f32[8,36,3,8,128]{4,3,2,1,0:T(8,128)S(1)} %get-tuple-element.46.p_ref, f32[8,36,3,8,128]{4,3,2,1,0:T(8,128)S(1)} %get-tuple-element.48.excess_ref, ...), custom_call_target="tpu_custom_call" | custom-call | flops 7077888 | bytes 10616832 | tf_op jit(solution)/shard_map/local_rate/pallas_call | solution.py:766
  27.3 3.8 %collective-permute-done.3.refs_4_.refs_5_ = f32[65,8,128]{2,1,0:T(8,128)S(1)} collective-permute-done((f32[65,8,128]{2,1,0:T(8,128)S(1)}, f32[65,8,128]{2,1,0:T(8,128)S(1)}, u32[]{:S(2)}, u32[]{:S(2)}) %collective-permute-start.3) | collective-permute-done | bytes 266272 | tf_op jit(solution)/shard_map/ppermute | solution.py:763
  31.1 0.0 collective-permute-start.4
  31.1 3.1 %grow_near.2 = (f32[8,36,3,8,128]{4,3,2,1,0:T(8,128)S(1)}, f32[36,8,128]{2,1,0:T(8,128)S(1)}) custom-call(f32[7168]{0:T(1024)S(1)} %copy-done, f32[8,36,3,8,128]{4,3,2,1,0:T(8,128)S(1)} %get-tuple-element.50.refs_1_, f32[119,8,128]{2,1,0:T(8,128)S(1)} %get-tuple-element.45.sums_ref.refs_2_, f32[119,8,128]{2,1,0:T(8,128)S(1)} %collective-permute-done.2.other_ref.refs_3_, ...), custom_call_target="tpu_custom_call" | custom-call | flops 10616832 | bytes 3538944 | tf_op jit(solution)/shard_map/grow_near/pallas_call | solution.py:789
  34.2 0.0 collective-permute-done.4.refs_5_
  34.2 2.8 %grow_far.2.refs_2_ = f32[8,36,3,8,128]{4,3,2,1,0:T(8,128)S(1)} custom-call(f32[7168]{0:T(1024)S(1)} %copy-done, f32[8,36,3,8,128]{4,3,2,1,0:T(8,128)S(1)} %get-tuple-element.50.refs_1_, f32[119,8,128]{2,1,0:T(8,128)S(1)} %get-tuple-element.45.sums_ref.refs_2_, ...), custom_call_target="tpu_custom_call", output_to_operand_aliasing={{}: (8, {})} | custom-call | flops 10616832 | bytes 3538944 | tf_op jit(solution)/shard_map/grow_far/pallas_call | solution.py:789
  37.0 4.6 %sources.3 = (f32[8,36,3,8,128]{4,3,2,1,0:T(8,128)S(1)}, f32[8,36,3,8,128]{4,3,2,1,0:T(8,128)S(1)}, f32[114,8,128]{2,1,0:T(8,128)S(1)}) custom-call(f32[7168]{0:T(1024)S(1)} %copy-done, f32[4,6,8,128]{3,2,1,0:T(8,128)S(1)} %copy-done.1, f32[8,36,3,8,128]{4,3,2,1,0:T(8,128)S(1)} %grow_far.2.refs_2_, f32[8,36,3,8,128]{4,3,2,1,0:T(8,128)S(1)} %get-tuple-element.56.refs_3_, ...), custom_call_target="tpu_custom_call" | custom-call | flops 26542080 | bytes 10616832 | tf_op jit(solution)/shard_map/sources/pallas_call | solution.py:741
  41.7 0.6 %collective-permute-start.5 = (f32[114,8,128]{2,1,0:T(8,128)S(1)}, f32[114,8,128]{2,1,0:T(8,128)S(1)}, u32[]{:S(2)}, u32[]{:S(2)}) collective-permute-start(f32[114,8,128]{2,1,0:T(8,128)S(1)} %get-tuple-element.58.sums_ref.refs_2_), channel_id=1, source_target_pairs={{0,1},{1,0},{2,3},{3,2},{4,5},{5,4},{6,7},{7,6},{8,9},{9,8},{10,11... | collective-permute-start | bytes 1400840 | tf_op jit(solution)/shard_map/ppermute | solution.py:753
  42.2 1.5 %collective-permute-done.5.other_ref.refs_3_ = f32[114,8,128]{2,1,0:T(8,128)S(1)} collective-permute-done((f32[114,8,128]{2,1,0:T(8,128)S(1)}, f32[114,8,128]{2,1,0:T(8,128)S(1)}, u32[]{:S(2)}, u32[]{:S(2)}) %collective-permute-start.5) | collective-permute-done | bytes 466976 | tf_op jit(solution)/shard_map/ppermute | solution.py:753
  43.7 1.6 %collective-permute-start.6 = (f32[60,8,128]{2,1,0:T(8,128)S(1)}, f32[60,8,128]{2,1,0:T(8,128)S(1)}, u32[]{:S(2)}, u32[]{:S(2)}) collective-permute-start(f32[60,8,128]{2,1,0:T(8,128)S(1)} %pair_sums.3), channel_id=1, source_target_pairs={{0,2},{2,0},{1,3},{3,1},{4,6},{6,4},{5,7},{7,5},{8,10},{10,8},{9,1... | collective-permute-start | bytes 737288 | tf_op jit(solution)/shard_map/ppermute | solution.py:763
  45.3 2.2 %local_rate.3.refs_1_ = f32[8,36,3,8,128]{4,3,2,1,0:T(8,128)S(1)} custom-call(f32[7168]{0:T(1024)S(1)} %copy-done, f32[8,36,3,8,128]{4,3,2,1,0:T(8,128)S(1)} %get-tuple-element.59.p_ref, f32[8,36,3,8,128]{4,3,2,1,0:T(8,128)S(1)} %get-tuple-element.61.excess_ref), custom_call_target="tpu_custom_call" | custom-call | flops 7077888 | bytes 10616832 | tf_op jit(solution)/shard_map/local_rate/pallas_call | solution.py:766
  47.5 4.5 %collective-permute-done.6.refs_4_.refs_5_ = f32[60,8,128]{2,1,0:T(8,128)S(1)} collective-permute-done((f32[60,8,128]{2,1,0:T(8,128)S(1)}, f32[60,8,128]{2,1,0:T(8,128)S(1)}, u32[]{:S(2)}, u32[]{:S(2)}) %collective-permute-start.6) | collective-permute-done | bytes 245792 | tf_op jit(solution)/shard_map/ppermute | solution.py:763
  52.0 0.0 collective-permute-start.7
  52.0 1.6 %grow_near.3 = (f32[8,18,24,128]{3,2,1,0:T(8,128)S(1)}, f32[24,128]{1,0:T(8,128)}) custom-call(f32[7168]{0:T(1024)S(1)} %copy-done, f32[8,36,3,8,128]{4,3,2,1,0:T(8,128)S(1)} %local_rate.3.refs_1_, f32[114,8,128]{2,1,0:T(8,128)S(1)} %get-tuple-element.58.sums_ref.refs_2_, f32[114,8,128]{2,1,0:T(8,128)S(1)} %collective-permute-done.5.other_ref.refs_3_, ...), custom_call_target="tpu_custom_call" | custom-call | flops 5308416 | bytes 3538944 | tf_op jit(solution)/shard_map/grow_near/pallas_call | solution.py:789
  53.6 0.0 collective-permute-done.7.refs_5_
  53.7 2.9 %grow_far.3 = f32[8,36,24,128]{3,2,1,0:T(8,128)} custom-call(f32[7168]{0:T(1024)S(1)} %copy-done, f32[8,36,3,8,128]{4,3,2,1,0:T(8,128)S(1)} %local_rate.3.refs_1_, f32[114,8,128]{2,1,0:T(8,128)S(1)} %get-tuple-element.58.sums_ref.refs_2_, f32[114,8,128]{2,1,0:T(8,128)S(1)} %collective-permute-done.5.other_ref.refs_3_, ...), custom_call_target="tpu_custom_call" | custom-call | flops 5308416 | bytes 3538944 | tf_op jit(solution)/shard_map/grow_far/pallas_call | solution.py:789
  (2 shorter events, 0.1 us)
Async XLA Ops:
  0.6 10.2 %copy-start = (f32[7168]{0:T(1024)S(1)}, f32[7168]{0:T(1024)}, u32[]{:S(2)}) copy-start(f32[7168]{0:T(1024)} %constant.4.clone.scal_ref.refs_0_) | copy-start | bytes 86020
  0.6 14.1 %copy-start.1 = (f32[4,6,8,128]{3,2,1,0:T(8,128)S(1)}, f32[4,6,8,128]{3,2,1,0:T(8,128)}, u32[]{:S(2)}) copy-start(f32[4,6,8,128]{3,2,1,0:T(8,128)} %constant.5.clone.refs_1_.refs_8_) | copy-start | bytes 294916
  4.2 10.2 %collective-permute-start = (f32[28,8,128]{2,1,0:T(8,128)S(1)}, f32[28,8,128]{2,1,0:T(8,128)S(1)}, u32[]{:S(2)}, u32[]{:S(2)}) collective-permute-start(f32[28,8,128]{2,1,0:T(8,128)S(1)} %get-tuple-element.43), channel_id=1, source_target_pairs={{0,4},{4,0},{8,12},{12,8},{16,20},{20,16},{24,28},{28,24},{1,5},{5... | collective-permute-start | bytes 344072 | tf_op jit(solution)/shard_map/ppermute | solution.py:722
  7.2 7.5 %collective-permute-start.1 = (f32[28,8,128]{2,1,0:T(8,128)S(1)}, f32[28,8,128]{2,1,0:T(8,128)S(1)}, u32[]{:S(2)}, u32[]{:S(2)}) collective-permute-start(f32[28,8,128]{2,1,0:T(8,128)S(1)} %get-tuple-element.44), channel_id=1, source_target_pairs={{0,28},{4,8},{8,4},{12,16},{16,12},{20,24},{24,20},{28,0},{1,29},{... | collective-permute-start | bytes 344072 | tf_op jit(solution)/shard_map/ppermute | solution.py:723
  20.7 1.9 %collective-permute-start.2 = (f32[119,8,128]{2,1,0:T(8,128)S(1)}, f32[119,8,128]{2,1,0:T(8,128)S(1)}, u32[]{:S(2)}, u32[]{:S(2)}) collective-permute-start(f32[119,8,128]{2,1,0:T(8,128)S(1)} %get-tuple-element.45.sums_ref.refs_2_), channel_id=1, source_target_pairs={{0,1},{1,0},{2,3},{3,2},{4,5},{5,4},{6,7},{7,6},{8,9},{9,8},{10,11... | collective-permute-start | bytes 1462280 | tf_op jit(solution)/shard_map/ppermute | solution.py:753
  22.6 8.5 %collective-permute-start.3 = (f32[65,8,128]{2,1,0:T(8,128)S(1)}, f32[65,8,128]{2,1,0:T(8,128)S(1)}, u32[]{:S(2)}, u32[]{:S(2)}) collective-permute-start(f32[65,8,128]{2,1,0:T(8,128)S(1)} %pair_sums.2), channel_id=1, source_target_pairs={{0,2},{2,0},{1,3},{3,1},{4,6},{6,4},{5,7},{7,5},{8,10},{10,8},{9,1... | collective-permute-start | bytes 798728 | tf_op jit(solution)/shard_map/ppermute | solution.py:763
  31.1 3.1 %collective-permute-start.4 = (f32[65,8,128]{2,1,0:T(8,128)S(1)}, f32[65,8,128]{2,1,0:T(8,128)S(1)}, u32[]{:S(2)}, u32[]{:S(2)}) collective-permute-start(f32[65,8,128]{2,1,0:T(8,128)S(1)} %collective-permute-done.3.refs_4_.refs_5_), channel_id=1, source_target_pairs={{0,1},{1,0},{2,3},{3,2},{4,5},{5,4},{6,7},{7,6},{8,9},{9,8},{10,11... | collective-permute-start | bytes 798728 | tf_op jit(solution)/shard_map/ppermute | solution.py:777
  41.7 2.0 %collective-permute-start.5 = (f32[114,8,128]{2,1,0:T(8,128)S(1)}, f32[114,8,128]{2,1,0:T(8,128)S(1)}, u32[]{:S(2)}, u32[]{:S(2)}) collective-permute-start(f32[114,8,128]{2,1,0:T(8,128)S(1)} %get-tuple-element.58.sums_ref.refs_2_), channel_id=1, source_target_pairs={{0,1},{1,0},{2,3},{3,2},{4,5},{5,4},{6,7},{7,6},{8,9},{9,8},{10,11... | collective-permute-start | bytes 1400840 | tf_op jit(solution)/shard_map/ppermute | solution.py:753
  43.7 8.3 %collective-permute-start.6 = (f32[60,8,128]{2,1,0:T(8,128)S(1)}, f32[60,8,128]{2,1,0:T(8,128)S(1)}, u32[]{:S(2)}, u32[]{:S(2)}) collective-permute-start(f32[60,8,128]{2,1,0:T(8,128)S(1)} %pair_sums.3), channel_id=1, source_target_pairs={{0,2},{2,0},{1,3},{3,1},{4,6},{6,4},{5,7},{7,5},{8,10},{10,8},{9,1... | collective-permute-start | bytes 737288 | tf_op jit(solution)/shard_map/ppermute | solution.py:763
  52.0 1.6 %collective-permute-start.7 = (f32[60,8,128]{2,1,0:T(8,128)S(1)}, f32[60,8,128]{2,1,0:T(8,128)S(1)}, u32[]{:S(2)}, u32[]{:S(2)}) collective-permute-start(f32[60,8,128]{2,1,0:T(8,128)S(1)} %collective-permute-done.6.refs_4_.refs_5_), channel_id=1, source_target_pairs={{0,1},{1,0},{2,3},{3,2},{4,5},{5,4},{6,7},{7,6},{8,9},{9,8},{10,11... | collective-permute-start | bytes 737288 | tf_op jit(solution)/shard_map/ppermute | solution.py:777

commit v8 on v7

--- a/solution.py
+++ b/solution.py
@@ -53,9 +53,7 @@
 BANDS = 8
 SENT = HALF + QUARTER + 1
 FIELDS = 5
-SLOPE_AT = ND * TILES
-STRESS_AT = SLOPE_AT + TILES
-PACKED_AT = STRESS_AT + TILES
+PACKED_AT = ND * TILES
 PACKED_SUMS = 5
 HALF_TILES = HALF * TILES
 SCALE = 0.25 * DTHETA
@@ -110,53 +108,51 @@
     return slice(8 * r, 8 * r + 8)
 
 
-CHUNK = 4
-
-
 def pack_kernel(spec_ref, *refs):
     sources, (copy_ref, right_ref, left_ref), held_refs = refs[:4], refs[4:7], refs[7:11]
-    to_even_ref, to_odd_ref, arrived = refs[11:]
-
-    def fetch(c):
-        part = pl.ds(CHUNK * c, CHUNK)
-        return pltpu.make_async_copy(spec_ref.at[:, part], copy_ref.at[:, part], arrived.at[c])
+    to_even_ref, to_odd_ref, arrived, four_ref, two_ref = refs[11:]
+
+    def fetch(k):
+        return pltpu.make_async_copy(spec_ref.at[k], copy_ref.at[k], arrived.at[k])
 
     small = [
-        pltpu.make_async_copy(source, target, arrived.at[ND // CHUNK + i])
+        pltpu.make_async_copy(source, target, arrived.at[BANDS + i])
         for i, (source, target) in enumerate(zip(sources, held_refs))
     ]
-    for c in range(ND // CHUNK):
-        fetch(c).start()
+    for k in range(BANDS):
+        fetch(k).start()
     for copy in small:
         copy.start()
     lane = lanes()
     zero = jnp.zeros((8, WIDTH), jnp.float32)
+
+    def by_tile(spot, tiles):
+        return jnp.where(spot < GROUP, tiles[0], jnp.where(spot < 2 * GROUP, tiles[1], tiles[2]))
+
+    first = {True: WIDTH - 4, False: 0}
+    aside = {True: 4, False: -2}
+    spot = {back: (lane - aside[back]) % WIDTH for back in aside}
+    for k in range(BANDS):
+        fetch(k).wait()
+        for j in range(ND):
+            back = BACK_LON[j]
+            tiles = [
+                turn(copy_ref[k, j, tile_rows(r), :], GROUP * r + 4 * k - first[back])
+                for r in range(TILES)
+            ]
+            four, two = by_tile(lane, tiles), by_tile(spot[back], tiles)
+            if k:
+                four = jnp.where(lane // 4 % BANDS == k, four, four_ref[j])
+                two = jnp.where(spot[back] // 4 % BANDS == k, two, two_ref[j])
+            four_ref[j] = four
+            two_ref[j] = two
     held = [zero, zero]
-    spot = {True: (lane + (WIDTH - 4)) % WIDTH, False: (lane + 2) % WIDTH}
     for j in range(ND):
-        if j % CHUNK == 0:
-            fetch(j // CHUNK).wait()
         back = BACK_LON[j]
         wide, narrow = (right_ref, left_ref) if back else (left_ref, right_ref)
         half = RANK[j] % 2
-        first, aside = (WIDTH - 4, 4) if back else (0, -2)
-        fours, twos = [], []
-        for r in range(TILES):
-            four, two = zero, zero
-            for k in range(BANDS):
-                place = GROUP * r + 4 * k
-                tile = turn(copy_ref[k, j, tile_rows(r), :], place - first)
-                four = jnp.where(lane // 4 % BANDS == k, tile, four)
-                two = jnp.where(spot[back] // 4 % BANDS == k, tile, two)
-            fours.append(four)
-            twos.append(two)
-        four = jnp.where(lane < GROUP, fours[0], jnp.where(lane < 2 * GROUP, fours[1], fours[2]))
-        two = jnp.where(
-            spot[back] < GROUP, twos[0], jnp.where(spot[back] < 2 * GROUP, twos[1], twos[2])
-        )
-        four = jnp.where(lane < TILES * GROUP, four, 0.0)
-        wide[RANK[j]] = four
-        two = turn(two, 2 * half - aside)
+        wide[RANK[j]] = jnp.where(lane < TILES * GROUP, four_ref[j], 0.0)
+        two = turn(two_ref[j], 2 * half - aside[back])
         if half:
             narrow[HALF + RANK[j] // 2] = jnp.where(lane % 4 < 2, held[back], two)
         else:
@@ -466,8 +462,8 @@
 
 
 def source_kernel(first, *refs):
-    scal_ref, table_ref, x_ref, spec_ref, drive_ref, land_ref, rows_ref = refs[:7]
-    refs = refs[7:]
+    table_ref, x_ref, spec_ref, land_ref, rows_ref = refs[:5]
+    refs = refs[5:]
     freq = lax.axis_index("freq")
     bands = x_ref.shape[0]
 
@@ -499,7 +495,6 @@
     at_edge = {True: lane < 2, False: lane >= WIDTH - 2}
 
     def band(k, carry):
-        extra = (freq * bands + k) * STRIDE + 6 * ND
         for r in range(TILES):
             rows = tile_rows(r)
             held, sea = held_and_sea(r, land_ref, rows_ref)
@@ -517,16 +512,33 @@
                         x = jnp.maximum(x * free, spec_ref[k, j, r])
                     p_ref[k, j, r] = x
                     p[j] = x
-            slope = tree(p)
-            stress = tree([p[j] * drive_ref[j, r] for j in range(ND)])
-            sums_ref[SLOPE_AT + r] += slope * scal_ref[extra + 2]
-            sums_ref[STRESS_AT + r] += stress * scal_ref[extra + 3]
             for j, excess in enumerate(excess_of(p)):
                 excess_ref[k, j, r] = excess
                 sums_ref[TILES * j + r] += excess
         return carry
 
     lax.fori_loop(0, bands, band, 0)
+
+
+def weights_kernel(scal_ref, p_ref, drive_ref, out_ref):
+    bands = p_ref.shape[0]
+    for i in range(2 * TILES):
+        out_ref[i] = jnp.zeros((8, WIDTH), jnp.float32)
+
+    def band(k, carry):
+        extra = (lax.axis_index("freq") * bands + k) * STRIDE + 6 * ND
+        for r in range(TILES):
+            p = [p_ref[k, j, r] for j in range(ND)]
+            out_ref[r] += tree(p) * scal_ref[extra + 2]
+            out_ref[TILES + r] += tree([p[j] * drive_ref[j, r] for j in range(ND)]) * scal_ref[extra + 3]
+        return carry
+
+    lax.fori_loop(0, bands, band, 0)
+
+
+def add_kernel(one_ref, other_ref, out_ref):
+    for i in range(out_ref.shape[0]):
+        out_ref[i] = one_ref[i] + other_ref[i]
 
 
 def local_kernel(last, scal_ref, p_ref, excess_ref, *refs):
@@ -567,7 +579,7 @@
     for i in range(HALF_TILES):
         out_ref[i] = sums_ref[first + i] + other_ref[first + i]
     for i in range(out_ref.shape[0] - HALF_TILES):
-        out_ref[HALF_TILES + i] = sums_ref[SLOPE_AT + i] + other_ref[SLOPE_AT + i]
+        out_ref[HALF_TILES + i] = sums_ref[PACKED_AT + i] + other_ref[PACKED_AT + i]
 
 
 def damp_and_gain(slope, stress, ice):
@@ -576,20 +588,16 @@
 
 
 def grow_half(half, last, near, refs):
-    scal_ref, part_ref, sums_ref, other_ref, mine_ref, lower_ref = refs[:6]
-    drive_ref, land_ref, out_ref, rate_ref, near_ref, field_ref, sent = refs[6:]
+    scal_ref, part_ref, other_ref, lower_ref, pair_ref, rest_ref, drive_ref, land_ref = refs[:8]
+    out_ref, rate_ref, near_ref, field_ref, written_ref, sent = refs[8:]
     bands = part_ref.shape[0]
     freq = lax.axis_index("freq")
     odd = jnp.where(freq % 2 == 1, 1.0, 0.0)
     upper = jnp.where(freq >= 2, 1.0, 0.0)
-    after = SLOPE_AT - HALF_TILES
     for r in range(TILES):
         rows = tile_rows(r)
         ice = jnp.where(land_ref[rows, :] == 2, 1.0, 0.0)
-        slope, stress = (
-            (sums_ref[at + r] + other_ref[at + r]) + mine_ref[at + r - after]
-            for at in (SLOPE_AT, STRESS_AT)
-        )
+        slope, stress = (pair_ref[at + r] + rest_ref[at + r] for at in (0, TILES))
         damp, gain = damp_and_gain(slope, stress, ice)
         for i in range(HALF):
             j = half * HALF + i
@@ -600,8 +608,8 @@
     target_ref = out_ref if near else field_ref
 
     def send(k, mine):
-        source, which = (field_ref, half) if mine else (near_ref, 1 - half)
-        place = out_ref.at[k, pl.ds(which * HALF, HALF)]
+        source, which = (target_ref, half) if mine else (near_ref, 1 - half)
+        place = written_ref.at[k, pl.ds(which * HALF, HALF)]
         return pltpu.make_async_copy(source.at[k], place, sent.at[int(mine), k])
 
     def band(k, carry):
@@ -616,41 +624,52 @@
             else:
                 for r, tile in enumerate(drift(j, base, tiles, scal_ref, inside)):
                     out_ref[k, j, r] = tile
-        if last and not near:
-            send(k, True).start()
         return carry
 
-    write = last and not near
-    if write:
-        for k in range(bands):
+    def sent_band(k, carry):
+        band(k, carry)
+        send(k, True).start()
+        return carry
+
+    early = EARLY if near else bands
+    if not last:
+        lax.fori_loop(0, bands, band, 0)
+        return
+    if not near:
+        for k in range(EARLY, bands):
             send(k, False).start()
-    lax.fori_loop(0, bands, band, 0)
-    if write:
-        for k in range(bands):
+    lax.fori_loop(0, early, sent_band, 0)
+    lax.fori_loop(early, bands, band, 0)
+    for k in range(early):
+        send(k, True).wait()
+    if not near:
+        for k in range(EARLY, bands):
             send(k, False).wait()
-            send(k, True).wait()
+
+
+EARLY = 4
 
 
 def growth_kernel(last, near, *refs):
     operands, refs = refs[:8], refs[8:]
-    scal_ref, part_ref, sums_ref, other_ref, mine_ref = operands[:5]
+    other_ref, mine_ref, pair_ref, rest_ref = operands[2:6]
     freq = lax.axis_index("freq")
-    rest = (None,) * 3
     if near and last:
-        out_ref, slope_out_ref, rate_ref, slope_ref, slope_sent = refs
+        half_ref, slope_out_ref, written_ref, rate_ref, slope_ref, slope_sent, sent = refs
+        results = (half_ref, rate_ref, None, None, written_ref, sent)
         for r in range(TILES):
-            at = SLOPE_AT + r
-            total = (sums_ref[at] + other_ref[at]) + mine_ref[at - SLOPE_AT + HALF_TILES]
-            slope_ref[tile_rows(r), :] = total
+            slope_ref[tile_rows(r), :] = pair_ref[r] + rest_ref[r]
         slope_copy = pltpu.make_async_copy(slope_ref, slope_out_ref, slope_sent)
         slope_copy.start()
     elif near:
-        table_ref, packed_part_ref, packed_drive_ref, ice_ref, out_ref, columns_ref, rate_ref = refs
+        table_ref, sums_ref, packed_part_ref, packed_drive_ref, ice_ref = refs[:5]
+        out_ref, columns_ref, rate_ref = refs[5:]
+        results = (out_ref, rate_ref, None, None, None, None)
         odd = jnp.where(freq % 2 == 1, 1.0, 0.0)
         upper = jnp.where(freq >= 2, 1.0, 0.0)
         total, lower = [], []
         for i in range(PACKED_SUMS):
-            here, there = PACKED_AT + i, HALF_TILES + 2 * TILES + i
+            here, there = PACKED_AT + i, HALF_TILES + i
             total.append((sums_ref[here] + other_ref[here]) + mine_ref[there])
             lower.append(odd * other_ref[here] + upper * mine_ref[there])
         slope, stress = (spread(total[i // BANDS], i % BANDS) for i in (ND, ND + 1))
@@ -660,14 +679,17 @@
             under = spread(lower[j // BANDS], j % BANDS)
             rate = gain * packed_drive_ref[j] - damp - LOWER * under
             columns_ref[j] = packed_part_ref[j] * jnp.exp(root * rate)
+    elif last:
+        half_ref, _, out_ref, rate_ref, field_ref, sent = refs
+        results = (out_ref, rate_ref, half_ref, field_ref, out_ref, sent)
     else:
-        before_ref, out_ref, rate_ref, *rest = refs
-        rest = (before_ref, *rest) if last else (None,) * 3
+        _, out_ref, rate_ref = refs
+        results = (out_ref, rate_ref, None, None, None, None)
     for half in range(2):
 
         @pl.when(freq % 2 == (half if near else 1 - half))
         def _():
-            grow_half(half, last, near, operands + (out_ref, rate_ref, *rest))
+            grow_half(half, last, near, operands + results)
 
     if near and last:
         slope_copy.wait()
@@ -714,7 +736,7 @@
         out_shape=[field, tiles(SENT), tiles(SENT)]
         + [jax.ShapeDtypeStruct(x.shape, x.dtype) for x in arguments[1:]]
         + [tiles(SENT), tiles(SENT)],
-        scratch_shapes=[pltpu.SemaphoreType.DMA((ND // CHUNK + 4,))],
+        scratch_shapes=[pltpu.SemaphoreType.DMA((bands + 4,)), packed, packed],
         compiler_params=params,
         cost_estimate=cost(whole, 6, 2),
         name="pack_columns",
@@ -731,16 +753,15 @@
         name="drift",
     )(scalars, spectrum, east_wind, north_wind, land_sea)
 
-    fields = [drive, land_sea]
     for step in range(STEPS):
         first, last = step == 0, step == STEPS - 1
         sums = PACKED_AT + (PACKED_SUMS if first else 0)
-        half_sums = sums - SLOPE_AT + HALF_TILES
-        operands = [scalars, table, drifted, spectrum if first else kept, *fields, edge_rows]
+        half_sums = sums - PACKED_AT + HALF_TILES
+        operands = [table, drifted, spectrum if first else kept, land_sea, edge_rows]
         operands += [right, left, even, odd] if first else [columns]
         p, excess, mine, *packed_state = pl.pallas_call(
             functools.partial(source_kernel, first),
-            in_specs=[smem] + [vmem] * (len(operands) - 1),
+            in_specs=[vmem] * len(operands),
             out_specs=[vmem] * (6 if first else 3),
             out_shape=[spread_field, spread_field, tiles(sums)]
             + ([tiles(ND), tiles(ND), tile] if first else []),
@@ -761,7 +782,18 @@
             name="pair_sums",
         )(mine, other)
         near = lax.ppermute(pair, "freq", swap_chip)
-        excess, _ = lax.optimization_barrier((excess, pair))
+        p, _ = lax.optimization_barrier((p, pair))
+        weights = pl.pallas_call(
+            weights_kernel,
+            in_specs=[smem] + [vmem] * 2,
+            out_specs=vmem,
+            out_shape=tiles(2 * TILES),
+            compiler_params=params,
+            cost_estimate=cost(whole, 3, 1),
+            name="slope_and_stress",
+        )(scalars, p, drive)
+        p, excess, weights = lax.optimization_barrier((p, excess, weights))
+        weights_other = lax.ppermute(weights, "freq", swap_core)
         operands = [scalars, p, excess] + ([] if last else [spectrum, land_sea, edge_rows])
         part, *kept = pl.pallas_call(
             functools.partial(local_kernel, last),
@@ -773,37 +805,50 @@
             name="local_rate",
         )(*operands)
         kept = None if last else kept[0]
-        near, part = lax.optimization_barrier((near, part))
+        weights_other, part = lax.optimization_barrier((weights_other, part))
+        weights_pair = pl.pallas_call(
+            add_kernel,
+            in_specs=[vmem] * 2,
+            out_specs=vmem,
+            out_shape=tiles(2 * TILES),
+            compiler_params=params,
+            cost_estimate=cost(2 * TILES, 1, 3),
+            name="pair_slope_and_stress",
+        )(weights, weights_other)
+        weights_rest = lax.ppermute(weights_pair, "freq", swap_chip)
+        near, weights_rest = lax.optimization_barrier((near, weights_rest))
         far = lax.ppermute(near, "freq", swap_core)
 
-        near_half = jax.ShapeDtypeStruct((bands, HALF, LAT, WIDTH), f32)
-
-        def grow(is_near, operands, shapes):
-            write = last and not is_near
-            scratch = [pltpu.VMEM((HALF, TILES, 8, WIDTH), f32)]
-            if write:
-                scratch += [pltpu.VMEM(near_half.shape, f32), pltpu.SemaphoreType.DMA((2, bands))]
-            elif last:
-                scratch += [pltpu.VMEM(plane.shape, f32), pltpu.SemaphoreType.DMA(())]
-            alias = not last and not is_near
+        common = [weights_pair, weights_rest, drive, land_sea]
+        half_rate = pltpu.VMEM((HALF, TILES, 8, WIDTH), f32)
+        half_field = (bands, HALF, LAT, WIDTH)
+        sent = pltpu.SemaphoreType.DMA((2, bands))
+
+        def grow(is_near, lower, extra, specs, results, shapes, scratch, alias):
+            operands = [scalars, part, other, lower, *common, *extra]
             return pl.pallas_call(
                 functools.partial(growth_kernel, last, is_near),
-                in_specs=[smem] + [vmem] * (len(operands) - 1),
-                out_specs=[hbm] if write else [vmem, hbm if last else vmem][: len(shapes)],
+                in_specs=[smem] + [vmem] * (len(operands) - 1 - len(specs)) + specs,
+                out_specs=results,
                 out_shape=shapes,
                 input_output_aliases={len(operands) - 1: 0} if alias else {},
-                scratch_shapes=scratch,
+                scratch_shapes=[half_rate] + scratch,
                 compiler_params=params,
                 cost_estimate=cost(whole, 6 if last else 12, 1),
                 name="grow_near" if is_near else "grow_far",
             )(*operands)
 
-        operands = [scalars, part, mine, other, near]
-        extra = [] if last else [table, *packed_state]
-        shapes = [near_half, plane] if last else [spread_field, tiles(ND)]
-        made, columns = grow(True, operands + [near, *fields, *extra], shapes)
-        shapes = [field if last else spread_field]
-        (drifted,) = grow(False, operands + [far, *fields, made], shapes)
+        if last:
+            shapes = [jax.ShapeDtypeStruct(half_field, f32), plane, field]
+            scratch = [pltpu.VMEM(plane.shape, f32), pltpu.SemaphoreType.DMA(()), sent]
+            made, columns, written = grow(True, near, [], [], [vmem, hbm, hbm], shapes, scratch, False)
+            scratch = [pltpu.VMEM(half_field, f32), sent]
+            (drifted,) = grow(False, far, [made, written], [hbm], [hbm], [field], scratch, True)
+        else:
+            shapes = [spread_field, tiles(ND)]
+            extra = [table, mine, *packed_state]
+            made, columns = grow(True, near, extra, [], [vmem] * 2, shapes, [], False)
+            (drifted,) = grow(False, far, [made], [], [vmem], [spread_field], [], True)
     return drifted, columns
 
 

time: 56.8 us -> 55.1 us (0.970)
  waiting for transfers between devices: 11.9 us -> 9.23 us
  starting transfers between devices: 10.4 us -> 11.8 us
    ppermute x2, waiting for transfers between devices: 8.31 us -> 0.01 us  [per_device(): near = lax.ppermute(pair, 'freq', swap_chip)]
    ppermute x0 -> x4, waiting for transfers between devices: none -> 5.7 us  [the longest x2 5.7 us: per_device(): weights_rest = lax.ppermute(weights_pair, 'freq', swap_chip)]
    ppermute x0 -> x4, starting transfers between devices: none -> 2.37 us  [the longest x2 2.16 us: per_device(): weights_rest = lax.ppermute(weights_pair, 'freq', swap_chip)]
    ppermute x2, starting transfers between devices: 3.18 us -> 2.17 us  [per_device(): near = lax.ppermute(pair, 'freq', swap_chip)]
    pallas_call x1, Pallas kernels: 3.54 us -> 2.77 us  [per_device(): pl.pallas_call(pack_kernel, in_specs=[hbm] * 5, out_specs=[vmem] * 9, out...]
    pallas_call x2 -> x6, Pallas kernels: 10.6 us -> 10.8 us  [the longest x2 7.86 us: per_device(): pl.pallas_call(functools.partial(source_kernel, first), in_specs=[vmem] *...]
  transfers between devices with their start and end apart: 8 -> 12, of which waited for: 5 -> 5; matrix products, arithmetic and copies ran while one was open for 0% -> 0% of each run, Pallas kernels for 24% -> 31%
where the time goes in v8:
time: 55.1 us; the launch traced here: 54.9 us
  Pallas kernels  33.1 us (60%)
  starting transfers between devices  11.8 us (21%)
  waiting for transfers between devices  9.23 us (17%)
  between operations  0.81 us (1%)
    pallas_call x4, Pallas kernels, grow(): pl.pallas_call(functools.partial(growth_kernel, last, is_near), in_specs=...  10.7 us
    pallas_call x2, Pallas kernels, per_device(): pl.pallas_call(functools.partial(source_kernel, first), in_specs=[vmem] *...  7.86 us
    ppermute x2, waiting for transfers between devices, per_device(): weights_rest = lax.ppermute(weights_pair, 'freq', swap_chip)  5.7 us
    pallas_call x2, Pallas kernels, per_device(): pl.pallas_call(functools.partial(local_kernel, last), in_specs=[smem] + [...  5.19 us
    pallas_call x1, Pallas kernels, per_device(): pl.pallas_call(drift_kernel, in_specs=[smem] + [vmem] * 4, out_specs=[vme...  3.61 us
    ppermute x1, starting transfers between devices, per_device(): odd = lax.ppermute(odd, 'lon', swap_odd)  3.57 us
    ppermute x2, waiting for transfers between devices, per_device(): other = lax.ppermute(mine, 'freq', swap_core)  3.23 us
    ppermute x1, starting transfers between devices, per_device(): even = lax.ppermute(even, 'lon', swap_even)  3 us
  transfers between devices with their start and end apart: 12, of which 5 were waited for; matrix products, arithmetic and copies ran while one was open for 0% of the time, Pallas kernels for 31%

profile of v8, /device:TPU:0, one launch (start us, length us, event | category | flops | bytes accessed | tf_op | source)
XLA Modules:
  0.0 54.9 jit_solution(3142309090054966733)
XLA Ops:
  0.6 0.0 copy-start
  0.6 0.0 copy-start.1
  0.7 2.8 %pack_columns.1 = (f32[8,36,24,128]{3,2,1,0:T(8,128)S(1)}, f32[28,8,128]{2,1,0:T(8,128)S(1)}, f32[28,8,128]{2,1,0:T(8,128)S(1)}, f32[24,128]{1,0:T(8,128)S(1)}, ...) custom-call(f32[8,36,24,128]{3,2,1,0:T(8,128)} %spec_ref.1, ...), custom_call_target="tpu_custom_call" | custom-call | flops 5308416 | bytes 7077888 | tf_op jit(solution)/shard_map/pack_columns/pallas_call | solution.py:732
  3.4 3.0 %collective-permute-start = (f32[28,8,128]{2,1,0:T(8,128)S(1)}, f32[28,8,128]{2,1,0:T(8,128)S(1)}, u32[]{:S(2)}, u32[]{:S(2)}) collective-permute-start(f32[28,8,128]{2,1,0:T(8,128)S(1)} %get-tuple-element.53), channel_id=1, source_target_pairs={{0,4},{4,0},{8,12},{12,8},{16,20},{20,16},{24,28},{28,24},{1,5},{5... | collective-permute-start | bytes 344072 | tf_op jit(solution)/shard_map/ppermute | solution.py:744
  6.4 3.6 %collective-permute-start.1 = (f32[28,8,128]{2,1,0:T(8,128)S(1)}, f32[28,8,128]{2,1,0:T(8,128)S(1)}, u32[]{:S(2)}, u32[]{:S(2)}) collective-permute-start(f32[28,8,128]{2,1,0:T(8,128)S(1)} %get-tuple-element.54), channel_id=1, source_target_pairs={{0,28},{4,8},{8,4},{12,16},{16,12},{20,24},{24,20},{28,0},{1,29},{... | collective-permute-start | bytes 344072 | tf_op jit(solution)/shard_map/ppermute | solution.py:745
  10.0 3.6 %drift.1 = (f32[8,36,3,8,128]{4,3,2,1,0:T(8,128)S(1)}, f32[36,3,8,128]{3,2,1,0:T(8,128)S(1)}) custom-call(f32[7168]{0:T(1024)S(1)} %copy-done, f32[8,36,24,128]{3,2,1,0:T(8,128)S(1)} %get-tuple-element.45.q_ref.refs_2_.refs_0_, f32[24,128]{1,0:T(8,128)S(1)} %get-tuple-element.46.east_ref, f32[24,128]{1,0:T(8,128)S(1)} %get-tuple-element.47.north_ref, ...), custom_call_target="tpu_custom_call" | custom-call | flops 10616832 | bytes 7077888 | tf_op jit(solution)/shard_map/drift/pallas_call | solution.py:746
  13.6 0.3 collective-permute-done.1.refs_8_
  13.9 4.6 %sources.2 = (f32[8,36,3,8,128]{4,3,2,1,0:T(8,128)S(1)}, f32[8,36,3,8,128]{4,3,2,1,0:T(8,128)S(1)}, f32[113,8,128]{2,1,0:T(8,128)S(1)}, f32[36,8,128]{2,1,0:T(8,...) custom-call(f32[4,6,8,128]{3,2,1,0:T(8,128)S(1)} %copy-done.1, ...), custom_call_target="tpu_custom_call" | custom-call | flops 26542080 | bytes 10616832 | tf_op jit(solution)/shard_map/sources/pallas_call | solution.py:762
  18.6 0.1 collective-permute-start.2
  18.7 1.8 %collective-permute-done.2.other_ref.refs_2_ = f32[113,8,128]{2,1,0:T(8,128)S(1)} collective-permute-done((f32[113,8,128]{2,1,0:T(8,128)S(1)}, f32[113,8,128]{2,1,0:T(8,128)S(1)}, u32[]{:S(2)}, u32[]{:S(2)}) %collective-permute-start.2) | collective-permute-done | bytes 462880 | tf_op jit(solution)/shard_map/ppermute | solution.py:774
  20.5 1.6 %collective-permute-start.4 = (f32[59,8,128]{2,1,0:T(8,128)S(1)}, f32[59,8,128]{2,1,0:T(8,128)S(1)}, u32[]{:S(2)}, u32[]{:S(2)}) collective-permute-start(f32[59,8,128]{2,1,0:T(8,128)S(1)} %pair_sums.2), channel_id=1, source_target_pairs={{0,2},{2,0},{1,3},{3,1},{4,6},{6,4},{5,7},{7,5},{8,10},{10,8},{9,1... | collective-permute-start | bytes 725000 | tf_op jit(solution)/shard_map/ppermute | solution.py:784
  22.1 1.4 %slope_and_stress.2.one_ref = f32[6,8,128]{2,1,0:T(8,128)S(1)} custom-call(f32[7168]{0:T(1024)S(1)} %copy-done, f32[8,36,3,8,128]{4,3,2,1,0:T(8,128)S(1)} %get-tuple-element.61.p_ref, f32[36,3,8,128]{3,2,1,0:T(8,128)S(1)} %get-tuple-element.59.drive_ref.refs_6_), custom_call_target="tpu_custom_call" | custom-call | flops 2654208 | bytes 3538944 | tf_op jit(solution)/shard_map/slope_and_stress/pallas_call | solution.py:786
  23.5 0.1 collective-permute-start.3
  23.6 3.1 %local_rate.2 = (f32[8,36,3,8,128]{4,3,2,1,0:T(8,128)S(1)}, f32[8,36,3,8,128]{4,3,2,1,0:T(8,128)S(1)}) custom-call(f32[7168]{0:T(1024)S(1)} %copy-done, f32[8,36,3,8,128]{4,3,2,1,0:T(8,128)S(1)} %get-tuple-element.61.p_ref, f32[8,36,3,8,128]{4,3,2,1,0:T(8,128)S(1)} %get-tuple-element.62.excess_ref, ...), custom_call_target="tpu_custom_call" | custom-call | flops 7077888 | bytes 10616832 | tf_op jit(solution)/shard_map/local_rate/pallas_call | solution.py:798
  26.7 0.0 collective-permute-done.3.other_ref
  26.7 0.6 %collective-permute-start.5 = (f32[6,8,128]{2,1,0:T(8,128)S(1)}, f32[6,8,128]{2,1,0:T(8,128)S(1)}, u32[]{:S(2)}, u32[]{:S(2)}) collective-permute-start(f32[6,8,128]{2,1,0:T(8,128)S(1)} %pair_slope_and_stress.2.refs_4_), channel_id=1, source_target_pairs={{0,2},{2,0},{1,3},{3,1},{4,6},{6,4},{5,7},{7,5},{8,10},{10,8},{9,1... | collective-permute-start | bytes 73736 | tf_op jit(solution)/shard_map/ppermute | solution.py:818
  27.3 3.3 %collective-permute-done.5.refs_5_ = f32[6,8,128]{2,1,0:T(8,128)S(1)} collective-permute-done((f32[6,8,128]{2,1,0:T(8,128)S(1)}, f32[6,8,128]{2,1,0:T(8,128)S(1)}, u32[]{:S(2)}, u32[]{:S(2)}) %collective-permute-start.5) | collective-permute-done | bytes 24608 | tf_op jit(solution)/shard_map/ppermute | solution.py:818
  30.6 3.1 %grow_near.2 = (f32[8,36,3,8,128]{4,3,2,1,0:T(8,128)S(1)}, f32[36,8,128]{2,1,0:T(8,128)S(1)}) custom-call(f32[7168]{0:T(1024)S(1)} %copy-done, f32[8,36,3,8,128]{4,3,2,1,0:T(8,128)S(1)} %get-tuple-element.64.refs_1_, f32[113,8,128]{2,1,0:T(8,128)S(1)} %collective-permute-done.2.other_ref.refs_2_, f32[59,8,128]{2,1,0:T(8,128)S(1)} %collective-permute-done.4.refs_3_, ...), custom_call_target="tpu_custom_call" | custom-call | flops 10616832 | bytes 3538944 | tf_op jit(solution)/shard_map/grow_near/pallas_call | solution.py:829
  33.7 2.8 %grow_far.2.refs_1_ = f32[8,36,3,8,128]{4,3,2,1,0:T(8,128)S(1)} custom-call(f32[7168]{0:T(1024)S(1)} %copy-done, f32[8,36,3,8,128]{4,3,2,1,0:T(8,128)S(1)} %get-tuple-element.64.refs_1_, f32[113,8,128]{2,1,0:T(8,128)S(1)} %collective-permute-done.2.other_ref.refs_2_, ...), custom_call_target="tpu_custom_call", output_to_operand_aliasing={{}: (8, {})} | custom-call | flops 10616832 | bytes 3538944 | tf_op jit(solution)/shard_map/grow_far/pallas_call | solution.py:829
  36.5 3.2 %sources.3 = (f32[8,36,3,8,128]{4,3,2,1,0:T(8,128)S(1)}, f32[8,36,3,8,128]{4,3,2,1,0:T(8,128)S(1)}, f32[108,8,128]{2,1,0:T(8,128)S(1)}) custom-call(f32[4,6,8,128]{3,2,1,0:T(8,128)S(1)} %copy-done.1, f32[8,36,3,8,128]{4,3,2,1,0:T(8,128)S(1)} %grow_far.2.refs_1_, f32[8,36,3,8,128]{4,3,2,1,0:T(8,128)S(1)} %get-tuple-element.72.refs_2_, ...), custom_call_target="tpu_custom_call" | custom-call | flops 26542080 | bytes 10616832 | tf_op jit(solution)/shard_map/sources/pallas_call | solution.py:762
  39.7 0.6 %collective-permute-start.7 = (f32[108,8,128]{2,1,0:T(8,128)S(1)}, f32[108,8,128]{2,1,0:T(8,128)S(1)}, u32[]{:S(2)}, u32[]{:S(2)}) collective-permute-start(f32[108,8,128]{2,1,0:T(8,128)S(1)} %get-tuple-element.75.sums_ref), channel_id=1, source_target_pairs={{0,1},{1,0},{2,3},{3,2},{4,5},{5,4},{6,7},{7,6},{8,9},{9,8},{10,11... | collective-permute-start | bytes 1327112 | tf_op jit(solution)/shard_map/ppermute | solution.py:774
  40.3 1.4 %collective-permute-done.7.other_ref.refs_2_ = f32[108,8,128]{2,1,0:T(8,128)S(1)} collective-permute-done((f32[108,8,128]{2,1,0:T(8,128)S(1)}, f32[108,8,128]{2,1,0:T(8,128)S(1)}, u32[]{:S(2)}, u32[]{:S(2)}) %collective-permute-start.7) | collective-permute-done | bytes 442400 | tf_op jit(solution)/shard_map/ppermute | solution.py:774
  41.7 0.6 %collective-permute-start.9 = (f32[54,8,128]{2,1,0:T(8,128)S(1)}, f32[54,8,128]{2,1,0:T(8,128)S(1)}, u32[]{:S(2)}, u32[]{:S(2)}) collective-permute-start(f32[54,8,128]{2,1,0:T(8,128)S(1)} %pair_sums.3), channel_id=1, source_target_pairs={{0,2},{2,0},{1,3},{3,1},{4,6},{6,4},{5,7},{7,5},{8,10},{10,8},{9,1... | collective-permute-start | bytes 663560 | tf_op jit(solution)/shard_map/ppermute | solution.py:784
  42.3 1.5 %slope_and_stress.3.one_ref = f32[6,8,128]{2,1,0:T(8,128)S(1)} custom-call(f32[7168]{0:T(1024)S(1)} %copy-done, f32[8,36,3,8,128]{4,3,2,1,0:T(8,128)S(1)} %get-tuple-element.79.p_ref, f32[36,3,8,128]{3,2,1,0:T(8,128)S(1)} %get-tuple-element.59.drive_ref.refs_6_), custom_call_target="tpu_custom_call" | custom-call | flops 2654208 | bytes 3538944 | tf_op jit(solution)/shard_map/slope_and_stress/pallas_call | solution.py:786
  43.8 0.1 collective-permute-start.8
  43.9 2.1 %local_rate.3.refs_1_ = f32[8,36,3,8,128]{4,3,2,1,0:T(8,128)S(1)} custom-call(f32[7168]{0:T(1024)S(1)} %copy-done, f32[8,36,3,8,128]{4,3,2,1,0:T(8,128)S(1)} %get-tuple-element.79.p_ref, f32[8,36,3,8,128]{4,3,2,1,0:T(8,128)S(1)} %get-tuple-element.80.excess_ref), custom_call_target="tpu_custom_call" | custom-call | flops 7077888 | bytes 10616832 | tf_op jit(solution)/shard_map/local_rate/pallas_call | solution.py:798
  46.1 0.0 collective-permute-done.8.other_ref
  46.1 1.6 %collective-permute-start.10 = (f32[6,8,128]{2,1,0:T(8,128)S(1)}, f32[6,8,128]{2,1,0:T(8,128)S(1)}, u32[]{:S(2)}, u32[]{:S(2)}) collective-permute-start(f32[6,8,128]{2,1,0:T(8,128)S(1)} %pair_slope_and_stress.3.refs_4_), channel_id=1, source_target_pairs={{0,2},{2,0},{1,3},{3,1},{4,6},{6,4},{5,7},{7,5},{8,10},{10,8},{9,1... | collective-permute-start | bytes 73736 | tf_op jit(solution)/shard_map/ppermute | solution.py:818
  47.7 2.4 %collective-permute-done.10.refs_5_ = f32[6,8,128]{2,1,0:T(8,128)S(1)} collective-permute-done((f32[6,8,128]{2,1,0:T(8,128)S(1)}, f32[6,8,128]{2,1,0:T(8,128)S(1)}, u32[]{:S(2)}, u32[]{:S(2)}) %collective-permute-start.10) | collective-permute-done | bytes 24608 | tf_op jit(solution)/shard_map/ppermute | solution.py:818
  50.0 0.0 collective-permute-done.9.refs_3_
  50.1 2.2 %grow_near.3 = (f32[8,18,24,128]{3,2,1,0:T(8,128)S(1)}, f32[24,128]{1,0:T(8,128)}, f32[8,36,24,128]{3,2,1,0:T(8,128)}) custom-call(f32[7168]{0:T(1024)S(1)} %copy-done, f32[8,36,3,8,128]{4,3,2,1,0:T(8,128)S(1)} %local_rate.3.refs_1_, f32[108,8,128]{2,1,0:T(8,128)S(1)} %collective-permute-done.7.other_ref.refs_2_, ...), custom_call_target="tpu_custom_call" | custom-call | flops 5308416 | bytes 3538944 | tf_op jit(solution)/shard_map/grow_near/pallas_call | solution.py:829
  52.3 2.7 %grow_far.3 = f32[8,36,24,128]{3,2,1,0:T(8,128)} custom-call(f32[7168]{0:T(1024)S(1)} %copy-done, f32[8,36,3,8,128]{4,3,2,1,0:T(8,128)S(1)} %local_rate.3.refs_1_, f32[108,8,128]{2,1,0:T(8,128)S(1)} %collective-permute-done.7.other_ref.refs_2_, f32[54,8,128]{2,1,0:T(8,128)S(1)} %collective-permute-done.11.refs_3_, ...), custom_call_target="tpu_custom_call", output_to_operand_aliasing={{}: (9, {})} | custom-call | flops 5308416 | bytes 3538944 | tf_op jit(solution)/shard_map/grow_far/pallas_call | solution.py:829
  (12 shorter events, 0.1 us)
Async XLA Ops:
  0.6 9.4 %copy-start = (f32[7168]{0:T(1024)S(1)}, f32[7168]{0:T(1024)}, u32[]{:S(2)}) copy-start(f32[7168]{0:T(1024)} %constant.4.clone.scal_ref.refs_0_) | copy-start | bytes 86020
  0.6 13.3 %copy-start.1 = (f32[4,6,8,128]{3,2,1,0:T(8,128)S(1)}, f32[4,6,8,128]{3,2,1,0:T(8,128)}, u32[]{:S(2)}) copy-start(f32[4,6,8,128]{3,2,1,0:T(8,128)} %constant.5.clone.refs_0_.refs_8_) | copy-start | bytes 294916
  3.4 10.2 %collective-permute-start = (f32[28,8,128]{2,1,0:T(8,128)S(1)}, f32[28,8,128]{2,1,0:T(8,128)S(1)}, u32[]{:S(2)}, u32[]{:S(2)}) collective-permute-start(f32[28,8,128]{2,1,0:T(8,128)S(1)} %get-tuple-element.53), channel_id=1, source_target_pairs={{0,4},{4,0},{8,12},{12,8},{16,20},{20,16},{24,28},{28,24},{1,5},{5... | collective-permute-start | bytes 344072 | tf_op jit(solution)/shard_map/ppermute | solution.py:744
  6.4 7.5 %collective-permute-start.1 = (f32[28,8,128]{2,1,0:T(8,128)S(1)}, f32[28,8,128]{2,1,0:T(8,128)S(1)}, u32[]{:S(2)}, u32[]{:S(2)}) collective-permute-start(f32[28,8,128]{2,1,0:T(8,128)S(1)} %get-tuple-element.54), channel_id=1, source_target_pairs={{0,28},{4,8},{8,4},{12,16},{16,12},{20,24},{24,20},{28,0},{1,29},{... | collective-permute-start | bytes 344072 | tf_op jit(solution)/shard_map/ppermute | solution.py:745
  18.6 1.9 %collective-permute-start.2 = (f32[113,8,128]{2,1,0:T(8,128)S(1)}, f32[113,8,128]{2,1,0:T(8,128)S(1)}, u32[]{:S(2)}, u32[]{:S(2)}) collective-permute-start(f32[113,8,128]{2,1,0:T(8,128)S(1)} %get-tuple-element.56.sums_ref.refs_9_), channel_id=1, source_target_pairs={{0,1},{1,0},{2,3},{3,2},{4,5},{5,4},{6,7},{7,6},{8,9},{9,8},{10,11... | collective-permute-start | bytes 1388552 | tf_op jit(solution)/shard_map/ppermute | solution.py:774
  20.5 10.1 %collective-permute-start.4 = (f32[59,8,128]{2,1,0:T(8,128)S(1)}, f32[59,8,128]{2,1,0:T(8,128)S(1)}, u32[]{:S(2)}, u32[]{:S(2)}) collective-permute-start(f32[59,8,128]{2,1,0:T(8,128)S(1)} %pair_sums.2), channel_id=1, source_target_pairs={{0,2},{2,0},{1,3},{3,1},{4,6},{6,4},{5,7},{7,5},{8,10},{10,8},{9,1... | collective-permute-start | bytes 725000 | tf_op jit(solution)/shard_map/ppermute | solution.py:784
  23.5 3.2 %collective-permute-start.3 = (f32[6,8,128]{2,1,0:T(8,128)S(1)}, f32[6,8,128]{2,1,0:T(8,128)S(1)}, u32[]{:S(2)}, u32[]{:S(2)}) collective-permute-start(f32[6,8,128]{2,1,0:T(8,128)S(1)} %slope_and_stress.2.one_ref), channel_id=1, source_target_pairs={{0,1},{1,0},{2,3},{3,2},{4,5},{5,4},{6,7},{7,6},{8,9},{9,8},{10,11... | collective-permute-start | bytes 73736 | tf_op jit(solution)/shard_map/ppermute | solution.py:796
  26.7 3.9 %collective-permute-start.5 = (f32[6,8,128]{2,1,0:T(8,128)S(1)}, f32[6,8,128]{2,1,0:T(8,128)S(1)}, u32[]{:S(2)}, u32[]{:S(2)}) collective-permute-start(f32[6,8,128]{2,1,0:T(8,128)S(1)} %pair_slope_and_stress.2.refs_4_), channel_id=1, source_target_pairs={{0,2},{2,0},{1,3},{3,1},{4,6},{6,4},{5,7},{7,5},{8,10},{10,8},{9,1... | collective-permute-start | bytes 73736 | tf_op jit(solution)/shard_map/ppermute | solution.py:818
  30.6 3.1 %collective-permute-start.6 = (f32[59,8,128]{2,1,0:T(8,128)S(1)}, f32[59,8,128]{2,1,0:T(8,128)S(1)}, u32[]{:S(2)}, u32[]{:S(2)}) collective-permute-start(f32[59,8,128]{2,1,0:T(8,128)S(1)} %collective-permute-done.4.refs_3_), channel_id=1, source_target_pairs={{0,1},{1,0},{2,3},{3,2},{4,5},{5,4},{6,7},{7,6},{8,9},{9,8},{10,11... | collective-permute-start | bytes 725000 | tf_op jit(solution)/shard_map/ppermute | solution.py:820
  39.7 2.0 %collective-permute-start.7 = (f32[108,8,128]{2,1,0:T(8,128)S(1)}, f32[108,8,128]{2,1,0:T(8,128)S(1)}, u32[]{:S(2)}, u32[]{:S(2)}) collective-permute-start(f32[108,8,128]{2,1,0:T(8,128)S(1)} %get-tuple-element.75.sums_ref), channel_id=1, source_target_pairs={{0,1},{1,0},{2,3},{3,2},{4,5},{5,4},{6,7},{7,6},{8,9},{9,8},{10,11... | collective-permute-start | bytes 1327112 | tf_op jit(solution)/shard_map/ppermute | solution.py:774
  41.7 8.3 %collective-permute-start.9 = (f32[54,8,128]{2,1,0:T(8,128)S(1)}, f32[54,8,128]{2,1,0:T(8,128)S(1)}, u32[]{:S(2)}, u32[]{:S(2)}) collective-permute-start(f32[54,8,128]{2,1,0:T(8,128)S(1)} %pair_sums.3), channel_id=1, source_target_pairs={{0,2},{2,0},{1,3},{3,1},{4,6},{6,4},{5,7},{7,5},{8,10},{10,8},{9,1... | collective-permute-start | bytes 663560 | tf_op jit(solution)/shard_map/ppermute | solution.py:784
  43.8 2.3 %collective-permute-start.8 = (f32[6,8,128]{2,1,0:T(8,128)S(1)}, f32[6,8,128]{2,1,0:T(8,128)S(1)}, u32[]{:S(2)}, u32[]{:S(2)}) collective-permute-start(f32[6,8,128]{2,1,0:T(8,128)S(1)} %slope_and_stress.3.one_ref), channel_id=1, source_target_pairs={{0,1},{1,0},{2,3},{3,2},{4,5},{5,4},{6,7},{7,6},{8,9},{9,8},{10,11... | collective-permute-start | bytes 73736 | tf_op jit(solution)/shard_map/ppermute | solution.py:796
  46.1 4.0 %collective-permute-start.10 = (f32[6,8,128]{2,1,0:T(8,128)S(1)}, f32[6,8,128]{2,1,0:T(8,128)S(1)}, u32[]{:S(2)}, u32[]{:S(2)}) collective-permute-start(f32[6,8,128]{2,1,0:T(8,128)S(1)} %pair_slope_and_stress.3.refs_4_), channel_id=1, source_target_pairs={{0,2},{2,0},{1,3},{3,1},{4,6},{6,4},{5,7},{7,5},{8,10},{10,8},{9,1... | collective-permute-start | bytes 73736 | tf_op jit(solution)/shard_map/ppermute | solution.py:818
  50.1 2.2 %collective-permute-start.11 = (f32[54,8,128]{2,1,0:T(8,128)S(1)}, f32[54,8,128]{2,1,0:T(8,128)S(1)}, u32[]{:S(2)}, u32[]{:S(2)}) collective-permute-start(f32[54,8,128]{2,1,0:T(8,128)S(1)} %collective-permute-done.9.refs_3_), channel_id=1, source_target_pairs={{0,1},{1,0},{2,3},{3,2},{4,5},{5,4},{6,7},{7,6},{8,9},{9,8},{10,11... | collective-permute-start | bytes 663560 | tf_op jit(solution)/shard_map/ppermute | solution.py:820

commit v9 on v8

--- a/solution.py
+++ b/solution.py
@@ -647,7 +647,7 @@
             send(k, False).wait()
 
 
-EARLY = 4
+EARLY = 1
 
 
 def growth_kernel(last, near, *refs):
@@ -772,6 +772,17 @@
             name="sources",
         )(*operands)
         other = lax.ppermute(mine, "freq", swap_core)
+        weights = pl.pallas_call(
+            weights_kernel,
+            in_specs=[smem] + [vmem] * 2,
+            out_specs=vmem,
+            out_shape=tiles(2 * TILES),
+            compiler_params=params,
+            cost_estimate=cost(whole, 3, 1),
+            name="slope_and_stress",
+        )(scalars, p, drive)
+        other, weights = lax.optimization_barrier((other, weights))
+        weights_other = lax.ppermute(weights, "freq", swap_core)
         pair = pl.pallas_call(
             pair_kernel,
             in_specs=[vmem] * 2,
@@ -782,18 +793,18 @@
             name="pair_sums",
         )(mine, other)
         near = lax.ppermute(pair, "freq", swap_chip)
-        p, _ = lax.optimization_barrier((p, pair))
-        weights = pl.pallas_call(
-            weights_kernel,
-            in_specs=[smem] + [vmem] * 2,
+        weights_other, _ = lax.optimization_barrier((weights_other, pair))
+        weights_pair = pl.pallas_call(
+            add_kernel,
+            in_specs=[vmem] * 2,
             out_specs=vmem,
             out_shape=tiles(2 * TILES),
             compiler_params=params,
-            cost_estimate=cost(whole, 3, 1),
-            name="slope_and_stress",
-        )(scalars, p, drive)
-        p, excess, weights = lax.optimization_barrier((p, excess, weights))
-        weights_other = lax.ppermute(weights, "freq", swap_core)
+            cost_estimate=cost(2 * TILES, 1, 3),
+            name="pair_slope_and_stress",
+        )(weights, weights_other)
+        weights_rest = lax.ppermute(weights_pair, "freq", swap_chip)
+        excess, _ = lax.optimization_barrier((excess, weights_pair))
         operands = [scalars, p, excess] + ([] if last else [spectrum, land_sea, edge_rows])
         part, *kept = pl.pallas_call(
             functools.partial(local_kernel, last),
@@ -805,18 +816,7 @@
             name="local_rate",
         )(*operands)
         kept = None if last else kept[0]
-        weights_other, part = lax.optimization_barrier((weights_other, part))
-        weights_pair = pl.pallas_call(
-            add_kernel,
-            in_specs=[vmem] * 2,
-            out_specs=vmem,
-            out_shape=tiles(2 * TILES),
-            compiler_params=params,
-            cost_estimate=cost(2 * TILES, 1, 3),
-            name="pair_slope_and_stress",
-        )(weights, weights_other)
-        weights_rest = lax.ppermute(weights_pair, "freq", swap_chip)
-        near, weights_rest = lax.optimization_barrier((near, weights_rest))
+        near, weights_rest, part = lax.optimization_barrier((near, weights_rest, part))
         far = lax.ppermute(near, "freq", swap_core)
 
         common = [weights_pair, weights_rest, drive, land_sea]

time: 55.1 us -> 53.5 us (0.971)
  waiting for transfers between devices: 9.23 us -> 7.99 us
    ppermute x2, waiting for transfers between devices: 3.23 us -> 0.36 us  [per_device(): other = lax.ppermute(mine, 'freq', swap_core)]
    ppermute x2, waiting for transfers between devices: 0.01 us -> 2.35 us  [per_device(): weights_other = lax.ppermute(weights, 'freq', swap_core)]
    ppermute x2, starting transfers between devices: 2.16 us -> 1.01 us  [per_device(): weights_rest = lax.ppermute(weights_pair, 'freq', swap_chip)]
    ppermute x2, starting transfers between devices: 2.17 us -> 3.17 us  [per_device(): near = lax.ppermute(pair, 'freq', swap_chip)]
    ppermute x2, waiting for transfers between devices: 5.7 us -> 4.97 us  [per_device(): weights_rest = lax.ppermute(weights_pair, 'freq', swap_chip)]
  transfers between devices with their start and end apart: 12 -> 12, of which waited for: 5 -> 6; matrix products, arithmetic and copies ran while one was open for 0% -> 0% of each run, Pallas kernels for 31% -> 31%
where the time goes in v9:
time: 53.5 us; the launch traced here: 53.3 us
  Pallas kernels  33.1 us (62%)
  starting transfers between devices  11.5 us (21%)
  waiting for transfers between devices  7.99 us (15%)
  between operations  0.78 us (1%)
    pallas_call x4, Pallas kernels, grow(): pl.pallas_call(functools.partial(growth_kernel, last, is_near), in_specs=...  10.7 us
    pallas_call x2, Pallas kernels, per_device(): pl.pallas_call(functools.partial(source_kernel, first), in_specs=[vmem] *...  7.86 us
    pallas_call x2, Pallas kernels, per_device(): pl.pallas_call(functools.partial(local_kernel, last), in_specs=[smem] + [...  5.18 us
    ppermute x2, waiting for transfers between devices, per_device(): weights_rest = lax.ppermute(weights_pair, 'freq', swap_chip)  4.97 us
    pallas_call x1, Pallas kernels, per_device(): pl.pallas_call(drift_kernel, in_specs=[smem] + [vmem] * 4, out_specs=[vme...  3.61 us
    ppermute x1, starting transfers between devices, per_device(): odd = lax.ppermute(odd, 'lon', swap_odd)  3.57 us
    ppermute x2, starting transfers between devices, per_device(): near = lax.ppermute(pair, 'freq', swap_chip)  3.17 us
    ppermute x1, starting transfers between devices, per_device(): even = lax.ppermute(even, 'lon', swap_even)  3 us
  transfers between devices with their start and end apart: 12, of which 6 were waited for; matrix products, arithmetic and copies ran while one was open for 0% of the time, Pallas kernels for 31%

profile of v9, /device:TPU:0, one launch (start us, length us, event | category | flops | bytes accessed | tf_op | source)
XLA Modules:
  0.0 53.3 jit_solution(18316207596392166634)
XLA Ops:
  0.6 0.0 copy-start
  0.6 0.0 copy-start.1
  0.7 2.8 %pack_columns.1 = (f32[8,36,24,128]{3,2,1,0:T(8,128)S(1)}, f32[28,8,128]{2,1,0:T(8,128)S(1)}, f32[28,8,128]{2,1,0:T(8,128)S(1)}, f32[24,128]{1,0:T(8,128)S(1)}, ...) custom-call(f32[8,36,24,128]{3,2,1,0:T(8,128)} %spec_ref.1, ...), custom_call_target="tpu_custom_call" | custom-call | flops 5308416 | bytes 7077888 | tf_op jit(solution)/shard_map/pack_columns/pallas_call | solution.py:732
  3.4 3.0 %collective-permute-start = (f32[28,8,128]{2,1,0:T(8,128)S(1)}, f32[28,8,128]{2,1,0:T(8,128)S(1)}, u32[]{:S(2)}, u32[]{:S(2)}) collective-permute-start(f32[28,8,128]{2,1,0:T(8,128)S(1)} %get-tuple-element.51), channel_id=1, source_target_pairs={{0,4},{4,0},{8,12},{12,8},{16,20},{20,16},{24,28},{28,24},{1,5},{5... | collective-permute-start | bytes 344072 | tf_op jit(solution)/shard_map/ppermute | solution.py:744
  6.4 3.6 %collective-permute-start.1 = (f32[28,8,128]{2,1,0:T(8,128)S(1)}, f32[28,8,128]{2,1,0:T(8,128)S(1)}, u32[]{:S(2)}, u32[]{:S(2)}) collective-permute-start(f32[28,8,128]{2,1,0:T(8,128)S(1)} %get-tuple-element.52), channel_id=1, source_target_pairs={{0,28},{4,8},{8,4},{12,16},{16,12},{20,24},{24,20},{28,0},{1,29},{... | collective-permute-start | bytes 344072 | tf_op jit(solution)/shard_map/ppermute | solution.py:745
  10.0 3.6 %drift.1 = (f32[8,36,3,8,128]{4,3,2,1,0:T(8,128)S(1)}, f32[36,3,8,128]{3,2,1,0:T(8,128)S(1)}) custom-call(f32[7168]{0:T(1024)S(1)} %copy-done, f32[8,36,24,128]{3,2,1,0:T(8,128)S(1)} %get-tuple-element.43.q_ref.refs_2_.refs_0_, f32[24,128]{1,0:T(8,128)S(1)} %get-tuple-element.44.east_ref, f32[24,128]{1,0:T(8,128)S(1)} %get-tuple-element.45.north_ref, ...), custom_call_target="tpu_custom_call" | custom-call | flops 10616832 | bytes 7077888 | tf_op jit(solution)/shard_map/drift/pallas_call | solution.py:746
  13.6 0.3 collective-permute-done.1.refs_8_
  13.9 4.6 %sources.2 = (f32[8,36,3,8,128]{4,3,2,1,0:T(8,128)S(1)}, f32[8,36,3,8,128]{4,3,2,1,0:T(8,128)S(1)}, f32[113,8,128]{2,1,0:T(8,128)S(1)}, f32[36,8,128]{2,1,0:T(8,...) custom-call(f32[4,6,8,128]{3,2,1,0:T(8,128)S(1)} %copy-done.1, ...), custom_call_target="tpu_custom_call" | custom-call | flops 26542080 | bytes 10616832 | tf_op jit(solution)/shard_map/sources/pallas_call | solution.py:762
  18.6 0.1 collective-permute-start.2
  18.7 1.4 %slope_and_stress.2.one_ref = f32[6,8,128]{2,1,0:T(8,128)S(1)} custom-call(f32[7168]{0:T(1024)S(1)} %copy-done, f32[8,36,3,8,128]{4,3,2,1,0:T(8,128)S(1)} %get-tuple-element.54.p_ref, f32[36,3,8,128]{3,2,1,0:T(8,128)S(1)} %get-tuple-element.55.drive_ref.refs_6_), custom_call_target="tpu_custom_call" | custom-call | flops 2654208 | bytes 3538944 | tf_op jit(solution)/shard_map/slope_and_stress/pallas_call | solution.py:775
  20.1 0.4 collective-permute-done.2.other_ref.refs_2_
  20.5 1.6 %collective-permute-start.3 = (f32[59,8,128]{2,1,0:T(8,128)S(1)}, f32[59,8,128]{2,1,0:T(8,128)S(1)}, u32[]{:S(2)}, u32[]{:S(2)}) collective-permute-start(f32[59,8,128]{2,1,0:T(8,128)S(1)} %pair_sums.2), channel_id=1, source_target_pairs={{0,2},{2,0},{1,3},{3,1},{4,6},{6,4},{5,7},{7,5},{8,10},{10,8},{9,1... | collective-permute-start | bytes 725000 | tf_op jit(solution)/shard_map/ppermute | solution.py:795
  22.1 0.0 collective-permute-start.4
  22.1 1.2 %collective-permute-done.4.other_ref = f32[6,8,128]{2,1,0:T(8,128)S(1)} collective-permute-done((f32[6,8,128]{2,1,0:T(8,128)S(1)}, f32[6,8,128]{2,1,0:T(8,128)S(1)}, u32[]{:S(2)}, u32[]{:S(2)}) %collective-permute-start.4) | collective-permute-done | bytes 24608 | tf_op jit(solution)/shard_map/ppermute | solution.py:785
  23.3 0.5 collective-permute-start.5
  23.8 3.1 %local_rate.2 = (f32[8,36,3,8,128]{4,3,2,1,0:T(8,128)S(1)}, f32[8,36,3,8,128]{4,3,2,1,0:T(8,128)S(1)}) custom-call(f32[7168]{0:T(1024)S(1)} %copy-done, f32[8,36,3,8,128]{4,3,2,1,0:T(8,128)S(1)} %get-tuple-element.54.p_ref, f32[8,36,3,8,128]{4,3,2,1,0:T(8,128)S(1)} %get-tuple-element.60.excess_ref, ...), custom_call_target="tpu_custom_call" | custom-call | flops 7077888 | bytes 10616832 | tf_op jit(solution)/shard_map/local_rate/pallas_call | solution.py:809
  26.9 2.1 %collective-permute-done.5.refs_5_ = f32[6,8,128]{2,1,0:T(8,128)S(1)} collective-permute-done((f32[6,8,128]{2,1,0:T(8,128)S(1)}, f32[6,8,128]{2,1,0:T(8,128)S(1)}, u32[]{:S(2)}, u32[]{:S(2)}) %collective-permute-start.5) | collective-permute-done | bytes 24608 | tf_op jit(solution)/shard_map/ppermute | solution.py:806
  29.0 0.0 collective-permute-done.3.refs_3_
  29.0 0.0 collective-permute-start.6
  29.0 3.1 %grow_near.2 = (f32[8,36,3,8,128]{4,3,2,1,0:T(8,128)S(1)}, f32[36,8,128]{2,1,0:T(8,128)S(1)}) custom-call(f32[7168]{0:T(1024)S(1)} %copy-done, f32[8,36,3,8,128]{4,3,2,1,0:T(8,128)S(1)} %get-tuple-element.62.refs_1_, f32[113,8,128]{2,1,0:T(8,128)S(1)} %collective-permute-done.2.other_ref.refs_2_, f32[59,8,128]{2,1,0:T(8,128)S(1)} %collective-permute-done.3.refs_3_, ...), custom_call_target="tpu_custom_call" | custom-call | flops 10616832 | bytes 3538944 | tf_op jit(solution)/shard_map/grow_near/pallas_call | solution.py:829
  32.1 2.8 %grow_far.2.refs_1_ = f32[8,36,3,8,128]{4,3,2,1,0:T(8,128)S(1)} custom-call(f32[7168]{0:T(1024)S(1)} %copy-done, f32[8,36,3,8,128]{4,3,2,1,0:T(8,128)S(1)} %get-tuple-element.62.refs_1_, f32[113,8,128]{2,1,0:T(8,128)S(1)} %collective-permute-done.2.other_ref.refs_2_, ...), custom_call_target="tpu_custom_call", output_to_operand_aliasing={{}: (8, {})} | custom-call | flops 10616832 | bytes 3538944 | tf_op jit(solution)/shard_map/grow_far/pallas_call | solution.py:829
  34.9 3.2 %sources.3 = (f32[8,36,3,8,128]{4,3,2,1,0:T(8,128)S(1)}, f32[8,36,3,8,128]{4,3,2,1,0:T(8,128)S(1)}, f32[108,8,128]{2,1,0:T(8,128)S(1)}) custom-call(f32[4,6,8,128]{3,2,1,0:T(8,128)S(1)} %copy-done.1, f32[8,36,3,8,128]{4,3,2,1,0:T(8,128)S(1)} %grow_far.2.refs_1_, f32[8,36,3,8,128]{4,3,2,1,0:T(8,128)S(1)} %get-tuple-element.69.refs_2_, ...), custom_call_target="tpu_custom_call" | custom-call | flops 26542080 | bytes 10616832 | tf_op jit(solution)/shard_map/sources/pallas_call | solution.py:762
  38.1 0.6 %collective-permute-start.7 = (f32[108,8,128]{2,1,0:T(8,128)S(1)}, f32[108,8,128]{2,1,0:T(8,128)S(1)}, u32[]{:S(2)}, u32[]{:S(2)}) collective-permute-start(f32[108,8,128]{2,1,0:T(8,128)S(1)} %get-tuple-element.71.sums_ref), channel_id=1, source_target_pairs={{0,1},{1,0},{2,3},{3,2},{4,5},{5,4},{6,7},{7,6},{8,9},{9,8},{10,11... | collective-permute-start | bytes 1327112 | tf_op jit(solution)/shard_map/ppermute | solution.py:774
  38.7 1.5 %slope_and_stress.3.one_ref = f32[6,8,128]{2,1,0:T(8,128)S(1)} custom-call(f32[7168]{0:T(1024)S(1)} %copy-done, f32[8,36,3,8,128]{4,3,2,1,0:T(8,128)S(1)} %get-tuple-element.72.p_ref, f32[36,3,8,128]{3,2,1,0:T(8,128)S(1)} %get-tuple-element.55.drive_ref.refs_6_), custom_call_target="tpu_custom_call" | custom-call | flops 2654208 | bytes 3538944 | tf_op jit(solution)/shard_map/slope_and_stress/pallas_call | solution.py:775
  40.2 1.6 %collective-permute-start.8 = (f32[54,8,128]{2,1,0:T(8,128)S(1)}, f32[54,8,128]{2,1,0:T(8,128)S(1)}, u32[]{:S(2)}, u32[]{:S(2)}) collective-permute-start(f32[54,8,128]{2,1,0:T(8,128)S(1)} %pair_sums.3), channel_id=1, source_target_pairs={{0,2},{2,0},{1,3},{3,1},{4,6},{6,4},{5,7},{7,5},{8,10},{10,8},{9,1... | collective-permute-start | bytes 663560 | tf_op jit(solution)/shard_map/ppermute | solution.py:795
  41.8 0.0 collective-permute-start.9
  41.8 1.2 %collective-permute-done.9.other_ref = f32[6,8,128]{2,1,0:T(8,128)S(1)} collective-permute-done((f32[6,8,128]{2,1,0:T(8,128)S(1)}, f32[6,8,128]{2,1,0:T(8,128)S(1)}, u32[]{:S(2)}, u32[]{:S(2)}) %collective-permute-start.9) | collective-permute-done | bytes 24608 | tf_op jit(solution)/shard_map/ppermute | solution.py:785
  43.0 0.5 collective-permute-start.10
  43.5 2.1 %local_rate.3.refs_1_ = f32[8,36,3,8,128]{4,3,2,1,0:T(8,128)S(1)} custom-call(f32[7168]{0:T(1024)S(1)} %copy-done, f32[8,36,3,8,128]{4,3,2,1,0:T(8,128)S(1)} %get-tuple-element.72.p_ref, f32[8,36,3,8,128]{4,3,2,1,0:T(8,128)S(1)} %get-tuple-element.77.excess_ref), custom_call_target="tpu_custom_call" | custom-call | flops 7077888 | bytes 10616832 | tf_op jit(solution)/shard_map/local_rate/pallas_call | solution.py:809
  45.6 2.8 %collective-permute-done.10.refs_5_ = f32[6,8,128]{2,1,0:T(8,128)S(1)} collective-permute-done((f32[6,8,128]{2,1,0:T(8,128)S(1)}, f32[6,8,128]{2,1,0:T(8,128)S(1)}, u32[]{:S(2)}, u32[]{:S(2)}) %collective-permute-start.10) | collective-permute-done | bytes 24608 | tf_op jit(solution)/shard_map/ppermute | solution.py:806
  48.5 2.0 %grow_near.3 = (f32[8,18,24,128]{3,2,1,0:T(8,128)S(1)}, f32[24,128]{1,0:T(8,128)}, f32[8,36,24,128]{3,2,1,0:T(8,128)}) custom-call(f32[7168]{0:T(1024)S(1)} %copy-done, f32[8,36,3,8,128]{4,3,2,1,0:T(8,128)S(1)} %local_rate.3.refs_1_, f32[108,8,128]{2,1,0:T(8,128)S(1)} %collective-permute-done.7.other_ref.refs_2_, ...), custom_call_target="tpu_custom_call" | custom-call | flops 5308416 | bytes 3538944 | tf_op jit(solution)/shard_map/grow_near/pallas_call | solution.py:829
  50.4 2.9 %grow_far.3 = f32[8,36,24,128]{3,2,1,0:T(8,128)} custom-call(f32[7168]{0:T(1024)S(1)} %copy-done, f32[8,36,3,8,128]{4,3,2,1,0:T(8,128)S(1)} %local_rate.3.refs_1_, f32[108,8,128]{2,1,0:T(8,128)S(1)} %collective-permute-done.7.other_ref.refs_2_, f32[54,8,128]{2,1,0:T(8,128)S(1)} %collective-permute-done.11.refs_3_, ...), custom_call_target="tpu_custom_call", output_to_operand_aliasing={{}: (9, {})} | custom-call | flops 5308416 | bytes 3538944 | tf_op jit(solution)/shard_map/grow_far/pallas_call | solution.py:829
  (12 shorter events, 0.1 us)
Async XLA Ops:
  0.6 9.4 %copy-start = (f32[7168]{0:T(1024)S(1)}, f32[7168]{0:T(1024)}, u32[]{:S(2)}) copy-start(f32[7168]{0:T(1024)} %constant.4.clone.scal_ref.refs_0_) | copy-start | bytes 86020
  0.6 13.3 %copy-start.1 = (f32[4,6,8,128]{3,2,1,0:T(8,128)S(1)}, f32[4,6,8,128]{3,2,1,0:T(8,128)}, u32[]{:S(2)}) copy-start(f32[4,6,8,128]{3,2,1,0:T(8,128)} %constant.5.clone.refs_0_.refs_8_) | copy-start | bytes 294916
  3.4 10.2 %collective-permute-start = (f32[28,8,128]{2,1,0:T(8,128)S(1)}, f32[28,8,128]{2,1,0:T(8,128)S(1)}, u32[]{:S(2)}, u32[]{:S(2)}) collective-permute-start(f32[28,8,128]{2,1,0:T(8,128)S(1)} %get-tuple-element.51), channel_id=1, source_target_pairs={{0,4},{4,0},{8,12},{12,8},{16,20},{20,16},{24,28},{28,24},{1,5},{5... | collective-permute-start | bytes 344072 | tf_op jit(solution)/shard_map/ppermute | solution.py:744
  6.4 7.5 %collective-permute-start.1 = (f32[28,8,128]{2,1,0:T(8,128)S(1)}, f32[28,8,128]{2,1,0:T(8,128)S(1)}, u32[]{:S(2)}, u32[]{:S(2)}) collective-permute-start(f32[28,8,128]{2,1,0:T(8,128)S(1)} %get-tuple-element.52), channel_id=1, source_target_pairs={{0,28},{4,8},{8,4},{12,16},{16,12},{20,24},{24,20},{28,0},{1,29},{... | collective-permute-start | bytes 344072 | tf_op jit(solution)/shard_map/ppermute | solution.py:745
  18.6 1.9 %collective-permute-start.2 = (f32[113,8,128]{2,1,0:T(8,128)S(1)}, f32[113,8,128]{2,1,0:T(8,128)S(1)}, u32[]{:S(2)}, u32[]{:S(2)}) collective-permute-start(f32[113,8,128]{2,1,0:T(8,128)S(1)} %get-tuple-element.53.sums_ref.refs_9_), channel_id=1, source_target_pairs={{0,1},{1,0},{2,3},{3,2},{4,5},{5,4},{6,7},{7,6},{8,9},{9,8},{10,11... | collective-permute-start | bytes 1388552 | tf_op jit(solution)/shard_map/ppermute | solution.py:774
  20.5 8.5 %collective-permute-start.3 = (f32[59,8,128]{2,1,0:T(8,128)S(1)}, f32[59,8,128]{2,1,0:T(8,128)S(1)}, u32[]{:S(2)}, u32[]{:S(2)}) collective-permute-start(f32[59,8,128]{2,1,0:T(8,128)S(1)} %pair_sums.2), channel_id=1, source_target_pairs={{0,2},{2,0},{1,3},{3,1},{4,6},{6,4},{5,7},{7,5},{8,10},{10,8},{9,1... | collective-permute-start | bytes 725000 | tf_op jit(solution)/shard_map/ppermute | solution.py:795
  22.1 1.2 %collective-permute-start.4 = (f32[6,8,128]{2,1,0:T(8,128)S(1)}, f32[6,8,128]{2,1,0:T(8,128)S(1)}, u32[]{:S(2)}, u32[]{:S(2)}) collective-permute-start(f32[6,8,128]{2,1,0:T(8,128)S(1)} %slope_and_stress.2.one_ref), channel_id=1, source_target_pairs={{0,1},{1,0},{2,3},{3,2},{4,5},{5,4},{6,7},{7,6},{8,9},{9,8},{10,11... | collective-permute-start | bytes 73736 | tf_op jit(solution)/shard_map/ppermute | solution.py:785
  23.3 5.7 %collective-permute-start.5 = (f32[6,8,128]{2,1,0:T(8,128)S(1)}, f32[6,8,128]{2,1,0:T(8,128)S(1)}, u32[]{:S(2)}, u32[]{:S(2)}) collective-permute-start(f32[6,8,128]{2,1,0:T(8,128)S(1)} %pair_slope_and_stress.2.refs_4_), channel_id=1, source_target_pairs={{0,2},{2,0},{1,3},{3,1},{4,6},{6,4},{5,7},{7,5},{8,10},{10,8},{9,1... | collective-permute-start | bytes 73736 | tf_op jit(solution)/shard_map/ppermute | solution.py:806
  29.0 3.1 %collective-permute-start.6 = (f32[59,8,128]{2,1,0:T(8,128)S(1)}, f32[59,8,128]{2,1,0:T(8,128)S(1)}, u32[]{:S(2)}, u32[]{:S(2)}) collective-permute-start(f32[59,8,128]{2,1,0:T(8,128)S(1)} %collective-permute-done.3.refs_3_), channel_id=1, source_target_pairs={{0,1},{1,0},{2,3},{3,2},{4,5},{5,4},{6,7},{7,6},{8,9},{9,8},{10,11... | collective-permute-start | bytes 725000 | tf_op jit(solution)/shard_map/ppermute | solution.py:820
  38.1 2.0 %collective-permute-start.7 = (f32[108,8,128]{2,1,0:T(8,128)S(1)}, f32[108,8,128]{2,1,0:T(8,128)S(1)}, u32[]{:S(2)}, u32[]{:S(2)}) collective-permute-start(f32[108,8,128]{2,1,0:T(8,128)S(1)} %get-tuple-element.71.sums_ref), channel_id=1, source_target_pairs={{0,1},{1,0},{2,3},{3,2},{4,5},{5,4},{6,7},{7,6},{8,9},{9,8},{10,11... | collective-permute-start | bytes 1327112 | tf_op jit(solution)/shard_map/ppermute | solution.py:774
  40.2 8.2 %collective-permute-start.8 = (f32[54,8,128]{2,1,0:T(8,128)S(1)}, f32[54,8,128]{2,1,0:T(8,128)S(1)}, u32[]{:S(2)}, u32[]{:S(2)}) collective-permute-start(f32[54,8,128]{2,1,0:T(8,128)S(1)} %pair_sums.3), channel_id=1, source_target_pairs={{0,2},{2,0},{1,3},{3,1},{4,6},{6,4},{5,7},{7,5},{8,10},{10,8},{9,1... | collective-permute-start | bytes 663560 | tf_op jit(solution)/shard_map/ppermute | solution.py:795
  41.8 1.2 %collective-permute-start.9 = (f32[6,8,128]{2,1,0:T(8,128)S(1)}, f32[6,8,128]{2,1,0:T(8,128)S(1)}, u32[]{:S(2)}, u32[]{:S(2)}) collective-permute-start(f32[6,8,128]{2,1,0:T(8,128)S(1)} %slope_and_stress.3.one_ref), channel_id=1, source_target_pairs={{0,1},{1,0},{2,3},{3,2},{4,5},{5,4},{6,7},{7,6},{8,9},{9,8},{10,11... | collective-permute-start | bytes 73736 | tf_op jit(solution)/shard_map/ppermute | solution.py:785
  43.0 5.5 %collective-permute-start.10 = (f32[6,8,128]{2,1,0:T(8,128)S(1)}, f32[6,8,128]{2,1,0:T(8,128)S(1)}, u32[]{:S(2)}, u32[]{:S(2)}) collective-permute-start(f32[6,8,128]{2,1,0:T(8,128)S(1)} %pair_slope_and_stress.3.refs_4_), channel_id=1, source_target_pairs={{0,2},{2,0},{1,3},{3,1},{4,6},{6,4},{5,7},{7,5},{8,10},{10,8},{9,1... | collective-permute-start | bytes 73736 | tf_op jit(solution)/shard_map/ppermute | solution.py:806
  48.5 2.0 %collective-permute-start.11 = (f32[54,8,128]{2,1,0:T(8,128)S(1)}, f32[54,8,128]{2,1,0:T(8,128)S(1)}, u32[]{:S(2)}, u32[]{:S(2)}) collective-permute-start(f32[54,8,128]{2,1,0:T(8,128)S(1)} %collective-permute-done.8.refs_3_), channel_id=1, source_target_pairs={{0,1},{1,0},{2,3},{3,2},{4,5},{5,4},{6,7},{7,6},{8,9},{9,8},{10,11... | collective-permute-start | bytes 663560 | tf_op jit(solution)/shard_map/ppermute | solution.py:820

commit v10 on v9

--- a/solution.py
+++ b/solution.py
@@ -410,7 +410,7 @@
     ice = jnp.where(land > 1.5, 1.0, 0.0)
     ice_ref[...] = ice
     inverse = table(5)
-    p, stress = [], []
+    p, slope, stress = [], [None] * 4, [None] * 4
     for j in range(ND):
         lon = packed_coefficients(inverse, COURANT_MAX * COS[j])
         lat = packed_coefficients(inverse, 0.5 * COURANT_MAX * SIN[j])
@@ -420,8 +420,10 @@
         p.append(jnp.where(held, centre, jnp.maximum(x, 0.0)) * sea)
         drive = drive_of(j, east, north, 1.0 - ice)
         drive_ref[j] = drive
-        stress.append(p[j] * drive)
-    slope, stress = tree(p), tree(stress)
+        push = p[j] * drive
+        slope[j % 4] = p[j] if j < 4 else slope[j % 4] + p[j]
+        stress[j % 4] = push if j < 4 else stress[j % 4] + push
+    slope, stress = tree(slope), tree(stress)
 
     def running(tile):
         for step in (1, 2, 4):
@@ -528,9 +530,14 @@
     def band(k, carry):
         extra = (lax.axis_index("freq") * bands + k) * STRIDE + 6 * ND
         for r in range(TILES):
-            p = [p_ref[k, j, r] for j in range(ND)]
-            out_ref[r] += tree(p) * scal_ref[extra + 2]
-            out_ref[TILES + r] += tree([p[j] * drive_ref[j, r] for j in range(ND)]) * scal_ref[extra + 3]
+            slope, stress = [None] * 4, [None] * 4
+            for j in range(ND):
+                p = p_ref[k, j, r]
+                push = p * drive_ref[j, r]
+                slope[j % 4] = p if j < 4 else slope[j % 4] + p
+                stress[j % 4] = push if j < 4 else stress[j % 4] + push
+            out_ref[r] += tree(slope) * scal_ref[extra + 2]
+            out_ref[TILES + r] += tree(stress) * scal_ref[extra + 3]
         return carry
 
     lax.fori_loop(0, bands, band, 0)
@@ -647,7 +654,7 @@
             send(k, False).wait()
 
 
-EARLY = 1
+EARLY = 0
 
 
 def growth_kernel(last, near, *refs):

time: 53.5 us -> 53.4 us (level)
  no operation moved by 1% of the time
where the time goes in v10:
time: 53.4 us; the launch traced here: 53.2 us
  Pallas kernels  33 us (62%)
  starting transfers between devices  11.4 us (21%)
  waiting for transfers between devices  7.98 us (15%)
  between operations  0.78 us (1%)
    pallas_call x4, Pallas kernels, grow(): pl.pallas_call(functools.partial(growth_kernel, last, is_near), in_specs=...  10.6 us
    pallas_call x2, Pallas kernels, per_device(): pl.pallas_call(functools.partial(source_kernel, first), in_specs=[vmem] *...  7.85 us
    pallas_call x2, Pallas kernels, per_device(): pl.pallas_call(functools.partial(local_kernel, last), in_specs=[smem] + [...  5.18 us
    ppermute x2, waiting for transfers between devices, per_device(): weights_rest = lax.ppermute(weights_pair, 'freq', swap_chip)  4.92 us
    pallas_call x1, Pallas kernels, per_device(): pl.pallas_call(drift_kernel, in_specs=[smem] + [vmem] * 4, out_specs=[vme...  3.61 us
    ppermute x1, starting transfers between devices, per_device(): odd = lax.ppermute(odd, 'lon', swap_odd)  3.57 us
    ppermute x2, starting transfers between devices, per_device(): near = lax.ppermute(pair, 'freq', swap_chip)  3.17 us
    ppermute x1, starting transfers between devices, per_device(): even = lax.ppermute(even, 'lon', swap_even)  3 us
  transfers between devices with their start and end apart: 12, of which 6 were waited for; matrix products, arithmetic and copies ran while one was open for 0% of the time, Pallas kernels for 31%

profile of v10, /device:TPU:0, one launch (start us, length us, event | category | flops | bytes accessed | tf_op | source)
XLA Modules:
  0.0 53.2 jit_solution(2915163782941011691)
XLA Ops:
  0.6 0.0 copy-start
  0.6 0.0 copy-start.1
  0.7 2.8 %pack_columns.1 = (f32[8,36,24,128]{3,2,1,0:T(8,128)S(1)}, f32[28,8,128]{2,1,0:T(8,128)S(1)}, f32[28,8,128]{2,1,0:T(8,128)S(1)}, f32[24,128]{1,0:T(8,128)S(1)}, ...) custom-call(f32[8,36,24,128]{3,2,1,0:T(8,128)} %spec_ref.1, ...), custom_call_target="tpu_custom_call" | custom-call | flops 5308416 | bytes 7077888 | tf_op jit(solution)/shard_map/pack_columns/pallas_call | solution.py:739
  3.4 3.0 %collective-permute-start = (f32[28,8,128]{2,1,0:T(8,128)S(1)}, f32[28,8,128]{2,1,0:T(8,128)S(1)}, u32[]{:S(2)}, u32[]{:S(2)}) collective-permute-start(f32[28,8,128]{2,1,0:T(8,128)S(1)} %get-tuple-element.51), channel_id=1, source_target_pairs={{0,4},{4,0},{8,12},{12,8},{16,20},{20,16},{24,28},{28,24},{1,5},{5... | collective-permute-start | bytes 344072 | tf_op jit(solution)/shard_map/ppermute | solution.py:751
  6.4 3.6 %collective-permute-start.1 = (f32[28,8,128]{2,1,0:T(8,128)S(1)}, f32[28,8,128]{2,1,0:T(8,128)S(1)}, u32[]{:S(2)}, u32[]{:S(2)}) collective-permute-start(f32[28,8,128]{2,1,0:T(8,128)S(1)} %get-tuple-element.52), channel_id=1, source_target_pairs={{0,28},{4,8},{8,4},{12,16},{16,12},{20,24},{24,20},{28,0},{1,29},{... | collective-permute-start | bytes 344072 | tf_op jit(solution)/shard_map/ppermute | solution.py:752
  10.0 3.6 %drift.1 = (f32[8,36,3,8,128]{4,3,2,1,0:T(8,128)S(1)}, f32[36,3,8,128]{3,2,1,0:T(8,128)S(1)}) custom-call(f32[7168]{0:T(1024)S(1)} %copy-done, f32[8,36,24,128]{3,2,1,0:T(8,128)S(1)} %get-tuple-element.43.q_ref.refs_2_.refs_0_, f32[24,128]{1,0:T(8,128)S(1)} %get-tuple-element.44.east_ref, f32[24,128]{1,0:T(8,128)S(1)} %get-tuple-element.45.north_ref, ...), custom_call_target="tpu_custom_call" | custom-call | flops 10616832 | bytes 7077888 | tf_op jit(solution)/shard_map/drift/pallas_call | solution.py:753
  13.6 0.0 collective-permute-done.refs_7_
  13.6 0.3 collective-permute-done.1.refs_8_
  13.9 4.6 %sources.2 = (f32[8,36,3,8,128]{4,3,2,1,0:T(8,128)S(1)}, f32[8,36,3,8,128]{4,3,2,1,0:T(8,128)S(1)}, f32[113,8,128]{2,1,0:T(8,128)S(1)}, f32[36,8,128]{2,1,0:T(8,...) custom-call(f32[4,6,8,128]{3,2,1,0:T(8,128)S(1)} %copy-done.1, ...), custom_call_target="tpu_custom_call" | custom-call | flops 26542080 | bytes 10616832 | tf_op jit(solution)/shard_map/sources/pallas_call | solution.py:769
  18.6 0.1 collective-permute-start.2
  18.6 1.4 %slope_and_stress.2.one_ref = f32[6,8,128]{2,1,0:T(8,128)S(1)} custom-call(f32[7168]{0:T(1024)S(1)} %copy-done, f32[8,36,3,8,128]{4,3,2,1,0:T(8,128)S(1)} %get-tuple-element.54.p_ref, f32[36,3,8,128]{3,2,1,0:T(8,128)S(1)} %get-tuple-element.55.drive_ref.refs_6_), custom_call_target="tpu_custom_call" | custom-call | flops 2654208 | bytes 3538944 | tf_op jit(solution)/shard_map/slope_and_stress/pallas_call | solution.py:782
  20.1 0.4 collective-permute-done.2.other_ref.refs_2_
  20.5 1.6 %collective-permute-start.3 = (f32[59,8,128]{2,1,0:T(8,128)S(1)}, f32[59,8,128]{2,1,0:T(8,128)S(1)}, u32[]{:S(2)}, u32[]{:S(2)}) collective-permute-start(f32[59,8,128]{2,1,0:T(8,128)S(1)} %pair_sums.2), channel_id=1, source_target_pairs={{0,2},{2,0},{1,3},{3,1},{4,6},{6,4},{5,7},{7,5},{8,10},{10,8},{9,1... | collective-permute-start | bytes 725000 | tf_op jit(solution)/shard_map/ppermute | solution.py:802
  22.1 0.0 collective-permute-start.4
  22.1 1.2 %collective-permute-done.4.other_ref = f32[6,8,128]{2,1,0:T(8,128)S(1)} collective-permute-done((f32[6,8,128]{2,1,0:T(8,128)S(1)}, f32[6,8,128]{2,1,0:T(8,128)S(1)}, u32[]{:S(2)}, u32[]{:S(2)}) %collective-permute-start.4) | collective-permute-done | bytes 24608 | tf_op jit(solution)/shard_map/ppermute | solution.py:792
  23.3 0.5 collective-permute-start.5
  23.8 3.1 %local_rate.2 = (f32[8,36,3,8,128]{4,3,2,1,0:T(8,128)S(1)}, f32[8,36,3,8,128]{4,3,2,1,0:T(8,128)S(1)}) custom-call(f32[7168]{0:T(1024)S(1)} %copy-done, f32[8,36,3,8,128]{4,3,2,1,0:T(8,128)S(1)} %get-tuple-element.54.p_ref, f32[8,36,3,8,128]{4,3,2,1,0:T(8,128)S(1)} %get-tuple-element.60.excess_ref, ...), custom_call_target="tpu_custom_call" | custom-call | flops 7077888 | bytes 10616832 | tf_op jit(solution)/shard_map/local_rate/pallas_call | solution.py:816
  26.9 2.1 %collective-permute-done.5.refs_5_ = f32[6,8,128]{2,1,0:T(8,128)S(1)} collective-permute-done((f32[6,8,128]{2,1,0:T(8,128)S(1)}, f32[6,8,128]{2,1,0:T(8,128)S(1)}, u32[]{:S(2)}, u32[]{:S(2)}) %collective-permute-start.5) | collective-permute-done | bytes 24608 | tf_op jit(solution)/shard_map/ppermute | solution.py:813
  29.0 0.0 collective-permute-done.3.refs_3_
  29.0 0.0 collective-permute-start.6
  29.0 3.1 %grow_near.2 = (f32[8,36,3,8,128]{4,3,2,1,0:T(8,128)S(1)}, f32[36,8,128]{2,1,0:T(8,128)S(1)}) custom-call(f32[7168]{0:T(1024)S(1)} %copy-done, f32[8,36,3,8,128]{4,3,2,1,0:T(8,128)S(1)} %get-tuple-element.62.refs_1_, f32[113,8,128]{2,1,0:T(8,128)S(1)} %collective-permute-done.2.other_ref.refs_2_, f32[59,8,128]{2,1,0:T(8,128)S(1)} %collective-permute-done.3.refs_3_, ...), custom_call_target="tpu_custom_call" | custom-call | flops 10616832 | bytes 3538944 | tf_op jit(solution)/shard_map/grow_near/pallas_call | solution.py:836
  32.1 2.8 %grow_far.2.refs_1_ = f32[8,36,3,8,128]{4,3,2,1,0:T(8,128)S(1)} custom-call(f32[7168]{0:T(1024)S(1)} %copy-done, f32[8,36,3,8,128]{4,3,2,1,0:T(8,128)S(1)} %get-tuple-element.62.refs_1_, f32[113,8,128]{2,1,0:T(8,128)S(1)} %collective-permute-done.2.other_ref.refs_2_, ...), custom_call_target="tpu_custom_call", output_to_operand_aliasing={{}: (8, {})} | custom-call | flops 10616832 | bytes 3538944 | tf_op jit(solution)/shard_map/grow_far/pallas_call | solution.py:836
  34.9 3.2 %sources.3 = (f32[8,36,3,8,128]{4,3,2,1,0:T(8,128)S(1)}, f32[8,36,3,8,128]{4,3,2,1,0:T(8,128)S(1)}, f32[108,8,128]{2,1,0:T(8,128)S(1)}) custom-call(f32[4,6,8,128]{3,2,1,0:T(8,128)S(1)} %copy-done.1, f32[8,36,3,8,128]{4,3,2,1,0:T(8,128)S(1)} %grow_far.2.refs_1_, f32[8,36,3,8,128]{4,3,2,1,0:T(8,128)S(1)} %get-tuple-element.69.refs_2_, ...), custom_call_target="tpu_custom_call" | custom-call | flops 26542080 | bytes 10616832 | tf_op jit(solution)/shard_map/sources/pallas_call | solution.py:769
  38.1 0.6 %collective-permute-start.7 = (f32[108,8,128]{2,1,0:T(8,128)S(1)}, f32[108,8,128]{2,1,0:T(8,128)S(1)}, u32[]{:S(2)}, u32[]{:S(2)}) collective-permute-start(f32[108,8,128]{2,1,0:T(8,128)S(1)} %get-tuple-element.71.sums_ref), channel_id=1, source_target_pairs={{0,1},{1,0},{2,3},{3,2},{4,5},{5,4},{6,7},{7,6},{8,9},{9,8},{10,11... | collective-permute-start | bytes 1327112 | tf_op jit(solution)/shard_map/ppermute | solution.py:781
  38.7 1.5 %slope_and_stress.3.one_ref = f32[6,8,128]{2,1,0:T(8,128)S(1)} custom-call(f32[7168]{0:T(1024)S(1)} %copy-done, f32[8,36,3,8,128]{4,3,2,1,0:T(8,128)S(1)} %get-tuple-element.72.p_ref, f32[36,3,8,128]{3,2,1,0:T(8,128)S(1)} %get-tuple-element.55.drive_ref.refs_6_), custom_call_target="tpu_custom_call" | custom-call | flops 2654208 | bytes 3538944 | tf_op jit(solution)/shard_map/slope_and_stress/pallas_call | solution.py:782
  40.2 1.6 %collective-permute-start.8 = (f32[54,8,128]{2,1,0:T(8,128)S(1)}, f32[54,8,128]{2,1,0:T(8,128)S(1)}, u32[]{:S(2)}, u32[]{:S(2)}) collective-permute-start(f32[54,8,128]{2,1,0:T(8,128)S(1)} %pair_sums.3), channel_id=1, source_target_pairs={{0,2},{2,0},{1,3},{3,1},{4,6},{6,4},{5,7},{7,5},{8,10},{10,8},{9,1... | collective-permute-start | bytes 663560 | tf_op jit(solution)/shard_map/ppermute | solution.py:802
  41.8 1.2 %collective-permute-done.9.other_ref = f32[6,8,128]{2,1,0:T(8,128)S(1)} collective-permute-done((f32[6,8,128]{2,1,0:T(8,128)S(1)}, f32[6,8,128]{2,1,0:T(8,128)S(1)}, u32[]{:S(2)}, u32[]{:S(2)}) %collective-permute-start.9) | collective-permute-done | bytes 24608 | tf_op jit(solution)/shard_map/ppermute | solution.py:792
  43.0 0.5 collective-permute-start.10
  43.5 2.1 %local_rate.3.refs_1_ = f32[8,36,3,8,128]{4,3,2,1,0:T(8,128)S(1)} custom-call(f32[7168]{0:T(1024)S(1)} %copy-done, f32[8,36,3,8,128]{4,3,2,1,0:T(8,128)S(1)} %get-tuple-element.72.p_ref, f32[8,36,3,8,128]{4,3,2,1,0:T(8,128)S(1)} %get-tuple-element.77.excess_ref), custom_call_target="tpu_custom_call" | custom-call | flops 7077888 | bytes 10616832 | tf_op jit(solution)/shard_map/local_rate/pallas_call | solution.py:816
  45.7 2.8 %collective-permute-done.10.refs_5_ = f32[6,8,128]{2,1,0:T(8,128)S(1)} collective-permute-done((f32[6,8,128]{2,1,0:T(8,128)S(1)}, f32[6,8,128]{2,1,0:T(8,128)S(1)}, u32[]{:S(2)}, u32[]{:S(2)}) %collective-permute-start.10) | collective-permute-done | bytes 24608 | tf_op jit(solution)/shard_map/ppermute | solution.py:813
  48.4 1.8 %grow_near.3 = (f32[8,18,24,128]{3,2,1,0:T(8,128)S(1)}, f32[24,128]{1,0:T(8,128)}, f32[8,36,24,128]{3,2,1,0:T(8,128)}) custom-call(f32[7168]{0:T(1024)S(1)} %copy-done, f32[8,36,3,8,128]{4,3,2,1,0:T(8,128)S(1)} %local_rate.3.refs_1_, f32[108,8,128]{2,1,0:T(8,128)S(1)} %collective-permute-done.7.other_ref.refs_2_, ...), custom_call_target="tpu_custom_call" | custom-call | flops 5308416 | bytes 3538944 | tf_op jit(solution)/shard_map/grow_near/pallas_call | solution.py:836
  50.2 3.0 %grow_far.3 = f32[8,36,24,128]{3,2,1,0:T(8,128)} custom-call(f32[7168]{0:T(1024)S(1)} %copy-done, f32[8,36,3,8,128]{4,3,2,1,0:T(8,128)S(1)} %local_rate.3.refs_1_, f32[108,8,128]{2,1,0:T(8,128)S(1)} %collective-permute-done.7.other_ref.refs_2_, f32[54,8,128]{2,1,0:T(8,128)S(1)} %collective-permute-done.11.refs_3_, ...), custom_call_target="tpu_custom_call", output_to_operand_aliasing={{}: (9, {})} | custom-call | flops 5308416 | bytes 3538944 | tf_op jit(solution)/shard_map/grow_far/pallas_call | solution.py:836
  (12 shorter events, 0.1 us)
Async XLA Ops:
  0.6 9.4 %copy-start = (f32[7168]{0:T(1024)S(1)}, f32[7168]{0:T(1024)}, u32[]{:S(2)}) copy-start(f32[7168]{0:T(1024)} %constant.4.clone.scal_ref.refs_0_) | copy-start | bytes 86020
  0.6 13.3 %copy-start.1 = (f32[4,6,8,128]{3,2,1,0:T(8,128)S(1)}, f32[4,6,8,128]{3,2,1,0:T(8,128)}, u32[]{:S(2)}) copy-start(f32[4,6,8,128]{3,2,1,0:T(8,128)} %constant.5.clone.refs_0_.refs_8_) | copy-start | bytes 294916
  3.4 10.2 %collective-permute-start = (f32[28,8,128]{2,1,0:T(8,128)S(1)}, f32[28,8,128]{2,1,0:T(8,128)S(1)}, u32[]{:S(2)}, u32[]{:S(2)}) collective-permute-start(f32[28,8,128]{2,1,0:T(8,128)S(1)} %get-tuple-element.51), channel_id=1, source_target_pairs={{0,4},{4,0},{8,12},{12,8},{16,20},{20,16},{24,28},{28,24},{1,5},{5... | collective-permute-start | bytes 344072 | tf_op jit(solution)/shard_map/ppermute | solution.py:751
  6.4 7.5 %collective-permute-start.1 = (f32[28,8,128]{2,1,0:T(8,128)S(1)}, f32[28,8,128]{2,1,0:T(8,128)S(1)}, u32[]{:S(2)}, u32[]{:S(2)}) collective-permute-start(f32[28,8,128]{2,1,0:T(8,128)S(1)} %get-tuple-element.52), channel_id=1, source_target_pairs={{0,28},{4,8},{8,4},{12,16},{16,12},{20,24},{24,20},{28,0},{1,29},{... | collective-permute-start | bytes 344072 | tf_op jit(solution)/shard_map/ppermute | solution.py:752
  18.6 1.9 %collective-permute-start.2 = (f32[113,8,128]{2,1,0:T(8,128)S(1)}, f32[113,8,128]{2,1,0:T(8,128)S(1)}, u32[]{:S(2)}, u32[]{:S(2)}) collective-permute-start(f32[113,8,128]{2,1,0:T(8,128)S(1)} %get-tuple-element.53.sums_ref.refs_9_), channel_id=1, source_target_pairs={{0,1},{1,0},{2,3},{3,2},{4,5},{5,4},{6,7},{7,6},{8,9},{9,8},{10,11... | collective-permute-start | bytes 1388552 | tf_op jit(solution)/shard_map/ppermute | solution.py:781
  20.5 8.5 %collective-permute-start.3 = (f32[59,8,128]{2,1,0:T(8,128)S(1)}, f32[59,8,128]{2,1,0:T(8,128)S(1)}, u32[]{:S(2)}, u32[]{:S(2)}) collective-permute-start(f32[59,8,128]{2,1,0:T(8,128)S(1)} %pair_sums.2), channel_id=1, source_target_pairs={{0,2},{2,0},{1,3},{3,1},{4,6},{6,4},{5,7},{7,5},{8,10},{10,8},{9,1... | collective-permute-start | bytes 725000 | tf_op jit(solution)/shard_map/ppermute | solution.py:802
  22.1 1.2 %collective-permute-start.4 = (f32[6,8,128]{2,1,0:T(8,128)S(1)}, f32[6,8,128]{2,1,0:T(8,128)S(1)}, u32[]{:S(2)}, u32[]{:S(2)}) collective-permute-start(f32[6,8,128]{2,1,0:T(8,128)S(1)} %slope_and_stress.2.one_ref), channel_id=1, source_target_pairs={{0,1},{1,0},{2,3},{3,2},{4,5},{5,4},{6,7},{7,6},{8,9},{9,8},{10,11... | collective-permute-start | bytes 73736 | tf_op jit(solution)/shard_map/ppermute | solution.py:792
  23.3 5.7 %collective-permute-start.5 = (f32[6,8,128]{2,1,0:T(8,128)S(1)}, f32[6,8,128]{2,1,0:T(8,128)S(1)}, u32[]{:S(2)}, u32[]{:S(2)}) collective-permute-start(f32[6,8,128]{2,1,0:T(8,128)S(1)} %pair_slope_and_stress.2.refs_4_), channel_id=1, source_target_pairs={{0,2},{2,0},{1,3},{3,1},{4,6},{6,4},{5,7},{7,5},{8,10},{10,8},{9,1... | collective-permute-start | bytes 73736 | tf_op jit(solution)/shard_map/ppermute | solution.py:813
  29.0 3.1 %collective-permute-start.6 = (f32[59,8,128]{2,1,0:T(8,128)S(1)}, f32[59,8,128]{2,1,0:T(8,128)S(1)}, u32[]{:S(2)}, u32[]{:S(2)}) collective-permute-start(f32[59,8,128]{2,1,0:T(8,128)S(1)} %collective-permute-done.3.refs_3_), channel_id=1, source_target_pairs={{0,1},{1,0},{2,3},{3,2},{4,5},{5,4},{6,7},{7,6},{8,9},{9,8},{10,11... | collective-permute-start | bytes 725000 | tf_op jit(solution)/shard_map/ppermute | solution.py:827
  38.1 2.1 %collective-permute-start.7 = (f32[108,8,128]{2,1,0:T(8,128)S(1)}, f32[108,8,128]{2,1,0:T(8,128)S(1)}, u32[]{:S(2)}, u32[]{:S(2)}) collective-permute-start(f32[108,8,128]{2,1,0:T(8,128)S(1)} %get-tuple-element.71.sums_ref), channel_id=1, source_target_pairs={{0,1},{1,0},{2,3},{3,2},{4,5},{5,4},{6,7},{7,6},{8,9},{9,8},{10,11... | collective-permute-start | bytes 1327112 | tf_op jit(solution)/shard_map/ppermute | solution.py:781
  40.2 8.2 %collective-permute-start.8 = (f32[54,8,128]{2,1,0:T(8,128)S(1)}, f32[54,8,128]{2,1,0:T(8,128)S(1)}, u32[]{:S(2)}, u32[]{:S(2)}) collective-permute-start(f32[54,8,128]{2,1,0:T(8,128)S(1)} %pair_sums.3), channel_id=1, source_target_pairs={{0,2},{2,0},{1,3},{3,1},{4,6},{6,4},{5,7},{7,5},{8,10},{10,8},{9,1... | collective-permute-start | bytes 663560 | tf_op jit(solution)/shard_map/ppermute | solution.py:802
  41.8 1.2 %collective-permute-start.9 = (f32[6,8,128]{2,1,0:T(8,128)S(1)}, f32[6,8,128]{2,1,0:T(8,128)S(1)}, u32[]{:S(2)}, u32[]{:S(2)}) collective-permute-start(f32[6,8,128]{2,1,0:T(8,128)S(1)} %slope_and_stress.3.one_ref), channel_id=1, source_target_pairs={{0,1},{1,0},{2,3},{3,2},{4,5},{5,4},{6,7},{7,6},{8,9},{9,8},{10,11... | collective-permute-start | bytes 73736 | tf_op jit(solution)/shard_map/ppermute | solution.py:792
  43.0 5.4 %collective-permute-start.10 = (f32[6,8,128]{2,1,0:T(8,128)S(1)}, f32[6,8,128]{2,1,0:T(8,128)S(1)}, u32[]{:S(2)}, u32[]{:S(2)}) collective-permute-start(f32[6,8,128]{2,1,0:T(8,128)S(1)} %pair_slope_and_stress.3.refs_4_), channel_id=1, source_target_pairs={{0,2},{2,0},{1,3},{3,1},{4,6},{6,4},{5,7},{7,5},{8,10},{10,8},{9,1... | collective-permute-start | bytes 73736 | tf_op jit(solution)/shard_map/ppermute | solution.py:813
  48.4 1.8 %collective-permute-start.11 = (f32[54,8,128]{2,1,0:T(8,128)S(1)}, f32[54,8,128]{2,1,0:T(8,128)S(1)}, u32[]{:S(2)}, u32[]{:S(2)}) collective-permute-start(f32[54,8,128]{2,1,0:T(8,128)S(1)} %collective-permute-done.8.refs_3_), channel_id=1, source_target_pairs={{0,1},{1,0},{2,3},{3,2},{4,5},{5,4},{6,7},{7,6},{8,9},{9,8},{10,11... | collective-permute-start | bytes 663560 | tf_op jit(solution)/shard_map/ppermute | solution.py:827

commit v11 on v10

--- a/solution.py
+++ b/solution.py
@@ -192,6 +192,14 @@
     return drive * drive * open_water
 
 
+def in_pairs(count, body):
+    def both(i, carry):
+        body(2 * i, carry)
+        return body(2 * i + 1, carry)
+
+    lax.fori_loop(0, count // 2, both, 0)
+
+
 def tree(values):
     values = list(values)
     while len(values) > 1:
@@ -519,7 +527,7 @@
                 sums_ref[TILES * j + r] += excess
         return carry
 
-    lax.fori_loop(0, bands, band, 0)
+    in_pairs(bands, band)
 
 
 def weights_kernel(scal_ref, p_ref, drive_ref, out_ref):
@@ -638,23 +646,18 @@
         send(k, True).start()
         return carry
 
-    early = EARLY if near else bands
     if not last:
-        lax.fori_loop(0, bands, band, 0)
+        in_pairs(bands, band)
         return
-    if not near:
-        for k in range(EARLY, bands):
-            send(k, False).start()
-    lax.fori_loop(0, early, sent_band, 0)
-    lax.fori_loop(early, bands, band, 0)
-    for k in range(early):
+    if near:
+        in_pairs(bands, band)
+        return
+    for k in range(bands):
+        send(k, False).start()
+    in_pairs(bands, sent_band)
+    for k in range(bands):
         send(k, True).wait()
-    if not near:
-        for k in range(EARLY, bands):
-            send(k, False).wait()
-
-
-EARLY = 0
+        send(k, False).wait()
 
 
 def growth_kernel(last, near, *refs):

time: 53.4 us -> 52.1 us (0.976)
  Pallas kernels: 33 us -> 31.7 us
    pallas_call x4, Pallas kernels: 10.6 us -> 9.83 us  [grow(): pl.pallas_call(functools.partial(growth_kernel, last, is_near), in_specs=...]
    pallas_call x2, Pallas kernels: 7.85 us -> 7.3 us  [per_device(): pl.pallas_call(functools.partial(source_kernel, first), in_specs=[vmem] *...]
where the time goes in v11:
time: 52.1 us; the launch traced here: 51.9 us
  Pallas kernels  31.7 us (61%)
  starting transfers between devices  11.4 us (22%)
  waiting for transfers between devices  7.98 us (15%)
  between operations  0.78 us (1%)
    pallas_call x4, Pallas kernels, grow(): pl.pallas_call(functools.partial(growth_kernel, last, is_near), in_specs=...  9.83 us
    pallas_call x2, Pallas kernels, per_device(): pl.pallas_call(functools.partial(source_kernel, first), in_specs=[vmem] *...  7.3 us
    pallas_call x2, Pallas kernels, per_device(): pl.pallas_call(functools.partial(local_kernel, last), in_specs=[smem] + [...  5.18 us
    ppermute x2, waiting for transfers between devices, per_device(): weights_rest = lax.ppermute(weights_pair, 'freq', swap_chip)  4.92 us
    pallas_call x1, Pallas kernels, per_device(): pl.pallas_call(drift_kernel, in_specs=[smem] + [vmem] * 4, out_specs=[vme...  3.61 us
    ppermute x1, starting transfers between devices, per_device(): odd = lax.ppermute(odd, 'lon', swap_odd)  3.57 us
    ppermute x2, starting transfers between devices, per_device(): near = lax.ppermute(pair, 'freq', swap_chip)  3.17 us
    ppermute x1, starting transfers between devices, per_device(): even = lax.ppermute(even, 'lon', swap_even)  3 us
  transfers between devices with their start and end apart: 12, of which 6 were waited for; matrix products, arithmetic and copies ran while one was open for 0% of the time, Pallas kernels for 31%

profile of v11, /device:TPU:0, one launch (start us, length us, event | category | flops | bytes accessed | tf_op | source)
XLA Modules:
  0.0 51.9 jit_solution(5034117720292061695)
XLA Ops:
  0.6 0.0 copy-start
  0.6 0.0 copy-start.1
  0.7 2.8 %pack_columns.1 = (f32[8,36,24,128]{3,2,1,0:T(8,128)S(1)}, f32[28,8,128]{2,1,0:T(8,128)S(1)}, f32[28,8,128]{2,1,0:T(8,128)S(1)}, f32[24,128]{1,0:T(8,128)S(1)}, ...) custom-call(f32[8,36,24,128]{3,2,1,0:T(8,128)} %spec_ref.1, ...), custom_call_target="tpu_custom_call" | custom-call | flops 5308416 | bytes 7077888 | tf_op jit(solution)/shard_map/pack_columns/pallas_call | solution.py:742
  3.4 3.0 %collective-permute-start = (f32[28,8,128]{2,1,0:T(8,128)S(1)}, f32[28,8,128]{2,1,0:T(8,128)S(1)}, u32[]{:S(2)}, u32[]{:S(2)}) collective-permute-start(f32[28,8,128]{2,1,0:T(8,128)S(1)} %get-tuple-element.51), channel_id=1, source_target_pairs={{0,4},{4,0},{8,12},{12,8},{16,20},{20,16},{24,28},{28,24},{1,5},{5... | collective-permute-start | bytes 344072 | tf_op jit(solution)/shard_map/ppermute | solution.py:754
  6.4 3.6 %collective-permute-start.1 = (f32[28,8,128]{2,1,0:T(8,128)S(1)}, f32[28,8,128]{2,1,0:T(8,128)S(1)}, u32[]{:S(2)}, u32[]{:S(2)}) collective-permute-start(f32[28,8,128]{2,1,0:T(8,128)S(1)} %get-tuple-element.52), channel_id=1, source_target_pairs={{0,28},{4,8},{8,4},{12,16},{16,12},{20,24},{24,20},{28,0},{1,29},{... | collective-permute-start | bytes 344072 | tf_op jit(solution)/shard_map/ppermute | solution.py:755
  10.0 3.6 %drift.1 = (f32[8,36,3,8,128]{4,3,2,1,0:T(8,128)S(1)}, f32[36,3,8,128]{3,2,1,0:T(8,128)S(1)}) custom-call(f32[7168]{0:T(1024)S(1)} %copy-done, f32[8,36,24,128]{3,2,1,0:T(8,128)S(1)} %get-tuple-element.43.q_ref.refs_2_.refs_0_, f32[24,128]{1,0:T(8,128)S(1)} %get-tuple-element.44.east_ref, f32[24,128]{1,0:T(8,128)S(1)} %get-tuple-element.45.north_ref, ...), custom_call_target="tpu_custom_call" | custom-call | flops 10616832 | bytes 7077888 | tf_op jit(solution)/shard_map/drift/pallas_call | solution.py:756
  13.6 0.0 collective-permute-done.refs_7_
  13.6 0.3 collective-permute-done.1.refs_8_
  13.9 4.4 %sources.2 = (f32[8,36,3,8,128]{4,3,2,1,0:T(8,128)S(1)}, f32[8,36,3,8,128]{4,3,2,1,0:T(8,128)S(1)}, f32[113,8,128]{2,1,0:T(8,128)S(1)}, f32[36,8,128]{2,1,0:T(8,...) custom-call(f32[4,6,8,128]{3,2,1,0:T(8,128)S(1)} %copy-done.1, ...), custom_call_target="tpu_custom_call" | custom-call | flops 26542080 | bytes 10616832 | tf_op jit(solution)/shard_map/sources/pallas_call | solution.py:772
  18.3 0.1 collective-permute-start.2
  18.4 1.4 %slope_and_stress.2.one_ref = f32[6,8,128]{2,1,0:T(8,128)S(1)} custom-call(f32[7168]{0:T(1024)S(1)} %copy-done, f32[8,36,3,8,128]{4,3,2,1,0:T(8,128)S(1)} %get-tuple-element.54.p_ref, f32[36,3,8,128]{3,2,1,0:T(8,128)S(1)} %get-tuple-element.55.drive_ref.refs_6_), custom_call_target="tpu_custom_call" | custom-call | flops 2654208 | bytes 3538944 | tf_op jit(solution)/shard_map/slope_and_stress/pallas_call | solution.py:785
  19.8 0.4 collective-permute-done.2.other_ref.refs_2_
  20.2 1.6 %collective-permute-start.3 = (f32[59,8,128]{2,1,0:T(8,128)S(1)}, f32[59,8,128]{2,1,0:T(8,128)S(1)}, u32[]{:S(2)}, u32[]{:S(2)}) collective-permute-start(f32[59,8,128]{2,1,0:T(8,128)S(1)} %pair_sums.2), channel_id=1, source_target_pairs={{0,2},{2,0},{1,3},{3,1},{4,6},{6,4},{5,7},{7,5},{8,10},{10,8},{9,1... | collective-permute-start | bytes 725000 | tf_op jit(solution)/shard_map/ppermute | solution.py:805
  21.8 1.2 %collective-permute-done.4.other_ref = f32[6,8,128]{2,1,0:T(8,128)S(1)} collective-permute-done((f32[6,8,128]{2,1,0:T(8,128)S(1)}, f32[6,8,128]{2,1,0:T(8,128)S(1)}, u32[]{:S(2)}, u32[]{:S(2)}) %collective-permute-start.4) | collective-permute-done | bytes 24608 | tf_op jit(solution)/shard_map/ppermute | solution.py:795
  23.0 0.5 collective-permute-start.5
  23.5 3.1 %local_rate.2 = (f32[8,36,3,8,128]{4,3,2,1,0:T(8,128)S(1)}, f32[8,36,3,8,128]{4,3,2,1,0:T(8,128)S(1)}) custom-call(f32[7168]{0:T(1024)S(1)} %copy-done, f32[8,36,3,8,128]{4,3,2,1,0:T(8,128)S(1)} %get-tuple-element.54.p_ref, f32[8,36,3,8,128]{4,3,2,1,0:T(8,128)S(1)} %get-tuple-element.60.excess_ref, ...), custom_call_target="tpu_custom_call" | custom-call | flops 7077888 | bytes 10616832 | tf_op jit(solution)/shard_map/local_rate/pallas_call | solution.py:819
  26.6 2.1 %collective-permute-done.5.refs_5_ = f32[6,8,128]{2,1,0:T(8,128)S(1)} collective-permute-done((f32[6,8,128]{2,1,0:T(8,128)S(1)}, f32[6,8,128]{2,1,0:T(8,128)S(1)}, u32[]{:S(2)}, u32[]{:S(2)}) %collective-permute-start.5) | collective-permute-done | bytes 24608 | tf_op jit(solution)/shard_map/ppermute | solution.py:816
  28.7 0.0 collective-permute-done.3.refs_3_
  28.7 2.7 %grow_near.2 = (f32[8,36,3,8,128]{4,3,2,1,0:T(8,128)S(1)}, f32[36,8,128]{2,1,0:T(8,128)S(1)}) custom-call(f32[7168]{0:T(1024)S(1)} %copy-done, f32[8,36,3,8,128]{4,3,2,1,0:T(8,128)S(1)} %get-tuple-element.62.refs_1_, f32[113,8,128]{2,1,0:T(8,128)S(1)} %collective-permute-done.2.other_ref.refs_2_, f32[59,8,128]{2,1,0:T(8,128)S(1)} %collective-permute-done.3.refs_3_, ...), custom_call_target="tpu_custom_call" | custom-call | flops 10616832 | bytes 3538944 | tf_op jit(solution)/shard_map/grow_near/pallas_call | solution.py:839
  31.5 2.4 %grow_far.2.refs_1_ = f32[8,36,3,8,128]{4,3,2,1,0:T(8,128)S(1)} custom-call(f32[7168]{0:T(1024)S(1)} %copy-done, f32[8,36,3,8,128]{4,3,2,1,0:T(8,128)S(1)} %get-tuple-element.62.refs_1_, f32[113,8,128]{2,1,0:T(8,128)S(1)} %collective-permute-done.2.other_ref.refs_2_, ...), custom_call_target="tpu_custom_call", output_to_operand_aliasing={{}: (8, {})} | custom-call | flops 10616832 | bytes 3538944 | tf_op jit(solution)/shard_map/grow_far/pallas_call | solution.py:839
  33.9 2.9 %sources.3 = (f32[8,36,3,8,128]{4,3,2,1,0:T(8,128)S(1)}, f32[8,36,3,8,128]{4,3,2,1,0:T(8,128)S(1)}, f32[108,8,128]{2,1,0:T(8,128)S(1)}) custom-call(f32[4,6,8,128]{3,2,1,0:T(8,128)S(1)} %copy-done.1, f32[8,36,3,8,128]{4,3,2,1,0:T(8,128)S(1)} %grow_far.2.refs_1_, f32[8,36,3,8,128]{4,3,2,1,0:T(8,128)S(1)} %get-tuple-element.69.refs_2_, ...), custom_call_target="tpu_custom_call" | custom-call | flops 26542080 | bytes 10616832 | tf_op jit(solution)/shard_map/sources/pallas_call | solution.py:772
  36.8 0.6 %collective-permute-start.7 = (f32[108,8,128]{2,1,0:T(8,128)S(1)}, f32[108,8,128]{2,1,0:T(8,128)S(1)}, u32[]{:S(2)}, u32[]{:S(2)}) collective-permute-start(f32[108,8,128]{2,1,0:T(8,128)S(1)} %get-tuple-element.71.sums_ref), channel_id=1, source_target_pairs={{0,1},{1,0},{2,3},{3,2},{4,5},{5,4},{6,7},{7,6},{8,9},{9,8},{10,11... | collective-permute-start | bytes 1327112 | tf_op jit(solution)/shard_map/ppermute | solution.py:784
  37.4 1.5 %slope_and_stress.3.one_ref = f32[6,8,128]{2,1,0:T(8,128)S(1)} custom-call(f32[7168]{0:T(1024)S(1)} %copy-done, f32[8,36,3,8,128]{4,3,2,1,0:T(8,128)S(1)} %get-tuple-element.72.p_ref, f32[36,3,8,128]{3,2,1,0:T(8,128)S(1)} %get-tuple-element.55.drive_ref.refs_6_), custom_call_target="tpu_custom_call" | custom-call | flops 2654208 | bytes 3538944 | tf_op jit(solution)/shard_map/slope_and_stress/pallas_call | solution.py:785
  38.9 0.0 collective-permute-done.7.other_ref.refs_2_
  39.0 1.6 %collective-permute-start.8 = (f32[54,8,128]{2,1,0:T(8,128)S(1)}, f32[54,8,128]{2,1,0:T(8,128)S(1)}, u32[]{:S(2)}, u32[]{:S(2)}) collective-permute-start(f32[54,8,128]{2,1,0:T(8,128)S(1)} %pair_sums.3), channel_id=1, source_target_pairs={{0,2},{2,0},{1,3},{3,1},{4,6},{6,4},{5,7},{7,5},{8,10},{10,8},{9,1... | collective-permute-start | bytes 663560 | tf_op jit(solution)/shard_map/ppermute | solution.py:805
  40.6 0.0 collective-permute-start.9
  40.6 1.2 %collective-permute-done.9.other_ref = f32[6,8,128]{2,1,0:T(8,128)S(1)} collective-permute-done((f32[6,8,128]{2,1,0:T(8,128)S(1)}, f32[6,8,128]{2,1,0:T(8,128)S(1)}, u32[]{:S(2)}, u32[]{:S(2)}) %collective-permute-start.9) | collective-permute-done | bytes 24608 | tf_op jit(solution)/shard_map/ppermute | solution.py:795
  41.8 0.5 collective-permute-start.10
  42.3 2.1 %local_rate.3.refs_1_ = f32[8,36,3,8,128]{4,3,2,1,0:T(8,128)S(1)} custom-call(f32[7168]{0:T(1024)S(1)} %copy-done, f32[8,36,3,8,128]{4,3,2,1,0:T(8,128)S(1)} %get-tuple-element.72.p_ref, f32[8,36,3,8,128]{4,3,2,1,0:T(8,128)S(1)} %get-tuple-element.77.excess_ref), custom_call_target="tpu_custom_call" | custom-call | flops 7077888 | bytes 10616832 | tf_op jit(solution)/shard_map/local_rate/pallas_call | solution.py:819
  44.4 2.8 %collective-permute-done.10.refs_5_ = f32[6,8,128]{2,1,0:T(8,128)S(1)} collective-permute-done((f32[6,8,128]{2,1,0:T(8,128)S(1)}, f32[6,8,128]{2,1,0:T(8,128)S(1)}, u32[]{:S(2)}, u32[]{:S(2)}) %collective-permute-start.10) | collective-permute-done | bytes 24608 | tf_op jit(solution)/shard_map/ppermute | solution.py:816
  47.2 1.8 %grow_near.3 = (f32[8,18,24,128]{3,2,1,0:T(8,128)S(1)}, f32[24,128]{1,0:T(8,128)}, f32[8,36,24,128]{3,2,1,0:T(8,128)}) custom-call(f32[7168]{0:T(1024)S(1)} %copy-done, f32[8,36,3,8,128]{4,3,2,1,0:T(8,128)S(1)} %local_rate.3.refs_1_, f32[108,8,128]{2,1,0:T(8,128)S(1)} %collective-permute-done.7.other_ref.refs_2_, ...), custom_call_target="tpu_custom_call" | custom-call | flops 5308416 | bytes 3538944 | tf_op jit(solution)/shard_map/grow_near/pallas_call | solution.py:839
  49.0 2.9 %grow_far.3 = f32[8,36,24,128]{3,2,1,0:T(8,128)} custom-call(f32[7168]{0:T(1024)S(1)} %copy-done, f32[8,36,3,8,128]{4,3,2,1,0:T(8,128)S(1)} %local_rate.3.refs_1_, f32[108,8,128]{2,1,0:T(8,128)S(1)} %collective-permute-done.7.other_ref.refs_2_, f32[54,8,128]{2,1,0:T(8,128)S(1)} %collective-permute-done.11.refs_3_, ...), custom_call_target="tpu_custom_call", output_to_operand_aliasing={{}: (9, {})} | custom-call | flops 5308416 | bytes 3538944 | tf_op jit(solution)/shard_map/grow_far/pallas_call | solution.py:839
  (12 shorter events, 0.1 us)
Async XLA Ops:
  0.6 9.4 %copy-start = (f32[7168]{0:T(1024)S(1)}, f32[7168]{0:T(1024)}, u32[]{:S(2)}) copy-start(f32[7168]{0:T(1024)} %constant.4.clone.scal_ref.refs_0_) | copy-start | bytes 86020
  0.6 13.3 %copy-start.1 = (f32[4,6,8,128]{3,2,1,0:T(8,128)S(1)}, f32[4,6,8,128]{3,2,1,0:T(8,128)}, u32[]{:S(2)}) copy-start(f32[4,6,8,128]{3,2,1,0:T(8,128)} %constant.5.clone.refs_0_.refs_8_) | copy-start | bytes 294916
  3.4 10.2 %collective-permute-start = (f32[28,8,128]{2,1,0:T(8,128)S(1)}, f32[28,8,128]{2,1,0:T(8,128)S(1)}, u32[]{:S(2)}, u32[]{:S(2)}) collective-permute-start(f32[28,8,128]{2,1,0:T(8,128)S(1)} %get-tuple-element.51), channel_id=1, source_target_pairs={{0,4},{4,0},{8,12},{12,8},{16,20},{20,16},{24,28},{28,24},{1,5},{5... | collective-permute-start | bytes 344072 | tf_op jit(solution)/shard_map/ppermute | solution.py:754
  6.4 7.5 %collective-permute-start.1 = (f32[28,8,128]{2,1,0:T(8,128)S(1)}, f32[28,8,128]{2,1,0:T(8,128)S(1)}, u32[]{:S(2)}, u32[]{:S(2)}) collective-permute-start(f32[28,8,128]{2,1,0:T(8,128)S(1)} %get-tuple-element.52), channel_id=1, source_target_pairs={{0,28},{4,8},{8,4},{12,16},{16,12},{20,24},{24,20},{28,0},{1,29},{... | collective-permute-start | bytes 344072 | tf_op jit(solution)/shard_map/ppermute | solution.py:755
  18.3 1.9 %collective-permute-start.2 = (f32[113,8,128]{2,1,0:T(8,128)S(1)}, f32[113,8,128]{2,1,0:T(8,128)S(1)}, u32[]{:S(2)}, u32[]{:S(2)}) collective-permute-start(f32[113,8,128]{2,1,0:T(8,128)S(1)} %get-tuple-element.53.sums_ref.refs_9_), channel_id=1, source_target_pairs={{0,1},{1,0},{2,3},{3,2},{4,5},{5,4},{6,7},{7,6},{8,9},{9,8},{10,11... | collective-permute-start | bytes 1388552 | tf_op jit(solution)/shard_map/ppermute | solution.py:784
  20.2 8.5 %collective-permute-start.3 = (f32[59,8,128]{2,1,0:T(8,128)S(1)}, f32[59,8,128]{2,1,0:T(8,128)S(1)}, u32[]{:S(2)}, u32[]{:S(2)}) collective-permute-start(f32[59,8,128]{2,1,0:T(8,128)S(1)} %pair_sums.2), channel_id=1, source_target_pairs={{0,2},{2,0},{1,3},{3,1},{4,6},{6,4},{5,7},{7,5},{8,10},{10,8},{9,1... | collective-permute-start | bytes 725000 | tf_op jit(solution)/shard_map/ppermute | solution.py:805
  21.8 1.2 %collective-permute-start.4 = (f32[6,8,128]{2,1,0:T(8,128)S(1)}, f32[6,8,128]{2,1,0:T(8,128)S(1)}, u32[]{:S(2)}, u32[]{:S(2)}) collective-permute-start(f32[6,8,128]{2,1,0:T(8,128)S(1)} %slope_and_stress.2.one_ref), channel_id=1, source_target_pairs={{0,1},{1,0},{2,3},{3,2},{4,5},{5,4},{6,7},{7,6},{8,9},{9,8},{10,11... | collective-permute-start | bytes 73736 | tf_op jit(solution)/shard_map/ppermute | solution.py:795
  23.0 5.7 %collective-permute-start.5 = (f32[6,8,128]{2,1,0:T(8,128)S(1)}, f32[6,8,128]{2,1,0:T(8,128)S(1)}, u32[]{:S(2)}, u32[]{:S(2)}) collective-permute-start(f32[6,8,128]{2,1,0:T(8,128)S(1)} %pair_slope_and_stress.2.refs_4_), channel_id=1, source_target_pairs={{0,2},{2,0},{1,3},{3,1},{4,6},{6,4},{5,7},{7,5},{8,10},{10,8},{9,1... | collective-permute-start | bytes 73736 | tf_op jit(solution)/shard_map/ppermute | solution.py:816
  28.7 2.7 %collective-permute-start.6 = (f32[59,8,128]{2,1,0:T(8,128)S(1)}, f32[59,8,128]{2,1,0:T(8,128)S(1)}, u32[]{:S(2)}, u32[]{:S(2)}) collective-permute-start(f32[59,8,128]{2,1,0:T(8,128)S(1)} %collective-permute-done.3.refs_3_), channel_id=1, source_target_pairs={{0,1},{1,0},{2,3},{3,2},{4,5},{5,4},{6,7},{7,6},{8,9},{9,8},{10,11... | collective-permute-start | bytes 725000 | tf_op jit(solution)/shard_map/ppermute | solution.py:830
  36.8 2.1 %collective-permute-start.7 = (f32[108,8,128]{2,1,0:T(8,128)S(1)}, f32[108,8,128]{2,1,0:T(8,128)S(1)}, u32[]{:S(2)}, u32[]{:S(2)}) collective-permute-start(f32[108,8,128]{2,1,0:T(8,128)S(1)} %get-tuple-element.71.sums_ref), channel_id=1, source_target_pairs={{0,1},{1,0},{2,3},{3,2},{4,5},{5,4},{6,7},{7,6},{8,9},{9,8},{10,11... | collective-permute-start | bytes 1327112 | tf_op jit(solution)/shard_map/ppermute | solution.py:784
  39.0 8.2 %collective-permute-start.8 = (f32[54,8,128]{2,1,0:T(8,128)S(1)}, f32[54,8,128]{2,1,0:T(8,128)S(1)}, u32[]{:S(2)}, u32[]{:S(2)}) collective-permute-start(f32[54,8,128]{2,1,0:T(8,128)S(1)} %pair_sums.3), channel_id=1, source_target_pairs={{0,2},{2,0},{1,3},{3,1},{4,6},{6,4},{5,7},{7,5},{8,10},{10,8},{9,1... | collective-permute-start | bytes 663560 | tf_op jit(solution)/shard_map/ppermute | solution.py:805
  40.6 1.2 %collective-permute-start.9 = (f32[6,8,128]{2,1,0:T(8,128)S(1)}, f32[6,8,128]{2,1,0:T(8,128)S(1)}, u32[]{:S(2)}, u32[]{:S(2)}) collective-permute-start(f32[6,8,128]{2,1,0:T(8,128)S(1)} %slope_and_stress.3.one_ref), channel_id=1, source_target_pairs={{0,1},{1,0},{2,3},{3,2},{4,5},{5,4},{6,7},{7,6},{8,9},{9,8},{10,11... | collective-permute-start | bytes 73736 | tf_op jit(solution)/shard_map/ppermute | solution.py:795
  41.8 5.4 %collective-permute-start.10 = (f32[6,8,128]{2,1,0:T(8,128)S(1)}, f32[6,8,128]{2,1,0:T(8,128)S(1)}, u32[]{:S(2)}, u32[]{:S(2)}) collective-permute-start(f32[6,8,128]{2,1,0:T(8,128)S(1)} %pair_slope_and_stress.3.refs_4_), channel_id=1, source_target_pairs={{0,2},{2,0},{1,3},{3,1},{4,6},{6,4},{5,7},{7,5},{8,10},{10,8},{9,1... | collective-permute-start | bytes 73736 | tf_op jit(solution)/shard_map/ppermute | solution.py:816
  47.2 1.8 %collective-permute-start.11 = (f32[54,8,128]{2,1,0:T(8,128)S(1)}, f32[54,8,128]{2,1,0:T(8,128)S(1)}, u32[]{:S(2)}, u32[]{:S(2)}) collective-permute-start(f32[54,8,128]{2,1,0:T(8,128)S(1)} %collective-permute-done.8.refs_3_), channel_id=1, source_target_pairs={{0,1},{1,0},{2,3},{3,2},{4,5},{5,4},{6,7},{7,6},{8,9},{9,8},{10,11... | collective-permute-start | bytes 663560 | tf_op jit(solution)/shard_map/ppermute | solution.py:830
